TPU v7x, 32 devices: a whole 2x2x4 slice. The times are simulated.
32 devices in a mesh: dp: 8 (over y, x, core), expert: 4 (over z).
Axes of the slice: x: 2, y: 2, z: 4, core: 2. Of those that a mesh axis runs over, the one named last changes fastest.
Arguments:
- frames: bfloat16 [16384, 512], P(('dp', 'expert')), may hold values from -8 to 8
- lengths: int32 [32, 4], replicated, may hold values from 1 to 380, as said below
- choice_first: int32 [16384, 1], P(('dp', 'expert')), may hold values from 0 to 3; in each aligned block of 512 rows (0 to 511, 512 to 1023, ...) at most 256 rows name the same one
- choice_second: int32 [16384, 1], P(('dp', 'expert')), may hold values from 0 to 3; in each aligned block of 512 rows (0 to 511, 512 to 1023, ...) at most 256 rows name the same one
- embed_weight: bfloat16 [512, 512], replicated, may hold values from -0.25 to 0.25
- routers: bfloat16 [2, 512, 4], P(None, ('dp', 'expert')), may hold values from -0.25 to 0.25
- norm_gains: bfloat16 [6, 512], P(None, ('dp', 'expert')), may hold values from 0.25 to 1.75
- attn_in: bfloat16 [512, 1536], P(('dp', 'expert')), may hold values from -0.25 to 0.25
- attn_out: bfloat16 [512, 512], P(('dp', 'expert')), may hold values from -1 to 1
- conv_in: bfloat16 [512, 1024], P(('dp', 'expert')), may hold values from -0.25 to 0.25
- conv_kernel: bfloat16 [15, 512], P(None, ('dp', 'expert')), may hold values from -1.5 to 1.5
- bn_shift: bfloat16 [512], P(('dp', 'expert')), may hold values from -3 to 3
- conv_out: bfloat16 [512, 512], P(('dp', 'expert')), may hold values from -0.375 to 0.375
- expert_in: bfloat16 [2, 4, 512, 2048], P(None, 'expert', 'dp'), may hold values from -0.25 to 0.25
- expert_out: bfloat16 [2, 4, 2048, 512], P(None, 'expert', 'dp'), may hold values from -2 to 2
- cotangent: bfloat16 [16384, 512], P(('dp', 'expert')), may hold values from -6 to 6
Outputs:
- block_out: bfloat16 [16384, 512], P(('dp', 'expert'))
- frames_grad: float32 [16384, 512], P(('dp', 'expert'))
- embed_grad: float32 [512, 512], replicated
- routers_grad: float32 [2, 512, 4], P(None, ('dp', 'expert'))
- norm_gains_grad: float32 [6, 512], P(None, ('dp', 'expert'))
- attn_in_grad: float32 [512, 1536], P(('dp', 'expert'))
- attn_out_grad: float32 [512, 512], P(('dp', 'expert'))
- conv_in_grad: float32 [512, 1024], P(('dp', 'expert'))
- conv_kernel_grad: float32 [15, 512], P(None, ('dp', 'expert'))
- bn_shift_grad: float32 [512], P(('dp', 'expert'))
- conv_out_grad: float32 [512, 512], P(('dp', 'expert'))
- expert_in_grad: float32 [2, 4, 512, 2048], P(None, 'expert', 'dp')
- expert_out_grad: float32 [2, 4, 2048, 512], P(None, 'expert', 'dp')
Inputs may be any that keep to these rules, and one draw needn't show every extreme that they name: `lengths`: A row lists, in order, the frame counts of the 4 segments of one device's 512 frames and sums to 512; the last segment is padding of at most 32 frames, the others hold 50 frames or more, and each row's largest entry is 380. `choice_first`: among the frames of one device no expert is chosen more than 256 times, and in every draw some expert is chosen exactly 256 times by the frames of some device. `choice_second`: among the frames of one device no expert is chosen more than 256 times, and in every draw some expert is chosen exactly 256 times by the frames of some device.
All inputs are finite; a program needn't handle non-finite values.
Results may differ from a plain program's by a relative error of at most 0.018.
Values may be sent and summed in bfloat16 or wider, within the bound.
No kernel may reach another device: no remote copies, remote signals or barrier semaphores. Data moves between devices by JAX's collectives and lax.ppermute only.
A program may use at most 192 MiB of HBM per device.

v0:
```python
import jax
import jax.numpy as jnp
from jax import lax
from jax.sharding import PartitionSpec as P

H = 8
DH = 64


EPSILON = 1e-05
MASK_FILL = 1000000000.0
HIGHEST = lax.Precision.HIGHEST


def silu_slope(preactivation):
    logistic = jax.nn.sigmoid(preactivation)
    return logistic * (1.0 + preactivation * (1.0 - logistic))


def segments(lengths_row, row_count):
    seg_ends = jnp.cumsum(lengths_row, dtype=jnp.int32)
    seg_starts = seg_ends - lengths_row
    positions = jnp.arange(row_count, dtype=jnp.int32)
    segment = jnp.sum((positions[:, None] >= seg_ends[None, :]).astype(jnp.int32), 1)
    member = segment[:, None] == jnp.arange(lengths_row.shape[0], dtype=jnp.int32)[None, :]
    offsets = positions - jnp.sum(jnp.where(member, seg_starts[None, :], 0), 1)
    validity = (segment < lengths_row.shape[0] - 1).astype(jnp.float32)
    return (segment, offsets, validity)


def rotation(offsets, head_dim):
    half_dim = head_dim // 2
    frequency = 10000.0 ** (-jnp.arange(half_dim, dtype=jnp.float32) / half_dim)
    angles = offsets.astype(jnp.float32)[:, None] * frequency[None, :]
    return (jnp.cos(angles)[:, None, :], jnp.sin(angles)[:, None, :])


def rotate(values, cosine, sine_table):
    half_dim = values.shape[-1] // 2
    first_half = values[..., :half_dim]
    second_half = values[..., half_dim:]
    return jnp.concatenate(
        [
            first_half * cosine - second_half * sine_table,
            first_half * sine_table + second_half * cosine,
        ],
        -1,
    )


def norm_forward(rows_in, gain_row):
    centred = rows_in - jnp.mean(rows_in, -1, keepdims=True)
    inverse = lax.rsqrt(jnp.mean(centred * centred, -1, keepdims=True) + EPSILON)
    normed = centred * inverse
    return (normed * gain_row, normed, inverse)


def norm_backward(grad_out, gain_row, normed, inverse):
    scaled = grad_out * gain_row
    gain_grad = jnp.sum(grad_out * normed, 0)
    rows_grad = inverse * (
        scaled
        - jnp.mean(scaled, -1, keepdims=True)
        - normed * jnp.mean(scaled * normed, -1, keepdims=True)
    )
    return (rows_grad, gain_grad)


def depthwise(values, kernel, segment):
    row_count = values.shape[0]
    reach_half = kernel.shape[0] // 2
    padded = jnp.pad(values, ((reach_half, reach_half), (0, 0)))
    seg_padded = jnp.pad(segment, (reach_half, reach_half), constant_values=-1)
    result = jnp.zeros(values.shape, jnp.float32)
    for tap_index in range(kernel.shape[0]):
        same_segment = (seg_padded[tap_index : tap_index + row_count] == segment).astype(
            jnp.float32
        )[:, None]
        result = (
            result + kernel[tap_index] * padded[tap_index : tap_index + row_count] * same_segment
        )
    return result


def depthwise_backward(grad_out, values, kernel, segment):
    row_count = values.shape[0]
    reach_half = kernel.shape[0] // 2
    padded = jnp.pad(values, ((reach_half, reach_half), (0, 0)))
    seg_padded = jnp.pad(segment, (reach_half, reach_half), constant_values=-1)
    values_grad = jnp.zeros(values.shape, jnp.float32)
    kernel_rows = []
    for tap_index in range(kernel.shape[0]):
        same_segment = (seg_padded[tap_index : tap_index + row_count] == segment).astype(
            jnp.float32
        )[:, None]
        masked = grad_out * same_segment
        kernel_rows.append(jnp.sum(masked * padded[tap_index : tap_index + row_count], 0))
        start_row = 2 * reach_half - tap_index
        shifted = jnp.pad(masked, ((reach_half, reach_half), (0, 0)))[
            start_row : start_row + row_count
        ]
        values_grad = values_grad + kernel[tap_index] * shifted
    return (values_grad, jnp.stack(kernel_rows))


def attend_forward(query_rows, key_rows, value_rows, segment, block_rows):
    row_count, head_count, head_dim = query_rows.shape
    block_count = row_count // block_rows
    score_scale = head_dim ** (-0.5)

    def one_block(inputs):
        query_block, segment_block = inputs
        scores = (
            jnp.einsum("bhd,thd->hbt", query_block, key_rows, preferred_element_type=jnp.float32)
            * score_scale
        )
        allowed = (segment_block[:, None] == segment[None, :])[None]
        scores = jnp.where(allowed, scores, -MASK_FILL)
        row_max = jnp.max(scores, -1, keepdims=True)
        weights = jnp.exp(scores - row_max)
        row_total = jnp.sum(weights, -1, keepdims=True)
        probabilities = (weights / row_total).astype(jnp.bfloat16)
        attended = jnp.einsum(
            "hbt,thd->bhd", probabilities, value_rows, preferred_element_type=jnp.float32
        )
        return (attended, (row_max + jnp.log(row_total))[..., 0])

    attended, logsum = lax.map(
        one_block,
        (
            query_rows.reshape(block_count, block_rows, head_count, head_dim),
            segment.reshape(block_count, block_rows),
        ),
    )
    return (attended.reshape(row_count, head_count, head_dim), logsum)


def attend_backward(query_rows, key_rows, value_rows, segment, logsum, attended_grad, block_rows):
    row_count, head_count, head_dim = query_rows.shape
    block_count = row_count // block_rows
    score_scale = head_dim ** (-0.5)

    def one_block(running, inputs):
        key_grad, value_grad = running
        query_block, segment_block, logsum_block, grad_block = inputs
        scores = (
            jnp.einsum("bhd,thd->hbt", query_block, key_rows, preferred_element_type=jnp.float32)
            * score_scale
        )
        allowed = (segment_block[:, None] == segment[None, :])[None]
        probabilities = jnp.where(allowed, jnp.exp(scores - logsum_block[:, :, None]), 0.0)
        prob_grad = jnp.einsum(
            "bhd,thd->hbt", grad_block, value_rows, preferred_element_type=jnp.float32
        )
        row_inner = jnp.sum(probabilities * prob_grad, -1, keepdims=True)
        score_grad = (probabilities * (prob_grad - row_inner)).astype(jnp.bfloat16)
        query_grad = (
            jnp.einsum("hbt,thd->bhd", score_grad, key_rows, preferred_element_type=jnp.float32)
            * score_scale
        )
        key_grad = (
            key_grad
            + jnp.einsum(
                "hbt,bhd->thd", score_grad, query_block, preferred_element_type=jnp.float32
            )
            * score_scale
        )
        value_grad = value_grad + jnp.einsum(
            "hbt,bhd->thd",
            probabilities.astype(jnp.bfloat16),
            grad_block,
            preferred_element_type=jnp.float32,
        )
        return ((key_grad, value_grad), query_grad)

    zero_grad = jnp.zeros(query_rows.shape, jnp.float32)
    (key_grad, value_grad), query_grad = lax.scan(
        one_block,
        (zero_grad, zero_grad),
        (
            query_rows.reshape(block_count, block_rows, head_count, head_dim),
            segment.reshape(block_count, block_rows),
            logsum,
            attended_grad.reshape(block_count, block_rows, head_count, head_dim),
        ),
    )
    return (query_grad.reshape(row_count, head_count, head_dim), key_grad, value_grad)


def expert_slots(choice_col, expert_total, capacity, local_experts, peer_count):
    chosen = choice_col[:, 0]
    onehot = (chosen[:, None] == jnp.arange(expert_total, dtype=jnp.int32)[None, :]).astype(
        jnp.int32
    )
    rank_within = jnp.sum((jnp.cumsum(onehot, 0, dtype=jnp.int32) - onehot) * onehot, 1)
    slot_index = (
        chosen % local_experts * (peer_count * capacity)
        + chosen // local_experts * capacity
        + rank_within
    )
    return (slot_index, onehot.astype(jnp.float32))


def scatter_rows(rows_low, slot_index, local_experts, peer_count, capacity):
    buffer = jnp.zeros((local_experts * peer_count * capacity, rows_low.shape[1]), jnp.bfloat16)
    buffer = buffer.at[slot_index].set(rows_low)
    return buffer.reshape(local_experts, peer_count, capacity, rows_low.shape[1])


def to_experts(sent_rows):
    return lax.all_to_all(sent_rows, "expert", split_axis=1, concat_axis=1, tiled=True)


def from_experts(back_rows):
    return lax.all_to_all(back_rows, "expert", split_axis=1, concat_axis=1, tiled=True)


def moe_forward(rows_in, gain_row, embedded, router, choice_col, input_weight, output_weight):
    expert_total = router.shape[1]
    local_experts = input_weight.shape[0]
    peer_count = lax.axis_size("expert")
    capacity = 2 * rows_in.shape[0] // expert_total
    model_width = rows_in.shape[1]
    normed_out, normed, inverse = norm_forward(rows_in, gain_row)
    rows_low = normed_out.astype(jnp.bfloat16)
    slot_index, onehot = expert_slots(choice_col, expert_total, capacity, local_experts, peer_count)
    arrived_rows = to_experts(
        scatter_rows(rows_low, slot_index, local_experts, peer_count, capacity)
    )
    arrived_rows = arrived_rows.reshape(local_experts, peer_count * capacity, model_width)
    preactivation = jnp.einsum(
        "zve,zeg->zvg", arrived_rows, input_weight, preferred_element_type=jnp.float32
    )
    hidden_reduced = jax.nn.silu(preactivation).astype(jnp.bfloat16)
    produced = jnp.einsum(
        "gzm,gmb->gzb", hidden_reduced, output_weight, preferred_element_type=jnp.float32
    ).astype(jnp.bfloat16)
    returned = from_experts(produced.reshape(local_experts, peer_count, capacity, model_width))
    expert_rows = returned.reshape(-1, model_width)[slot_index].astype(jnp.float32)
    router_probs = jax.nn.softmax(jnp.dot(embedded, router, precision=HIGHEST), -1)
    gate_value = jnp.sum(router_probs * onehot, 1)
    output = rows_in + 0.5 * gate_value[:, None] * expert_rows
    saved = (
        normed,
        inverse,
        slot_index,
        onehot,
        arrived_rows,
        preactivation,
        hidden_reduced,
        expert_rows,
        router_probs,
        gate_value,
    )
    return (output, saved)


def moe_backward(grad_out, gain_row, input_weight, output_weight, saved):
    (
        normed,
        inverse,
        slot_index,
        onehot,
        arrived_rows,
        preactivation,
        hidden_reduced,
        expert_rows,
        router_probs,
        gate_value,
    ) = saved
    local_experts, row_total, model_width = arrived_rows.shape
    peer_count = lax.axis_size("expert")
    capacity = row_total // peer_count
    sent_grad = (0.5 * gate_value[:, None] * grad_out).astype(jnp.bfloat16)
    gate_grad = 0.5 * jnp.sum(expert_rows * grad_out, 1)
    logit_grad = (gate_grad * gate_value)[:, None] * (onehot - router_probs)
    row_gradients = to_experts(
        scatter_rows(sent_grad, slot_index, local_experts, peer_count, capacity)
    )
    row_gradients = row_gradients.reshape(local_experts, row_total, model_width)
    out_weight_grad = jnp.einsum(
        "ymv,yml->yvl", hidden_reduced, row_gradients, preferred_element_type=jnp.float32
    )
    hidden_grad = jnp.einsum(
        "ysi,yzi->ysz", row_gradients, output_weight, preferred_element_type=jnp.float32
    )
    preactivation_grad = (hidden_grad * silu_slope(preactivation)).astype(jnp.bfloat16)
    in_weight_grad = jnp.einsum(
        "keo,keu->kou", arrived_rows, preactivation_grad, preferred_element_type=jnp.float32
    )
    input_grad = jnp.einsum(
        "wot,wqt->woq", preactivation_grad, input_weight, preferred_element_type=jnp.float32
    ).astype(jnp.bfloat16)
    returned = from_experts(input_grad.reshape(local_experts, peer_count, capacity, model_width))
    normed_grad = returned.reshape(-1, model_width)[slot_index].astype(jnp.float32)
    rows_grad, gain_grad = norm_backward(normed_grad, gain_row, normed, inverse)
    return (grad_out + rows_grad, gain_grad, logit_grad, in_weight_grad, out_weight_grad)


def shards(
    frames,
    lengths,
    choice_first,
    choice_second,
    embed_weight,
    routers,
    norm_gains,
    attn_in,
    attn_out,
    conv_in,
    conv_kernel,
    bn_shift,
    conv_out,
    expert_in,
    expert_out,
    cotangent,
):
    row_count, model_width = frames.shape
    own_lengths = lax.dynamic_index_in_dim(
        lengths, lax.axis_index(("dp", "expert")), 0, keepdims=False
    )
    segment, offsets, validity = segments(own_lengths, row_count)
    frame_count = jnp.sum(lengths[:, :-1]).astype(jnp.float32)
    block_rows = min(512, row_count)
    cosine, sine_table = rotation(offsets, DH)
    (
        routers_all,
        gains_all,
        attn_in_all,
        attn_out_all,
        conv_in_all,
        kernel_all,
        shift_all,
        conv_out_all,
    ) = (
        lax.all_gather(routers, ("dp", "expert"), axis=1, tiled=True),
        lax.all_gather(norm_gains, ("dp", "expert"), axis=1, tiled=True),
        lax.all_gather(attn_in, ("dp", "expert"), axis=0, tiled=True),
        lax.all_gather(attn_out, ("dp", "expert"), axis=0, tiled=True),
        lax.all_gather(conv_in, ("dp", "expert"), axis=0, tiled=True),
        lax.all_gather(conv_kernel, ("dp", "expert"), axis=1, tiled=True),
        lax.all_gather(bn_shift, ("dp", "expert"), axis=0, tiled=True),
        lax.all_gather(conv_out, ("dp", "expert"), axis=0, tiled=True),
    )
    experts_in_all, experts_out_all = (
        lax.all_gather(expert_in, "dp", axis=2, tiled=True),
        lax.all_gather(expert_out, "dp", axis=2, tiled=True),
    )
    first_in, second_in = (experts_in_all[0], experts_in_all[1])
    first_out, second_out = (experts_out_all[0], experts_out_all[1])
    gain_rows = gains_all.astype(jnp.float32)
    router_pair = routers_all.astype(jnp.float32)
    rows_in = frames.astype(jnp.float32)
    embed_pre = jnp.dot(frames, embed_weight, preferred_element_type=jnp.float32)
    embedded = jax.nn.silu(embed_pre)
    after_first, saved_first = moe_forward(
        rows_in, gain_rows[0], embedded, router_pair[0], choice_first, first_in, first_out
    )
    attn_norm, attn_hat, attn_inverse = norm_forward(after_first, gain_rows[1])
    attn_low = attn_norm.astype(jnp.bfloat16)
    projected = jnp.dot(attn_low, attn_in_all, preferred_element_type=jnp.float32)
    query_rows = rotate(
        projected[:, :model_width].reshape(row_count, H, DH), cosine, sine_table
    ).astype(jnp.bfloat16)
    key_rows = rotate(
        projected[:, model_width : 2 * model_width].reshape(row_count, H, DH), cosine, sine_table
    ).astype(jnp.bfloat16)
    value_rows = projected[:, 2 * model_width :].reshape(row_count, H, DH).astype(jnp.bfloat16)
    attended, logsum = attend_forward(query_rows, key_rows, value_rows, segment, block_rows)
    attended_low = attended.reshape(row_count, model_width).astype(jnp.bfloat16)
    after_attention = after_first + jnp.dot(
        attended_low, attn_out_all, preferred_element_type=jnp.float32
    )
    conv_norm, conv_hat, conv_inverse = norm_forward(after_attention, gain_rows[2])
    conv_low = conv_norm.astype(jnp.bfloat16)
    gates_in = jnp.dot(conv_low, conv_in_all, preferred_element_type=jnp.float32)
    logistic = jax.nn.sigmoid(gates_in[:, model_width:])
    glu_out = gates_in[:, :model_width] * logistic
    kernel = kernel_all.astype(jnp.float32)
    conv_depth = depthwise(glu_out, kernel, segment)
    weighted = validity[:, None] * conv_depth
    first_sum, second_sum = lax.psum(
        (jnp.sum(weighted, 0), jnp.sum(weighted * conv_depth, 0)), ("dp", "expert")
    )
    batch_mean = first_sum / frame_count
    batch_var = second_sum / frame_count - batch_mean * batch_mean
    batch_inverse = lax.rsqrt(batch_var + EPSILON)
    centred_depth = conv_depth - batch_mean
    batch_hat = centred_depth * batch_inverse
    batch_out = batch_hat * gain_rows[5] + shift_all.astype(jnp.float32)
    swish_low = jax.nn.silu(batch_out).astype(jnp.bfloat16)
    after_conv = after_attention + jnp.dot(
        swish_low, conv_out_all, preferred_element_type=jnp.float32
    )
    after_second, saved_second = moe_forward(
        after_conv, gain_rows[3], embedded, router_pair[1], choice_second, second_in, second_out
    )
    final_norm, final_hat, final_inverse = norm_forward(after_second, gain_rows[4])
    block_out = (final_norm * validity[:, None]).astype(jnp.bfloat16)
    grad_final = cotangent.astype(jnp.float32) * validity[:, None]
    grad_second, final_gain_grad = norm_backward(grad_final, gain_rows[4], final_hat, final_inverse)
    grad_conv, second_gain_grad, second_logit_grad, second_in_grad, second_out_grad = moe_backward(
        grad_second, gain_rows[3], second_in, second_out, saved_second
    )
    conv_grad_low = grad_conv.astype(jnp.bfloat16)
    conv_out_grad = jnp.einsum(
        "td,te->de", swish_low, conv_grad_low, preferred_element_type=jnp.float32
    )
    swish_grad = jnp.einsum(
        "te,de->td", conv_grad_low, conv_out_all, preferred_element_type=jnp.float32
    )
    batch_grad = swish_grad * silu_slope(batch_out)
    shift_grad = jnp.sum(batch_grad, 0)
    bn_gain_grad = jnp.sum(batch_grad * batch_hat, 0)
    hat_grad = batch_grad * gain_rows[5]
    hat_total, hat_moment = lax.psum(
        (jnp.sum(hat_grad, 0), jnp.sum(hat_grad * centred_depth, 0)), ("dp", "expert")
    )
    var_grad = -0.5 * hat_moment * batch_inverse * batch_inverse * batch_inverse
    mean_grad = -batch_inverse * hat_total - 2.0 * batch_mean * var_grad
    depth_grad = (
        hat_grad * batch_inverse
        + validity[:, None] * (mean_grad + 2.0 * conv_depth * var_grad) / frame_count
    )
    glu_grad, kernel_grad = depthwise_backward(depth_grad, glu_out, kernel, segment)
    gates_grad = jnp.concatenate(
        [glu_grad * logistic, glu_grad * gates_in[:, :model_width] * logistic * (1.0 - logistic)], 1
    ).astype(jnp.bfloat16)
    conv_in_grad = jnp.einsum("td,te->de", conv_low, gates_grad, preferred_element_type=jnp.float32)
    conv_norm_grad = jnp.einsum(
        "te,de->td", gates_grad, conv_in_all, preferred_element_type=jnp.float32
    )
    rows_grad, conv_gain_grad = norm_backward(conv_norm_grad, gain_rows[2], conv_hat, conv_inverse)
    grad_attention = grad_conv + rows_grad
    attention_grad_low = grad_attention.astype(jnp.bfloat16)
    attn_out_grad = jnp.einsum(
        "td,te->de", attended_low, attention_grad_low, preferred_element_type=jnp.float32
    )
    attended_grad = (
        jnp.einsum(
            "te,de->td", attention_grad_low, attn_out_all, preferred_element_type=jnp.float32
        )
        .astype(jnp.bfloat16)
        .reshape(row_count, H, DH)
    )
    query_grad, key_grad, value_grad = attend_backward(
        query_rows, key_rows, value_rows, segment, logsum, attended_grad, block_rows
    )
    projected_grad = jnp.concatenate(
        [
            rotate(query_grad, cosine, -sine_table).reshape(row_count, model_width),
            rotate(key_grad, cosine, -sine_table).reshape(row_count, model_width),
            value_grad.reshape(row_count, model_width),
        ],
        1,
    ).astype(jnp.bfloat16)
    attn_in_grad = jnp.einsum(
        "td,te->de", attn_low, projected_grad, preferred_element_type=jnp.float32
    )
    attn_norm_grad = jnp.einsum(
        "te,de->td", projected_grad, attn_in_all, preferred_element_type=jnp.float32
    )
    rows_grad, attn_gain_grad = norm_backward(attn_norm_grad, gain_rows[1], attn_hat, attn_inverse)
    grad_first = grad_attention + rows_grad
    grad_input, first_gain_grad, first_logit_grad, first_in_grad, first_out_grad = moe_backward(
        grad_first, gain_rows[0], first_in, first_out, saved_first
    )
    embed_rows_grad = jnp.dot(first_logit_grad, router_pair[0].T, precision=HIGHEST) + jnp.dot(
        second_logit_grad, router_pair[1].T, precision=HIGHEST
    )
    embed_pre_grad = (embed_rows_grad * silu_slope(embed_pre)).astype(jnp.bfloat16)
    embed_total = lax.psum(
        jnp.einsum("td,te->de", frames, embed_pre_grad, preferred_element_type=jnp.float32),
        ("dp", "expert"),
    )
    frames_grad = grad_input + jnp.einsum(
        "te,de->td", embed_pre_grad, embed_weight, preferred_element_type=jnp.float32
    )
    router_terms = jnp.stack(
        [
            jnp.dot(embedded.T, first_logit_grad, precision=HIGHEST),
            jnp.dot(embedded.T, second_logit_grad, precision=HIGHEST),
        ]
    )
    gain_terms = jnp.stack(
        [
            first_gain_grad,
            attn_gain_grad,
            conv_gain_grad,
            second_gain_grad,
            final_gain_grad,
            bn_gain_grad,
        ]
    )
    dense_parts = (
        lax.psum_scatter(router_terms, ("dp", "expert"), scatter_dimension=1, tiled=True),
        lax.psum_scatter(gain_terms, ("dp", "expert"), scatter_dimension=1, tiled=True),
        lax.psum_scatter(attn_in_grad, ("dp", "expert"), scatter_dimension=0, tiled=True),
        lax.psum_scatter(attn_out_grad, ("dp", "expert"), scatter_dimension=0, tiled=True),
        lax.psum_scatter(conv_in_grad, ("dp", "expert"), scatter_dimension=0, tiled=True),
        lax.psum_scatter(kernel_grad, ("dp", "expert"), scatter_dimension=1, tiled=True),
        lax.psum_scatter(shift_grad, ("dp", "expert"), scatter_dimension=0, tiled=True),
        lax.psum_scatter(conv_out_grad, ("dp", "expert"), scatter_dimension=0, tiled=True),
    )
    expert_parts = (
        lax.psum_scatter(
            jnp.stack([first_in_grad, second_in_grad]).astype(jnp.bfloat16),
            "dp",
            scatter_dimension=2,
            tiled=True,
        ).astype(jnp.float32),
        lax.psum_scatter(
            jnp.stack([first_out_grad, second_out_grad]).astype(jnp.bfloat16),
            "dp",
            scatter_dimension=2,
            tiled=True,
        ).astype(jnp.float32),
    )
    return (
        block_out,
        frames_grad,
        embed_total,
        dense_parts[0],
        dense_parts[1],
        dense_parts[2],
        dense_parts[3],
        dense_parts[4],
        dense_parts[5],
        dense_parts[6],
        dense_parts[7],
        expert_parts[0],
        expert_parts[1],
    )


def solution(mesh):
    in_specs = (
        P(("dp", "expert"), None),
        P(),
        P(("dp", "expert"), None),
        P(("dp", "expert"), None),
        P(),
        P(None, ("dp", "expert"), None),
        P(None, ("dp", "expert")),
        P(("dp", "expert"), None),
        P(("dp", "expert"), None),
        P(("dp", "expert"), None),
        P(None, ("dp", "expert")),
        P(("dp", "expert")),
        P(("dp", "expert"), None),
        P(None, "expert", "dp", None),
        P(None, "expert", "dp", None),
        P(("dp", "expert"), None),
    )
    out_specs = (
        P(("dp", "expert"), None),
        P(("dp", "expert"), None),
        P(),
        P(None, ("dp", "expert"), None),
        P(None, ("dp", "expert")),
        P(("dp", "expert"), None),
        P(("dp", "expert"), None),
        P(("dp", "expert"), None),
        P(None, ("dp", "expert")),
        P(("dp", "expert")),
        P(("dp", "expert"), None),
        P(None, "expert", "dp", None),
        P(None, "expert", "dp", None),
    )
    return jax.shard_map(shards, mesh=mesh, in_specs=in_specs, out_specs=out_specs, check_vma=False)
```

profile of v0, /device:TPU:0, one launch (start us, length us, event | category | flops | bytes accessed | tf_op | source)
XLA Modules:
  0.0 1953.3 jit_solution(16807625611152580971)
XLA Ops:
  11.8 71.2 %all-gather = bf16[32,16,6]{1,2,0:T(8,128)(2,1)S(1)} all-gather(bf16[1,16,6]{1,2,0:T(8,128)(2,1)} %bitcast.317), channel_id=1, replica_groups=mesh['dp'=8,'expert'=4] {'dp','expert'}, dimensions={0}, use_global_device_ids=true | all-gather | bytes 6336 | tf_op jit(solution)/shard_map/all_gather | solution.py:337
  87.9 4.1 scatter_custom_fusion
  92.1 3.5 all-to-all-start
  97.8 39.9 %all-reduce.16 = bf16[512]{0:T(512)(128)(2,1)S(1)} all-reduce(bf16[512]{0:T(512)(128)(2,1)S(1)} %dynamic-update-slice), channel_id=1, replica_groups=mesh['dp'=8,'expert'=4] {'dp','expert'}, use_global_device_ids=true, to_apply=%add.16 | all-reduce | flops 512 | bytes 2048
  140.4 67.4 %all_gather.36 = bf16[15,512]{0,1:T(8,128)(2,1)S(1)} all-gather(bf16[15,16]{0,1:T(8,128)(2,1)S(1)} %copy.144), channel_id=1, replica_groups=mesh['dp'=8,'expert'=4] {'dp','expert'}, dimensions={1}, use_global_device_ids=true | all-gather | bytes 15840 | tf_op jit(solution)/shard_map/all_gather | solution.py:341
  207.8 65.5 %all_gather.30 = bf16[2,512,4]{2,0,1:T(2,128)(2,1)S(1)} all-gather(bf16[2,16,4]{2,0,1:T(2,128)(2,1)S(1)} %copy.133), channel_id=1, replica_groups=mesh['dp'=8,'expert'=4] {'dp','expert'}, dimensions={1}, use_global_device_ids=true | all-gather | bytes 8448 | tf_op jit(solution)/shard_map/all_gather | solution.py:336
  278.1 8.1 multiply_convert_fusion.4
  286.3 6.2 fusion.18
  292.4 13.5 all-to-all-start.1
  306.0 2.7 slice_reduce_fusion.14
  311.1 83.0 %all_gather.35 = bf16[512,512]{1,0:T(8,128)(2,1)} all-gather(bf16[16,512]{1,0:T(8,128)(2,1)S(1)} %copy-done.148), channel_id=1, replica_groups=mesh['dp'=8,'expert'=4] {'dp','expert'}, dimensions={0}, use_global_device_ids=true | all-gather | bytes 540672 | tf_op jit(solution)/shard_map/all_gather | solution.py:339
  394.1 73.1 %all_gather.39 = bf16[512,512]{1,0:T(8,128)(2,1)} all-gather(bf16[16,512]{1,0:T(8,128)(2,1)S(1)} %copy-done.149), channel_id=1, replica_groups=mesh['dp'=8,'expert'=4] {'dp','expert'}, dimensions={0}, use_global_device_ids=true | all-gather | bytes 540672 | tf_op jit(solution)/shard_map/all_gather | solution.py:343
  470.1 2.5 fusion.199
  484.8 2.5 fusion.29
  493.6 3.8 fusion.81
  497.4 39.4 %all-reduce.19 = (f32[512]{0:T(512)S(1)}, f32[512]{0:T(512)S(1)}) all-reduce(f32[512]{0:T(512)S(1)} %get-tuple-element.164, f32[512]{0:T(512)S(1)} %get-tuple-element.163), channel_id=1, replica_groups=mesh['dp'=8,'expert'=4] {'dp','expert'}, use_global_device_ids=true, to_apply=%region_19.20 | all-reduce | flops 1024 | bytes 8192 | tf_op jit(solution)/shard_map/psum | solution.py:382
  539.7 3.7 scatter_custom_fusion.1
  543.5 28.7 %all_to_all.40 = bf16[1,4,256,512]{3,2,0,1:T(8,128)(2,1)S(1)} all-to-all(bf16[1,4,256,512]{3,2,0,1:T(8,128)(2,1)} %bitcast.228), channel_id=1, replica_groups=mesh['dp'=8,'expert'=4] {'expert'}, dimensions={1} | all-to-all | bytes 2097152 | tf_op jit(solution)/shard_map/all_to_all | solution.py:211
  572.2 7.3 multiply_convert_fusion.3
  579.5 3.3 fusion.16
  582.8 4.7 all-to-all-start.3
  594.0 18.3 all-to-all-done.3
  612.3 4.1 gather_fusion.1
  622.8 4.2 scatter_custom_fusion.2
  627.0 28.7 %all_to_all.41 = bf16[1,4,256,512]{3,2,0,1:T(8,128)(2,1)S(1)} all-to-all(bf16[1,4,256,512]{3,2,0,1:T(8,128)(2,1)} %bitcast.227), channel_id=1, replica_groups=mesh['dp'=8,'expert'=4] {'expert'}, dimensions={1} | all-to-all | bytes 2097152 | tf_op jit(solution)/shard_map/all_to_all | solution.py:211
  655.7 7.1 multiply_convert_fusion.2
  662.8 3.4 fusion.17
  666.2 4.2 all-to-all-start.5
  671.8 23.5 %all-to-all-done.5 = bf16[1,4,256,512]{3,2,0,1:T(8,128)(2,1)} async-done(((bf16[1,4,256,512]{3,2,0,1:T(8,128)(2,1)}), bf16[1,4,256,512]{3,2,0,1:T(8,128)(2,1)}, u32[]{:S(2)}, u32[]{:S(2)}) %all-to-all-start.5) | async-done | bytes 1048608 | tf_op jit(solution)/shard_map/all_to_all | solution.py:215
  695.3 4.2 gather_fusion.2
  703.7 2.6 multiply_reduce_fusion.17
  706.2 38.1 %all-reduce.18 = (f32[512]{0:T(512)}, f32[512]{0:T(512)}, f32[512]{0:T(512)}) all-reduce(f32[512]{0:T(512)} %get-tuple-element.153, f32[512]{0:T(512)} %get-tuple-element.160, f32[512]{0:T(512)} %get-tuple-element.165), channel_id=1, replica_groups=mesh['dp'=8,'expert'=4] {'dp','expert'}, use_global_device_ids=true, to_apply=%region_42.43 | all-reduce | flops 1536 | bytes 12288 | tf_op jit(solution)/shard_map/psum | solution.py:416
  745.1 5.0 multiply_reduce_fusion.2
  752.2 2.5 multiply_convert_fusion.7
  761.3 3.0 multiply_reduce_fusion
  764.4 2.9 multiply_convert_fusion.1
  773.7 4.2 scatter_custom_fusion.3
  778.0 4.2 all-to-all-start.6
  785.4 23.2 %all-to-all-done.6 = bf16[1,4,256,512]{3,2,0,1:T(8,128)(2,1)} async-done(((bf16[1,4,256,512]{3,2,0,1:T(8,128)(2,1)}), bf16[1,4,256,512]{3,2,0,1:T(8,128)(2,1)}, u32[]{:S(2)}, u32[]{:S(2)}) %all-to-all-start.6) | async-done | bytes 1048608 | tf_op jit(solution)/shard_map/all_to_all | solution.py:211
  808.6 8.2 multiply_convert_fusion
  816.8 3.3 fusion.19
  820.1 3.5 all-to-all-start.7
  823.9 6.2 fusion.7
  836.5 6.3 fusion.6
  842.8 7.0 all-to-all-done.7
  849.9 2.6 gather_fusion.3
  855.2 4.6 pad_maximum_fusion
  861.0 4.7 fusion.9
  865.7 3.7 fusion.8
  872.3 3.2 fusion.113
  875.6 2.4 fusion.110
  878.2 3.5 fusion.88
  882.0 4.2 fusion.90
  887.6 35.5 %reduce-scatter.28.cloned.1.call-done = f32[16,8]{1,0:T(8,128)} async-done(((f32[512,8]{1,0:T(8,128)}), f32[16,8]{1,0:T(8,128)}) %reduce-scatter.28.cloned.1.call-update) | async-done | bytes 528
  924.6 132.2 %reduce-scatter.32.cloned.1.call-done = f32[16,15]{1,0:T(8,128)} async-done(((f32[512,15]{1,0:T(8,128)}), f32[16,15]{1,0:T(8,128)}) %reduce-scatter.32.cloned.1.call-update) | async-done | bytes 976
  1058.1 130.4 %all-reduce.22.cloned.1.call-done = f32[512,512]{0,1:T(8,128)} async-done(((f32[512,512]{0,1:T(8,128)}), f32[512,512]{0,1:T(8,128)}) %all-reduce.22.cloned.1.call-update) | async-done | bytes 1048592 | tf_op jit(solution)/shard_map/psum | solution.py:472
  1188.5 2.5 copy.157
  1192.6 131.0 %reduce-scatter.30.cloned.1.call-done = f32[16,6]{1,0:T(8,128)} async-done(((f32[512,6]{1,0:T(8,128)}), f32[16,6]{1,0:T(8,128)}) %reduce-scatter.30.cloned.1.call-update) | async-done | bytes 400
  1325.0 49.4 %reduce-scatter.24.cloned.1.call-done = bf16[2,1,64,2048]{3,2,1,0:T(8,128)(2,1)} async-done(((bf16[2,1,512,2048]{3,2,1,0:T(8,128)(2,1)}), bf16[2,1,64,2048]{3,2,1,0:T(8,128)(2,1)}) %reduce-scatter.24.cloned.1.call-update) | async-done | bytes 524304 | tf_op jit(solution)/shard_map/reduce_scatter | solution.py:506
  1376.5 52.8 %reduce-scatter.26.cloned.1.call-done = bf16[2,1,256,512]{3,2,1,0:T(8,128)(2,1)} async-done(((bf16[2,1,2048,512]{3,2,1,0:T(8,128)(2,1)}), bf16[2,1,256,512]{3,2,1,0:T(8,128)(2,1)}) %reduce-scatter.26.cloned.1.call-update) | async-done | bytes 524304 | tf_op jit(solution)/shard_map/reduce_scatter | solution.py:512
  1431.5 136.3 %reduce-scatter.22.cloned.1.call-done = f32[16,512]{1,0:T(8,128)} async-done(((f32[512,512]{1,0:T(8,128)}), f32[16,512]{1,0:T(8,128)}) %reduce-scatter.22.cloned.1.call-update) | async-done | bytes 32784 | tf_op jit(solution)/shard_map/reduce_scatter | solution.py:503
  1567.8 134.4 %reduce-scatter.18.cloned.1.call-done = f32[16,512]{1,0:T(8,128)} async-done(((f32[512,512]{1,0:T(8,128)}), f32[16,512]{1,0:T(8,128)}) %reduce-scatter.18.cloned.1.call-update) | async-done | bytes 32784 | tf_op jit(solution)/shard_map/reduce_scatter | solution.py:499
  1702.2 137.6 %reduce-scatter.20.cloned.1.call-done = f32[16,1024]{1,0:T(8,128)} async-done(((f32[512,1024]{1,0:T(8,128)}), f32[16,1024]{1,0:T(8,128)}) %reduce-scatter.20.cloned.1.call-update) | async-done | bytes 65552 | tf_op jit(solution)/shard_map/reduce_scatter | solution.py:500
  1839.8 106.8 %reduce-scatter.16.cloned.1.call-done = f32[16,1536]{1,0:T(8,128)} async-done(((f32[512,1536]{1,0:T(8,128)}), f32[16,1536]{1,0:T(8,128)}) %reduce-scatter.16.cloned.1.call-update) | async-done | bytes 98320 | tf_op jit(solution)/shard_map/reduce_scatter | solution.py:498
  (565 shorter events, 105.7 us)
Async XLA Ops:
  7.2 267.4 %copy-start = (bf16[512,512]{1,0:T(8,128)(2,1)S(1)}, bf16[512,512]{1,0:T(8,128)(2,1)}, u32[]{:S(2)}) copy-start(bf16[512,512]{1,0:T(8,128)(2,1)} %param.20) | copy-start | bytes 1572868
  7.2 267.4 %copy-start.2 = (bf16[512,512]{1,0:T(8,128)(2,1)S(1)}, bf16[512,512]{1,0:T(8,128)(2,1)}, u32[]{:S(2)}) copy-start(bf16[512,512]{1,0:T(8,128)(2,1)} %param.16) | copy-start | bytes 1572868
  7.2 89.0 %copy-start.170 = (s32[32,4]{0,1:T(4,128)S(1)}, s32[32,4]{0,1:T(4,128)}, u32[]{:S(2)}) copy-start(s32[32,4]{0,1:T(4,128)} %param.17) | copy-start | bytes 1540
  7.2 90.3 %copy-start.190 = (bf16[16]{0:T(256)(128)(2,1)S(1)}, bf16[16]{0:T(256)(128)(2,1)}, u32[]{:S(2)}) copy-start(bf16[16]{0:T(256)(128)(2,1)} %param.27) | copy-start | bytes 100
  7.2 131.3 %copy-start.180 = (bf16[15,16]{1,0:T(8,128)(2,1)S(1)}, bf16[15,16]{1,0:T(8,128)(2,1)}, u32[]{:S(2)}) copy-start(bf16[15,16]{1,0:T(8,128)(2,1)} %param.26) | copy-start | bytes 1444
  7.2 131.4 %copy-start.183 = (bf16[2,16,4]{1,2,0:T(4,128)(2,1)S(1)}, bf16[2,16,4]{1,2,0:T(4,128)(2,1)}, u32[]{:S(2)}) copy-start(bf16[2,16,4]{1,2,0:T(4,128)(2,1)} %param.21) | copy-start | bytes 772
  7.2 131.5 %copy-start.62 = (s32[512,1]{0,1:T(1,128)S(1)}, s32[512,1]{0,1:T(1,128)}, u32[]{:S(2)}) copy-start(s32[512,1]{0,1:T(1,128)} %param.19) | copy-start | bytes 6148
  7.3 270.8 %all-gather.6.cloned.1.call-start = ((), (), s32[]{:S(2)}) async-start(), calls=%async_computation.17 | async-start | bytes 4718592 | tf_op jit(solution)/shard_map/all_gather | solution.py:346
  8.0 278.3 %all-gather.8.cloned.1.call-start = ((), (), s32[]{:S(2)}) async-start(), calls=%async_computation.18 | async-start | bytes 4718592 | tf_op jit(solution)/shard_map/all_gather | solution.py:347
  8.7 461.3 %all-gather.10.cloned.1.call-start = ((), (), s32[]{:S(2)}) async-start(), calls=%async_computation.19 | async-start | bytes 1622016 | tf_op jit(solution)/shard_map/all_gather | solution.py:338
  85.3 55.1 %copy-start.55 = (f32[512]{0:T(512)}, f32[512]{0:T(512)S(1)}, u32[]{:S(2)}) copy-start(f32[512]{0:T(512)S(1)} %broadcast_multiply_fusion.28) | copy-start | bytes 6148
  86.6 53.8 %copy-start.74 = (f32[512]{0:T(512)}, f32[512]{0:T(512)S(1)}, u32[]{:S(2)}) copy-start(f32[512]{0:T(512)S(1)} %add_rsqrt_fusion.5) | copy-start | bytes 6148
  87.3 51.2 %copy-start.168 = (s32[512,1]{0,1:T(1,128)}, s32[512,1]{0,1:T(1,128)S(1)}, u32[]{:S(2)}) copy-start(s32[512,1]{0,1:T(1,128)S(1)} %compare_select_fusion.1) | copy-start | bytes 6148
  87.9 52.5 %copy-start.69 = (f32[1,512]{1,0:T(1,128)}, f32[1,512]{1,0:T(1,128)S(1)}, u32[]{:S(2)}) copy-start(f32[1,512]{1,0:T(1,128)S(1)} %get-tuple-element.252) | copy-start | bytes 6148
  87.9 382.1 %copy-start.152 = (f32[1,512]{1,0:T(1,128)}, f32[1,512]{1,0:T(1,128)S(1)}, u32[]{:S(2)}) copy-start(f32[1,512]{1,0:T(1,128)S(1)} %get-tuple-element.251) | copy-start | bytes 6148
  92.1 186.0 %all-to-all-start = ((bf16[1,4,256,512]{3,2,0,1:T(8,128)(2,1)}), bf16[1,4,256,512]{3,2,0,1:T(8,128)(2,1)S(1)}, u32[]{:S(2)}, u32[]{:S(2)}) async-start(bf16[1,4,256,512]{3,2,0,1:T(8,128)(2,1)} %bitcast.10), calls=%async_computation | async-start | bytes 2097152 | tf_op jit(solution)/shard_map/all_to_all | solution.py:211
  95.6 393.1 %all-gather.12.cloned.1.call-start = ((), (), s32[]{:S(2)}) async-start(), calls=%async_computation.20 | async-start | bytes 1081344 | tf_op jit(solution)/shard_map/all_gather | solution.py:340
  96.2 371.0 %copy-start.146 = (s32[1024]{0:T(1024)}, s32[1024]{0:T(1024)S(1)}, u32[]{:S(2)}) copy-start(s32[1024]{0:T(1024)S(1)} %pad_clamp_fusion.1) | copy-start | bytes 12292
  274.6 11.7 copy-start.67
  278.0 209.3 %copy-start.51 = (f32[512]{0:T(512)}, f32[512]{0:T(512)S(1)}, u32[]{:S(2)}) copy-start(f32[512]{0:T(512)S(1)} %broadcast_multiply_fusion.30) | copy-start | bytes 6148
  292.4 18.7 copy-start.148
  292.4 101.7 %copy-start.149 = (bf16[16,512]{1,0:T(8,128)(2,1)S(1)}, bf16[16,512]{1,0:T(8,128)(2,1)}, u32[]{:S(2)}) copy-start(bf16[16,512]{1,0:T(8,128)(2,1)} %param.28) | copy-start | bytes 49156
  292.4 174.8 %all-to-all-start.1 = ((bf16[1,4,256,512]{3,2,0,1:T(8,128)(2,1)}), bf16[1,4,256,512]{3,2,0,1:T(8,128)(2,1)S(1)}, u32[]{:S(2)}, u32[]{:S(2)}) async-start(bf16[1,4,256,512]{3,2,0,1:T(8,128)(2,1)} %bitcast.243), calls=%async_computation.1 | async-start | bytes 2097152 | tf_op jit(solution)/shard_map/all_to_all | solution.py:215
  309.9 182.4 %copy-start.64 = (f32[512]{0:T(512)}, f32[512]{0:T(512)S(1)}, u32[]{:S(2)}) copy-start(f32[512]{0:T(512)S(1)} %get-tuple-element.272) | copy-start | bytes 6148
  497.4 42.3 %copy-start.83 = (f32[1,512]{1,0:T(1,128)S(1)}, f32[1,512]{1,0:T(1,128)}, u32[]{:S(2)}) copy-start(f32[1,512]{1,0:T(1,128)} %get-tuple-element.248) | copy-start | bytes 6148
  538.9 40.6 %copy-start.66 = (f32[512]{0:T(512)}, f32[512]{0:T(512)S(1)}, u32[]{:S(2)}) copy-start(f32[512]{0:T(512)S(1)} %broadcast_multiply_fusion.25) | copy-start | bytes 6148
  579.5 9.7 copy-start.169
  582.8 29.5 %all-to-all-start.3 = ((bf16[1,4,256,512]{3,2,0,1:T(8,128)(2,1)}), bf16[1,4,256,512]{3,2,0,1:T(8,128)(2,1)}, u32[]{:S(2)}, u32[]{:S(2)}) async-start(bf16[1,4,256,512]{3,2,0,1:T(8,128)(2,1)} %bitcast.244), calls=%async_computation.3 | async-start | bytes 2097152 | tf_op jit(solution)/shard_map/all_to_all | solution.py:215
  666.2 29.1 %all-to-all-start.5 = ((bf16[1,4,256,512]{3,2,0,1:T(8,128)(2,1)}), bf16[1,4,256,512]{3,2,0,1:T(8,128)(2,1)}, u32[]{:S(2)}, u32[]{:S(2)}) async-start(bf16[1,4,256,512]{3,2,0,1:T(8,128)(2,1)} %bitcast.245), calls=%async_computation.5 | async-start | bytes 2097152 | tf_op jit(solution)/shard_map/all_to_all | solution.py:215
  703.7 41.4 %copy-start.10 = (f32[512,512]{1,0:T(8,128)S(1)}, f32[512,512]{1,0:T(8,128)}, u32[]{:S(2)}) copy-start(f32[512,512]{1,0:T(8,128)} %copy-done.9) | copy-start | bytes 3145732
  757.1 14.7 copy-start.7
  771.9 10.8 copy-start.95
  771.9 10.8 copy-start.156
  771.9 10.8 copy-start.6
  771.9 10.8 copy-start.63
  771.9 10.8 copy-start.82
  771.9 10.8 copy-start.91
  771.9 11.5 copy-start.93
  771.9 11.5 copy-start.50
  771.9 11.5 copy-start.61
  772.0 11.5 copy-start.80
  778.0 30.6 %all-to-all-start.6 = ((bf16[1,4,256,512]{3,2,0,1:T(8,128)(2,1)}), bf16[1,4,256,512]{3,2,0,1:T(8,128)(2,1)}, u32[]{:S(2)}, u32[]{:S(2)}) async-start(bf16[1,4,256,512]{3,2,0,1:T(8,128)(2,1)} %bitcast.226), calls=%async_computation.6 | async-start | bytes 2097152 | tf_op jit(solution)/shard_map/all_to_all | solution.py:211
  782.2 140.9 %reduce-scatter.28.cloned.1.call-start = ((), (), s32[]{:S(2)}) async-start(), calls=%async_computation.28 | async-start | bytes 270336
  820.1 29.7 %all-to-all-start.7 = ((bf16[1,4,256,512]{3,2,0,1:T(8,128)(2,1)}), bf16[1,4,256,512]{3,2,0,1:T(8,128)(2,1)S(1)}, u32[]{:S(2)}, u32[]{:S(2)}) async-start(bf16[1,4,256,512]{3,2,0,1:T(8,128)(2,1)} %bitcast.242), calls=%async_computation.7 | async-start | bytes 2097152 | tf_op jit(solution)/shard_map/all_to_all | solution.py:215
  823.8 232.9 %reduce-scatter.32.cloned.1.call-start = ((), (), s32[]{:S(2)}) async-start(), calls=%async_computation.30 | async-start | bytes 270336
  831.2 357.3 %all-reduce.22.cloned.1.call-start = ((), (), s32[]{:S(2)}) async-start(), calls=%async_computation.21 | async-start | bytes 2097152 | tf_op jit(solution)/shard_map/psum | solution.py:472
  836.3 13.6 copy-start.147
  836.3 487.3 %reduce-scatter.30.cloned.1.call-start = ((), (), s32[]{:S(2)}) async-start(), calls=%async_computation.29 | async-start | bytes 270336
  842.8 9.7 copy-start.56
  842.8 9.7 copy-start.70
  842.8 9.7 copy-start.75
  842.8 11.4 copy-start.150
  842.8 11.4 copy-start.151
  842.8 11.4 copy-start.181
  842.8 11.4 copy-start.182
  855.2 519.3 %reduce-scatter.24.cloned.1.call-start = ((), (), s32[]{:S(2)}) async-start(), calls=%async_computation.26 | async-start | bytes 4718592 | tf_op jit(solution)/shard_map/reduce_scatter | solution.py:506
  859.8 569.6 %reduce-scatter.26.cloned.1.call-start = ((), (), s32[]{:S(2)}) async-start(), calls=%async_computation.27 | async-start | bytes 4718592 | tf_op jit(solution)/shard_map/reduce_scatter | solution.py:512
  871.8 696.0 %reduce-scatter.22.cloned.1.call-start = ((), (), s32[]{:S(2)}) async-start(), calls=%async_computation.25 | async-start | bytes 1081344 | tf_op jit(solution)/shard_map/reduce_scatter | solution.py:503
  875.6 826.6 %reduce-scatter.18.cloned.1.call-start = ((), (), s32[]{:S(2)}) async-start(), calls=%async_computation.23 | async-start | bytes 1081344 | tf_op jit(solution)/shard_map/reduce_scatter | solution.py:499
  878.1 961.6 %reduce-scatter.20.cloned.1.call-start = ((), (), s32[]{:S(2)}) async-start(), calls=%async_computation.24 | async-start | bytes 2162688 | tf_op jit(solution)/shard_map/reduce_scatter | solution.py:500
  881.7 1064.8 %reduce-scatter.16.cloned.1.call-start = ((), (), s32[]{:S(2)}) async-start(), calls=%async_computation.22 | async-start | bytes 3244032 | tf_op jit(solution)/shard_map/reduce_scatter | solution.py:498
  886.2 304.8 %copy-start.15 = (f32[512,512]{1,0:T(8,128)S(1)}, f32[512,512]{1,0:T(8,128)}, u32[]{:S(2)}) copy-start(f32[512,512]{1,0:T(8,128)} %get-tuple-element.222) | copy-start | bytes 3145732
  886.2 304.8 %copy-start.19 = (bf16[512,512]{1,0:T(8,128)(2,1)S(1)}, bf16[512,512]{1,0:T(8,128)(2,1)}, u32[]{:S(2)}) copy-start(bf16[512,512]{1,0:T(8,128)(2,1)} %gather_fusion.3) | copy-start | bytes 1572868
  886.2 304.8 %copy-start.30 = (bf16[512,512]{1,0:T(8,128)(2,1)S(1)}, bf16[512,512]{1,0:T(8,128)(2,1)}, u32[]{:S(2)}) copy-start(bf16[512,512]{1,0:T(8,128)(2,1)} %copy-done.29) | copy-start | bytes 1572868
  (154 other events, 609.9 us)
Sparse Core Ops, SparseCore 0:
  10.0 39.4 all-gather.5
  51.4 36.8 all-gather.7
  91.2 58.7 all-gather.9
  152.8 52.7 all-gather.11
  785.6 137.5 reduce-scatter.27
  925.3 131.3 reduce-scatter.31
  1062.5 125.9 all-reduce.21
  1190.8 132.7 reduce-scatter.29
  1327.0 47.3 reduce-scatter.23
  1378.0 51.3 reduce-scatter.25
  1432.2 135.5 reduce-scatter.21
  1570.6 131.5 reduce-scatter.17
  1705.0 134.7 reduce-scatter.19
  1846.5 99.9 reduce-scatter.15
where the time goes:
time: 1960 us; the launch traced here: 1950 us
  waiting for transfers between devices  1120 us (57%)
  blocking collectives  535 us (27%)
  matrix products  116 us (6%)
  other arithmetic  79.1 us (4%)
  local copies, waits for them, and re-layouts  49 us (2%)
  starting transfers between devices  35 us (2%)
    unnamed x17, waiting for transfers between devices  301 us
    reduce_scatter x1, waiting for transfers between devices, shards(): lax.psum_scatter(conv_in_grad, ('dp', 'expert'), scatter_dimension=0, til...  138 us
    reduce_scatter x1, waiting for transfers between devices, shards(): lax.psum_scatter(conv_out_grad, ('dp', 'expert'), scatter_dimension=0, ti...  136 us
    reduce_scatter x1, waiting for transfers between devices, shards(): lax.psum_scatter(attn_out_grad, ('dp', 'expert'), scatter_dimension=0, ti...  134 us
    psum x1, waiting for transfers between devices, shards(): lax.psum(jnp.einsum('td,te->de', frames, embed_pre_grad, preferred_elemen...  130 us
    reduce_scatter x1, waiting for transfers between devices, shards(): lax.psum_scatter(attn_in_grad, ('dp', 'expert'), scatter_dimension=0, til...  107 us
    all_gather x1, blocking collectives, shards(): lax.all_gather(attn_out, ('dp', 'expert'), axis=0, tiled=True)  83 us
    all_gather x1, blocking collectives, shards(): lax.all_gather(conv_out, ('dp', 'expert'), axis=0, tiled=True)  73.1 us
  transfers between devices with their start and end apart: 20, of which 14 were waited for; matrix products, arithmetic and copies ran while one was open for 7% of the time, Pallas kernels for 0%

commit v1 on v0

--- a/solution.py
+++ b/solution.py
@@ -10,6 +10,81 @@
 EPSILON = 1e-05
 MASK_FILL = 1000000000.0
 HIGHEST = lax.Precision.HIGHEST
+
+
+AXES = ("dp", "expert")
+
+
+def position(axes):
+    return lax.axis_index(axes)
+
+
+def bit_count(axes):
+    total = 1
+    for name in axes:
+        total *= lax.axis_size(name)
+    return total.bit_length() - 1
+
+
+def exchange(values, axes, mask):
+    total = 1 << bit_count(axes)
+    return lax.ppermute(values, axes, [(i, i ^ mask) for i in range(total)])
+
+
+def spread_order(axes):
+    expert_bits = bit_count(("expert",)) if "expert" in axes else 0
+    dp_bits = bit_count(("dp",)) if "dp" in axes else 0
+    dp_list = [expert_bits + i for i in range(dp_bits)]
+    return dp_list + list(range(expert_bits))
+
+
+def reduce_scatter_bits(values, axes, order):
+    count = bit_count(axes)
+    index = position(axes)
+    left = list(range(count - 1, -1, -1))
+    for bit in order:
+        dim = left.index(bit)
+        own_bit = (index >> bit) & 1
+        sent = lax.dynamic_index_in_dim(values, 1 - own_bit, dim, False)
+        kept = lax.dynamic_index_in_dim(values, own_bit, dim, False)
+        arrived = exchange(sent, axes, 1 << bit)
+        values = (kept.astype(jnp.float32) + arrived.astype(jnp.float32)).astype(values.dtype)
+        left.remove(bit)
+    return values
+
+
+def all_gather_bits(values, axes, order):
+    index = position(axes)
+    held = []
+    for bit in order:
+        own_bit = (index >> bit) & 1
+        arrived = exchange(values, axes, 1 << bit)
+        dim = sum(1 for other in held if other > bit)
+        values = jnp.stack(
+            [jnp.where(own_bit == 0, values, arrived), jnp.where(own_bit == 0, arrived, values)],
+            dim,
+        )
+        held.append(bit)
+    return values
+
+
+def sum_everywhere(values):
+    order = spread_order(AXES)
+    expert_bits = bit_count(("expert",))
+    groups = [order[:1]]
+    rest = [order[1 : len(order) - expert_bits], order[len(order) - expert_bits :]]
+    for bits in rest:
+        groups += [bits[i : i + 2] for i in range(0, len(bits), 2)]
+    for bits in groups:
+        if len(bits) == 1:
+            values = values + exchange(values, AXES, 1 << bits[0])
+        else:
+            low, high = 1 << bits[0], 1 << bits[1]
+            near = exchange(values, AXES, low)
+            far = exchange(values, AXES, high)
+            across = exchange(values, AXES, low | high)
+            values = (values + near) + (far + across)
+    return values
 
 
 def silu_slope(preactivation):
@@ -215,86 +290,37 @@
     return lax.all_to_all(back_rows, "expert", split_axis=1, concat_axis=1, tiled=True)
 
 
-def moe_forward(rows_in, gain_row, embedded, router, choice_col, input_weight, output_weight):
-    expert_total = router.shape[1]
-    local_experts = input_weight.shape[0]
-    peer_count = lax.axis_size("expert")
-    capacity = 2 * rows_in.shape[0] // expert_total
-    model_width = rows_in.shape[1]
-    normed_out, normed, inverse = norm_forward(rows_in, gain_row)
-    rows_low = normed_out.astype(jnp.bfloat16)
-    slot_index, onehot = expert_slots(choice_col, expert_total, capacity, local_experts, peer_count)
-    arrived_rows = to_experts(
-        scatter_rows(rows_low, slot_index, local_experts, peer_count, capacity)
-    )
-    arrived_rows = arrived_rows.reshape(local_experts, peer_count * capacity, model_width)
+def gates(embedded, router, onehot):
+    router_probs = jax.nn.softmax(jnp.dot(embedded, router, precision=HIGHEST), -1)
+    return (router_probs, jnp.sum(router_probs * onehot, 1))
+
+
+def expert_forward(arrived_rows, input_weight, output_weight):
     preactivation = jnp.einsum(
         "zve,zeg->zvg", arrived_rows, input_weight, preferred_element_type=jnp.float32
     )
-    hidden_reduced = jax.nn.silu(preactivation).astype(jnp.bfloat16)
+    hidden = jax.nn.silu(preactivation).astype(jnp.bfloat16)
     produced = jnp.einsum(
-        "gzm,gmb->gzb", hidden_reduced, output_weight, preferred_element_type=jnp.float32
-    ).astype(jnp.bfloat16)
-    returned = from_experts(produced.reshape(local_experts, peer_count, capacity, model_width))
-    expert_rows = returned.reshape(-1, model_width)[slot_index].astype(jnp.float32)
-    router_probs = jax.nn.softmax(jnp.dot(embedded, router, precision=HIGHEST), -1)
-    gate_value = jnp.sum(router_probs * onehot, 1)
-    output = rows_in + 0.5 * gate_value[:, None] * expert_rows
-    saved = (
-        normed,
-        inverse,
-        slot_index,
-        onehot,
-        arrived_rows,
-        preactivation,
-        hidden_reduced,
-        expert_rows,
-        router_probs,
-        gate_value,
-    )
-    return (output, saved)
-
-
-def moe_backward(grad_out, gain_row, input_weight, output_weight, saved):
-    (
-        normed,
-        inverse,
-        slot_index,
-        onehot,
-        arrived_rows,
-        preactivation,
-        hidden_reduced,
-        expert_rows,
-        router_probs,
-        gate_value,
-    ) = saved
-    local_experts, row_total, model_width = arrived_rows.shape
-    peer_count = lax.axis_size("expert")
-    capacity = row_total // peer_count
-    sent_grad = (0.5 * gate_value[:, None] * grad_out).astype(jnp.bfloat16)
-    gate_grad = 0.5 * jnp.sum(expert_rows * grad_out, 1)
-    logit_grad = (gate_grad * gate_value)[:, None] * (onehot - router_probs)
-    row_gradients = to_experts(
-        scatter_rows(sent_grad, slot_index, local_experts, peer_count, capacity)
-    )
-    row_gradients = row_gradients.reshape(local_experts, row_total, model_width)
+        "gzm,gmb->gzb", hidden, output_weight, preferred_element_type=jnp.float32
+    ).astype(jnp.bfloat16)
+    return (preactivation, hidden, produced)
+
+
+def expert_backward(row_grads, arrived_rows, preactivation, hidden, input_weight, output_weight):
+    hidden_grad = jnp.einsum(
+        "ysi,yzi->ysz", row_grads, output_weight, preferred_element_type=jnp.float32
+    )
+    preactivation_grad = (hidden_grad * silu_slope(preactivation)).astype(jnp.bfloat16)
+    input_grad = jnp.einsum(
+        "wot,wqt->woq", preactivation_grad, input_weight, preferred_element_type=jnp.float32
+    ).astype(jnp.bfloat16)
     out_weight_grad = jnp.einsum(
-        "ymv,yml->yvl", hidden_reduced, row_gradients, preferred_element_type=jnp.float32
-    )
-    hidden_grad = jnp.einsum(
-        "ysi,yzi->ysz", row_gradients, output_weight, preferred_element_type=jnp.float32
-    )
-    preactivation_grad = (hidden_grad * silu_slope(preactivation)).astype(jnp.bfloat16)
+        "ymv,yml->yvl", hidden, row_grads, preferred_element_type=jnp.float32
+    ).astype(jnp.bfloat16)
     in_weight_grad = jnp.einsum(
         "keo,keu->kou", arrived_rows, preactivation_grad, preferred_element_type=jnp.float32
-    )
-    input_grad = jnp.einsum(
-        "wot,wqt->woq", preactivation_grad, input_weight, preferred_element_type=jnp.float32
-    ).astype(jnp.bfloat16)
-    returned = from_experts(input_grad.reshape(local_experts, peer_count, capacity, model_width))
-    normed_grad = returned.reshape(-1, model_width)[slot_index].astype(jnp.float32)
-    rows_grad, gain_grad = norm_backward(normed_grad, gain_row, normed, inverse)
-    return (grad_out + rows_grad, gain_grad, logit_grad, in_weight_grad, out_weight_grad)
+    ).astype(jnp.bfloat16)
+    return (input_grad, in_weight_grad, out_weight_grad)
 
 
 def shards(
@@ -316,46 +342,95 @@
     cotangent,
 ):
     row_count, model_width = frames.shape
-    own_lengths = lax.dynamic_index_in_dim(
-        lengths, lax.axis_index(("dp", "expert")), 0, keepdims=False
-    )
+    router_count, slice_width, expert_total = routers.shape
+    tap_count = conv_kernel.shape[0]
+    gain_count = norm_gains.shape[0]
+    peer_count = lax.axis_size("expert")
+    dp_count = lax.axis_size("dp")
+    device_total = peer_count * dp_count
+    local_experts = expert_in.shape[1]
+    capacity = 2 * row_count // expert_total
+    dp_bits = bit_count(("dp",))
+    expert_bits = bit_count(("expert",))
+    hidden_width = expert_in.shape[3]
+    slots = peer_count * capacity
+
+    def scattered(rows_low, slot_index):
+        return scatter_rows(rows_low, slot_index, local_experts, peer_count, capacity)
+
+    def arrived_of(sent):
+        return to_experts(sent).reshape(local_experts, slots, model_width)
+
+    def returned_of(back, slot_index):
+        back = from_experts(back.reshape(local_experts, peer_count, capacity, model_width))
+        return back.reshape(-1, model_width)[slot_index].astype(jnp.float32)
+
+    slot_first, onehot_first = expert_slots(
+        choice_first, expert_total, capacity, local_experts, peer_count
+    )
+    slot_second, onehot_second = expert_slots(
+        choice_second, expert_total, capacity, local_experts, peer_count
+    )
+    arrived_frames = arrived_of(scattered(frames, slot_first))
+    dp_order = list(range(dp_bits))
+    outer_bits = dp_order[1:]
+    first_in = all_gather_bits(expert_in[0], ("dp",), outer_bits + [0])
+    first_out = all_gather_bits(expert_out[0], ("dp",), outer_bits[::-1] + [0])
+
+    def whole_weight(pieces, depth):
+        pieces = pieces.reshape((dp_count,) + pieces.shape[dp_bits:])
+        return jnp.moveaxis(pieces, 0, 1).reshape(local_experts, depth, -1)
+
+    first_in = whole_weight(first_in, model_width)
+    first_out = whole_weight(first_out, hidden_width)
+    small_width = router_count * expert_total + gain_count + tap_count + 1
+    small = jnp.concatenate(
+        [
+            jnp.moveaxis(routers, 1, 0).reshape(slice_width, -1),
+            norm_gains.T,
+            conv_kernel.T,
+            bn_shift[:, None],
+            jnp.zeros((slice_width, -small_width % 128), jnp.bfloat16),
+        ],
+        1,
+    )
+    dense = lax.all_gather(
+        jnp.concatenate([attn_in, attn_out, conv_in, conv_out, small], 1), AXES, axis=0, tiled=True
+    )
+    second_in = lax.all_gather(expert_in[1], "dp", axis=1, tiled=True)
+    second_out = lax.all_gather(expert_out[1], "dp", axis=1, tiled=True)
+
+    width = model_width
+    attn_in_all = dense[:, : 3 * width]
+    attn_out_all = dense[:, 3 * width : 4 * width]
+    conv_in_all = dense[:, 4 * width : 6 * width]
+    conv_out_all = dense[:, 6 * width : 7 * width]
+    small_all = dense[:, 7 * width :].astype(jnp.float32)
+    start = router_count * expert_total
+    router_pair = jnp.moveaxis(small_all[:, :start].reshape(width, router_count, expert_total), 1, 0)
+    gain_rows = small_all[:, start : start + gain_count].T
+    kernel = small_all[:, start + gain_count : start + gain_count + tap_count].T
+    shift_row = small_all[:, start + gain_count + tap_count]
+
+    own_lengths = lax.dynamic_index_in_dim(lengths, lax.axis_index(AXES), 0, keepdims=False)
     segment, offsets, validity = segments(own_lengths, row_count)
     frame_count = jnp.sum(lengths[:, :-1]).astype(jnp.float32)
     block_rows = min(512, row_count)
     cosine, sine_table = rotation(offsets, DH)
-    (
-        routers_all,
-        gains_all,
-        attn_in_all,
-        attn_out_all,
-        conv_in_all,
-        kernel_all,
-        shift_all,
-        conv_out_all,
-    ) = (
-        lax.all_gather(routers, ("dp", "expert"), axis=1, tiled=True),
-        lax.all_gather(norm_gains, ("dp", "expert"), axis=1, tiled=True),
-        lax.all_gather(attn_in, ("dp", "expert"), axis=0, tiled=True),
-        lax.all_gather(attn_out, ("dp", "expert"), axis=0, tiled=True),
-        lax.all_gather(conv_in, ("dp", "expert"), axis=0, tiled=True),
-        lax.all_gather(conv_kernel, ("dp", "expert"), axis=1, tiled=True),
-        lax.all_gather(bn_shift, ("dp", "expert"), axis=0, tiled=True),
-        lax.all_gather(conv_out, ("dp", "expert"), axis=0, tiled=True),
-    )
-    experts_in_all, experts_out_all = (
-        lax.all_gather(expert_in, "dp", axis=2, tiled=True),
-        lax.all_gather(expert_out, "dp", axis=2, tiled=True),
-    )
-    first_in, second_in = (experts_in_all[0], experts_in_all[1])
-    first_out, second_out = (experts_out_all[0], experts_out_all[1])
-    gain_rows = gains_all.astype(jnp.float32)
-    router_pair = routers_all.astype(jnp.float32)
     rows_in = frames.astype(jnp.float32)
     embed_pre = jnp.dot(frames, embed_weight, preferred_element_type=jnp.float32)
     embedded = jax.nn.silu(embed_pre)
-    after_first, saved_first = moe_forward(
-        rows_in, gain_rows[0], embedded, router_pair[0], choice_first, first_in, first_out
-    )
+    probs_first, gate_first = gates(embedded, router_pair[0], onehot_first)
+    probs_second, gate_second = gates(embedded, router_pair[1], onehot_second)
+
+    first_norm, first_hat_arrived, _ = norm_forward(
+        arrived_frames.astype(jnp.float32), gain_rows[0]
+    )
+    first_arrived = first_norm.astype(jnp.bfloat16)
+    first_pre, first_hidden, first_produced = expert_forward(first_arrived, first_in, first_out)
+    first_expert = returned_of(first_produced, slot_first)
+    after_first = rows_in + 0.5 * gate_first[:, None] * first_expert
+
     attn_norm, attn_hat, attn_inverse = norm_forward(after_first, gain_rows[1])
     attn_low = attn_norm.astype(jnp.bfloat16)
     projected = jnp.dot(attn_low, attn_in_all, preferred_element_type=jnp.float32)
@@ -376,32 +451,47 @@
     gates_in = jnp.dot(conv_low, conv_in_all, preferred_element_type=jnp.float32)
     logistic = jax.nn.sigmoid(gates_in[:, model_width:])
     glu_out = gates_in[:, :model_width] * logistic
-    kernel = kernel_all.astype(jnp.float32)
     conv_depth = depthwise(glu_out, kernel, segment)
     weighted = validity[:, None] * conv_depth
-    first_sum, second_sum = lax.psum(
-        (jnp.sum(weighted, 0), jnp.sum(weighted * conv_depth, 0)), ("dp", "expert")
-    )
-    batch_mean = first_sum / frame_count
-    batch_var = second_sum / frame_count - batch_mean * batch_mean
+    moments = sum_everywhere(jnp.stack([jnp.sum(weighted, 0), jnp.sum(weighted * conv_depth, 0)]))
+    batch_mean = moments[0] / frame_count
+    batch_var = moments[1] / frame_count - batch_mean * batch_mean
     batch_inverse = lax.rsqrt(batch_var + EPSILON)
     centred_depth = conv_depth - batch_mean
     batch_hat = centred_depth * batch_inverse
-    batch_out = batch_hat * gain_rows[5] + shift_all.astype(jnp.float32)
+    batch_out = batch_hat * gain_rows[5] + shift_row
     swish_low = jax.nn.silu(batch_out).astype(jnp.bfloat16)
     after_conv = after_attention + jnp.dot(
         swish_low, conv_out_all, preferred_element_type=jnp.float32
     )
-    after_second, saved_second = moe_forward(
-        after_conv, gain_rows[3], embedded, router_pair[1], choice_second, second_in, second_out
-    )
+
+    second_norm, second_hat, second_inverse = norm_forward(after_conv, gain_rows[3])
+    second_arrived = arrived_of(scattered(second_norm.astype(jnp.bfloat16), slot_second))
+    second_pre, second_hidden, second_produced = expert_forward(
+        second_arrived, second_in, second_out
+    )
+    second_expert = returned_of(second_produced, slot_second)
+    after_second = after_conv + 0.5 * gate_second[:, None] * second_expert
     final_norm, final_hat, final_inverse = norm_forward(after_second, gain_rows[4])
     block_out = (final_norm * validity[:, None]).astype(jnp.bfloat16)
+
     grad_final = cotangent.astype(jnp.float32) * validity[:, None]
     grad_second, final_gain_grad = norm_backward(grad_final, gain_rows[4], final_hat, final_inverse)
-    grad_conv, second_gain_grad, second_logit_grad, second_in_grad, second_out_grad = moe_backward(
-        grad_second, gain_rows[3], second_in, second_out, saved_second
-    )
+    second_sent = (0.5 * gate_second[:, None] * grad_second).astype(jnp.bfloat16)
+    second_row_grads = arrived_of(scattered(second_sent, slot_second))
+    second_gate_grad = 0.5 * jnp.sum(second_expert * grad_second, 1)
+    second_logit_grad = (second_gate_grad * gate_second)[:, None] * (onehot_second - probs_second)
+    second_input_grad, second_in_grad, second_out_grad = expert_backward(
+        second_row_grads, second_arrived, second_pre, second_hidden, second_in, second_out
+    )
+    second_norm_grad = returned_of(second_input_grad, slot_second)
+    rows_grad, second_gain_grad = norm_backward(
+        second_norm_grad, gain_rows[3], second_hat, second_inverse
+    )
+    grad_conv = grad_second + rows_grad
+    second_in_grad = lax.psum_scatter(second_in_grad, "dp", scatter_dimension=1, tiled=True)
+    second_out_grad = lax.psum_scatter(second_out_grad, "dp", scatter_dimension=1, tiled=True)
+
     conv_grad_low = grad_conv.astype(jnp.bfloat16)
     conv_out_grad = jnp.einsum(
         "td,te->de", swish_low, conv_grad_low, preferred_element_type=jnp.float32
@@ -413,9 +503,10 @@
     shift_grad = jnp.sum(batch_grad, 0)
     bn_gain_grad = jnp.sum(batch_grad * batch_hat, 0)
     hat_grad = batch_grad * gain_rows[5]
-    hat_total, hat_moment = lax.psum(
-        (jnp.sum(hat_grad, 0), jnp.sum(hat_grad * centred_depth, 0)), ("dp", "expert")
-    )
+    hat_sums = sum_everywhere(
+        jnp.stack([jnp.sum(hat_grad, 0), jnp.sum(hat_grad * centred_depth, 0)])
+    )
+    hat_total, hat_moment = (hat_sums[0], hat_sums[1])
     var_grad = -0.5 * hat_moment * batch_inverse * batch_inverse * batch_inverse
     mean_grad = -batch_inverse * hat_total - 2.0 * batch_mean * var_grad
     depth_grad = (
@@ -462,74 +553,99 @@
     )
     rows_grad, attn_gain_grad = norm_backward(attn_norm_grad, gain_rows[1], attn_hat, attn_inverse)
     grad_first = grad_attention + rows_grad
-    grad_input, first_gain_grad, first_logit_grad, first_in_grad, first_out_grad = moe_backward(
-        grad_first, gain_rows[0], first_in, first_out, saved_first
-    )
+
+    first_sent = (0.5 * gate_first[:, None] * grad_first).astype(jnp.bfloat16)
+    first_row_grads = arrived_of(scattered(first_sent, slot_first))
+    first_gate_grad = 0.5 * jnp.sum(first_expert * grad_first, 1)
+    first_logit_grad = (first_gate_grad * gate_first)[:, None] * (onehot_first - probs_first)
+
+    def to_owners(term):
+        term = lax.psum_scatter(term.astype(jnp.bfloat16), "dp", scatter_dimension=0, tiled=True)
+        return lax.psum_scatter(term, "expert", scatter_dimension=0, tiled=True).astype(jnp.float32)
+
+    conv_terms = to_owners(jnp.concatenate([attn_out_grad, conv_in_grad, conv_out_grad], 1))
+    attn_terms = to_owners(attn_in_grad)
+
     embed_rows_grad = jnp.dot(first_logit_grad, router_pair[0].T, precision=HIGHEST) + jnp.dot(
         second_logit_grad, router_pair[1].T, precision=HIGHEST
     )
     embed_pre_grad = (embed_rows_grad * silu_slope(embed_pre)).astype(jnp.bfloat16)
-    embed_total = lax.psum(
-        jnp.einsum("td,te->de", frames, embed_pre_grad, preferred_element_type=jnp.float32),
-        ("dp", "expert"),
-    )
-    frames_grad = grad_input + jnp.einsum(
+    embed_term = jnp.einsum("td,te->de", frames, embed_pre_grad, preferred_element_type=jnp.float32)
+    all_bits = dp_bits + expert_bits
+    order = spread_order(AXES)
+    embed_own = reduce_scatter_bits(
+        embed_term.astype(jnp.bfloat16).reshape((2,) * all_bits + (slice_width, width)), AXES, order
+    )
+    embed_total = (
+        all_gather_bits(embed_own, AXES, order[::-1]).reshape(width, width).astype(jnp.float32)
+    )
+    embed_rows = jnp.einsum(
         "te,de->td", embed_pre_grad, embed_weight, preferred_element_type=jnp.float32
     )
-    router_terms = jnp.stack(
+
+    first_input_grad, first_in_grad, first_out_grad = expert_backward(
+        first_row_grads, first_arrived, first_pre, first_hidden, first_in, first_out
+    )
+    first_gain_grad = jnp.sum(first_input_grad.astype(jnp.float32) * first_hat_arrived, (0, 1))
+
+    def to_expert_owners(term, order):
+        pieces = term.reshape(local_experts, dp_count, -1, term.shape[2])
+        pieces = jnp.moveaxis(pieces, 1, 0)
+        pieces = pieces.reshape((2,) * dp_bits + pieces.shape[1:])
+        return reduce_scatter_bits(pieces, ("dp",), order)
+
+    first_out_own = to_expert_owners(first_out_grad, [0] + outer_bits[::-1])
+    first_in_own = to_expert_owners(first_in_grad, [0] + outer_bits)
+
+    router_terms = jnp.concatenate(
         [
             jnp.dot(embedded.T, first_logit_grad, precision=HIGHEST),
             jnp.dot(embedded.T, second_logit_grad, precision=HIGHEST),
-        ]
-    )
-    gain_terms = jnp.stack(
+        ],
+        1,
+    ).T
+    small_terms = jnp.concatenate(
         [
-            first_gain_grad,
-            attn_gain_grad,
-            conv_gain_grad,
-            second_gain_grad,
-            final_gain_grad,
-            bn_gain_grad,
-        ]
-    )
-    dense_parts = (
-        lax.psum_scatter(router_terms, ("dp", "expert"), scatter_dimension=1, tiled=True),
-        lax.psum_scatter(gain_terms, ("dp", "expert"), scatter_dimension=1, tiled=True),
-        lax.psum_scatter(attn_in_grad, ("dp", "expert"), scatter_dimension=0, tiled=True),
-        lax.psum_scatter(attn_out_grad, ("dp", "expert"), scatter_dimension=0, tiled=True),
-        lax.psum_scatter(conv_in_grad, ("dp", "expert"), scatter_dimension=0, tiled=True),
-        lax.psum_scatter(kernel_grad, ("dp", "expert"), scatter_dimension=1, tiled=True),
-        lax.psum_scatter(shift_grad, ("dp", "expert"), scatter_dimension=0, tiled=True),
-        lax.psum_scatter(conv_out_grad, ("dp", "expert"), scatter_dimension=0, tiled=True),
-    )
-    expert_parts = (
-        lax.psum_scatter(
-            jnp.stack([first_in_grad, second_in_grad]).astype(jnp.bfloat16),
-            "dp",
-            scatter_dimension=2,
-            tiled=True,
-        ).astype(jnp.float32),
-        lax.psum_scatter(
-            jnp.stack([first_out_grad, second_out_grad]).astype(jnp.bfloat16),
-            "dp",
-            scatter_dimension=2,
-            tiled=True,
-        ).astype(jnp.float32),
-    )
+            router_terms,
+            first_gain_grad[None],
+            attn_gain_grad[None],
+            conv_gain_grad[None],
+            second_gain_grad[None],
+            final_gain_grad[None],
+            bn_gain_grad[None],
+            kernel_grad,
+            shift_grad[None],
+        ],
+        0,
+    )
+    small_sums = lax.dynamic_slice_in_dim(
+        sum_everywhere(small_terms), lax.axis_index(AXES) * slice_width, slice_width, 1
+    )
+    routers_out = jnp.moveaxis(
+        small_sums[:start].reshape(router_count, expert_total, slice_width), 1, 2
+    )
+    gains_out = small_sums[start : start + gain_count]
+    kernel_out = small_sums[start + gain_count : start + gain_count + tap_count]
+    shift_out = small_sums[start + gain_count + tap_count]
+
+    first_norm_grad = returned_of(first_input_grad, slot_first)
+    _, first_hat, first_inverse = norm_forward(rows_in, gain_rows[0])
+    rows_grad, _ = norm_backward(first_norm_grad, gain_rows[0], first_hat, first_inverse)
+    frames_grad = grad_first + rows_grad + embed_rows
     return (
         block_out,
         frames_grad,
         embed_total,
-        dense_parts[0],
-        dense_parts[1],
-        dense_parts[2],
-        dense_parts[3],
-        dense_parts[4],
-        dense_parts[5],
-        dense_parts[6],
-        dense_parts[7],
-        expert_parts[0],
-        expert_parts[1],
+        routers_out,
+        gains_out,
+        attn_terms,
+        conv_terms[:, :width],
+        conv_terms[:, width : 3 * width],
+        kernel_out,
+        shift_out,
+        conv_terms[:, 3 * width :],
+        jnp.stack([first_in_own, second_in_grad]).astype(jnp.float32),
+        jnp.stack([first_out_own, second_out_grad]).astype(jnp.float32),
     )
 
 

time: 1960 us -> 613 us (0.31)
  waiting for transfers between devices: 1120 us -> 208 us
  blocking collectives: 535 us -> 56.7 us
  starting transfers between devices: 35 us -> 74 us
    reduce_scatter x6, waiting for transfers between devices: 617 us -> 32.7 us  [the longest x2 32.7 us: to_owners(): lax.psum_scatter(term.astype(jnp.bfloat16), 'dp', scatter_dimension=0, ti...]
    all_gather x5 -> x0, blocking collectives: 360 us -> none  [the longest x1 83 us: shards(): lax.all_gather(attn_out, ('dp', 'expert'), axis=0, tiled=True)]
    unnamed x17 -> x9, waiting for transfers between devices: 301 us -> 0.84 us
    psum x1 -> x0, waiting for transfers between devices: 130 us -> none  [shards(): lax.psum(jnp.einsum('td,te->de', frames, embed_pre_grad, preferred_elemen...]
    ppermute x0 -> x43, waiting for transfers between devices: none -> 78.3 us  [exchange(): return lax.ppermute(values, axes, [(i, i ^ mask) for i in range(total)])]
    psum x2 -> x0, blocking collectives: 77.5 us -> none  [the longest x1 39.4 us: shards(): lax.psum((jnp.sum(weighted, 0), jnp.sum(weighted * conv_depth, 0)), ('dp'...]
    ppermute x0 -> x43, starting transfers between devices: none -> 48.9 us  [exchange(): return lax.ppermute(values, axes, [(i, i ^ mask) for i in range(total)])]
    unnamed x1 -> x0, blocking collectives: 39.9 us -> none
  transfers between devices with their start and end apart: 20 -> 58, of which waited for: 14 -> 33; matrix products, arithmetic and copies ran while one was open for 7% -> 28% of each run, Pallas kernels for 0% -> 0%
where the time goes in v1:
time: 613 us; the launch traced here: 603 us
  waiting for transfers between devices  208 us (34%)
  matrix products  106 us (17%)
  other arithmetic  81.7 us (13%)
  starting transfers between devices  74 us (12%)
  local copies, waits for them, and re-layouts  58.9 us (10%)
  blocking collectives  56.7 us (9%)
  between operations  18.3 us (3%)
    ppermute x43, waiting for transfers between devices, exchange(): return lax.ppermute(values, axes, [(i, i ^ mask) for i in range(total)])  78.3 us
    ppermute x43, starting transfers between devices, exchange(): return lax.ppermute(values, axes, [(i, i ^ mask) for i in range(total)])  48.9 us
    all_to_all x3, waiting for transfers between devices, to_experts(): lax.all_to_all(sent_rows, 'expert', split_axis=1, concat_axis=1, tiled=True)  43.8 us
    all_to_all x3, waiting for transfers between devices, from_experts(): lax.all_to_all(back_rows, 'expert', split_axis=1, concat_axis=1, tiled=True)  40.3 us
    reduce_scatter x2, waiting for transfers between devices, to_owners(): lax.psum_scatter(term.astype(jnp.bfloat16), 'dp', scatter_dimension=0, ti...  32.7 us
    all_to_all x1, blocking collectives, to_experts(): lax.all_to_all(sent_rows, 'expert', split_axis=1, concat_axis=1, tiled=True)  28.7 us
    all_to_all x1, blocking collectives, from_experts(): lax.all_to_all(back_rows, 'expert', split_axis=1, concat_axis=1, tiled=True)  28 us
    dot_general x2, matrix products, expert_backward(): jnp.einsum('ysi,yzi->ysz', row_grads, output_weight, preferred_element_ty...  15.2 us
  transfers between devices with their start and end apart: 58, of which 33 were waited for; matrix products, arithmetic and copies ran while one was open for 28% of the time, Pallas kernels for 0%

profile of v1, /device:TPU:0, one launch (start us, length us, event | category | flops | bytes accessed | tf_op | source)
XLA Modules:
  0.0 603.1 jit_solution(1681709075983066149)
XLA Ops:
  13.9 3.0 collective-permute-start
  26.9 4.0 scatter_custom_fusion
  30.9 4.9 all-to-all-start
  40.6 13.0 %collective-permute-done.4 = bf16[2,1,256,512]{3,2,0,1:T(8,128)(2,1)S(1)} collective-permute-done((bf16[2,1,256,512]{3,2,0,1:T(8,128)(2,1)S(1)}, bf16[2,1,256,512]{3,2,0,1:T(8,128)(2,1)S(1)}, u32[]{:S(2)}, u32[]{:S(2)}) %collective-permute-start.4) | collective-permute-done | bytes 524320 | tf_op jit(solution)/shard_map/ppermute | solution.py:31
  56.5 9.5 %all-to-all-done = bf16[1,4,256,512]{3,2,0,1:T(8,128)(2,1)S(1)} async-done(((bf16[1,4,256,512]{3,2,0,1:T(8,128)(2,1)}), bf16[1,4,256,512]{3,2,0,1:T(8,128)(2,1)S(1)}, u32[]{:S(2)}, u32[]{:S(2)}) %all-to-all-start) | async-done | bytes 1048608 | tf_op jit(solution)/shard_map/all_to_all | solution.py:286
  72.7 11.8 %all-gather.6.cloned.1.call-done = bf16[512,3712]{1,0:T(8,128)(2,1)} async-done(((bf16[16,3712]{1,0:T(8,128)(2,1)}), bf16[512,3712]{1,0:T(8,128)(2,1)}) %all-gather.6.cloned.1.call-update) | async-done | bytes 3801104 | tf_op jit(solution)/shard_map/all_gather | solution.py:397
  87.5 5.3 multiply_convert_fusion.4
  92.9 3.3 convolution_convert_fusion.7
  96.2 3.8 all-to-all-start.1
  104.7 2.6 slice_reduce_fusion.19
  107.3 19.0 %all-to-all-done.1 = bf16[1,4,256,512]{3,2,0,1:T(8,128)(2,1)S(1)} async-done(((bf16[1,4,256,512]{3,2,0,1:T(8,128)(2,1)}), bf16[1,4,256,512]{3,2,0,1:T(8,128)(2,1)S(1)}, u32[]{:S(2)}, u32[]{:S(2)}) %all-to-all-start.1) | async-done | bytes 1048608 | tf_op jit(solution)/shard_map/all_to_all | solution.py:290
  126.4 2.8 gather_fusion
  132.1 2.7 fusion.26
  146.0 2.7 fusion.34
  153.7 3.8 multiply_reduce_fusion.3
  166.7 3.0 collective-permute-start.10
  173.6 3.6 scatter_custom_fusion.1
  177.2 3.6 all-to-all-start.2
  180.9 23.0 %all-to-all-done.2 = bf16[1,4,256,512]{3,2,0,1:T(8,128)(2,1)S(1)} async-done(((bf16[1,4,256,512]{3,2,0,1:T(8,128)(2,1)}), bf16[1,4,256,512]{3,2,0,1:T(8,128)(2,1)S(1)}, u32[]{:S(2)}, u32[]{:S(2)}) %all-to-all-start.2) | async-done | bytes 1048608 | tf_op jit(solution)/shard_map/all_to_all | solution.py:286
  203.9 8.1 %multiply_convert_fusion.3 = (bf16[1024,2048]{1,0:T(8,128)(2,1)}, f32[1024,2048]{1,0:T(8,128)}) fusion(bf16[1024,512]{1,0:T(8,128)(2,1)S(1)} %bitcast.390, bf16[1,1,512,2048]{3,2,1,0:T(8,128)(2,1)} %all-gather.8.cloned.1.call-done), kind=kOutput, calls=%fused_computation.13 | convolution fusion | flops 2157969408 | bytes 15728640 | tf_op jit(solution)/shard_map/zve,zeg->zvg/dot_general | solution.py:299
  212.0 6.2 %fusion.21 = bf16[1024,512]{1,0:T(8,128)(2,1)} fusion(bf16[1024,2048]{1,0:T(8,128)(2,1)} %get-tuple-element.235, bf16[1,1,2048,512]{3,2,1,0:T(8,128)(2,1)} %all-gather.10.cloned.1.call-done), kind=kOutput, calls=%fused_computation.61 | convolution fusion | flops 2148007936 | bytes 7340032 | tf_op jit(solution)/shard_map/gzm,gmb->gzb/dot_general | solution.py:303
  218.2 3.5 all-to-all-start.3
  225.4 21.2 %all-to-all-done.3 = bf16[1,4,256,512]{3,2,0,1:T(8,128)(2,1)S(1)} async-done(((bf16[1,4,256,512]{3,2,0,1:T(8,128)(2,1)}), bf16[1,4,256,512]{3,2,0,1:T(8,128)(2,1)S(1)}, u32[]{:S(2)}, u32[]{:S(2)}) %all-to-all-start.3) | async-done | bytes 1048608 | tf_op jit(solution)/shard_map/all_to_all | solution.py:290
  246.6 3.1 gather_fusion.1
  255.4 3.7 scatter_custom_fusion.2
  259.0 28.7 %all_to_all.40 = bf16[1,4,256,512]{3,2,0,1:T(8,128)(2,1)S(1)} all-to-all(bf16[1,4,256,512]{3,2,0,1:T(8,128)(2,1)} %bitcast.375), channel_id=1, replica_groups=mesh['dp'=8,'expert'=4] {'expert'}, dimensions={1} | all-to-all | bytes 2097152 | tf_op jit(solution)/shard_map/all_to_all | solution.py:286
  287.7 7.1 %multiply_convert_fusion.2 = bf16[1024,2048]{1,0:T(8,128)(2,1)S(1)} fusion(f32[1024,2048]{1,0:T(8,128)} %get-tuple-element.236, bf16[1024,512]{1,0:T(8,128)(2,1)S(1)} %bitcast.392, bf16[1,1,2048,512]{3,2,1,0:T(8,128)(2,1)} %all-gather.10.cloned.1.call-done), kind=kOutput, calls=%fused_computation.12 | convolution fusion | flops 2166358016 | bytes 15728640 | tf_op jit(solution)/shard_map/ysi,yzi->ysz/dot_general | solution.py:310
  294.9 2.4 fusion.18
  297.3 28.0 %all_to_all.41 = bf16[1,4,256,512]{3,2,0,1:T(8,128)(2,1)S(1)} all-to-all(bf16[1,4,256,512]{3,2,0,1:T(8,128)(2,1)S(1)} %bitcast.397), channel_id=1, replica_groups=mesh['dp'=8,'expert'=4] {'expert'}, dimensions={1} | all-to-all | bytes 2097152 | tf_op jit(solution)/shard_map/all_to_all | solution.py:290
  325.3 2.6 gather_fusion.2
  327.9 2.3 fusion.83
  342.6 2.7 collective-permute-start.17
  347.1 3.3 multiply_reduce_fusion.4
  352.6 2.5 multiply_convert_fusion.9
  360.9 3.0 multiply_reduce_fusion
  363.9 2.9 multiply_convert_fusion.1
  370.5 2.5 convolution_convert_fusion.4
  373.2 3.2 convolution_convert_fusion.8
  378.2 32.7 %reduce-scatter.7.cloned.1.call-done = bf16[64,1536]{1,0:T(8,128)(2,1)} async-done(((bf16[512,1536]{1,0:T(8,128)(2,1)}), bf16[64,1536]{1,0:T(8,128)(2,1)}) %reduce-scatter.7.cloned.1.call-update) | async-done | bytes 196624 | tf_op jit(solution)/shard_map/reduce_scatter | solution.py:563
  413.5 3.2 pad_maximum_fusion.2
  417.1 3.3 multiply_reduce_fusion.22
  425.8 3.7 fusion.7
  431.7 4.1 collective-permute-done.21
  437.4 2.8 collective-permute-done.22
  441.8 2.4 collective-permute-done.23
  444.2 2.6 collective-permute-start.24
  446.9 2.1 collective-permute-done.24
  448.9 2.7 collective-permute-start.25
  459.2 6.3 %fusion.6 = bf16[1,512,2048]{2,1,0:T(8,128)(2,1)} fusion(bf16[1024,512]{1,0:T(8,128)(2,1)} %bitcast.391, bf16[1024,2048]{1,0:T(8,128)(2,1)} %copy-done.206), kind=kOutput, calls=%fused_computation.30 | convolution fusion | flops 2148532224 | bytes 7340032 | tf_op jit(solution)/shard_map/keo,keu->kou/dot_general | solution.py:320
  465.6 3.7 scatter_custom_fusion.3
  469.2 4.7 all-to-all-start.6
  475.3 3.7 collective-permute-done.28
  481.9 11.2 %all-to-all-done.6 = bf16[1,4,256,512]{3,2,0,1:T(8,128)(2,1)} async-done(((bf16[1,4,256,512]{3,2,0,1:T(8,128)(2,1)}), bf16[1,4,256,512]{3,2,0,1:T(8,128)(2,1)}, u32[]{:S(2)}, u32[]{:S(2)}) %all-to-all-start.6) | async-done | bytes 1048608 | tf_op jit(solution)/shard_map/all_to_all | solution.py:286
  493.2 8.1 %multiply_convert_fusion = bf16[1024,2048]{1,0:T(8,128)(2,1)S(1)} fusion(f32[1024,2048]{1,0:T(8,128)} %get-tuple-element.224, bf16[1024,512]{1,0:T(8,128)(2,1)} %bitcast.89, bf16[2048,512]{1,0:T(8,128)(2,1)} %bitcast.383), kind=kOutput, calls=%fused_computation.8 | convolution fusion | flops 2166358016 | bytes 15728640 | tf_op jit(solution)/shard_map/ysi,yzi->ysz/dot_general | solution.py:310
  501.6 3.5 multiply_convert_fusion.5
  505.5 4.6 convolution_convert_fusion.3
  516.4 5.2 convolution_convert_fusion.1
  521.6 3.5 all-to-all-start.7
  525.3 3.8 collective-permute-start.36
  531.1 17.5 %collective-permute-done.36 = f32[30,512]{1,0:T(8,128)S(1)} collective-permute-done((f32[30,512]{1,0:T(8,128)S(1)}, f32[30,512]{1,0:T(8,128)S(1)}, u32[]{:S(2)}, u32[]{:S(2)}) %collective-permute-start.36) | collective-permute-done | bytes 61472 | tf_op jit(solution)/shard_map/ppermute | solution.py:31
  548.6 7.4 %collective-permute-done.35 = f32[30,512]{1,0:T(8,128)S(1)} collective-permute-done((f32[30,512]{1,0:T(8,128)S(1)}, f32[30,512]{1,0:T(8,128)S(1)}, u32[]{:S(2)}, u32[]{:S(2)}) %collective-permute-start.35) | collective-permute-done | bytes 61472 | tf_op jit(solution)/shard_map/ppermute | solution.py:31
  567.9 2.6 gather_fusion.3
  570.6 6.6 %collective-permute-done.38 = bf16[2,1,64,2048]{3,2,1,0:T(8,128)(2,1)} collective-permute-done((bf16[2,1,64,2048]{3,2,1,0:T(8,128)(2,1)}, bf16[2,1,64,2048]{3,2,1,0:T(8,128)(2,1)}, u32[]{:S(2)}, u32[]{:S(2)}) %collective-permute-start.38) | collective-permute-done | bytes 524320 | tf_op jit(solution)/shard_map/ppermute | solution.py:31
  586.2 3.3 collective-permute-done.42
  (722 shorter events, 166.9 us)
Async XLA Ops:
  7.2 94.2 %copy-start = (bf16[512,512]{1,0:T(8,128)(2,1)S(1)}, bf16[512,512]{1,0:T(8,128)(2,1)}, u32[]{:S(2)}) copy-start(bf16[512,512]{1,0:T(8,128)(2,1)} %param.20) | copy-start | bytes 1572868
  7.2 77.3 %all-gather.6.cloned.1.call-start = ((), (), s32[]{:S(2)}) async-start(), calls=%async_computation.14 | async-start | bytes 3919872 | tf_op jit(solution)/shard_map/all_gather | solution.py:397
  12.0 168.9 %all-gather.8.cloned.1.call-start = ((), (), s32[]{:S(2)}) async-start(), calls=%async_computation.21 | async-start | bytes 2359296 | tf_op jit(solution)/shard_map/all_gather | solution.py:400
  13.9 24.1 %collective-permute-start = (bf16[1,64,2048]{2,1,0:T(8,128)(2,1)}, bf16[1,64,2048]{2,1,0:T(8,128)(2,1)}, u32[]{:S(2)}, u32[]{:S(2)}) collective-permute-start(bf16[1,64,2048]{2,1,0:T(8,128)(2,1)} %get-tuple-element.186), channel_id=1, source_target_pairs={{0,8},{4,12},{8,0},{12,4},{16,24},{20,28},{24,16},{28,20},{1,9},{5... | collective-permute-start | bytes 786440 | tf_op jit(solution)/shard_map/ppermute | solution.py:31
  18.7 18.6 %collective-permute-start.3 = (bf16[1,256,512]{2,1,0:T(8,128)(2,1)S(1)}, bf16[1,256,512]{2,1,0:T(8,128)(2,1)S(1)}, u32[]{:S(2)}, u32[]{:S(2)}) collective-permute-start(bf16[1,256,512]{2,1,0:T(8,128)(2,1)S(1)} %get-tuple-element.184), channel_id=1, source_target_pairs={{0,16},{4,20},{8,24},{12,28},{16,0},{20,4},{24,8},{28,12},{1,17},{... | collective-permute-start | bytes 786440 | tf_op jit(solution)/shard_map/ppermute | solution.py:31
  26.9 73.8 %copy-start.184 = (s32[512,1]{0,1:T(1,128)}, s32[512,1]{0,1:T(1,128)S(1)}, u32[]{:S(2)}) copy-start(s32[512,1]{0,1:T(1,128)S(1)} %compare_select_fusion.1) | copy-start | bytes 6148
  30.9 35.2 %all-to-all-start = ((bf16[1,4,256,512]{3,2,0,1:T(8,128)(2,1)}), bf16[1,4,256,512]{3,2,0,1:T(8,128)(2,1)S(1)}, u32[]{:S(2)}, u32[]{:S(2)}) async-start(bf16[1,4,256,512]{3,2,0,1:T(8,128)(2,1)} %bitcast.13), calls=%async_computation | async-start | bytes 2097152 | tf_op jit(solution)/shard_map/all_to_all | solution.py:286
  35.7 176.3 %all-gather.10.cloned.1.call-start = ((), (), s32[]{:S(2)}) async-start(), calls=%async_computation.22 | async-start | bytes 2359296 | tf_op jit(solution)/shard_map/all_gather | solution.py:401
  37.4 16.2 %collective-permute-start.4 = (bf16[2,1,256,512]{3,2,0,1:T(8,128)(2,1)S(1)}, bf16[2,1,256,512]{3,2,0,1:T(8,128)(2,1)S(1)}, u32[]{:S(2)}, u32[]{:S(2)}) collective-permute-start(bf16[2,1,256,512]{3,2,0,1:T(8,128)(2,1)S(1)} %pad_maximum_fusion.12), channel_id=1, source_target_pairs={{0,8},{4,12},{8,0},{12,4},{16,24},{20,28},{24,16},{28,20},{1,9},{5... | collective-permute-start | bytes 1572872 | tf_op jit(solution)/shard_map/ppermute | solution.py:31
  39.1 15.7 %collective-permute-start.1 = (bf16[2,1,64,2048]{3,2,0,1:T(8,128)(2,1)S(1)}, bf16[2,1,64,2048]{3,2,0,1:T(8,128)(2,1)S(1)}, u32[]{:S(2)}, u32[]{:S(2)}) collective-permute-start(bf16[2,1,64,2048]{3,2,0,1:T(8,128)(2,1)S(1)} %pad_maximum_fusion.11), channel_id=1, source_target_pairs={{0,16},{4,20},{8,24},{12,28},{16,0},{20,4},{24,8},{28,12},{1,17},{... | collective-permute-start | bytes 1572872 | tf_op jit(solution)/shard_map/ppermute | solution.py:31
  54.8 12.1 %collective-permute-start.5 = (bf16[2,2,1,256,512]{4,3,1,0,2:T(8,128)(2,1)}, bf16[2,2,1,256,512]{4,3,1,0,2:T(8,128)(2,1)}, u32[]{:S(2)}, u32[]{:S(2)}) collective-permute-start(bf16[2,2,1,256,512]{4,3,1,0,2:T(8,128)(2,1)} %pad_maximum_fusion.5), channel_id=1, source_target_pairs={{0,4},{4,0},{8,12},{12,8},{16,20},{20,16},{24,28},{28,24},{1,5},{5... | collective-permute-start | bytes 3145736 | tf_op jit(solution)/shard_map/ppermute | solution.py:31
  56.0 13.9 %collective-permute-start.2 = (bf16[2,2,1,64,2048]{4,3,1,0,2:T(8,128)(2,1)}, bf16[2,2,1,64,2048]{4,3,1,0,2:T(8,128)(2,1)}, u32[]{:S(2)}, u32[]{:S(2)}) collective-permute-start(bf16[2,2,1,64,2048]{4,3,1,0,2:T(8,128)(2,1)} %pad_maximum_fusion.4), channel_id=1, source_target_pairs={{0,4},{4,0},{8,12},{12,8},{16,20},{20,16},{24,28},{28,24},{1,5},{5... | collective-permute-start | bytes 3145736 | tf_op jit(solution)/shard_map/ppermute | solution.py:31
  96.2 30.2 %all-to-all-start.1 = ((bf16[1,4,256,512]{3,2,0,1:T(8,128)(2,1)}), bf16[1,4,256,512]{3,2,0,1:T(8,128)(2,1)S(1)}, u32[]{:S(2)}, u32[]{:S(2)}) async-start(bf16[1,4,256,512]{3,2,0,1:T(8,128)(2,1)} %bitcast.40), calls=%async_computation.1 | async-start | bytes 2097152 | tf_op jit(solution)/shard_map/all_to_all | solution.py:290
  157.5 1.2 collective-permute-start.6
  157.6 64.2 %copy-start.186 = (s32[512,1]{0,1:T(1,128)}, s32[512,1]{0,1:T(1,128)S(1)}, u32[]{:S(2)}) copy-start(s32[512,1]{0,1:T(1,128)S(1)} %compare_select_fusion) | copy-start | bytes 6148
  158.7 4.8 collective-permute-start.8
  160.3 4.5 collective-permute-start.9
  161.6 3.6 collective-permute-start.7
  165.2 5.5 collective-permute-start.12
  166.7 4.5 collective-permute-start.11
  166.7 4.6 collective-permute-start.10
  173.6 38.4 %copy-start.84 = (f32[512]{0:T(512)}, f32[512]{0:T(512)S(1)}, u32[]{:S(2)}) copy-start(f32[512]{0:T(512)S(1)} %add_rsqrt_fusion.3) | copy-start | bytes 6148
  177.2 26.7 %all-to-all-start.2 = ((bf16[1,4,256,512]{3,2,0,1:T(8,128)(2,1)}), bf16[1,4,256,512]{3,2,0,1:T(8,128)(2,1)S(1)}, u32[]{:S(2)}, u32[]{:S(2)}) async-start(bf16[1,4,256,512]{3,2,0,1:T(8,128)(2,1)} %bitcast.63), calls=%async_computation.2 | async-start | bytes 2097152 | tf_op jit(solution)/shard_map/all_to_all | solution.py:286
  218.2 28.4 %all-to-all-start.3 = ((bf16[1,4,256,512]{3,2,0,1:T(8,128)(2,1)}), bf16[1,4,256,512]{3,2,0,1:T(8,128)(2,1)S(1)}, u32[]{:S(2)}, u32[]{:S(2)}) async-start(bf16[1,4,256,512]{3,2,0,1:T(8,128)(2,1)} %bitcast.396), calls=%async_computation.3 | async-start | bytes 2097152 | tf_op jit(solution)/shard_map/all_to_all | solution.py:290
  221.7 189.1 %reduce-scatter.7.cloned.1.call-start = ((), (), s32[]{:S(2)}) async-start(), calls=%async_computation.15 | async-start | bytes 1769472 | tf_op jit(solution)/shard_map/reduce_scatter | solution.py:563
  255.4 39.5 %copy-start.16 = (f32[512,512]{1,0:T(8,128)}, f32[512,512]{1,0:T(8,128)S(1)}, u32[]{:S(2)}) copy-start(f32[512,512]{1,0:T(8,128)S(1)} %get-tuple-element.143) | copy-start | bytes 3145732
  333.8 1.2 collective-permute-start.13
  335.0 3.7 collective-permute-start.15
  336.0 4.5 collective-permute-start.16
  337.3 3.6 collective-permute-start.14
  340.9 5.5 collective-permute-start.19
  342.4 4.5 collective-permute-start.18
  342.6 4.3 collective-permute-start.17
  373.1 193.4 %reduce-scatter.9.cloned.1.call-start = ((), (), s32[]{:S(2)}) async-start(), calls=%async_computation.16 | async-start | bytes 245760 | tf_op jit(solution)/shard_map/reduce_scatter | solution.py:564
  410.9 157.0 %reduce-scatter.11.cloned.1.call-start = ((), (), s32[]{:S(2)}) async-start(), calls=%async_computation.17 | async-start | bytes 2359296 | tf_op jit(solution)/shard_map/reduce_scatter | solution.py:563
  416.8 172.9 %reduce-scatter.17.cloned.1.call-start = ((), (), s32[]{:S(2)}) async-start(), calls=%async_computation.20 | async-start | bytes 2359296 | tf_op jit(solution)/shard_map/reduce_scatter | solution.py:493
  425.3 4.8 collective-permute-start.20
  429.6 162.1 %reduce-scatter.15.cloned.1.call-start = ((), (), s32[]{:S(2)}) async-start(), calls=%async_computation.19 | async-start | bytes 2359296 | tf_op jit(solution)/shard_map/reduce_scatter | solution.py:492
  430.2 5.6 collective-permute-start.21
  435.8 4.3 collective-permute-start.22
  440.2 4.0 collective-permute-start.23
  444.2 4.7 collective-permute-start.24
  448.9 4.7 collective-permute-start.25
  453.7 4.0 collective-permute-start.26
  457.7 16.3 %collective-permute-start.27 = (bf16[2,2,16,512]{3,2,0,1:T(8,128)(2,1)S(1)}, bf16[2,2,16,512]{3,2,0,1:T(8,128)(2,1)S(1)}, u32[]{:S(2)}, u32[]{:S(2)}) collective-permute-start(bf16[2,2,16,512]{3,2,0,1:T(8,128)(2,1)S(1)} %pad_maximum_fusion.23), channel_id=1, source_target_pairs={{0,16},{1,17},{2,18},{3,19},{4,20},{5,21},{6,22},{7,23},{8,24},{9,... | collective-permute-start | bytes 196616 | tf_op jit(solution)/shard_map/ppermute | solution.py:31
  469.2 23.9 %all-to-all-start.6 = ((bf16[1,4,256,512]{3,2,0,1:T(8,128)(2,1)}), bf16[1,4,256,512]{3,2,0,1:T(8,128)(2,1)}, u32[]{:S(2)}, u32[]{:S(2)}) async-start(bf16[1,4,256,512]{3,2,0,1:T(8,128)(2,1)} %bitcast.374), calls=%async_computation.6 | async-start | bytes 2097152 | tf_op jit(solution)/shard_map/all_to_all | solution.py:286
  474.0 5.0 collective-permute-start.28
  479.1 1.6 collective-permute-start.29
  505.4 7.4 %collective-permute-start.30 = (f32[30,512]{1,0:T(8,128)S(1)}, f32[30,512]{1,0:T(8,128)S(1)}, u32[]{:S(2)}, u32[]{:S(2)}) collective-permute-start(f32[30,512]{1,0:T(8,128)S(1)} %concatenate.61), channel_id=1, source_target_pairs={{0,4},{1,5},{2,6},{3,7},{4,0},{5,1},{6,2},{7,3},{8,12},{9,13},{10,... | collective-permute-start | bytes 184328 | tf_op jit(solution)/shard_map/ppermute | solution.py:31
  512.3 45.6 %collective-permute-start.37 = (bf16[2,2,1,64,2048]{4,3,0,2,1:T(8,128)(2,1)}, bf16[2,2,1,64,2048]{4,3,0,2,1:T(8,128)(2,1)}, u32[]{:S(2)}, u32[]{:S(2)}) collective-permute-start(bf16[2,2,1,64,2048]{4,3,0,2,1:T(8,128)(2,1)} %bitcast.358), channel_id=1, source_target_pairs={{0,4},{4,0},{8,12},{12,8},{16,20},{20,16},{24,28},{28,24},{1,5},{5... | collective-permute-start | bytes 3145736 | tf_op jit(solution)/shard_map/ppermute | solution.py:31
  512.8 12.4 %collective-permute-start.33 = (f32[30,512]{1,0:T(8,128)S(1)}, f32[30,512]{1,0:T(8,128)S(1)}, u32[]{:S(2)}, u32[]{:S(2)}) collective-permute-start(f32[30,512]{1,0:T(8,128)S(1)} %add.634), channel_id=1, source_target_pairs={{0,24},{1,25},{2,26},{3,27},{4,28},{5,29},{6,30},{7,31},{8,16},{9,... | collective-permute-start | bytes 184328 | tf_op jit(solution)/shard_map/ppermute | solution.py:31
  514.4 10.8 %collective-permute-start.32 = (f32[30,512]{1,0:T(8,128)S(1)}, f32[30,512]{1,0:T(8,128)S(1)}, u32[]{:S(2)}, u32[]{:S(2)}) collective-permute-start(f32[30,512]{1,0:T(8,128)S(1)} %add.634), channel_id=1, source_target_pairs={{0,16},{1,17},{2,18},{3,19},{4,20},{5,21},{6,22},{7,23},{8,24},{9,... | collective-permute-start | bytes 184328 | tf_op jit(solution)/shard_map/ppermute | solution.py:31
  515.0 10.3 %collective-permute-start.31 = (f32[30,512]{1,0:T(8,128)S(1)}, f32[30,512]{1,0:T(8,128)S(1)}, u32[]{:S(2)}, u32[]{:S(2)}) collective-permute-start(f32[30,512]{1,0:T(8,128)S(1)} %add.634), channel_id=1, source_target_pairs={{0,8},{1,9},{2,10},{3,11},{4,12},{5,13},{6,14},{7,15},{8,0},{9,1},... | collective-permute-start | bytes 184328 | tf_op jit(solution)/shard_map/ppermute | solution.py:31
  521.6 46.3 %all-to-all-start.7 = ((bf16[1,4,256,512]{3,2,0,1:T(8,128)(2,1)}), bf16[1,4,256,512]{3,2,0,1:T(8,128)(2,1)S(1)}, u32[]{:S(2)}, u32[]{:S(2)}) async-start(bf16[1,4,256,512]{3,2,0,1:T(8,128)(2,1)} %bitcast.395), calls=%async_computation.7 | async-start | bytes 2097152 | tf_op jit(solution)/shard_map/all_to_all | solution.py:290
  525.1 68.5 %reduce-scatter.13.cloned.1.call-start = ((), (), s32[]{:S(2)}) async-start(), calls=%async_computation.18 | async-start | bytes 327680 | tf_op jit(solution)/shard_map/reduce_scatter | solution.py:564
  525.2 37.7 %copy-start.32 = (bf16[2048,512]{1,0:T(8,128)(2,1)S(1)}, bf16[2048,512]{1,0:T(8,128)(2,1)}, u32[]{:S(2)}) copy-start(bf16[2048,512]{1,0:T(8,128)(2,1)} %convolution_convert_fusion.1) | copy-start | bytes 6291460
  525.3 23.4 %collective-permute-start.36 = (f32[30,512]{1,0:T(8,128)S(1)}, f32[30,512]{1,0:T(8,128)S(1)}, u32[]{:S(2)}, u32[]{:S(2)}) collective-permute-start(f32[30,512]{1,0:T(8,128)S(1)} %add_add_fusion), channel_id=1, source_target_pairs={{0,3},{1,2},{2,1},{3,0},{4,7},{5,6},{6,5},{7,4},{8,11},{9,10},{10,... | collective-permute-start | bytes 184328 | tf_op jit(solution)/shard_map/ppermute | solution.py:31
  529.1 27.0 %collective-permute-start.35 = (f32[30,512]{1,0:T(8,128)S(1)}, f32[30,512]{1,0:T(8,128)S(1)}, u32[]{:S(2)}, u32[]{:S(2)}) collective-permute-start(f32[30,512]{1,0:T(8,128)S(1)} %add_add_fusion), channel_id=1, source_target_pairs={{0,2},{1,3},{2,0},{3,1},{4,6},{5,7},{6,4},{7,5},{8,10},{9,11},{10,... | collective-permute-start | bytes 184328 | tf_op jit(solution)/shard_map/ppermute | solution.py:31
  529.1 27.0 %collective-permute-start.34 = (f32[30,512]{1,0:T(8,128)S(1)}, f32[30,512]{1,0:T(8,128)S(1)}, u32[]{:S(2)}, u32[]{:S(2)}) collective-permute-start(f32[30,512]{1,0:T(8,128)S(1)} %add_add_fusion), channel_id=1, source_target_pairs={{0,1},{1,0},{2,3},{3,2},{4,5},{5,4},{6,7},{7,6},{8,9},{9,8},{10,11... | collective-permute-start | bytes 184328 | tf_op jit(solution)/shard_map/ppermute | solution.py:31
  531.1 31.8 %collective-permute-start.40 = (bf16[2,2,1,256,512]{4,3,1,2,0:T(8,128)(2,1)S(1)}, bf16[2,2,1,256,512]{4,3,1,2,0:T(8,128)(2,1)S(1)}, u32[]{:S(2)}, u32[]{:S(2)}) collective-permute-start(bf16[2,2,1,256,512]{4,3,1,2,0:T(8,128)(2,1)S(1)} %dynamic-slice_bitcast_fusion), channel_id=1, source_target_pairs={{0,4},{4,0},{8,12},{12,8},{16,20},{20,16},{24,28},{28,24},{1,5},{5... | collective-permute-start | bytes 3145736 | tf_op jit(solution)/shard_map/ppermute | solution.py:31
  561.7 15.5 %collective-permute-start.38 = (bf16[2,1,64,2048]{3,2,1,0:T(8,128)(2,1)}, bf16[2,1,64,2048]{3,2,1,0:T(8,128)(2,1)}, u32[]{:S(2)}, u32[]{:S(2)}) collective-permute-start(bf16[2,1,64,2048]{3,2,1,0:T(8,128)(2,1)} %dynamic-slice_bitcast_fusion.2), channel_id=1, source_target_pairs={{0,8},{4,12},{8,0},{12,4},{16,24},{20,28},{24,16},{28,20},{1,9},{5... | collective-permute-start | bytes 1572872 | tf_op jit(solution)/shard_map/ppermute | solution.py:31
  565.0 16.1 %collective-permute-start.41 = (bf16[2,1,256,512]{3,2,1,0:T(8,128)(2,1)}, bf16[2,1,256,512]{3,2,1,0:T(8,128)(2,1)}, u32[]{:S(2)}, u32[]{:S(2)}) collective-permute-start(bf16[2,1,256,512]{3,2,1,0:T(8,128)(2,1)} %dynamic-slice_bitcast_fusion.1), channel_id=1, source_target_pairs={{0,16},{4,20},{8,24},{12,28},{16,0},{20,4},{24,8},{28,12},{1,17},{... | collective-permute-start | bytes 1572872 | tf_op jit(solution)/shard_map/ppermute | solution.py:31
  578.6 7.6 %collective-permute-start.39 = (bf16[1,64,2048]{2,1,0:T(8,128)(2,1)S(1)}, bf16[1,64,2048]{2,1,0:T(8,128)(2,1)S(1)}, u32[]{:S(2)}, u32[]{:S(2)}) collective-permute-start(bf16[1,64,2048]{2,1,0:T(8,128)(2,1)S(1)} %dynamic-slice_bitcast_fusion.4), channel_id=1, source_target_pairs={{0,16},{4,20},{8,24},{12,28},{16,0},{20,4},{24,8},{28,12},{1,17},{... | collective-permute-start | bytes 786440 | tf_op jit(solution)/shard_map/ppermute | solution.py:31
  582.4 7.1 %collective-permute-start.42 = (bf16[1,256,512]{2,1,0:T(8,128)(2,1)S(1)}, bf16[1,256,512]{2,1,0:T(8,128)(2,1)S(1)}, u32[]{:S(2)}, u32[]{:S(2)}) collective-permute-start(bf16[1,256,512]{2,1,0:T(8,128)(2,1)S(1)} %dynamic-slice_bitcast_fusion.3), channel_id=1, source_target_pairs={{0,8},{4,12},{8,0},{12,4},{16,24},{20,28},{24,16},{28,20},{1,9},{5... | collective-permute-start | bytes 786440 | tf_op jit(solution)/shard_map/ppermute | solution.py:31
  (209 other events, 1310.3 us)
Sparse Core Ops, SparseCore 0:
  12.1 72.3 all-gather.5
  86.4 26.6 all-gather.7
  115.0 27.8 all-gather.9
  373.2 37.6 reduce-scatter.6
  413.0 19.3 reduce-scatter.8
  435.9 40.0 reduce-scatter.10
  479.3 43.7 reduce-scatter.16
  526.7 42.2 reduce-scatter.14
  571.2 20.3 reduce-scatter.12

commit v2 on v0

v2 whole, which is shorter than its diff:
```python
import functools

import jax
import jax.numpy as jnp
import numpy as np
from jax import lax
from jax.experimental import pallas as pl
from jax.experimental.pallas import tpu as pltpu
from jax.sharding import PartitionSpec as P

H = 8
DH = 64
LANES = 128

EPSILON = 1e-05
MASK_FILL = 1000000000.0
HIGHEST = lax.Precision.HIGHEST
AXES = ("dp", "expert")
BF16 = jnp.bfloat16
F32 = jnp.float32
I32 = jnp.int32
MIB = 1 << 20


def bit_count(axes):
    total = 1
    for name in axes:
        total *= lax.axis_size(name)
    return total.bit_length() - 1


def exchange(values, axes, mask):
    total = 1 << bit_count(axes)
    return lax.ppermute(values, axes, [(i, i ^ mask) for i in range(total)])


def device_groups():
    z_bits = bit_count(("expert",))
    dp_bits = bit_count(("dp",))
    chips = list(range(z_bits + 1, z_bits + dp_bits))
    rests = [chips, list(range(z_bits))]
    return [[z_bits]] + [bits[i : i + 2] for bits in rests for i in range(0, len(bits), 2)]


def masks_of(bits):
    if len(bits) == 1:
        return [1 << bits[0]]
    low, high = 1 << bits[0], 1 << bits[1]
    return [low, high, low | high]


def sum_everywhere(values):
    for bits in device_groups():
        arrived = [exchange(values, AXES, mask) for mask in masks_of(bits)]
        if len(arrived) == 1:
            values = values + arrived[0]
        else:
            values = (values + arrived[0]) + (arrived[1] + arrived[2])
    return values


def gather_everywhere(values):
    total = 1 << bit_count(AXES)
    sent = jnp.broadcast_to(values[None], (total,) + values.shape)
    return lax.all_to_all(sent, AXES, split_axis=0, concat_axis=0, tiled=True)


def sum_to_owners(values, axes):
    arrived = lax.all_to_all(values, axes, split_axis=0, concat_axis=0, tiled=True)
    return jnp.sum(arrived.astype(F32), 0)


def swap_blocks(blocks):
    total = lax.axis_size("expert")
    moved = [blocks[0]]
    for k in range(1, total):
        moved.append(lax.ppermute(blocks[k], "expert", [(i, i ^ k) for i in range(total)]))
    return moved


def chip_masks():
    return [core << 1 for core in range(lax.axis_size("dp") // 2)]


def call(body, outs, *args, specs=None, out_specs=None, scratch=(), vmem=60, **kw):
    vmem_spec = pl.BlockSpec(memory_space=pltpu.VMEM)
    if specs is None:
        specs = [None] * len(args)
    grid = kw.pop("grid", (1,))
    specs = [
        jax.tree.map(lambda _: vmem_spec, arg) if spec is None else spec
        for spec, arg in zip(specs, args)
    ]
    if out_specs is None:
        out_specs = jax.tree.map(lambda _: vmem_spec, outs)
    return pl.pallas_call(
        body,
        out_shape=outs,
        in_specs=specs,
        out_specs=out_specs,
        scratch_shapes=list(scratch),
        grid=grid,
        compiler_params=pltpu.CompilerParams(vmem_limit_bytes=vmem * MIB),
        cost_estimate=pl.CostEstimate(flops=0, bytes_accessed=0, transcendentals=0),
        **kw,
    )(*args)


def shaped(shape, dtype):
    return jax.ShapeDtypeStruct(shape, dtype)


SMEM = pl.BlockSpec(memory_space=pltpu.SMEM)
ANY = pl.BlockSpec(memory_space=pl.ANY)


def dot(left, right):
    return lax.dot_general(left, right, (((1,), (0,)), ((), ())), preferred_element_type=F32)


def dot_nt(left, right):
    return lax.dot_general(left, right, (((1,), (1,)), ((), ())), preferred_element_type=F32)


def dot_tn(left, right):
    return lax.dot_general(left, right, (((0,), (0,)), ((), ())), preferred_element_type=F32)


def iota(shape, dim):
    return lax.broadcasted_iota(I32, shape, dim)


def normalize(rows):
    centred = rows - jnp.mean(rows, -1, keepdims=True)
    inverse = lax.rsqrt(jnp.mean(centred * centred, -1, keepdims=True) + EPSILON)
    return centred * inverse, inverse


def norm_backward(grad, gain, hat, inverse):
    scaled = grad * gain
    return inverse * (
        scaled
        - jnp.mean(scaled, -1, keepdims=True)
        - hat * jnp.mean(scaled * hat, -1, keepdims=True)
    )


def sigmoid(values):
    return 1.0 / (1.0 + jnp.exp(-values))


def slope(values, logistic):
    return logistic * (1.0 + values * (1.0 - logistic))


def chunks(total, size):
    return [pl.ds(start, size) for start in range(0, total, size)]


def gathered(slot_col, blocks, rows):
    slot = slot_col[rows, :]
    total = None
    for k, block in enumerate(blocks):
        capacity = block.shape[0]
        pick = (slot == iota((slot.shape[0], capacity), 1) + k * capacity).astype(F32).astype(BF16)
        part = dot(pick, block[...])
        total = part if total is None else total + part
    return total


def scatter_to(slot_row, values, outs):
    for k, out in enumerate(outs):
        capacity = out.shape[0]
        pick = (slot_row[...] == iota((capacity, slot_row.shape[1]), 0) + k * capacity)
        out[...] = dot(pick.astype(F32).astype(BF16), values).astype(BF16)


def start_kernel(own, frames, col1, row1, col2, row2, sent, slot_col1, slot_row1, slot_col2, slot_row2):
    rows = frames.shape[0]
    capacity = sent[0].shape[0]
    below = (iota((rows, rows), 0) > iota((rows, rows), 1)).astype(F32).astype(BF16)
    above = (iota((rows, rows), 0) < iota((rows, rows), 1)).astype(F32).astype(BF16)
    for col, row, out_col, out_row in (
        (col1, row1, slot_col1, slot_row1),
        (col2, row2, slot_col2, slot_row2),
    ):
        hot = (col[...] == iota((rows, LANES), 1)).astype(F32)
        rank = jnp.sum(dot(below, hot.astype(BF16)) * hot, 1, keepdims=True)
        out_col[...] = (col[...] ^ own[0]) * capacity + rank.astype(I32)
        hot = (row[...] == iota((16, rows), 0)).astype(F32)
        rank = jnp.sum(dot(hot.astype(BF16), above) * hot, 0, keepdims=True)
        out_row[...] = (row[...] ^ own[0]) * capacity + rank.astype(I32)
    scatter_to(slot_row1, frames[...], sent)


def expert_specs(weights, hidden, tile):
    count, rows, width = weights.shape
    half = rows // 2
    in_rows = width // count
    first = pl.BlockSpec((count, in_rows, tile), lambda j: (0, half // in_rows + j, 0))
    second = pl.BlockSpec((tile // half, half, width), lambda j: (j, 0, 0))
    return first, second


def flat(ref):
    count, rows, width = ref.shape
    return ref[...].reshape(count * rows, width)


def expert_forward_kernel(with_norm, block, gain, w_in, w_out, out, total, inputs):
    step = pl.program_id(0)

    @pl.when(step == 0)
    def _():
        if with_norm:
            hat, _ = normalize(block[...].astype(F32))
            inputs[...] = (hat * gain[...]).astype(BF16)
        else:
            inputs[...] = block[...]
        total[...] = jnp.zeros_like(total)

    pre = dot(inputs[...], flat(w_in))
    hidden = (pre * sigmoid(pre)).astype(BF16)
    total[...] += dot(hidden, flat(w_out))

    @pl.when(step == pl.num_programs(0) - 1)
    def _():
        out[...] = total[...].astype(BF16)


def expert_forward(block, gain, weights, hidden, with_norm, tile=512):
    capacity, width = block.shape
    first, second = expert_specs(weights, hidden, tile)
    whole = pl.BlockSpec((capacity, width), lambda j: (0, 0))
    return call(
        functools.partial(expert_forward_kernel, with_norm),
        shaped((capacity, width), BF16),
        block,
        gain,
        weights,
        weights,
        specs=[whole, pl.BlockSpec((1, width), lambda j: (0, 0)), first, second],
        out_specs=whole,
        scratch=[pltpu.VMEM((capacity, width), F32), pltpu.VMEM((capacity, width), BF16)],
        grid=(hidden // tile,),
        vmem=12,
    )


def expert_backward_kernel(
    with_norm, block, grad, gain, w_in, w_out, out, hidden_out, pre_grad_out, input_out, gain_out, total, hats
):
    step = pl.program_id(0)

    @pl.when(step == 0)
    def _():
        if with_norm:
            hat, _ = normalize(block[...].astype(F32))
            hats[...] = hat
            input_out[...] = (hat * gain[...]).astype(BF16)
        else:
            input_out[...] = block[...]
        total[...] = jnp.zeros_like(total)

    first, second = flat(w_in), flat(w_out)
    pre = dot(input_out[...], first)
    logistic = sigmoid(pre)
    hidden_out[...] = (pre * logistic).astype(BF16)
    hidden_grad = dot_nt(grad[...], second)
    pre_grad = (hidden_grad * slope(pre, logistic)).astype(BF16)
    pre_grad_out[...] = pre_grad
    total[...] += dot_nt(pre_grad, first)

    @pl.when(step == pl.num_programs(0) - 1)
    def _():
        back = total[...].astype(BF16)
        out[...] = back
        if with_norm:
            gain_out[...] = jnp.sum(back.astype(F32) * hats[...], 0, keepdims=True)
        else:
            gain_out[...] = jnp.zeros_like(gain_out)


def expert_backward(block, grad, gain, weights, hidden, with_norm, tile=512):
    capacity, width = block.shape
    first, second = expert_specs(weights, hidden, tile)
    whole = pl.BlockSpec((capacity, width), lambda j: (0, 0))
    tiled = pl.BlockSpec((capacity, tile), lambda j: (0, j))
    one = pl.BlockSpec((1, width), lambda j: (0, 0))
    return call(
        functools.partial(expert_backward_kernel, with_norm),
        (
            shaped((capacity, width), BF16),
            shaped((capacity, hidden), BF16),
            shaped((capacity, hidden), BF16),
            shaped((capacity, width), BF16),
            shaped((1, width), F32),
        ),
        block,
        grad,
        gain,
        weights,
        weights,
        specs=[whole, whole, one, first, second],
        out_specs=(whole, tiled, tiled, whole, one),
        scratch=[pltpu.VMEM((capacity, width), F32), pltpu.VMEM((capacity, width), F32)],
        grid=(hidden // tile,),
        vmem=16,
    )


def weight_grad_kernel(relative, dp_index, inputs, grads, hidden, pre_grads, *refs):
    outs, (first, second) = refs[:-2], refs[-2:]
    step = pl.program_id(0)
    first_sum = second_sum = None
    for block, grad, hid, pre_grad in zip(inputs, grads, hidden, pre_grads):
        part = dot_tn(block[...], pre_grad[...])
        first_sum = part if first_sum is None else first_sum + part
        part = dot_tn(hid[...], grad[...])
        second_sum = part if second_sum is None else second_sum + part
    count = sum(out.shape[0] for out in outs)
    half = outs[0].shape[1] // 2
    in_rows = first_sum.shape[0] // count
    tile = second_sum.shape[0]
    owners = tile // half
    place = pl.ds(pl.multiple_of(half + step * in_rows, in_rows), in_rows)
    if not relative:
        for device in range(count):
            outs[0][device, place, :] = first_sum[device * in_rows : (device + 1) * in_rows].astype(BF16)
        for number in range(owners):
            outs[0][step * owners + number, pl.ds(0, half), :] = second_sum[
                number * half : (number + 1) * half
            ].astype(BF16)
    else:
        first[...] = first_sum.astype(BF16)
        for number in range(count):
            source = pl.multiple_of((dp_index[0] ^ number) * in_rows, in_rows)
            outs[number % 2][number // 2, place, :] = first[pl.ds(source, in_rows), :]
        second[...] = second_sum.astype(BF16)
        for number in range(owners):
            owner = (step * owners + number) ^ dp_index[0]

            @pl.when(owner % 2 == 0)
            def _():
                outs[0][owner // 2, pl.ds(0, half), :] = second[pl.ds(number * half, half), :]

            @pl.when(owner % 2 == 1)
            def _():
                outs[1][owner // 2, pl.ds(0, half), :] = second[pl.ds(number * half, half), :]


def weight_grads(dp_index, inputs, grads, hidden, pre_grads, count, relative, tile=512):
    capacity, width = inputs[0].shape
    units = hidden[0].shape[1]
    whole = pl.BlockSpec((capacity, width), lambda j: (0, 0))
    tiled = pl.BlockSpec((capacity, tile), lambda j: (0, j))
    rows = 2 * units // count
    if relative:
        outs = (shaped((count // 2, rows, width), BF16),) * 2
    else:
        outs = (shaped((count, rows, width), BF16),)
    peers = len(inputs)
    return call(
        functools.partial(weight_grad_kernel, relative),
        outs,
        dp_index,
        list(inputs),
        list(grads),
        list(hidden),
        list(pre_grads),
        specs=[SMEM, [whole] * peers, [whole] * peers, [tiled] * peers, [tiled] * peers],
        out_specs=tuple(pl.BlockSpec(o.shape, lambda j: (0, 0, 0)) for o in outs),
        scratch=[pltpu.VMEM((width, tile), BF16), pltpu.VMEM((tile, width), BF16)],
        grid=(units // tile,),
        vmem=28,
    )


def dense_grad_kernel(
    experts, ua, dproj, attended, dat, uc, dgin, swish, dco, gate_grad1, gate1, col1, gate_grad2, gate2, col2,
    probs, routers, pre, embedded, frames, out, dz, router_terms, logits,
):
    width = ua.shape[1]
    rows = frames.shape[0]
    for part in chunks(rows, 128):
        lane = iota((128, LANES), 1)
        grad = jnp.zeros((128, LANES), F32)
        for number, (gate_grad, gate, col) in enumerate(((gate_grad1, gate1, col1), (gate_grad2, gate2, col2))):
            inside = (lane >= number * experts) & (lane < (number + 1) * experts)
            hot = (lane == col[part, :] + number * experts).astype(F32)
            scale = gate_grad[part, :] * gate[part, :]
            grad = jnp.where(inside, scale * (hot - probs[part, :]), grad)
        logits[part, :] = grad
        demb = lax.dot_general(
            grad, routers[...], (((1,), (1,)), ((), ())), precision=HIGHEST, preferred_element_type=F32
        )
        held = pre[part, :]
        dz[part, :] = (demb * slope(held, sigmoid(held))).astype(BF16)
    router_terms[...] = lax.dot_general(
        logits[...], embedded[...], (((0,), (0,)), ((), ())), precision=HIGHEST, preferred_element_type=F32
    )
    start = 0
    for left, right in ((ua, dproj), (attended, dat), (uc, dgin), (swish, dco), (frames, dz)):
        for column in range(0, right.shape[1], width):
            out[:, pl.ds(start, width)] = dot_tn(left[...], right[:, pl.ds(column, width)]).astype(BF16)
            start += width


def embed_kernel(experts, ends, frames, weight, routers, col1, col2, pre_out, embedded_out, probs_out, gate1, gate2, seg_col, seg_row, taps_out, offset_out):
    rows = frames.shape[0]
    for part in chunks(rows, 128):
        pre = dot(frames[part, :], weight[...])
        pre_out[part, :] = pre
        embedded = pre * sigmoid(pre)
        embedded_out[part, :] = embedded
        logits = jnp.dot(embedded, routers[...], precision=HIGHEST, preferred_element_type=F32)
        lane = iota(logits.shape, 1)
        probs = jnp.zeros_like(logits)
        for number, (col, gate) in enumerate(((col1, gate1), (col2, gate2))):
            inside = (lane >= number * experts) & (lane < (number + 1) * experts)
            top = jnp.max(jnp.where(inside, logits, -MASK_FILL), 1, keepdims=True)
            weights = jnp.where(inside, jnp.exp(jnp.where(inside, logits - top, 0.0)), 0.0)
            own = weights / jnp.sum(weights, 1, keepdims=True)
            hot = lane == col[part, :] + number * experts
            gate[part, :] = jnp.sum(jnp.where(hot, own, 0.0), 1, keepdims=True)
            probs = probs + own
        probs_out[part, :] = probs

    def segment_of(place):
        found = jnp.zeros(place.shape, I32)
        for number in range(3):
            found += (place >= ends[number]).astype(I32)
        return found

    segment = segment_of(iota((rows, 1), 0))
    seg_col[...] = segment
    seg_row[...] = segment_of(iota((1, rows), 1))
    place = iota((rows, LANES), 0) + iota((rows, LANES), 1) - 7
    same = (segment_of(place) == segment) & (place >= 0) & (place < rows)
    taps_out[...] = same.astype(F32)
    first = jnp.zeros((rows, 1), I32)
    for number in range(3):
        first = jnp.where(segment > number, ends[number], first)
    offset_out[...] = (iota((rows, 1), 0) - first).astype(F32)


def partner(values):
    half = DH // 2
    lane = iota(values.shape, 1)
    return jnp.where(lane % DH < half, pltpu.roll(values, LANES - half, 1), pltpu.roll(values, half, 1))


def front_kernel(
    frames, blocks, slot_col, gate, table, attn_in, attn_out, conv_in, cosine, sine, seg_col, seg_row, taps,
    expert_out, x1_out, x2_out, ua_out, qkv_out, lse_out, attended_out, uc_out, gin_out, depth_out, moments,
    padded,
):
    rows, width = frames.shape
    gains = lambda n: table[pl.ds(n, 1), :]
    for part in chunks(rows, 128):
        found = gathered(slot_col, blocks, part)
        expert_out[part, :] = found.astype(BF16)
        x1 = frames[part, :].astype(F32) + 0.5 * gate[part, :] * found
        x1_out[part, :] = x1
        hat, _ = normalize(x1)
        ua = (hat * gains(1)).astype(BF16)
        ua_out[part, :] = ua
        for piece in range(3 * width // LANES):
            lanes = pl.ds(piece * LANES, LANES)
            if piece % 2 == 0:
                pair = dot(ua, attn_in[:, pl.ds(piece * LANES, 2 * LANES)])
            values = pair[:, :LANES] if piece % 2 == 0 else pair[:, LANES:]
            if piece < 2 * width // LANES:
                values = values * cosine[part, :] + partner(values) * sine[part, :]
            if piece < width // LANES:
                values = values * DH**-0.5
            qkv_out[part, lanes] = values.astype(BF16)

    lane = iota((1, LANES), 1)
    sides = ((lane < DH), (lane >= DH))
    zero = jnp.zeros((), BF16)

    def attend(part_index, carry):
        part = pl.ds(pl.multiple_of(part_index * 128, 128), 128)
        related = seg_col[part, :] == seg_row[...]
        lse = jnp.zeros((128, LANES), F32)
        for pair in range(width // LANES):
            q = qkv_out[part, pl.ds(pair * LANES, LANES)]
            k = qkv_out[:, pl.ds(width + pair * LANES, LANES)]
            v = qkv_out[:, pl.ds(2 * width + pair * LANES, LANES)]
            result = jnp.zeros((128, LANES), F32)
            for side in range(2):
                scores = dot_nt(jnp.where(sides[side], q, zero), k)
                scores = jnp.where(related, scores, -MASK_FILL)
                top = jnp.max(scores, 1, keepdims=True)
                weights = jnp.exp(scores - top)
                summed = jnp.sum(weights, 1, keepdims=True)
                probs = (weights * (1.0 / summed)).astype(BF16)
                result += dot(probs, jnp.where(sides[side], v, zero))
                lse = jnp.where(lane == 2 * pair + side, top + jnp.log(summed), lse)
            attended_out[part, pl.ds(pair * LANES, LANES)] = result.astype(BF16)
        lse_out[part, :] = lse
        return carry

    lax.fori_loop(0, rows // 128, attend, 0)

    edge = jnp.zeros((8, width), F32)
    padded[pl.ds(0, 8), :] = edge
    padded[pl.ds(rows + 8, 8), :] = edge
    for part in chunks(rows, 128):
        x2 = x1_out[part, :] + dot(attended_out[part, :], attn_out[...])
        x2_out[part, :] = x2
        hat, _ = normalize(x2)
        uc = (hat * gains(2)).astype(BF16)
        uc_out[part, :] = uc
        gin = dot(uc, conv_in[...])
        gin_out[part, :] = gin
        padded[pl.ds(part.start + 8, 128), :] = gin[:, :width] * sigmoid(gin[:, width:])

    sums = jnp.zeros((1, width), F32)
    squares = jnp.zeros((1, width), F32)
    for part in chunks(rows, 64):
        depth = jnp.zeros((64, width), F32)
        for tap in range(15):
            weight = table[pl.ds(6 + tap, 1), :]
            depth += weight * padded[pl.ds(part.start + tap + 1, 64), :] * taps[part, pl.ds(tap, 1)]
        depth_out[part, :] = depth
        weighted = jnp.where(seg_col[part, :] < 3, depth, 0.0)
        sums += jnp.sum(weighted, 0, keepdims=True)
        squares += jnp.sum(weighted * depth, 0, keepdims=True)
    moments[pl.ds(0, 1), :] = sums
    moments[pl.ds(1, 1), :] = squares
    moments[pl.ds(2, 6), :] = jnp.zeros((6, width), F32)


def batch_terms(moments, frame_count):
    mean = moments[pl.ds(0, 1), :] / frame_count[0]
    variance = moments[pl.ds(1, 1), :] / frame_count[0] - mean * mean
    return mean, lax.rsqrt(variance + EPSILON)


def middle_kernel(frame_count, depth, moments, x2, table, conv_out, slot_row, swish_out, x3_out, sent, normed):
    rows, width = depth.shape
    mean, scale = batch_terms(moments, frame_count)
    for part in chunks(rows, 128):
        bn = (depth[part, :] - mean) * scale * table[pl.ds(5, 1), :] + table[pl.ds(21, 1), :]
        swish = (bn * sigmoid(bn)).astype(BF16)
        swish_out[part, :] = swish
        x3 = x2[part, :] + dot(swish, conv_out[...])
        x3_out[part, :] = x3
        hat, _ = normalize(x3)
        normed[part, :] = (hat * table[pl.ds(3, 1), :]).astype(BF16)
    scatter_to(slot_row, normed[...], sent)


def turn_kernel(
    x3, blocks, slot_col, slot_row, gate, table, cotangent, seg_col,
    block_out, dx4_out, gate_grad, gain_out, sent, grads,
):
    rows, width = x3.shape
    gain = table[pl.ds(4, 1), :]
    gain_sum = jnp.zeros((1, width), F32)
    for part in chunks(rows, 128):
        found = gathered(slot_col, blocks, part)
        half = 0.5 * gate[part, :]
        x4 = x3[part, :] + half * found
        hat, inverse = normalize(x4)
        valid = seg_col[part, :] < 3
        block_out[part, :] = jnp.where(valid, hat * gain, 0.0).astype(BF16)
        grad = jnp.where(valid, cotangent[part, :].astype(F32), 0.0)
        gain_sum += jnp.sum(grad * hat, 0, keepdims=True)
        dx4 = norm_backward(grad, gain, hat, inverse)
        dx4_out[part, :] = dx4
        gate_grad[part, :] = 0.5 * jnp.sum(found * dx4, 1, keepdims=True)
        grads[part, :] = (half * dx4).astype(BF16)
    gain_out[...] = gain_sum
    scatter_to(slot_row, grads[...], sent)


def conv_back_kernel(
    frame_count, dx4, blocks, slot_col, x3, table, conv_out, depth, moments,
    dx3_out, dco_out, dh_out, sums,
):
    rows, width = x3.shape
    mean, scale = batch_terms(moments, frame_count)
    total = jnp.zeros((1, width), F32)
    moment = jnp.zeros((1, width), F32)
    shift = jnp.zeros((1, width), F32)
    gain5 = jnp.zeros((1, width), F32)
    gain3 = jnp.zeros((1, width), F32)
    for part in chunks(rows, 128):
        grad = gathered(slot_col, blocks, part)
        hat, inverse = normalize(x3[part, :])
        gain3 += jnp.sum(grad * hat, 0, keepdims=True)
        dx3 = dx4[part, :] + norm_backward(grad, table[pl.ds(3, 1), :], hat, inverse)
        dx3_out[part, :] = dx3
        dco = dx3.astype(BF16)
        dco_out[part, :] = dco
        centred = depth[part, :] - mean
        hat = centred * scale
        bn = hat * table[pl.ds(5, 1), :] + table[pl.ds(21, 1), :]
        dbn = dot_nt(dco, conv_out[...]) * slope(bn, sigmoid(bn))
        shift += jnp.sum(dbn, 0, keepdims=True)
        gain5 += jnp.sum(dbn * hat, 0, keepdims=True)
        dh = dbn * table[pl.ds(5, 1), :]
        dh_out[part, :] = dh
        total += jnp.sum(dh, 0, keepdims=True)
        moment += jnp.sum(dh * centred, 0, keepdims=True)
    for number, row in enumerate((total, moment, shift, gain5, gain3)):
        sums[pl.ds(number, 1), :] = row
    sums[pl.ds(5, 3), :] = jnp.zeros((3, width), F32)


def back_kernel(
    frame_count, dh, depth, moments, sums, dx3, gin, x2, x1, table, conv_in, attn_out, attn_in, qkv, lse,
    cosine, sine, seg_col, seg_row, taps, expert, gate, slot_row,
    dgin_out, dat_out, dproj_out, dx1_out, gate_grad, terms, sent,
    padded, glu, grad_rows, dk, dv, rows_sent,
):
    rows, width = dh.shape
    mean, scale = batch_terms(moments, frame_count)
    total, moment = sums[pl.ds(0, 1), :], sums[pl.ds(1, 1), :]
    var_grad = -0.5 * moment * scale * scale * scale
    mean_grad = -scale * total - 2.0 * mean * var_grad
    edge = jnp.zeros((8, width), F32)
    for ref in (padded, glu):
        ref[pl.ds(0, 8), :] = edge
        ref[pl.ds(rows + 8, 8), :] = edge
    for part in chunks(rows, 64):
        held = depth[part, :]
        grad = (mean_grad + 2.0 * held * var_grad) * (1.0 / frame_count[0])
        padded[pl.ds(part.start + 8, 64), :] = dh[part, :] * scale + jnp.where(seg_col[part, :] < 3, grad, 0.0)
        glu[pl.ds(part.start + 8, 64), :] = gin[part, :width] * sigmoid(gin[part, width:])
    kernel_sums = [jnp.zeros((1, width), F32) for _ in range(15)]
    gain2 = jnp.zeros((1, width), F32)
    for part in chunks(rows, 64):
        dglu = jnp.zeros((64, width), F32)
        own = padded[pl.ds(part.start + 8, 64), :]
        for tap in range(15):
            mask = taps[part, pl.ds(tap, 1)]
            dglu += table[pl.ds(20 - tap, 1), :] * padded[pl.ds(part.start + tap + 1, 64), :] * mask
            shifted = glu[pl.ds(part.start + tap + 1, 64), :]
            kernel_sums[tap] += jnp.sum(own * shifted * mask, 0, keepdims=True)
        logistic = sigmoid(gin[part, width:])
        dgin_out[part, :width] = (dglu * logistic).astype(BF16)
        dgin_out[part, width:] = (dglu * gin[part, :width] * logistic * (1.0 - logistic)).astype(BF16)
    for tap in range(15):
        terms[pl.ds(6 + tap, 1), :] = kernel_sums[tap]
    for part in chunks(rows, 128):
        grad = dot_nt(dgin_out[part, :], conv_in[...])
        hat, inverse = normalize(x2[part, :])
        gain2 += jnp.sum(grad * hat, 0, keepdims=True)
        dx2 = dx3[part, :] + norm_backward(grad, table[pl.ds(2, 1), :], hat, inverse)
        dx1_out[part, :] = dx2
        dat = dx2.astype(BF16)
        dat_out[part, :] = dat
        grad_rows[part, :] = dot_nt(dat, attn_out[...]).astype(BF16)
    terms[pl.ds(2, 1), :] = gain2

    lane = iota((1, LANES), 1)
    sides = ((lane < DH), (lane >= DH))
    zero = jnp.zeros((), BF16)
    dk[...] = jnp.zeros_like(dk)
    dv[...] = jnp.zeros_like(dv)

    def attend(part_index, carry):
        part = pl.ds(pl.multiple_of(part_index * 128, 128), 128)
        related = seg_col[part, :] == seg_row[...]
        for pair in range(width // LANES):
            own = pl.ds(pair * LANES, LANES)
            q = qkv[part, own]
            k = qkv[:, pl.ds(width + pair * LANES, LANES)]
            v = qkv[:, pl.ds(2 * width + pair * LANES, LANES)]
            da = grad_rows[part, own]
            dq = jnp.zeros((128, LANES), F32)
            for side in range(2):
                head = 2 * pair + side
                q_side = jnp.where(sides[side], q, zero)
                da_side = jnp.where(sides[side], da, zero)
                scores = dot_nt(q_side, k) - lse[part, pl.ds(head, 1)]
                probs = jnp.where(related, jnp.exp(jnp.where(related, scores, 0.0)), 0.0)
                dprobs = dot_nt(da_side, v)
                inner = jnp.sum(probs * dprobs, 1, keepdims=True)
                dscores = (probs * (dprobs - inner)).astype(BF16)
                dq += dot(dscores, jnp.where(sides[side], k, zero))
                dk[:, own] += dot_tn(dscores, q_side)
                dv[:, own] += dot_tn(probs.astype(BF16), da_side)
            dq = dq * DH**-0.5
            dproj_out[part, own] = (dq * cosine[part, :] - partner(dq) * sine[part, :]).astype(BF16)
        return carry

    lax.fori_loop(0, rows // 128, attend, 0)

    gain1 = jnp.zeros((1, width), F32)
    for part in chunks(rows, 128):
        for pair in range(width // LANES):
            own = pl.ds(pair * LANES, LANES)
            held = dk[part, own]
            dproj_out[part, pl.ds(width + pair * LANES, LANES)] = (
                held * cosine[part, :] - partner(held) * sine[part, :]
            ).astype(BF16)
            dproj_out[part, pl.ds(2 * width + pair * LANES, LANES)] = dv[part, own].astype(BF16)
        grad = dot_nt(dproj_out[part, :], attn_in[...])
        hat, inverse = normalize(x1[part, :])
        gain1 += jnp.sum(grad * hat, 0, keepdims=True)
        dx1 = dx1_out[part, :] + norm_backward(grad, table[pl.ds(1, 1), :], hat, inverse)
        dx1_out[part, :] = dx1
        gate_grad[part, :] = 0.5 * jnp.sum(expert[part, :].astype(F32) * dx1, 1, keepdims=True)
        rows_sent[part, :] = (0.5 * gate[part, :] * dx1).astype(BF16)
    terms[pl.ds(1, 1), :] = gain1
    scatter_to(slot_row, rows_sent[...], sent)


def final_kernel(frames, blocks, slot_col, table, dx1, dz, embed_weight, out):
    for part in chunks(frames.shape[0], 128):
        grad = gathered(slot_col, blocks, part)
        hat, inverse = normalize(frames[part, :].astype(F32))
        dx0 = dx1[part, :] + norm_backward(grad, table[pl.ds(0, 1), :], hat, inverse)
        out[part, :] = dx0 + dot_nt(dz[part, :], embed_weight[...])


def after(value, *others):
    return lax.optimization_barrier((value,) + others)[0]


def shards(
    frames,
    lengths,
    choice_first,
    choice_second,
    embed_weight,
    routers,
    norm_gains,
    attn_in,
    attn_out,
    conv_in,
    conv_kernel,
    bn_shift,
    conv_out,
    expert_in,
    expert_out,
    cotangent,
):
    rows, width = frames.shape
    layers, slice_width, experts = routers.shape
    taps = conv_kernel.shape[0]
    gains = norm_gains.shape[0]
    peers = lax.axis_size("expert")
    dp_count = lax.axis_size("dp")
    dp_bits = bit_count(("dp",))
    capacity = 2 * rows // experts
    hidden = expert_in.shape[3]
    device = lax.axis_index(AXES)
    block = shaped((capacity, width), BF16)
    wide = shaped((rows, width), F32)
    low = shaped((rows, width), BF16)
    column = shaped((rows, 1), F32)

    dp_index = lax.axis_index("dp")[None]

    def shard_of(layer):
        first = expert_in[layer, 0]
        tiles = [first[:, start : start + width] for start in range(0, hidden, width)]
        return jnp.concatenate([expert_out[layer, 0]] + tiles, 0)

    first_weights = lax.all_gather(shard_of(0), "dp", axis=0)
    sent, slot_col1, slot_row1, slot_col2, slot_row2 = call(
        start_kernel,
        ([block] * peers, shaped((rows, 1), I32), shaped((1, rows), I32), shaped((rows, 1), I32), shaped((1, rows), I32)),
        lax.axis_index("expert")[None],
        frames,
        choice_first,
        choice_first.reshape(1, rows),
        choice_second,
        choice_second.reshape(1, rows),
        specs=[SMEM] + [None] * 5,
    )
    first_blocks = swap_blocks(sent)

    small_width = gains + taps + 1 + layers * experts
    small = jnp.concatenate(
        [
            norm_gains.T,
            conv_kernel.T,
            bn_shift[:, None],
            jnp.moveaxis(routers, 1, 0).reshape(slice_width, -1),
            jnp.zeros((slice_width, -small_width % LANES), BF16),
        ],
        1,
    )
    small_all = gather_everywhere(small).reshape(width, LANES).astype(F32)
    table = small_all[:, : gains + taps + 3].T
    router_table = jnp.pad(
        small_all[:, gains + taps + 1 : small_width], ((0, 0), (0, LANES - layers * experts))
    )
    dense = after(jnp.concatenate([attn_in, attn_out, conv_in, conv_out], 1), small_all, *first_blocks)
    dense = lax.all_to_all(
        jnp.broadcast_to(dense[None], (peers,) + dense.shape), "expert", split_axis=0, concat_axis=0, tiled=True
    )
    dense = lax.all_gather(
        dense.reshape(peers * slice_width, 7 * width), "dp", axis=0, tiled=True
    )
    second_weights = lax.all_gather(shard_of(1), "dp", axis=0)

    own_lengths = lax.dynamic_index_in_dim(lengths, device, 0, keepdims=False)
    frame_count = jnp.sum(lengths[:, :-1]).astype(F32)[None]
    (embed_pre, embedded, probs, gate1, gate2, seg_col, seg_row, tap_masks, offsets) = call(
        functools.partial(embed_kernel, experts),
        [
            wide,
            wide,
            shaped((rows, LANES), F32),
            column,
            column,
            shaped((rows, 1), I32),
            shaped((1, rows), I32),
            shaped((rows, LANES), F32),
            column,
        ],
        jnp.cumsum(own_lengths, dtype=I32)[:-1],
        frames,
        embed_weight,
        router_table,
        choice_first,
        choice_second,
        specs=[SMEM] + [None] * 5,
    )
    half = DH // 2
    frequency = 10000.0 ** (-jnp.arange(half, dtype=F32) / half)
    angles = offsets * jnp.tile(frequency, LANES // half)[None, :]
    sign = jnp.asarray(np.where(np.arange(LANES) % DH < half, -1.0, 1.0), F32)
    cosine, sine = jnp.cos(angles), jnp.sin(angles) * sign[None, :]

    def gain(number):
        return table[number : number + 1]

    first_results = swap_blocks(
        [expert_forward(block, gain(0), first_weights, hidden, True) for block in first_blocks]
    )

    def dense_spec(columns, start):
        return pl.BlockSpec((width, columns), lambda i: (0, start // columns))

    attn_in_spec = dense_spec(3 * width, 0)
    attn_out_spec = dense_spec(width, 3 * width)
    conv_in_spec = dense_spec(2 * width, 4 * width)
    conv_out_spec = dense_spec(width, 6 * width)
    sums_shape = shaped((8, width), F32)
    padded = pltpu.VMEM((rows + 16, width), F32)

    first_expert, x1, x2, ua, qkv, lse, attended, uc, gin, depth, moments = call(
        front_kernel,
        [
            low,
            wide,
            wide,
            low,
            shaped((rows, 3 * width), BF16),
            shaped((rows, LANES), F32),
            low,
            low,
            shaped((rows, 2 * width), F32),
            wide,
            sums_shape,
        ],
        frames,
        first_results,
        slot_col1,
        gate1,
        table,
        dense,
        dense,
        dense,
        cosine,
        sine,
        seg_col,
        seg_row,
        tap_masks,
        specs=[None] * 5 + [attn_in_spec, attn_out_spec, conv_in_spec] + [None] * 5,
        scratch=[padded],
    )
    moments = sum_everywhere(moments)
    swish, x3, sent = call(
        middle_kernel,
        (low, wide, [block] * peers),
        frame_count,
        depth,
        moments,
        x2,
        table,
        dense,
        slot_row2,
        specs=[SMEM] + [None] * 4 + [conv_out_spec, None],
        scratch=[pltpu.VMEM((rows, width), BF16)],
    )

    second_blocks = swap_blocks(sent)
    second_results = swap_blocks(
        [expert_forward(block, gain(3), second_weights, hidden, False) for block in second_blocks]
    )
    block_out, dx4, gate_grad2, gain4, sent = call(
        turn_kernel,
        (low, wide, column, shaped((1, width), F32), [block] * peers),
        x3,
        second_results,
        slot_col2,
        slot_row2,
        gate2,
        table,
        cotangent,
        seg_col,
        scratch=[pltpu.VMEM((rows, width), BF16)],
    )
    second_grads = swap_blocks(sent)
    backs = [
        expert_backward(block, grad, gain(3), second_weights, hidden, False)
        for block, grad in zip(second_blocks, second_grads)
    ]
    back, hid, pre_grads, inputs, _ = zip(*backs)
    second_back = swap_blocks(back)
    (second_grad,) = weight_grads(
        dp_index, inputs, second_grads, hid, pre_grads, dp_count, False
    )
    second_back[1] = after(second_back[1], second_grad)
    second_own = lax.psum_scatter(second_grad, "dp", scatter_dimension=0, tiled=True)[0]

    dx3, dco, dh, sums = call(
        conv_back_kernel,
        [wide, low, wide, sums_shape],
        frame_count,
        dx4,
        second_back,
        slot_col2,
        x3,
        table,
        dense,
        depth,
        moments,
        specs=[SMEM] + [None] * 5 + [conv_out_spec] + [None] * 2,
    )
    all_sums = sum_everywhere(sums)
    dgin, dat, dproj, dx1, gate_grad1, terms, sent = call(
        back_kernel,
        (
            shaped((rows, 2 * width), BF16),
            low,
            shaped((rows, 3 * width), BF16),
            wide,
            column,
            shaped((24, width), F32),
            [block] * peers,
        ),
        frame_count,
        dh,
        depth,
        moments,
        all_sums,
        dx3,
        gin,
        x2,
        x1,
        table,
        dense,
        dense,
        dense,
        qkv,
        lse,
        cosine,
        sine,
        seg_col,
        seg_row,
        tap_masks,
        first_expert,
        gate1,
        slot_row1,
        specs=[SMEM] + [None] * 9 + [conv_in_spec, attn_out_spec, attn_in_spec] + [None] * 10,
        scratch=[padded, padded, pltpu.VMEM((rows, width), BF16), pltpu.VMEM((rows, width), F32), pltpu.VMEM((rows, width), F32), pltpu.VMEM((rows, width), BF16)],
    )
    first_grads = swap_blocks(sent)

    dense_terms, dz, router_terms = call(
        functools.partial(dense_grad_kernel, experts),
        (shaped((width, 8 * width), BF16), low, shaped((LANES, width), F32)),
        ua,
        dproj,
        attended,
        dat,
        uc,
        dgin,
        swish,
        dco,
        gate_grad1,
        gate1,
        choice_first,
        gate_grad2,
        gate2,
        choice_second,
        probs,
        router_table,
        embed_pre,
        embedded,
        frames,
        scratch=[pltpu.VMEM((rows, LANES), F32)],
    )
    dense_own = sum_to_owners(dense_terms.reshape(dp_count, -1, 8 * width), "dp").astype(BF16)
    dense_own = sum_to_owners(dense_own.reshape(peers, slice_width, 8 * width), "expert")
    embed_total = gather_everywhere(dense_own[:, 7 * width :].astype(BF16))
    embed_total = embed_total.reshape(width, width).astype(F32)

    first_grads[1] = after(first_grads[1], dense_terms)
    backs = [
        expert_backward(block, grad, gain(0), first_weights, hidden, True)
        for block, grad in zip(first_blocks, first_grads)
    ]
    back, hid, pre_grads, inputs, gain0 = zip(*backs)
    gain0 = sum(gain0)
    first_back = swap_blocks(back)
    kept, moved = weight_grads(dp_index, inputs, first_grads, hid, pre_grads, dp_count, True)
    moved = after(moved, *first_back[1:])

    def dp_exchange(values, mask):
        return lax.ppermute(values, "dp", [(i, i ^ mask) for i in range(dp_count)])

    pair_sum = (kept.astype(F32) + dp_exchange(moved, 1).astype(F32)).astype(BF16)
    first_own = pair_sum[0].astype(F32)
    for number, mask in enumerate(chip_masks()):
        if mask:
            first_own = first_own + dp_exchange(pair_sum[number], mask).astype(F32)

    small_terms = jnp.concatenate(
        [
            gain0,
            terms[1:3],
            sums[4:5],
            gain4,
            sums[3:4],
            terms[6 : 6 + taps],
            sums[2:3],
            router_terms[: layers * experts],
        ],
        0,
    )
    small_terms = jnp.pad(small_terms.T, ((0, 0), (0, LANES - small_width)))
    small_sums = sum_to_owners(small_terms.reshape(-1, slice_width, LANES), AXES).T
    frames_grad = call(
        final_kernel,
        wide,
        frames,
        first_back,
        slot_col1,
        table,
        dx1,
        dz,
        embed_weight,
    )
    def matrices(own):
        half = own.shape[0] // 2
        first = jnp.concatenate(jnp.split(own[half:], hidden // width, 0), 1)
        return first, own[:half]

    first_pair, second_pair = matrices(first_own), matrices(second_own.astype(F32))
    return (
        block_out,
        frames_grad,
        embed_total,
        jnp.moveaxis(
            small_sums[gains + taps + 1 : small_width].reshape(layers, experts, slice_width), 1, 2
        ),
        small_sums[:gains],
        dense_own[:, : 3 * width],
        dense_own[:, 3 * width : 4 * width],
        dense_own[:, 4 * width : 6 * width],
        small_sums[gains : gains + taps],
        small_sums[gains + taps],
        dense_own[:, 6 * width : 7 * width],
        jnp.stack([first_pair[0], second_pair[0]])[:, None],
        jnp.stack([first_pair[1], second_pair[1]])[:, None],
    )


def solution(mesh):
    in_specs = (
        P(("dp", "expert"), None),
        P(),
        P(("dp", "expert"), None),
        P(("dp", "expert"), None),
        P(),
        P(None, ("dp", "expert"), None),
        P(None, ("dp", "expert")),
        P(("dp", "expert"), None),
        P(("dp", "expert"), None),
        P(("dp", "expert"), None),
        P(None, ("dp", "expert")),
        P(("dp", "expert")),
        P(("dp", "expert"), None),
        P(None, "expert", "dp", None),
        P(None, "expert", "dp", None),
        P(("dp", "expert"), None),
    )
    out_specs = (
        P(("dp", "expert"), None),
        P(("dp", "expert"), None),
        P(),
        P(None, ("dp", "expert"), None),
        P(None, ("dp", "expert")),
        P(("dp", "expert"), None),
        P(("dp", "expert"), None),
        P(("dp", "expert"), None),
        P(None, ("dp", "expert")),
        P(("dp", "expert")),
        P(("dp", "expert"), None),
        P(None, "expert", "dp", None),
        P(None, "expert", "dp", None),
    )
    return jax.shard_map(shards, mesh=mesh, in_specs=in_specs, out_specs=out_specs, check_vma=False)
```

time: 1960 us -> 452 us (0.23)
  waiting for transfers between devices: 1120 us -> 104 us
  blocking collectives: 535 us -> 19.5 us
  Pallas kernels: 0 us -> 161 us
  matrix products: 116 us -> 0 us
  other arithmetic: 79.1 us -> 18.4 us
  starting transfers between devices: 35 us -> 91.7 us
    reduce_scatter x6 -> x1, waiting for transfers between devices: 617 us -> 0.01 us  [shards(): lax.psum_scatter(second_grad, 'dp', scatter_dimension=0, tiled=True)[0]]
    all_gather x5 -> x0, blocking collectives: 360 us -> none  [the longest x1 83 us: shards(): lax.all_gather(attn_out, ('dp', 'expert'), axis=0, tiled=True)]
    unnamed x17 -> x4, waiting for transfers between devices: 301 us -> 0.57 us
    pallas_call x0 -> x27, Pallas kernels: none -> 161 us  [call(): pl.pallas_call(body, out_shape=outs, in_specs=specs, out_specs=out_specs,...]
    psum x1 -> x0, waiting for transfers between devices: 130 us -> none  [shards(): lax.psum(jnp.einsum('td,te->de', frames, embed_pre_grad, preferred_elemen...]
    dot_general x39 -> x0, matrix products: 116 us -> none  [the longest x2 15.5 us: moe_forward(): jnp.einsum('zve,zeg->zvg', arrived_rows, input_weight, preferred_element_...]
    ppermute x0 -> x42, waiting for transfers between devices: none -> 96.4 us  [the longest x24 67.2 us: swap_blocks(): lax.ppermute(blocks[k], 'expert', [(i, i ^ k) for i in range(total)])]
    psum x2 -> x0, blocking collectives: 77.5 us -> none  [the longest x1 39.4 us: shards(): lax.psum((jnp.sum(weighted, 0), jnp.sum(weighted * conv_depth, 0)), ('dp'...]
  transfers between devices with their start and end apart: 20 -> 51, of which waited for: 14 -> 25; matrix products, arithmetic and copies ran while one was open for 7% -> 6% of each run, Pallas kernels for 0% -> 24%
where the time goes in v2:
time: 452 us; the launch traced here: 449 us
  Pallas kernels  161 us (36%)
  waiting for transfers between devices  104 us (23%)
  starting transfers between devices  91.7 us (20%)
  local copies, waits for them, and re-layouts  38.2 us (8%)
  blocking collectives  19.5 us (4%)
  other arithmetic  18.4 us (4%)
  between operations  15.6 us (3%)
    pallas_call x27, Pallas kernels, call(): pl.pallas_call(body, out_shape=outs, in_specs=specs, out_specs=out_specs,...  161 us
    ppermute x24, waiting for transfers between devices, swap_blocks(): lax.ppermute(blocks[k], 'expert', [(i, i ^ k) for i in range(total)])  67.2 us
    ppermute x24, starting transfers between devices, swap_blocks(): lax.ppermute(blocks[k], 'expert', [(i, i ^ k) for i in range(total)])  48.5 us
    unnamed x115, local copies, waits for them, and re-layouts  26.4 us
    all_to_all x1, blocking collectives, shards(): lax.all_to_all(jnp.broadcast_to(dense[None], (peers,) + dense.shape), 'ex...  19.5 us
    ppermute x14, starting transfers between devices, exchange(): return lax.ppermute(values, axes, [(i, i ^ mask) for i in range(total)])  16.1 us
    ppermute x4, waiting for transfers between devices, dp_exchange(): return lax.ppermute(values, 'dp', [(i, i ^ mask) for i in range(dp_count)])  15.9 us
    ppermute x14, waiting for transfers between devices, exchange(): return lax.ppermute(values, axes, [(i, i ^ mask) for i in range(total)])  13.3 us
  transfers between devices with their start and end apart: 51, of which 25 were waited for; matrix products, arithmetic and copies ran while one was open for 6% of the time, Pallas kernels for 24%

profile of v2, /device:TPU:0, one launch (start us, length us, event | category | flops | bytes accessed | tf_op | source)
XLA Modules:
  0.0 448.6 jit_solution(5507070826313071307)
XLA Ops:
  11.6 7.3 %all-to-all-start = ((bf16[32,16,128]{2,1,0:T(8,128)(2,1)}), bf16[32,16,128]{2,1,0:T(8,128)(2,1)S(1)}, u32[]{:S(2)}, u32[]{:S(2)}) async-start(bf16[32,16,128]{2,1,0:T(8,128)(2,1)} %broadcast_in_dim.44), calls=%async_computation | async-start | bytes 262144 | tf_op jit(solution)/shard_map/all_to_all | solution.py:65
  20.6 3.3 shard_map.264
  25.7 2.4 collective-permute-start.2
  28.4 9.2 %collective-permute-done.block = bf16[256,512]{1,0:T(8,128)(2,1)S(1)} collective-permute-done((bf16[256,512]{1,0:T(8,128)(2,1)}, bf16[256,512]{1,0:T(8,128)(2,1)S(1)}, u32[]{:S(2)}, u32[]{:S(2)}) %collective-permute-start) | collective-permute-done | bytes 262176 | tf_op jit(solution)/shard_map/ppermute | solution.py:77
  37.6 9.7 %collective-permute-done.2.block = bf16[256,512]{1,0:T(8,128)(2,1)S(1)} collective-permute-done((bf16[256,512]{1,0:T(8,128)(2,1)}, bf16[256,512]{1,0:T(8,128)(2,1)S(1)}, u32[]{:S(2)}, u32[]{:S(2)}) %collective-permute-start.2) | collective-permute-done | bytes 262176 | tf_op jit(solution)/shard_map/ppermute | solution.py:77
  47.3 19.5 %all_to_all.30 = bf16[4,16,3584]{2,1,0:T(8,128)(2,1)} all-to-all(bf16[4,16,3584]{2,1,0:T(8,128)(2,1)S(1)} %broadcast_in_dim.45), channel_id=1, replica_groups=mesh['dp'=8,'expert'=4] {'expert'}, dimensions={0} | all-to-all | bytes 917504 | tf_op jit(solution)/shard_map/all_to_all | solution.py:797
  69.0 2.2 copy-done
  71.1 3.0 shard_map.266
  74.6 3.0 shard_map.267
  79.3 3.0 shard_map.268
  82.3 2.4 collective-permute-start.5
  85.7 4.9 %shard_map.269 = (f32[512,512]{1,0:T(8,128)}, f32[512,512]{1,0:T(8,128)}, f32[512,128]{1,0:T(8,128)}, f32[512,1]{1,0:T(8,128)}, f32[512,1]{1,0:T(8,128)}, /*inde...) custom-call(s32[3]{0:T(128)} %slice_bitcast_fusion.11.ends, bf16[512,512]{1,0:T(8,128)(2,1)} %frames.9, ...), custom_call_target="tpu_custom_call" | custom-call | tf_op jit(solution)/shard_map/pallas_call | solution.py:96
  93.5 2.2 copy-done.1
  95.8 3.0 shard_map.265.blocks_0_
  101.4 21.4 %shard_map.270 = (bf16[512,512]{1,0:T(8,128)(2,1)}, f32[512,512]{1,0:T(8,128)}, f32[512,512]{1,0:T(8,128)}, bf16[512,512]{1,0:T(8,128)(2,1)}, bf16[512,1536]{1,0...) custom-call(bf16[512,512]{1,0:T(8,128)(2,1)} %frames.9, ...), custom_call_target="tpu_custom_call" | custom-call | tf_op jit(solution)/shard_map/pallas_call | solution.py:96
  131.9 3.4 collective-permute-start.12
  137.7 2.3 collective-permute-done.11
  140.6 3.9 shard_map.271
  146.5 2.4 collective-permute-start.17
  148.9 6.2 %collective-permute-done.13.block = bf16[256,512]{1,0:T(8,128)(2,1)S(1)} collective-permute-done((bf16[256,512]{1,0:T(8,128)(2,1)}, bf16[256,512]{1,0:T(8,128)(2,1)S(1)}, u32[]{:S(2)}, u32[]{:S(2)}) %collective-permute-start.13) | collective-permute-done | bytes 262176 | tf_op jit(solution)/shard_map/ppermute | solution.py:77
  155.1 2.2 copy-done.4
  157.3 2.8 shard_map.273
  160.2 4.5 %collective-permute-done.15.block = bf16[256,512]{1,0:T(8,128)(2,1)S(1)} collective-permute-done((bf16[256,512]{1,0:T(8,128)(2,1)}, bf16[256,512]{1,0:T(8,128)(2,1)S(1)}, u32[]{:S(2)}, u32[]{:S(2)}) %collective-permute-start.15) | collective-permute-done | bytes 262176 | tf_op jit(solution)/shard_map/ppermute | solution.py:77
  164.7 2.8 shard_map.274
  167.6 2.8 shard_map.275
  170.4 3.5 collective-permute-start.18
  173.9 2.8 shard_map.272.blocks_0_
  177.4 10.6 %collective-permute-done.16.blocks_2_ = bf16[256,512]{1,0:T(8,128)(2,1)S(1)} collective-permute-done((bf16[256,512]{1,0:T(8,128)(2,1)S(1)}, bf16[256,512]{1,0:T(8,128)(2,1)S(1)}, u32[]{:S(2)}, u32[]{:S(2)}) %collective-permute-start.16) | collective-permute-done | bytes 262176 | tf_op jit(solution)/shard_map/ppermute | solution.py:77
  188.8 4.9 %shard_map.276 = (bf16[512,512]{1,0:T(8,128)(2,1)}, f32[512,512]{1,0:T(8,128)}, f32[512,1]{1,0:T(8,128)}, f32[1,512]{1,0:T(1,128)}, bf16[256,512]{1,0:T(8,128)(2...) custom-call(f32[512,512]{1,0:T(8,128)} %get-tuple-element.129.x3, ...), custom_call_target="tpu_custom_call" | custom-call | tf_op jit(solution)/shard_map/pallas_call | solution.py:96
  193.7 2.5 collective-permute-start.22
  196.2 3.2 collective-permute-start.19
  199.3 5.5 %collective-permute-done.22.grad.grads_3_ = bf16[256,512]{1,0:T(8,128)(2,1)S(1)} collective-permute-done((bf16[256,512]{1,0:T(8,128)(2,1)}, bf16[256,512]{1,0:T(8,128)(2,1)S(1)}, u32[]{:S(2)}, u32[]{:S(2)}) %collective-permute-start.22) | collective-permute-done | bytes 262176 | tf_op jit(solution)/shard_map/ppermute | solution.py:77
  204.9 2.2 copy-done.6
  207.1 4.1 shard_map.280
  211.2 2.6 collective-permute-start.24
  213.8 4.1 shard_map.278
  217.9 12.0 %collective-permute-start.20 = (bf16[256,512]{1,0:T(8,128)(2,1)S(1)}, bf16[256,512]{1,0:T(8,128)(2,1)S(1)}, u32[]{:S(2)}, u32[]{:S(2)}) collective-permute-start(bf16[256,512]{1,0:T(8,128)(2,1)S(1)} %get-tuple-element.141), channel_id=1, source_target_pairs={{0,1},{1,0},{2,3},{3,2},{4,5},{5,4},{6,7},{7,6},{8,9},{9,8},{10,11... | collective-permute-start | bytes 786440 | tf_op jit(solution)/shard_map/ppermute | solution.py:77
  229.9 4.1 shard_map.279
  234.1 4.1 shard_map.277
  238.9 6.0 %shard_map.281 = bf16[8,512,512]{2,1,0:T(8,128)(2,1)S(1)} custom-call(s32[1]{0:T(128)} %bitcast.20.dp_index, bf16[256,512]{1,0:T(8,128)(2,1)S(1)} %get-tuple-element.142.inputs_0_, bf16[256,512]{1,0:T(8,128)(2,1)S(1)} %get-tuple-element.143.inputs_1_, bf16[256,512]{1,0:T(8,128)(2,1)S(1)} %get-tuple-element.145.inputs_2_, ...), custom_call_target="tpu_custom_call" | custom-call | tf_op jit(solution)/shard_map/pallas_call | solution.py:96
  247.9 6.1 %shard_map.282 = (f32[512,512]{1,0:T(8,128)}, bf16[512,512]{1,0:T(8,128)(2,1)}, f32[512,512]{1,0:T(8,128)}, f32[8,512]{1,0:T(8,128)}) custom-call(f32[1]{0:T(128)} %bitcast.frame_count, f32[512,512]{1,0:T(8,128)} %get-tuple-element.137.dx4, bf16[256,512]{1,0:T(8,128)(2,1)} %copy-done.16, bf16[256,512]{1,0:T(8,128)(2,1)} %copy-done.26, ...), custom_call_target="tpu_custom_call" | custom-call | tf_op jit(solution)/shard_map/pallas_call | solution.py:96
  261.8 2.4 collective-permute-start.31
  269.7 33.3 %shard_map.283 = (bf16[512,1024]{1,0:T(8,128)(2,1)}, bf16[512,512]{1,0:T(8,128)(2,1)}, bf16[512,1536]{1,0:T(8,128)(2,1)}, f32[512,512]{1,0:T(8,128)}, f32[512,1]...) custom-call(f32[1]{0:T(128)} %bitcast.frame_count, ...), custom_call_target="tpu_custom_call" | custom-call | tf_op jit(solution)/shard_map/pallas_call | solution.py:96
  303.0 9.8 %shard_map.285 = (bf16[512,4096]{1,0:T(8,128)(2,1)}, bf16[512,512]{1,0:T(8,128)(2,1)}, f32[128,512]{1,0:T(8,128)}) custom-call(bf16[512,512]{1,0:T(8,128)(2,1)} %get-tuple-element.171.ua, bf16[512,1536]{1,0:T(8,128)(2,1)} %get-tuple-element.172.dproj, bf16[512,512]{1,0:T(8,128)(2,1)} %get-tuple-element.173.attended, ...), custom_call_target="tpu_custom_call" | custom-call | tf_op jit(solution)/shard_map/pallas_call | solution.py:96
  312.8 4.6 %all-to-all-start.2 = ((bf16[8,64,4096]{2,1,0:T(8,128)(2,1)}), bf16[8,64,4096]{2,1,0:T(8,128)(2,1)}, u32[]{:S(2)}, u32[]{:S(2)}) async-start(bf16[8,64,4096]{2,1,0:T(8,128)(2,1)} %bitcast.107), calls=%async_computation.2 | async-start | bytes 8388608 | tf_op jit(solution)/shard_map/all_to_all | solution.py:69
  319.3 2.4 collective-permute-start.36
  321.8 5.1 %collective-permute-done.32.grad.grads_1_ = bf16[256,512]{1,0:T(8,128)(2,1)S(1)} collective-permute-done((bf16[256,512]{1,0:T(8,128)(2,1)S(1)}, bf16[256,512]{1,0:T(8,128)(2,1)S(1)}, u32[]{:S(2)}, u32[]{:S(2)}) %collective-permute-start.32) | collective-permute-done | bytes 262176 | tf_op jit(solution)/shard_map/ppermute | solution.py:77
  326.9 7.6 %collective-permute-done.36.grad.grads_3_ = bf16[256,512]{1,0:T(8,128)(2,1)S(1)} collective-permute-done((bf16[256,512]{1,0:T(8,128)(2,1)S(1)}, bf16[256,512]{1,0:T(8,128)(2,1)S(1)}, u32[]{:S(2)}, u32[]{:S(2)}) %collective-permute-start.36) | collective-permute-done | bytes 262176 | tf_op jit(solution)/shard_map/ppermute | solution.py:77
  334.5 2.3 copy-done.2
  336.8 4.1 shard_map.288
  342.7 8.7 %collective-permute-done.34.grad.grads_2_ = bf16[256,512]{1,0:T(8,128)(2,1)S(1)} collective-permute-done((bf16[256,512]{1,0:T(8,128)(2,1)S(1)}, bf16[256,512]{1,0:T(8,128)(2,1)S(1)}, u32[]{:S(2)}, u32[]{:S(2)}) %collective-permute-start.34) | collective-permute-done | bytes 262176 | tf_op jit(solution)/shard_map/ppermute | solution.py:77
  351.4 3.9 shard_map.287
  355.4 3.9 shard_map.286
  359.3 5.8 %collective-permute-start.33 = (bf16[256,512]{1,0:T(8,128)(2,1)S(1)}, bf16[256,512]{1,0:T(8,128)(2,1)S(1)}, u32[]{:S(2)}, u32[]{:S(2)}) collective-permute-start(bf16[256,512]{1,0:T(8,128)(2,1)S(1)} %get-tuple-element.186), channel_id=1, source_target_pairs={{0,1},{1,0},{2,3},{3,2},{4,5},{5,4},{6,7},{7,6},{8,9},{9,8},{10,11... | collective-permute-start | bytes 786440 | tf_op jit(solution)/shard_map/ppermute | solution.py:77
  365.1 3.9 shard_map.284
  369.7 7.5 %shard_map.290 = (bf16[4,512,512]{2,1,0:T(8,128)(2,1)S(1)}, bf16[4,512,512]{2,1,0:T(8,128)(2,1)}) custom-call(s32[1]{0:T(128)} %bitcast.20.dp_index, bf16[256,512]{1,0:T(8,128)(2,1)S(1)} %get-tuple-element.200.inputs_0_, bf16[256,512]{1,0:T(8,128)(2,1)S(1)} %get-tuple-element.201.inputs_1_, bf16[256,512]{1,0:T(8,128)(2,1)S(1)} %get-tuple-element.202.inputs_2_, ...), custom_call_target="tpu_custom_call" | custom-call | tf_op jit(solution)/shard_map/pallas_call | solution.py:96
  380.0 3.3 all-to-all-start.5
  383.3 3.8 reduce_sum.40
  387.2 6.4 %all-to-all-done.5 = f32[32,16,128]{2,1,0:T(8,128)S(1)} async-done(((f32[32,16,128]{2,1,0:T(8,128)}), f32[32,16,128]{2,1,0:T(8,128)S(1)}, u32[]{:S(2)}, u32[]{:S(2)}) %all-to-all-start.5) | async-done | bytes 262176 | tf_op jit(solution)/shard_map/all_to_all | solution.py:69
  393.6 3.5 all-to-all-start.3
  397.1 2.2 add_convert_fusion
  404.9 4.7 %shard_map.289 = f32[512,512]{1,0:T(8,128)} custom-call(bf16[512,512]{1,0:T(8,128)(2,1)} %frames.9, bf16[256,512]{1,0:T(8,128)(2,1)} %copy-done.15, bf16[256,512]{1,0:T(8,128)(2,1)} %copy-done.24, bf16[256,512]{1,0:T(8,128)(2,1)} %copy-done.23, bf16[256,512]{1,0:T(8,128)(2,1)} %copy-done.22, s32[512,1]{1,0:T(8,128)} %get-tuple-element.118.slot_col, ...), custom_call_target="tpu_custom_call" | custom-call | tf_op jit(solution)/shard_map/pallas_call | solution.py:96
  413.4 4.6 %all-to-all-start.4 = ((bf16[32,16,512]{2,1,0:T(8,128)(2,1)}), bf16[32,16,512]{2,1,0:T(8,128)(2,1)S(1)}, u32[]{:S(2)}, u32[]{:S(2)}) async-start(bf16[32,16,512]{2,1,0:T(8,128)(2,1)} %broadcast_in_dim.47), calls=%async_computation.4 | async-start | bytes 1048576 | tf_op jit(solution)/shard_map/all_to_all | solution.py:65
  418.0 14.0 %collective-permute-done.41 = bf16[512,512]{1,0:T(8,128)(2,1)S(1)} collective-permute-done((bf16[512,512]{1,0:T(8,128)(2,1)S(1)}, bf16[512,512]{1,0:T(8,128)(2,1)S(1)}, u32[]{:S(2)}, u32[]{:S(2)}) %collective-permute-start.41) | collective-permute-done | bytes 524320 | tf_op jit(solution)/shard_map/ppermute | solution.py:1022
  (248 shorter events, 77.6 us)
Async XLA Ops:
  7.2 11.7 %copy-start.39 = (s32[512,1]{0,1:T(1,128)S(1)}, s32[512,1]{0,1:T(1,128)}, u32[]{:S(2)}) copy-start(s32[512,1]{0,1:T(1,128)} %param.19) | copy-start | bytes 6148
  7.2 12.6 %copy-start.40 = (s32[512,1]{0,1:T(1,128)S(1)}, s32[512,1]{0,1:T(1,128)}, u32[]{:S(2)}) copy-start(s32[512,1]{0,1:T(1,128)} %param.20) | copy-start | bytes 6148
  7.2 61.7 %all-gather.8.cloned.1.call-start = ((), (), s32[]{:S(2)}) async-start(), calls=%async_computation.9 | async-start | bytes 4718592 | tf_op jit(solution)/shard_map/all_gather | solution.py:766
  8.4 19.9 %copy-start.34 = (bf16[16,1536]{1,0:T(8,128)(2,1)S(1)}, bf16[16,1536]{1,0:T(8,128)(2,1)}, u32[]{:S(2)}) copy-start(bf16[16,1536]{1,0:T(8,128)(2,1)} %param.24) | copy-start | bytes 147460
  8.4 19.9 %copy-start.35 = (bf16[16,1024]{1,0:T(8,128)(2,1)S(1)}, bf16[16,1024]{1,0:T(8,128)(2,1)}, u32[]{:S(2)}) copy-start(bf16[16,1024]{1,0:T(8,128)(2,1)} %param.26) | copy-start | bytes 98308
  8.4 19.9 %copy-start.37 = (bf16[16,512]{1,0:T(8,128)(2,1)S(1)}, bf16[16,512]{1,0:T(8,128)(2,1)}, u32[]{:S(2)}) copy-start(bf16[16,512]{1,0:T(8,128)(2,1)} %param.29) | copy-start | bytes 49156
  8.4 19.9 %copy-start.38 = (bf16[16,512]{1,0:T(8,128)(2,1)S(1)}, bf16[16,512]{1,0:T(8,128)(2,1)}, u32[]{:S(2)}) copy-start(bf16[16,512]{1,0:T(8,128)(2,1)} %param.25) | copy-start | bytes 49156
  11.6 16.8 %all-to-all-start = ((bf16[32,16,128]{2,1,0:T(8,128)(2,1)}), bf16[32,16,128]{2,1,0:T(8,128)(2,1)S(1)}, u32[]{:S(2)}, u32[]{:S(2)}) async-start(bf16[32,16,128]{2,1,0:T(8,128)(2,1)} %broadcast_in_dim.44), calls=%async_computation | async-start | bytes 262144 | tf_op jit(solution)/shard_map/all_to_all | solution.py:65
  18.9 81.6 %all-gather.6.cloned.1.call-start = ((), (), s32[]{:S(2)}) async-start(), calls=%async_computation.7 | async-start | bytes 4128768 | tf_op jit(solution)/shard_map/all_gather | solution.py:800
  20.6 47.3 %copy-start.41 = (s32[32,4]{0,1:T(4,128)S(1)}, s32[32,4]{0,1:T(4,128)}, u32[]{:S(2)}) copy-start(s32[32,4]{0,1:T(4,128)} %param.18) | copy-start | bytes 1540
  23.9 13.7 %collective-permute-start = (bf16[256,512]{1,0:T(8,128)(2,1)}, bf16[256,512]{1,0:T(8,128)(2,1)S(1)}, u32[]{:S(2)}, u32[]{:S(2)}) collective-permute-start(bf16[256,512]{1,0:T(8,128)(2,1)} %get-tuple-element.115), channel_id=1, source_target_pairs={{0,1},{1,0},{2,3},{3,2},{4,5},{5,4},{6,7},{7,6},{8,9},{9,8},{10,11... | collective-permute-start | bytes 786440 | tf_op jit(solution)/shard_map/ppermute | solution.py:77
  25.7 21.5 %collective-permute-start.2 = (bf16[256,512]{1,0:T(8,128)(2,1)}, bf16[256,512]{1,0:T(8,128)(2,1)S(1)}, u32[]{:S(2)}, u32[]{:S(2)}) collective-permute-start(bf16[256,512]{1,0:T(8,128)(2,1)} %get-tuple-element.116), channel_id=1, source_target_pairs={{0,2},{1,3},{2,0},{3,1},{4,6},{5,7},{6,4},{7,5},{8,10},{9,11},{10,... | collective-permute-start | bytes 786440 | tf_op jit(solution)/shard_map/ppermute | solution.py:77
  28.1 19.1 %collective-permute-start.4 = (bf16[256,512]{1,0:T(8,128)(2,1)}, bf16[256,512]{1,0:T(8,128)(2,1)S(1)}, u32[]{:S(2)}, u32[]{:S(2)}) collective-permute-start(bf16[256,512]{1,0:T(8,128)(2,1)} %get-tuple-element.117), channel_id=1, source_target_pairs={{0,3},{1,2},{2,1},{3,0},{4,7},{5,6},{6,5},{7,4},{8,11},{9,10},{10,... | collective-permute-start | bytes 786440 | tf_op jit(solution)/shard_map/ppermute | solution.py:77
  66.8 82.1 %all-gather.10.cloned.1.call-start = ((), (), s32[]{:S(2)}) async-start(), calls=%async_computation.10 | async-start | bytes 4718592 | tf_op jit(solution)/shard_map/all_gather | solution.py:803
  74.1 26.4 %collective-permute-start.1 = (bf16[256,512]{1,0:T(8,128)(2,1)S(1)}, bf16[256,512]{1,0:T(8,128)(2,1)S(1)}, u32[]{:S(2)}, u32[]{:S(2)}) collective-permute-start(bf16[256,512]{1,0:T(8,128)(2,1)S(1)} %shard_map.266), channel_id=1, source_target_pairs={{0,1},{1,0},{2,3},{3,2},{4,5},{5,4},{6,7},{7,6},{8,9},{9,8},{10,11... | collective-permute-start | bytes 786440 | tf_op jit(solution)/shard_map/ppermute | solution.py:77
  77.6 23.0 %collective-permute-start.3 = (bf16[256,512]{1,0:T(8,128)(2,1)S(1)}, bf16[256,512]{1,0:T(8,128)(2,1)S(1)}, u32[]{:S(2)}, u32[]{:S(2)}) collective-permute-start(bf16[256,512]{1,0:T(8,128)(2,1)S(1)} %shard_map.267), channel_id=1, source_target_pairs={{0,2},{1,3},{2,0},{3,1},{4,6},{5,7},{6,4},{7,5},{8,10},{9,11},{10,... | collective-permute-start | bytes 786440 | tf_op jit(solution)/shard_map/ppermute | solution.py:77
  82.3 9.4 %copy-start.47 = (f32[128]{0:T(128)S(1)}, f32[128]{0:T(128)}, u32[]{:S(2)}) copy-start(f32[128]{0:T(128)} %constant.34.clone) | copy-start | bytes 1540
  82.3 11.2 %copy-start.10 = (bf16[256,512]{1,0:T(8,128)(2,1)S(1)}, bf16[256,512]{1,0:T(8,128)(2,1)}, u32[]{:S(2)}) copy-start(bf16[256,512]{1,0:T(8,128)(2,1)} %get-tuple-element.114.block) | copy-start | bytes 786436
  82.3 18.2 %collective-permute-start.5 = (bf16[256,512]{1,0:T(8,128)(2,1)S(1)}, bf16[256,512]{1,0:T(8,128)(2,1)S(1)}, u32[]{:S(2)}, u32[]{:S(2)}) collective-permute-start(bf16[256,512]{1,0:T(8,128)(2,1)S(1)} %shard_map.268), channel_id=1, source_target_pairs={{0,3},{1,2},{2,1},{3,0},{4,7},{5,6},{6,5},{7,4},{8,11},{9,10},{10,... | collective-permute-start | bytes 786440 | tf_op jit(solution)/shard_map/ppermute | solution.py:77
  122.8 1.4 collective-permute-start.6
  124.9 5.0 %collective-permute-start.9 = (f32[8,512]{1,0:T(8,128)S(1)}, f32[8,512]{1,0:T(8,128)S(1)}, u32[]{:S(2)}, u32[]{:S(2)}) collective-permute-start(f32[8,512]{1,0:T(8,128)S(1)} %add.78), channel_id=1, source_target_pairs={{0,24},{1,25},{2,26},{3,27},{4,28},{5,29},{6,30},{7,31},{8,16},{9,... | collective-permute-start | bytes 49160 | tf_op jit(solution)/shard_map/ppermute | solution.py:34
  126.4 4.1 collective-permute-start.8
  127.9 4.1 collective-permute-start.7
  131.9 5.7 %collective-permute-start.12 = (f32[8,512]{1,0:T(8,128)S(1)}, f32[8,512]{1,0:T(8,128)S(1)}, u32[]{:S(2)}, u32[]{:S(2)}) collective-permute-start(f32[8,512]{1,0:T(8,128)S(1)} %add_add_fusion.3), channel_id=1, source_target_pairs={{0,3},{1,2},{2,1},{3,0},{4,7},{5,6},{6,5},{7,4},{8,11},{9,10},{10,... | collective-permute-start | bytes 49160 | tf_op jit(solution)/shard_map/ppermute | solution.py:34
  135.3 4.6 %collective-permute-start.11 = (f32[8,512]{1,0:T(8,128)S(1)}, f32[8,512]{1,0:T(8,128)S(1)}, u32[]{:S(2)}, u32[]{:S(2)}) collective-permute-start(f32[8,512]{1,0:T(8,128)S(1)} %add_add_fusion.3), channel_id=1, source_target_pairs={{0,2},{1,3},{2,0},{3,1},{4,6},{5,7},{6,4},{7,5},{8,10},{9,11},{10,... | collective-permute-start | bytes 49160 | tf_op jit(solution)/shard_map/ppermute | solution.py:34
  135.3 4.6 %collective-permute-start.10 = (f32[8,512]{1,0:T(8,128)S(1)}, f32[8,512]{1,0:T(8,128)S(1)}, u32[]{:S(2)}, u32[]{:S(2)}) collective-permute-start(f32[8,512]{1,0:T(8,128)S(1)} %add_add_fusion.3), channel_id=1, source_target_pairs={{0,1},{1,0},{2,3},{3,2},{4,5},{5,4},{6,7},{7,6},{8,9},{9,8},{10,11... | collective-permute-start | bytes 49160 | tf_op jit(solution)/shard_map/ppermute | solution.py:34
  144.5 10.6 %collective-permute-start.13 = (bf16[256,512]{1,0:T(8,128)(2,1)}, bf16[256,512]{1,0:T(8,128)(2,1)S(1)}, u32[]{:S(2)}, u32[]{:S(2)}) collective-permute-start(bf16[256,512]{1,0:T(8,128)(2,1)} %get-tuple-element.131), channel_id=1, source_target_pairs={{0,1},{1,0},{2,3},{3,2},{4,5},{5,4},{6,7},{7,6},{8,9},{9,8},{10,11... | collective-permute-start | bytes 786440 | tf_op jit(solution)/shard_map/ppermute | solution.py:77
  144.6 20.1 %collective-permute-start.15 = (bf16[256,512]{1,0:T(8,128)(2,1)}, bf16[256,512]{1,0:T(8,128)(2,1)S(1)}, u32[]{:S(2)}, u32[]{:S(2)}) collective-permute-start(bf16[256,512]{1,0:T(8,128)(2,1)} %get-tuple-element.132), channel_id=1, source_target_pairs={{0,2},{1,3},{2,0},{3,1},{4,6},{5,7},{6,4},{7,5},{8,10},{9,11},{10,... | collective-permute-start | bytes 786440 | tf_op jit(solution)/shard_map/ppermute | solution.py:77
  146.5 21.1 %collective-permute-start.17 = (bf16[256,512]{1,0:T(8,128)(2,1)}, bf16[256,512]{1,0:T(8,128)(2,1)S(1)}, u32[]{:S(2)}, u32[]{:S(2)}) collective-permute-start(bf16[256,512]{1,0:T(8,128)(2,1)} %get-tuple-element.133), channel_id=1, source_target_pairs={{0,3},{1,2},{2,1},{3,0},{4,7},{5,6},{6,5},{7,4},{8,11},{9,10},{10,... | collective-permute-start | bytes 786440 | tf_op jit(solution)/shard_map/ppermute | solution.py:77
  160.1 17.3 %collective-permute-start.14 = (bf16[256,512]{1,0:T(8,128)(2,1)S(1)}, bf16[256,512]{1,0:T(8,128)(2,1)S(1)}, u32[]{:S(2)}, u32[]{:S(2)}) collective-permute-start(bf16[256,512]{1,0:T(8,128)(2,1)S(1)} %shard_map.273), channel_id=1, source_target_pairs={{0,1},{1,0},{2,3},{3,2},{4,5},{5,4},{6,7},{7,6},{8,9},{9,8},{10,11... | collective-permute-start | bytes 786440 | tf_op jit(solution)/shard_map/ppermute | solution.py:77
  167.5 20.5 %collective-permute-start.16 = (bf16[256,512]{1,0:T(8,128)(2,1)S(1)}, bf16[256,512]{1,0:T(8,128)(2,1)S(1)}, u32[]{:S(2)}, u32[]{:S(2)}) collective-permute-start(bf16[256,512]{1,0:T(8,128)(2,1)S(1)} %shard_map.274), channel_id=1, source_target_pairs={{0,2},{1,3},{2,0},{3,1},{4,6},{5,7},{6,4},{7,5},{8,10},{9,11},{10,... | collective-permute-start | bytes 786440 | tf_op jit(solution)/shard_map/ppermute | solution.py:77
  170.4 17.6 %collective-permute-start.18 = (bf16[256,512]{1,0:T(8,128)(2,1)S(1)}, bf16[256,512]{1,0:T(8,128)(2,1)S(1)}, u32[]{:S(2)}, u32[]{:S(2)}) collective-permute-start(bf16[256,512]{1,0:T(8,128)(2,1)S(1)} %shard_map.275), channel_id=1, source_target_pairs={{0,3},{1,2},{2,1},{3,0},{4,7},{5,6},{6,5},{7,4},{8,11},{9,10},{10,... | collective-permute-start | bytes 786440 | tf_op jit(solution)/shard_map/ppermute | solution.py:77
  177.4 10.6 %copy-start.31 = (bf16[256,512]{1,0:T(8,128)(2,1)}, bf16[256,512]{1,0:T(8,128)(2,1)S(1)}, u32[]{:S(2)}) copy-start(bf16[256,512]{1,0:T(8,128)(2,1)S(1)} %collective-permute-done.14.blocks_1_) | copy-start | bytes 786436
  193.7 11.2 %collective-permute-start.22 = (bf16[256,512]{1,0:T(8,128)(2,1)}, bf16[256,512]{1,0:T(8,128)(2,1)S(1)}, u32[]{:S(2)}, u32[]{:S(2)}) collective-permute-start(bf16[256,512]{1,0:T(8,128)(2,1)} %get-tuple-element.146), channel_id=1, source_target_pairs={{0,3},{1,2},{2,1},{3,0},{4,7},{5,6},{6,5},{7,4},{8,11},{9,10},{10,... | collective-permute-start | bytes 786440 | tf_op jit(solution)/shard_map/ppermute | solution.py:77
  196.2 17.6 %collective-permute-start.19 = (bf16[256,512]{1,0:T(8,128)(2,1)}, bf16[256,512]{1,0:T(8,128)(2,1)S(1)}, u32[]{:S(2)}, u32[]{:S(2)}) collective-permute-start(bf16[256,512]{1,0:T(8,128)(2,1)} %get-tuple-element.140), channel_id=1, source_target_pairs={{0,1},{1,0},{2,3},{3,2},{4,5},{5,4},{6,7},{7,6},{8,9},{9,8},{10,11... | collective-permute-start | bytes 786440 | tf_op jit(solution)/shard_map/ppermute | solution.py:77
  199.3 30.6 %collective-permute-start.21 = (bf16[256,512]{1,0:T(8,128)(2,1)}, bf16[256,512]{1,0:T(8,128)(2,1)S(1)}, u32[]{:S(2)}, u32[]{:S(2)}) collective-permute-start(bf16[256,512]{1,0:T(8,128)(2,1)} %get-tuple-element.144), channel_id=1, source_target_pairs={{0,2},{1,3},{2,0},{3,1},{4,6},{5,7},{6,4},{7,5},{8,10},{9,11},{10,... | collective-permute-start | bytes 786440 | tf_op jit(solution)/shard_map/ppermute | solution.py:77
  211.2 35.8 %collective-permute-start.24 = (bf16[256,512]{1,0:T(8,128)(2,1)S(1)}, bf16[256,512]{1,0:T(8,128)(2,1)S(1)}, u32[]{:S(2)}, u32[]{:S(2)}) collective-permute-start(bf16[256,512]{1,0:T(8,128)(2,1)S(1)} %get-tuple-element.158), channel_id=1, source_target_pairs={{0,3},{1,2},{2,1},{3,0},{4,7},{5,6},{6,5},{7,4},{8,11},{9,10},{10,... | collective-permute-start | bytes 786440 | tf_op jit(solution)/shard_map/ppermute | solution.py:77
  217.9 16.2 %copy-start.9 = (bf16[256,512]{1,0:T(8,128)(2,1)S(1)}, bf16[256,512]{1,0:T(8,128)(2,1)}, u32[]{:S(2)}) copy-start(bf16[256,512]{1,0:T(8,128)(2,1)} %get-tuple-element.138.grad.grads_0_) | copy-start | bytes 786436
  217.9 29.1 %collective-permute-start.20 = (bf16[256,512]{1,0:T(8,128)(2,1)S(1)}, bf16[256,512]{1,0:T(8,128)(2,1)S(1)}, u32[]{:S(2)}, u32[]{:S(2)}) collective-permute-start(bf16[256,512]{1,0:T(8,128)(2,1)S(1)} %get-tuple-element.141), channel_id=1, source_target_pairs={{0,1},{1,0},{2,3},{3,2},{4,5},{5,4},{6,7},{7,6},{8,9},{9,8},{10,11... | collective-permute-start | bytes 786440 | tf_op jit(solution)/shard_map/ppermute | solution.py:77
  234.0 12.9 %collective-permute-start.23 = (bf16[256,512]{1,0:T(8,128)(2,1)S(1)}, bf16[256,512]{1,0:T(8,128)(2,1)S(1)}, u32[]{:S(2)}, u32[]{:S(2)}) collective-permute-start(bf16[256,512]{1,0:T(8,128)(2,1)S(1)} %get-tuple-element.157), channel_id=1, source_target_pairs={{0,2},{1,3},{2,0},{3,1},{4,6},{5,7},{6,4},{7,5},{8,10},{9,11},{10,... | collective-permute-start | bytes 786440 | tf_op jit(solution)/shard_map/ppermute | solution.py:77
  254.0 1.4 collective-permute-start.25
  256.1 4.6 %collective-permute-start.28 = (f32[8,512]{1,0:T(8,128)S(1)}, f32[8,512]{1,0:T(8,128)S(1)}, u32[]{:S(2)}, u32[]{:S(2)}) collective-permute-start(f32[8,512]{1,0:T(8,128)S(1)} %add.85), channel_id=1, source_target_pairs={{0,24},{1,25},{2,26},{3,27},{4,28},{5,29},{6,30},{7,31},{8,16},{9,... | collective-permute-start | bytes 49160 | tf_op jit(solution)/shard_map/ppermute | solution.py:34
  257.5 3.7 collective-permute-start.27
  258.1 3.7 collective-permute-start.26
  261.8 5.6 %collective-permute-start.31 = (f32[8,512]{1,0:T(8,128)S(1)}, f32[8,512]{1,0:T(8,128)S(1)}, u32[]{:S(2)}, u32[]{:S(2)}) collective-permute-start(f32[8,512]{1,0:T(8,128)S(1)} %add_add_fusion.1), channel_id=1, source_target_pairs={{0,3},{1,2},{2,1},{3,0},{4,7},{5,6},{6,5},{7,4},{8,11},{9,10},{10,... | collective-permute-start | bytes 49160 | tf_op jit(solution)/shard_map/ppermute | solution.py:34
  264.2 4.6 %collective-permute-start.30 = (f32[8,512]{1,0:T(8,128)S(1)}, f32[8,512]{1,0:T(8,128)S(1)}, u32[]{:S(2)}, u32[]{:S(2)}) collective-permute-start(f32[8,512]{1,0:T(8,128)S(1)} %add_add_fusion.1), channel_id=1, source_target_pairs={{0,2},{1,3},{2,0},{3,1},{4,6},{5,7},{6,4},{7,5},{8,10},{9,11},{10,... | collective-permute-start | bytes 49160 | tf_op jit(solution)/shard_map/ppermute | solution.py:34
  265.3 3.8 collective-permute-start.29
  312.8 67.2 %all-to-all-start.2 = ((bf16[8,64,4096]{2,1,0:T(8,128)(2,1)}), bf16[8,64,4096]{2,1,0:T(8,128)(2,1)}, u32[]{:S(2)}, u32[]{:S(2)}) async-start(bf16[8,64,4096]{2,1,0:T(8,128)(2,1)} %bitcast.107), calls=%async_computation.2 | async-start | bytes 8388608 | tf_op jit(solution)/shard_map/all_to_all | solution.py:69
  317.4 121.0 %reduce-scatter.2.cloned.1.call-start = ((), (), s32[]{:S(2)}) async-start(), calls=%async_computation.8 | async-start | bytes 4718592 | tf_op jit(solution)/shard_map/reduce_scatter | solution.py:925
  318.3 8.6 %collective-permute-start.32 = (bf16[256,512]{1,0:T(8,128)(2,1)S(1)}, bf16[256,512]{1,0:T(8,128)(2,1)S(1)}, u32[]{:S(2)}, u32[]{:S(2)}) collective-permute-start(bf16[256,512]{1,0:T(8,128)(2,1)S(1)} %copy-done.50), channel_id=1, source_target_pairs={{0,1},{1,0},{2,3},{3,2},{4,5},{5,4},{6,7},{7,6},{8,9},{9,8},{10,11... | collective-permute-start | bytes 786440 | tf_op jit(solution)/shard_map/ppermute | solution.py:77
  319.3 15.2 %collective-permute-start.36 = (bf16[256,512]{1,0:T(8,128)(2,1)S(1)}, bf16[256,512]{1,0:T(8,128)(2,1)S(1)}, u32[]{:S(2)}, u32[]{:S(2)}) collective-permute-start(bf16[256,512]{1,0:T(8,128)(2,1)S(1)} %copy-done.49), channel_id=1, source_target_pairs={{0,3},{1,2},{2,1},{3,0},{4,7},{5,6},{6,5},{7,4},{8,11},{9,10},{10,... | collective-permute-start | bytes 786440 | tf_op jit(solution)/shard_map/ppermute | solution.py:77
  321.7 29.8 %collective-permute-start.34 = (bf16[256,512]{1,0:T(8,128)(2,1)S(1)}, bf16[256,512]{1,0:T(8,128)(2,1)S(1)}, u32[]{:S(2)}, u32[]{:S(2)}) collective-permute-start(bf16[256,512]{1,0:T(8,128)(2,1)S(1)} %copy-done.48), channel_id=1, source_target_pairs={{0,2},{1,3},{2,0},{3,1},{4,6},{5,7},{6,4},{7,5},{8,10},{9,11},{10,... | collective-permute-start | bytes 786440 | tf_op jit(solution)/shard_map/ppermute | solution.py:77
  340.9 36.2 %collective-permute-start.37 = (bf16[256,512]{1,0:T(8,128)(2,1)S(1)}, bf16[256,512]{1,0:T(8,128)(2,1)S(1)}, u32[]{:S(2)}, u32[]{:S(2)}) collective-permute-start(bf16[256,512]{1,0:T(8,128)(2,1)S(1)} %get-tuple-element.190), channel_id=1, source_target_pairs={{0,3},{1,2},{2,1},{3,0},{4,7},{5,6},{6,5},{7,4},{8,11},{9,10},{10,... | collective-permute-start | bytes 786440 | tf_op jit(solution)/shard_map/ppermute | solution.py:77
  355.3 9.8 %copy-start.14 = (bf16[256,512]{1,0:T(8,128)(2,1)S(1)}, bf16[256,512]{1,0:T(8,128)(2,1)}, u32[]{:S(2)}) copy-start(bf16[256,512]{1,0:T(8,128)(2,1)} %get-tuple-element.168.grad.grads_0_) | copy-start | bytes 786436
  355.3 21.8 %collective-permute-start.35 = (bf16[256,512]{1,0:T(8,128)(2,1)S(1)}, bf16[256,512]{1,0:T(8,128)(2,1)S(1)}, u32[]{:S(2)}, u32[]{:S(2)}) collective-permute-start(bf16[256,512]{1,0:T(8,128)(2,1)S(1)} %get-tuple-element.188), channel_id=1, source_target_pairs={{0,2},{1,3},{2,0},{3,1},{4,6},{5,7},{6,4},{7,5},{8,10},{9,11},{10,... | collective-permute-start | bytes 786440 | tf_op jit(solution)/shard_map/ppermute | solution.py:77
  355.4 9.7 %copy-start.3 = (bf16[4096,512]{1,0:T(8,128)(2,1)S(1)}, bf16[4096,512]{1,0:T(8,128)(2,1)}, u32[]{:S(2)}) copy-start(bf16[4096,512]{1,0:T(8,128)(2,1)} %all-gather.8.cloned.1.call-done) | copy-start | bytes 12582916
  359.3 17.9 %collective-permute-start.33 = (bf16[256,512]{1,0:T(8,128)(2,1)S(1)}, bf16[256,512]{1,0:T(8,128)(2,1)S(1)}, u32[]{:S(2)}, u32[]{:S(2)}) collective-permute-start(bf16[256,512]{1,0:T(8,128)(2,1)S(1)} %get-tuple-element.186), channel_id=1, source_target_pairs={{0,1},{1,0},{2,3},{3,2},{4,5},{5,4},{6,7},{7,6},{8,9},{9,8},{10,11... | collective-permute-start | bytes 786440 | tf_op jit(solution)/shard_map/ppermute | solution.py:77
  377.2 19.9 %collective-permute-start.38 = (bf16[4,512,512]{2,1,0:T(8,128)(2,1)}, bf16[4,512,512]{2,1,0:T(8,128)(2,1)}, u32[]{:S(2)}, u32[]{:S(2)}) collective-permute-start(bf16[4,512,512]{2,1,0:T(8,128)(2,1)} %get-tuple-element.214), channel_id=1, source_target_pairs={{0,4},{4,0},{8,12},{12,8},{16,20},{20,16},{24,28},{28,24},{1,5},{5... | collective-permute-start | bytes 6291464 | tf_op jit(solution)/shard_map/ppermute | solution.py:1022
  380.0 13.5 %all-to-all-start.5 = ((f32[32,16,128]{2,1,0:T(8,128)}), f32[32,16,128]{2,1,0:T(8,128)S(1)}, u32[]{:S(2)}, u32[]{:S(2)}) async-start(f32[32,16,128]{2,1,0:T(8,128)} %bitcast.25), calls=%async_computation.5 | async-start | bytes 524288 | tf_op jit(solution)/shard_map/all_to_all | solution.py:69
  393.6 18.9 %all-to-all-start.3 = ((bf16[4,16,4096]{2,1,0:T(8,128)(2,1)}), bf16[4,16,4096]{2,1,0:T(8,128)(2,1)S(1)}, u32[]{:S(2)}, u32[]{:S(2)}) async-start(bf16[4,16,4096]{2,1,0:T(8,128)(2,1)} %bitcast.22), calls=%async_computation.3 | async-start | bytes 1048576 | tf_op jit(solution)/shard_map/all_to_all | solution.py:69
  401.4 16.6 %collective-permute-start.39 = (bf16[512,512]{1,0:T(8,128)(2,1)}, bf16[512,512]{1,0:T(8,128)(2,1)S(1)}, u32[]{:S(2)}, u32[]{:S(2)}) collective-permute-start(bf16[512,512]{1,0:T(8,128)(2,1)} %get-tuple-element.280), channel_id=1, source_target_pairs={{0,8},{4,12},{8,0},{12,4},{16,24},{20,28},{24,16},{28,20},{1,9},{5... | collective-permute-start | bytes 1572872 | tf_op jit(solution)/shard_map/ppermute | solution.py:1022
  402.4 29.6 %collective-permute-start.41 = (bf16[512,512]{1,0:T(8,128)(2,1)S(1)}, bf16[512,512]{1,0:T(8,128)(2,1)S(1)}, u32[]{:S(2)}, u32[]{:S(2)}) collective-permute-start(bf16[512,512]{1,0:T(8,128)(2,1)S(1)} %get-tuple-element.281), channel_id=1, source_target_pairs={{0,24},{4,28},{8,16},{12,20},{16,8},{20,12},{24,0},{28,4},{1,25},{... | collective-permute-start | bytes 1572872 | tf_op jit(solution)/shard_map/ppermute | solution.py:1022
  403.9 30.0 %collective-permute-start.40 = (bf16[512,512]{1,0:T(8,128)(2,1)S(1)}, bf16[512,512]{1,0:T(8,128)(2,1)S(1)}, u32[]{:S(2)}, u32[]{:S(2)}) collective-permute-start(bf16[512,512]{1,0:T(8,128)(2,1)S(1)} %get-tuple-element.282), channel_id=1, source_target_pairs={{0,16},{4,20},{8,24},{12,28},{16,0},{20,4},{24,8},{28,12},{1,17},{... | collective-permute-start | bytes 1572872 | tf_op jit(solution)/shard_map/ppermute | solution.py:1022
  413.4 23.8 %all-to-all-start.4 = ((bf16[32,16,512]{2,1,0:T(8,128)(2,1)}), bf16[32,16,512]{2,1,0:T(8,128)(2,1)S(1)}, u32[]{:S(2)}, u32[]{:S(2)}) async-start(bf16[32,16,512]{2,1,0:T(8,128)(2,1)} %broadcast_in_dim.47), calls=%async_computation.4 | async-start | bytes 1048576 | tf_op jit(solution)/shard_map/all_to_all | solution.py:65
  (38 other events, 91.9 us)
Sparse Core Ops, SparseCore 0:
  10.5 39.6 all-gather.7
  66.9 33.5 all-gather.5
  102.4 37.4 all-gather.9
  321.3 72.5 reduce-scatter.1

commit v3 on v2

--- a/solution.py
+++ b/solution.py
@@ -82,26 +82,113 @@
     return [core << 1 for core in range(lax.axis_size("dp") // 2)]
 
 
-def call(body, outs, *args, specs=None, out_specs=None, scratch=(), vmem=60, **kw):
+class Columns:
+    def __init__(self, array, start, count):
+        self.array, self.start, self.count = array, start, count
+
+
+class Stream:
+    def __init__(self, arrivals, results):
+        self.arrivals, self.results = arrivals, results
+        self.waited, self.sent = set(), []
+        self.begin(0)
+        self.begin(1)
+
+    def begin(self, stage):
+        for copy in self.arrivals.get(stage, ()):
+            copy.start()
+
+    def ready(self, stage):
+        for copy in self.arrivals.get(stage, ()):
+            copy.wait()
+        self.waited.add(stage)
+        self.begin(stage + 2)
+
+    def flush(self, *refs):
+        for ref in refs:
+            copy = self.results[id(ref)]
+            copy.start()
+            self.sent.append(copy)
+
+    def finish(self):
+        for copy in self.sent:
+            copy.wait()
+
+
+def call(body, outs, *args, specs=None, out_specs=None, scratch=(), stages=None, vmem=60, cost=5, **kw):
     vmem_spec = pl.BlockSpec(memory_space=pltpu.VMEM)
+    any_spec = pl.BlockSpec(memory_space=pl.ANY)
     if specs is None:
         specs = [None] * len(args)
+    columns = [arg if isinstance(arg, Columns) else None for arg in args]
+    args = [arg.array if isinstance(arg, Columns) else arg for arg in args]
     grid = kw.pop("grid", (1,))
-    specs = [
-        jax.tree.map(lambda _: vmem_spec, arg) if spec is None else spec
-        for spec, arg in zip(specs, args)
-    ]
-    if out_specs is None:
-        out_specs = jax.tree.map(lambda _: vmem_spec, outs)
+    scratch = list(scratch)
+    if stages is None:
+        specs = [
+            jax.tree.map(lambda _: vmem_spec, arg) if spec is None else spec
+            for spec, arg in zip(specs, args)
+        ]
+        if out_specs is None:
+            out_specs = jax.tree.map(lambda _: vmem_spec, outs)
+        wrapped = body
+    else:
+        specs = [
+            spec if spec is not None else jax.tree.map(lambda _: vmem_spec if stage is None else any_spec, arg)
+            for spec, arg, stage in zip(specs, args, stages)
+        ]
+        out_specs = jax.tree.map(lambda _: any_spec, outs)
+        buffers = []
+        for arg, part, stage in zip(args, columns, stages):
+            if stage is not None:
+                for leaf in jax.tree.leaves(arg):
+                    shape = leaf.shape if part is None else (leaf.shape[0], part.count)
+                    buffers.append(pltpu.VMEM(shape, leaf.dtype))
+        out_leaves, out_tree = jax.tree.flatten(outs)
+        buffers += [pltpu.VMEM(leaf.shape, leaf.dtype) for leaf in out_leaves]
+        own_scratch, total = len(scratch), len(buffers)
+        scratch = scratch + buffers + [pltpu.SemaphoreType.DMA((total,))]
+
+        def wrapped(*refs):
+            refs = list(refs)
+            ins, out_refs, rest = refs[: len(args)], refs[len(args) : len(args) + out_count], refs[len(args) + out_count :]
+            own, held, sems = rest[:own_scratch], rest[own_scratch:-1], rest[-1]
+            arrivals, given, used = {}, [], 0
+            for ref, part, stage in zip(ins, columns, stages):
+                if stage is None:
+                    given.append(ref)
+                    continue
+                leaves, tree = jax.tree.flatten(ref)
+                landed = []
+                for leaf in leaves:
+                    source = leaf if part is None else leaf.at[:, pl.ds(part.start, part.count)]
+                    arrivals.setdefault(stage, []).append(
+                        pltpu.make_async_copy(source, held[used], sems.at[used])
+                    )
+                    landed.append(held[used])
+                    used += 1
+                given.append(jax.tree.unflatten(tree, landed))
+            results, places = {}, []
+            for ref in jax.tree.leaves(out_refs):
+                results[id(held[used])] = pltpu.make_async_copy(held[used], ref, sems.at[used])
+                places.append(held[used])
+                used += 1
+            stream = Stream(arrivals, results)
+            given_outs = jax.tree.unflatten(out_tree, places)
+            given_outs = list(given_outs) if isinstance(given_outs, (tuple, list)) else [given_outs]
+            body(stream, *given, *given_outs, *own)
+            stream.finish()
+
+        out_count = len(outs) if isinstance(outs, (tuple, list)) else 1
     return pl.pallas_call(
-        body,
+        wrapped,
         out_shape=outs,
         in_specs=specs,
         out_specs=out_specs,
-        scratch_shapes=list(scratch),
+        scratch_shapes=scratch,
         grid=grid,
         compiler_params=pltpu.CompilerParams(vmem_limit_bytes=vmem * MIB),
-        cost_estimate=pl.CostEstimate(flops=0, bytes_accessed=0, transcendentals=0),
+        cost_estimate=pl.CostEstimate(flops=cost * 1153 * 10**6, bytes_accessed=0, transcendentals=0),
         **kw,
     )(*args)
 
@@ -244,6 +331,7 @@
         scratch=[pltpu.VMEM((capacity, width), F32), pltpu.VMEM((capacity, width), BF16)],
         grid=(hidden // tile,),
         vmem=12,
+        cost=8,
     )
 
 
@@ -306,6 +394,7 @@
         scratch=[pltpu.VMEM((capacity, width), F32), pltpu.VMEM((capacity, width), F32)],
         grid=(hidden // tile,),
         vmem=16,
+        cost=20,
     )
 
 
@@ -373,18 +462,27 @@
         scratch=[pltpu.VMEM((width, tile), BF16), pltpu.VMEM((tile, width), BF16)],
         grid=(units // tile,),
         vmem=28,
+        cost=8,
     )
 
 
 def dense_grad_kernel(
-    experts, ua, dproj, attended, dat, uc, dgin, swish, dco, gate_grad1, gate1, col1, gate_grad2, gate2, col2,
+    experts, stream, ua, dproj, attended, dat, uc, dgin, swish, dco, gate_grad1, gate1, col1, gate_grad2, gate2, col2,
     probs, routers, pre, embedded, frames, out, dz, router_terms, logits,
 ):
     width = ua.shape[1]
     rows = frames.shape[0]
-    for part in chunks(rows, 128):
-        lane = iota((128, LANES), 1)
-        grad = jnp.zeros((128, LANES), F32)
+    stream.ready(0)
+    stream.ready(1)
+    start = 0
+    for left, right in ((ua, dproj), (attended, dat)):
+        for column in range(0, right.shape[1], width):
+            out[:, pl.ds(start, width)] = dot_tn(left[...], right[:, pl.ds(column, width)]).astype(BF16)
+            start += width
+    stream.ready(2)
+    for part in chunks(rows, 256):
+        lane = iota((256, LANES), 1)
+        grad = jnp.zeros((256, LANES), F32)
         for number, (gate_grad, gate, col) in enumerate(((gate_grad1, gate1, col1), (gate_grad2, gate2, col2))):
             inside = (lane >= number * experts) & (lane < (number + 1) * experts)
             hot = (lane == col[part, :] + number * experts).astype(F32)
@@ -399,16 +497,28 @@
     router_terms[...] = lax.dot_general(
         logits[...], embedded[...], (((0,), (0,)), ((), ())), precision=HIGHEST, preferred_element_type=F32
     )
-    start = 0
-    for left, right in ((ua, dproj), (attended, dat), (uc, dgin), (swish, dco), (frames, dz)):
+    stream.flush(dz, router_terms)
+    for left, right in ((uc, dgin), (swish, dco), (frames, dz)):
         for column in range(0, right.shape[1], width):
             out[:, pl.ds(start, width)] = dot_tn(left[...], right[:, pl.ds(column, width)]).astype(BF16)
             start += width
+    stream.flush(out)
+
+
+def dense_out_kernel(arrived, *outs):
+    start = 0
+    for out in outs:
+        lanes = pl.ds(start, out.shape[1])
+        total = arrived[0, :, lanes].astype(F32)
+        for number in range(1, arrived.shape[0]):
+            total = total + arrived[number, :, lanes].astype(F32)
+        out[...] = total.astype(out.dtype)
+        start += out.shape[1]
 
 
 def embed_kernel(experts, ends, frames, weight, routers, col1, col2, pre_out, embedded_out, probs_out, gate1, gate2, seg_col, seg_row, taps_out, offset_out):
     rows = frames.shape[0]
-    for part in chunks(rows, 128):
+    for part in chunks(rows, 256):
         pre = dot(frames[part, :], weight[...])
         pre_out[part, :] = pre
         embedded = pre * sigmoid(pre)
@@ -450,21 +560,38 @@
     return jnp.where(lane % DH < half, pltpu.roll(values, LANES - half, 1), pltpu.roll(values, half, 1))
 
 
+def shifts(padded, part):
+    size = part.size
+    for offset in range(8):
+        held = padded[pl.ds(part.start + offset, size + 8), :]
+        if offset:
+            yield offset - 1, held[:size]
+        yield offset + 7, held[8:]
+
+
+def folded(values):
+    return jnp.sum(values.reshape(-1, 8, values.shape[1]), 0)
+
+
 def front_kernel(
-    frames, blocks, slot_col, gate, table, attn_in, attn_out, conv_in, cosine, sine, seg_col, seg_row, taps,
+    stream, frames, blocks, slot_col, gate, table, attn_in, attn_out, conv_in, cosine, sine, seg_col, seg_row, taps,
     expert_out, x1_out, x2_out, ua_out, qkv_out, lse_out, attended_out, uc_out, gin_out, depth_out, moments,
-    padded,
+    padded, flipped,
 ):
     rows, width = frames.shape
     gains = lambda n: table[pl.ds(n, 1), :]
-    for part in chunks(rows, 128):
+    stream.ready(0)
+    for part in chunks(rows, 256):
         found = gathered(slot_col, blocks, part)
         expert_out[part, :] = found.astype(BF16)
         x1 = frames[part, :].astype(F32) + 0.5 * gate[part, :] * found
         x1_out[part, :] = x1
         hat, _ = normalize(x1)
-        ua = (hat * gains(1)).astype(BF16)
-        ua_out[part, :] = ua
+        ua_out[part, :] = (hat * gains(1)).astype(BF16)
+    stream.flush(expert_out, x1_out, ua_out)
+    stream.ready(1)
+    for part in chunks(rows, 256):
+        ua = ua_out[part, :]
         for piece in range(3 * width // LANES):
             lanes = pl.ds(piece * LANES, LANES)
             if piece % 2 == 0:
@@ -476,38 +603,41 @@
                 values = values * DH**-0.5
             qkv_out[part, lanes] = values.astype(BF16)
 
-    lane = iota((1, LANES), 1)
-    sides = ((lane < DH), (lane >= DH))
+    stream.flush(qkv_out)
     zero = jnp.zeros((), BF16)
+    sides = tuple((iota((1, LANES), 1) < DH) == (side == 0) for side in range(2))
+    turned = tuple((iota((LANES, 1), 0) < DH) == (side == 0) for side in range(2))
+    for pair in range(width // LANES):
+        flipped[pl.ds(pair * LANES, LANES), :] = qkv_out[:, pl.ds(2 * width + pair * LANES, LANES)].T
 
     def attend(part_index, carry):
-        part = pl.ds(pl.multiple_of(part_index * 128, 128), 128)
-        related = seg_col[part, :] == seg_row[...]
-        lse = jnp.zeros((128, LANES), F32)
+        part = pl.ds(pl.multiple_of(part_index * 512, 512), 512)
+        related = seg_col[...] == seg_row[:, part]
         for pair in range(width // LANES):
             q = qkv_out[part, pl.ds(pair * LANES, LANES)]
             k = qkv_out[:, pl.ds(width + pair * LANES, LANES)]
-            v = qkv_out[:, pl.ds(2 * width + pair * LANES, LANES)]
-            result = jnp.zeros((128, LANES), F32)
+            v = flipped[pl.ds(pair * LANES, LANES), :]
+            result = jnp.zeros((LANES, 512), F32)
             for side in range(2):
-                scores = dot_nt(jnp.where(sides[side], q, zero), k)
+                scores = dot_nt(k, jnp.where(sides[side], q, zero))
                 scores = jnp.where(related, scores, -MASK_FILL)
-                top = jnp.max(scores, 1, keepdims=True)
+                top = jnp.max(scores, 0, keepdims=True)
                 weights = jnp.exp(scores - top)
-                summed = jnp.sum(weights, 1, keepdims=True)
+                summed = jnp.sum(weights, 0, keepdims=True)
                 probs = (weights * (1.0 / summed)).astype(BF16)
-                result += dot(probs, jnp.where(sides[side], v, zero))
-                lse = jnp.where(lane == 2 * pair + side, top + jnp.log(summed), lse)
-            attended_out[part, pl.ds(pair * LANES, LANES)] = result.astype(BF16)
-        lse_out[part, :] = lse
+                result += dot(jnp.where(turned[side], v, zero), probs)
+                lse_out[pl.ds(2 * pair + side, 1), part] = top + jnp.log(summed)
+            attended_out[part, pl.ds(pair * LANES, LANES)] = result.T.astype(BF16)
         return carry
 
-    lax.fori_loop(0, rows // 128, attend, 0)
+    lax.fori_loop(0, rows // 512, attend, 0)
+    stream.flush(attended_out, lse_out)
+    stream.ready(2)
 
     edge = jnp.zeros((8, width), F32)
     padded[pl.ds(0, 8), :] = edge
     padded[pl.ds(rows + 8, 8), :] = edge
-    for part in chunks(rows, 128):
+    for part in chunks(rows, 256):
         x2 = x1_out[part, :] + dot(attended_out[part, :], attn_out[...])
         x2_out[part, :] = x2
         hat, _ = normalize(x2)
@@ -515,15 +645,15 @@
         uc_out[part, :] = uc
         gin = dot(uc, conv_in[...])
         gin_out[part, :] = gin
-        padded[pl.ds(part.start + 8, 128), :] = gin[:, :width] * sigmoid(gin[:, width:])
-
+        padded[pl.ds(part.start + 8, 256), :] = gin[:, :width] * sigmoid(gin[:, width:])
+
+    stream.flush(x2_out, uc_out, gin_out)
     sums = jnp.zeros((1, width), F32)
     squares = jnp.zeros((1, width), F32)
     for part in chunks(rows, 64):
         depth = jnp.zeros((64, width), F32)
-        for tap in range(15):
-            weight = table[pl.ds(6 + tap, 1), :]
-            depth += weight * padded[pl.ds(part.start + tap + 1, 64), :] * taps[part, pl.ds(tap, 1)]
+        for tap, shifted in shifts(padded, part):
+            depth += table[pl.ds(6 + tap, 1), :] * shifted * taps[part, pl.ds(tap, 1)]
         depth_out[part, :] = depth
         weighted = jnp.where(seg_col[part, :] < 3, depth, 0.0)
         sums += jnp.sum(weighted, 0, keepdims=True)
@@ -531,6 +661,7 @@
     moments[pl.ds(0, 1), :] = sums
     moments[pl.ds(1, 1), :] = squares
     moments[pl.ds(2, 6), :] = jnp.zeros((6, width), F32)
+    stream.flush(depth_out, moments)
 
 
 def batch_terms(moments, frame_count):
@@ -539,10 +670,11 @@
     return mean, lax.rsqrt(variance + EPSILON)
 
 
-def middle_kernel(frame_count, depth, moments, x2, table, conv_out, slot_row, swish_out, x3_out, sent, normed):
+def middle_kernel(stream, frame_count, depth, moments, x2, table, conv_out, slot_row, swish_out, x3_out, sent, normed):
     rows, width = depth.shape
+    stream.ready(0)
     mean, scale = batch_terms(moments, frame_count)
-    for part in chunks(rows, 128):
+    for part in chunks(rows, 256):
         bn = (depth[part, :] - mean) * scale * table[pl.ds(5, 1), :] + table[pl.ds(21, 1), :]
         swish = (bn * sigmoid(bn)).astype(BF16)
         swish_out[part, :] = swish
@@ -550,17 +682,20 @@
         x3_out[part, :] = x3
         hat, _ = normalize(x3)
         normed[part, :] = (hat * table[pl.ds(3, 1), :]).astype(BF16)
+    stream.flush(swish_out, x3_out)
     scatter_to(slot_row, normed[...], sent)
+    stream.flush(*sent)
 
 
 def turn_kernel(
-    x3, blocks, slot_col, slot_row, gate, table, cotangent, seg_col,
+    stream, x3, blocks, slot_col, slot_row, gate, table, cotangent, seg_col,
     block_out, dx4_out, gate_grad, gain_out, sent, grads,
 ):
     rows, width = x3.shape
     gain = table[pl.ds(4, 1), :]
+    stream.ready(0)
     gain_sum = jnp.zeros((1, width), F32)
-    for part in chunks(rows, 128):
+    for part in chunks(rows, 256):
         found = gathered(slot_col, blocks, part)
         half = 0.5 * gate[part, :]
         x4 = x3[part, :] + half * found
@@ -574,21 +709,24 @@
         gate_grad[part, :] = 0.5 * jnp.sum(found * dx4, 1, keepdims=True)
         grads[part, :] = (half * dx4).astype(BF16)
     gain_out[...] = gain_sum
+    stream.flush(block_out, dx4_out, gate_grad, gain_out)
     scatter_to(slot_row, grads[...], sent)
+    stream.flush(*sent)
 
 
 def conv_back_kernel(
-    frame_count, dx4, blocks, slot_col, x3, table, conv_out, depth, moments,
+    stream, frame_count, dx4, blocks, slot_col, x3, table, conv_out, depth, moments,
     dx3_out, dco_out, dh_out, sums,
 ):
     rows, width = x3.shape
     mean, scale = batch_terms(moments, frame_count)
+    stream.ready(0)
     total = jnp.zeros((1, width), F32)
     moment = jnp.zeros((1, width), F32)
     shift = jnp.zeros((1, width), F32)
     gain5 = jnp.zeros((1, width), F32)
     gain3 = jnp.zeros((1, width), F32)
-    for part in chunks(rows, 128):
+    for part in chunks(rows, 256):
         grad = gathered(slot_col, blocks, part)
         hat, inverse = normalize(x3[part, :])
         gain3 += jnp.sum(grad * hat, 0, keepdims=True)
@@ -609,13 +747,14 @@
     for number, row in enumerate((total, moment, shift, gain5, gain3)):
         sums[pl.ds(number, 1), :] = row
     sums[pl.ds(5, 3), :] = jnp.zeros((3, width), F32)
+    stream.flush(dx3_out, dco_out, dh_out, sums)
 
 
 def back_kernel(
-    frame_count, dh, depth, moments, sums, dx3, gin, x2, x1, table, conv_in, attn_out, attn_in, qkv, lse,
+    stream, frame_count, dh, depth, moments, sums, dx3, gin, x2, x1, table, conv_in, attn_out, attn_in, qkv, lse,
     cosine, sine, seg_col, seg_row, taps, expert, gate, slot_row,
     dgin_out, dat_out, dproj_out, dx1_out, gate_grad, terms, sent,
-    padded, glu, grad_rows, dk, dv, rows_sent,
+    padded, glu, grad_rows, dk, dv, rows_sent, flipped,
 ):
     rows, width = dh.shape
     mean, scale = batch_terms(moments, frame_count)
@@ -626,27 +765,31 @@
     for ref in (padded, glu):
         ref[pl.ds(0, 8), :] = edge
         ref[pl.ds(rows + 8, 8), :] = edge
+    stream.ready(0)
     for part in chunks(rows, 64):
         held = depth[part, :]
         grad = (mean_grad + 2.0 * held * var_grad) * (1.0 / frame_count[0])
         padded[pl.ds(part.start + 8, 64), :] = dh[part, :] * scale + jnp.where(seg_col[part, :] < 3, grad, 0.0)
+    stream.ready(1)
+    for part in chunks(rows, 64):
         glu[pl.ds(part.start + 8, 64), :] = gin[part, :width] * sigmoid(gin[part, width:])
-    kernel_sums = [jnp.zeros((1, width), F32) for _ in range(15)]
+    kernel_sums = [jnp.zeros((8, width), F32) for _ in range(15)]
     gain2 = jnp.zeros((1, width), F32)
     for part in chunks(rows, 64):
         dglu = jnp.zeros((64, width), F32)
         own = padded[pl.ds(part.start + 8, 64), :]
-        for tap in range(15):
+        for (tap, grad), (_, value) in zip(shifts(padded, part), shifts(glu, part)):
             mask = taps[part, pl.ds(tap, 1)]
-            dglu += table[pl.ds(20 - tap, 1), :] * padded[pl.ds(part.start + tap + 1, 64), :] * mask
-            shifted = glu[pl.ds(part.start + tap + 1, 64), :]
-            kernel_sums[tap] += jnp.sum(own * shifted * mask, 0, keepdims=True)
+            dglu += table[pl.ds(20 - tap, 1), :] * grad * mask
+            kernel_sums[tap] += folded(own * value * mask)
         logistic = sigmoid(gin[part, width:])
         dgin_out[part, :width] = (dglu * logistic).astype(BF16)
         dgin_out[part, width:] = (dglu * gin[part, :width] * logistic * (1.0 - logistic)).astype(BF16)
     for tap in range(15):
-        terms[pl.ds(6 + tap, 1), :] = kernel_sums[tap]
-    for part in chunks(rows, 128):
+        terms[pl.ds(6 + tap, 1), :] = jnp.sum(kernel_sums[tap], 0, keepdims=True)
+    stream.flush(dgin_out)
+    stream.ready(2)
+    for part in chunks(rows, 256):
         grad = dot_nt(dgin_out[part, :], conv_in[...])
         hat, inverse = normalize(x2[part, :])
         gain2 += jnp.sum(grad * hat, 0, keepdims=True)
@@ -657,42 +800,51 @@
         grad_rows[part, :] = dot_nt(dat, attn_out[...]).astype(BF16)
     terms[pl.ds(2, 1), :] = gain2
 
-    lane = iota((1, LANES), 1)
-    sides = ((lane < DH), (lane >= DH))
+    stream.flush(dat_out)
+    stream.ready(3)
     zero = jnp.zeros((), BF16)
+    sides = tuple((iota((1, LANES), 1) < DH) == (side == 0) for side in range(2))
+    turned = tuple((iota((LANES, 1), 0) < DH) == (side == 0) for side in range(2))
+    for pair in range(width // LANES):
+        flipped[pl.ds(pair * LANES, LANES), :] = qkv[:, pl.ds(width + pair * LANES, LANES)].T
     dk[...] = jnp.zeros_like(dk)
     dv[...] = jnp.zeros_like(dv)
 
     def attend(part_index, carry):
-        part = pl.ds(pl.multiple_of(part_index * 128, 128), 128)
-        related = seg_col[part, :] == seg_row[...]
+        part = pl.ds(pl.multiple_of(part_index * 512, 512), 512)
+        related = seg_col[...] == seg_row[:, part]
         for pair in range(width // LANES):
             own = pl.ds(pair * LANES, LANES)
             q = qkv[part, own]
             k = qkv[:, pl.ds(width + pair * LANES, LANES)]
             v = qkv[:, pl.ds(2 * width + pair * LANES, LANES)]
             da = grad_rows[part, own]
-            dq = jnp.zeros((128, LANES), F32)
+            dq = jnp.zeros((LANES, 512), F32)
+            dk_sum = jnp.zeros((rows, LANES), F32)
+            dv_sum = jnp.zeros((rows, LANES), F32)
             for side in range(2):
                 head = 2 * pair + side
                 q_side = jnp.where(sides[side], q, zero)
                 da_side = jnp.where(sides[side], da, zero)
-                scores = dot_nt(q_side, k) - lse[part, pl.ds(head, 1)]
-                probs = jnp.where(related, jnp.exp(jnp.where(related, scores, 0.0)), 0.0)
-                dprobs = dot_nt(da_side, v)
-                inner = jnp.sum(probs * dprobs, 1, keepdims=True)
+                scores = dot_nt(k, q_side) - lse[pl.ds(head, 1), part]
+                probs = jnp.exp(jnp.where(related, scores, -MASK_FILL))
+                dprobs = dot_nt(v, da_side)
+                inner = jnp.sum(probs * dprobs, 0, keepdims=True)
                 dscores = (probs * (dprobs - inner)).astype(BF16)
-                dq += dot(dscores, jnp.where(sides[side], k, zero))
-                dk[:, own] += dot_tn(dscores, q_side)
-                dv[:, own] += dot_tn(probs.astype(BF16), da_side)
-            dq = dq * DH**-0.5
+                dq += dot(jnp.where(turned[side], flipped[own, :], zero), dscores)
+                dk_sum += dot(dscores, q_side)
+                dv_sum += dot(probs.astype(BF16), da_side)
+            dk[:, own] += dk_sum
+            dv[:, own] += dv_sum
+            dq = dq.T * DH**-0.5
             dproj_out[part, own] = (dq * cosine[part, :] - partner(dq) * sine[part, :]).astype(BF16)
         return carry
 
-    lax.fori_loop(0, rows // 128, attend, 0)
-
+    lax.fori_loop(0, rows // 512, attend, 0)
+
+    stream.ready(4)
     gain1 = jnp.zeros((1, width), F32)
-    for part in chunks(rows, 128):
+    for part in chunks(rows, 256):
         for pair in range(width // LANES):
             own = pl.ds(pair * LANES, LANES)
             held = dk[part, own]
@@ -708,10 +860,12 @@
         gate_grad[part, :] = 0.5 * jnp.sum(expert[part, :].astype(F32) * dx1, 1, keepdims=True)
         rows_sent[part, :] = (0.5 * gate[part, :] * dx1).astype(BF16)
     terms[pl.ds(1, 1), :] = gain1
+    stream.flush(dproj_out, dx1_out, gate_grad, terms)
     scatter_to(slot_row, rows_sent[...], sent)
-
-
-def final_kernel(frames, blocks, slot_col, table, dx1, dz, embed_weight, out):
+    stream.flush(*sent)
+
+
+def final_kernel(frames, blocks, slot_col, table, dx1, dz, embed_weight, _, out):
     for part in chunks(frames.shape[0], 128):
         grad = gathered(slot_col, blocks, part)
         hat, inverse = normalize(frames[part, :].astype(F32))
@@ -788,12 +942,13 @@
         ],
         1,
     )
+    small = after(small, sent[0])
     small_all = gather_everywhere(small).reshape(width, LANES).astype(F32)
     table = small_all[:, : gains + taps + 3].T
     router_table = jnp.pad(
         small_all[:, gains + taps + 1 : small_width], ((0, 0), (0, LANES - layers * experts))
     )
-    dense = after(jnp.concatenate([attn_in, attn_out, conv_in, conv_out], 1), small_all, *first_blocks)
+    dense = jnp.concatenate([attn_in, attn_out, conv_in, conv_out], 1)
     dense = lax.all_to_all(
         jnp.broadcast_to(dense[None], (peers,) + dense.shape), "expert", split_axis=0, concat_axis=0, tiled=True
     )
@@ -856,7 +1011,7 @@
             wide,
             low,
             shaped((rows, 3 * width), BF16),
-            shaped((rows, LANES), F32),
+            shaped((8, rows), F32),
             low,
             low,
             shaped((rows, 2 * width), F32),
@@ -868,16 +1023,17 @@
         slot_col1,
         gate1,
         table,
-        dense,
-        dense,
-        dense,
+        Columns(dense, 0, 3 * width),
+        Columns(dense, 3 * width, width),
+        Columns(dense, 4 * width, 2 * width),
         cosine,
         sine,
         seg_col,
         seg_row,
         tap_masks,
-        specs=[None] * 5 + [attn_in_spec, attn_out_spec, conv_in_spec] + [None] * 5,
-        scratch=[padded],
+        stages=[0, 0, None, None, None, 1, 2, 2, 1, 1, None, None, 2],
+        cost=20,
+        scratch=[padded, pltpu.VMEM((width, rows), BF16)],
     )
     moments = sum_everywhere(moments)
     swish, x3, sent = call(
@@ -888,9 +1044,10 @@
         moments,
         x2,
         table,
-        dense,
+        Columns(dense, 6 * width, width),
         slot_row2,
-        specs=[SMEM] + [None] * 4 + [conv_out_spec, None],
+        specs=[SMEM] + [None] * 6,
+        stages=[None, 0, None, 0, None, 0, None],
         scratch=[pltpu.VMEM((rows, width), BF16)],
     )
 
@@ -909,6 +1066,7 @@
         table,
         cotangent,
         seg_col,
+        stages=[0, 0, None, None, None, None, 0, None],
         scratch=[pltpu.VMEM((rows, width), BF16)],
     )
     second_grads = swap_blocks(sent)
@@ -933,10 +1091,11 @@
         slot_col2,
         x3,
         table,
-        dense,
+        Columns(dense, 6 * width, width),
         depth,
         moments,
-        specs=[SMEM] + [None] * 5 + [conv_out_spec] + [None] * 2,
+        specs=[SMEM] + [None] * 8,
+        stages=[None, 0, 0, None, 0, None, 0, 0, None],
     )
     all_sums = sum_everywhere(sums)
     dgin, dat, dproj, dx1, gate_grad1, terms, sent = call(
@@ -960,9 +1119,9 @@
         x2,
         x1,
         table,
-        dense,
-        dense,
-        dense,
+        Columns(dense, 4 * width, 2 * width),
+        Columns(dense, 3 * width, width),
+        Columns(dense, 0, 3 * width),
         qkv,
         lse,
         cosine,
@@ -973,8 +1132,10 @@
         first_expert,
         gate1,
         slot_row1,
-        specs=[SMEM] + [None] * 9 + [conv_in_spec, attn_out_spec, attn_in_spec] + [None] * 10,
-        scratch=[padded, padded, pltpu.VMEM((rows, width), BF16), pltpu.VMEM((rows, width), F32), pltpu.VMEM((rows, width), F32), pltpu.VMEM((rows, width), BF16)],
+        specs=[SMEM] + [None] * 22,
+        stages=[None, 0, 0, None, None, 2, 1, 2, 4, None, 2, 2, 4, 3, 3, 3, 3, None, None, 1, 4, None, None],
+        cost=30,
+        scratch=[padded, padded, pltpu.VMEM((rows, width), BF16), pltpu.VMEM((rows, width), F32), pltpu.VMEM((rows, width), F32), pltpu.VMEM((rows, width), BF16), pltpu.VMEM((width, rows), BF16)],
     )
     first_grads = swap_blocks(sent)
 
@@ -1000,14 +1161,24 @@
         embed_pre,
         embedded,
         frames,
+        stages=[0, 0, 1, 1, 2, 2, 2, 2] + [None] * 7 + [None, 2, 2, 2],
+        cost=1,
         scratch=[pltpu.VMEM((rows, LANES), F32)],
     )
     dense_own = sum_to_owners(dense_terms.reshape(dp_count, -1, 8 * width), "dp").astype(BF16)
-    dense_own = sum_to_owners(dense_own.reshape(peers, slice_width, 8 * width), "expert")
-    embed_total = gather_everywhere(dense_own[:, 7 * width :].astype(BF16))
+    dense_own = lax.all_to_all(
+        dense_own.reshape(peers, slice_width, 8 * width), "expert", split_axis=0, concat_axis=0, tiled=True
+    )
+    owned = [shaped((slice_width, count * width), F32) for count in (3, 1, 2, 1)]
+    *dense_own, embed_own = call(
+        dense_out_kernel,
+        (*owned, shaped((slice_width, width), BF16)),
+        dense_own,
+        cost=10,
+    )
+    embed_total = gather_everywhere(embed_own)
     embed_total = embed_total.reshape(width, width).astype(F32)
 
-    first_grads[1] = after(first_grads[1], dense_terms)
     backs = [
         expert_backward(block, grad, gain(0), first_weights, hidden, True)
         for block, grad in zip(first_blocks, first_grads)
@@ -1052,6 +1223,9 @@
         dx1,
         dz,
         embed_weight,
+        second_own,
+        specs=[None] * 7 + [ANY],
+        cost=40,
     )
     def matrices(own):
         half = own.shape[0] // 2
@@ -1067,12 +1241,10 @@
             small_sums[gains + taps + 1 : small_width].reshape(layers, experts, slice_width), 1, 2
         ),
         small_sums[:gains],
-        dense_own[:, : 3 * width],
-        dense_own[:, 3 * width : 4 * width],
-        dense_own[:, 4 * width : 6 * width],
+        *dense_own[:3],
         small_sums[gains : gains + taps],
         small_sums[gains + taps],
-        dense_own[:, 6 * width : 7 * width],
+        dense_own[3],
         jnp.stack([first_pair[0], second_pair[0]])[:, None],
         jnp.stack([first_pair[1], second_pair[1]])[:, None],
     )

time: 452 us -> 433 us (0.958); the launches traced: 449 us -> 425 us
  Pallas kernels: 161 us -> 149 us
    ppermute x24, waiting for transfers between devices: 67.2 us -> 44.8 us  [swap_blocks(): lax.ppermute(blocks[k], 'expert', [(i, i ^ k) for i in range(total)])]
    pallas_call x27 -> x28, Pallas kernels: 161 us -> 149 us  [call(): pl.pallas_call(wrapped, out_shape=outs, in_specs=specs, out_specs=out_spe...]
    all_gather x1, waiting for transfers between devices: 1.06 us -> 11.3 us  [shards(): lax.all_gather(dense.reshape(peers * slice_width, 7 * width), 'dp', axis=...]
    all_to_all x2, starting transfers between devices: 11.9 us -> 6.32 us  [gather_everywhere(): return lax.all_to_all(sent, AXES, split_axis=0, concat_axis=0, tiled=True)]
    all_to_all x0 -> x1, waiting for transfers between devices: none -> 4.57 us  [shards(): lax.all_to_all(dense_own.reshape(peers, slice_width, 8 * width), 'expert'...]
    all_to_all x3 -> x2, starting transfers between devices: 11.3 us -> 8.37 us  [sum_to_owners(): lax.all_to_all(values, axes, split_axis=0, concat_axis=0, tiled=True)]
    unnamed x115 -> x111, local copies, waits for them, and re-layouts: 26.4 us -> 24.6 us
  transfers between devices with their start and end apart: 51 -> 51, of which waited for: 25 -> 28; matrix products, arithmetic and copies ran while one was open for 6% -> 6% of each run, Pallas kernels for 24% -> 31%
where the time goes in v3:
time: 433 us; the launch traced here: 425 us
  Pallas kernels  149 us (34%)
  waiting for transfers between devices  100 us (23%)
  starting transfers between devices  87.4 us (20%)
  local copies, waits for them, and re-layouts  35.2 us (8%)
  blocking collectives  19.3 us (4%)
  other arithmetic  18.3 us (4%)
  between operations  15.8 us (4%)
    pallas_call x28, Pallas kernels, call(): pl.pallas_call(wrapped, out_shape=outs, in_specs=specs, out_specs=out_spe...  149 us
    ppermute x24, starting transfers between devices, swap_blocks(): lax.ppermute(blocks[k], 'expert', [(i, i ^ k) for i in range(total)])  48.2 us
    ppermute x24, waiting for transfers between devices, swap_blocks(): lax.ppermute(blocks[k], 'expert', [(i, i ^ k) for i in range(total)])  44.8 us
    unnamed x111, local copies, waits for them, and re-layouts  24.6 us
    all_to_all x1, blocking collectives, shards(): lax.all_to_all(jnp.broadcast_to(dense[None], (peers,) + dense.shape), 'ex...  19.3 us
    ppermute x4, waiting for transfers between devices, dp_exchange(): return lax.ppermute(values, 'dp', [(i, i ^ mask) for i in range(dp_count)])  17.8 us
    ppermute x14, starting transfers between devices, exchange(): return lax.ppermute(values, axes, [(i, i ^ mask) for i in range(total)])  17.4 us
    ppermute x14, waiting for transfers between devices, exchange(): return lax.ppermute(values, axes, [(i, i ^ mask) for i in range(total)])  13.2 us
  transfers between devices with their start and end apart: 51, of which 28 were waited for; matrix products, arithmetic and copies ran while one was open for 6% of the time, Pallas kernels for 31%

profile of v3, /device:TPU:0, one launch (start us, length us, event | category | flops | bytes accessed | tf_op | source)
XLA Modules:
  0.0 424.9 jit_solution(10893142017306299090)
XLA Ops:
  10.5 19.3 %all_to_all.30 = bf16[4,16,3584]{2,1,0:T(8,128)(2,1)} all-to-all(bf16[4,16,3584]{2,1,0:T(8,128)(2,1)S(1)} %broadcast_in_dim.45), channel_id=1, replica_groups=mesh['dp'=8,'expert'=4] {'expert'}, dimensions={0} | all-to-all | bytes 917504 | tf_op jit(solution)/shard_map/all_to_all | solution.py:952
  32.1 3.2 shard_map.264
  36.0 3.7 all-to-all-start
  41.6 2.4 collective-permute-start.2
  46.2 2.2 all-to-all-done
  49.4 4.6 %shard_map.269 = (f32[512,512]{1,0:T(8,128)}, f32[512,512]{1,0:T(8,128)}, f32[512,128]{1,0:T(8,128)}, f32[512,1]{1,0:T(8,128)}, f32[512,1]{1,0:T(8,128)}, /*inde...) custom-call(s32[3]{0:T(128)} %slice_bitcast_fusion.8.ends, bf16[512,512]{1,0:T(8,128)(2,1)} %frames.5, ...), custom_call_target="tpu_custom_call" | custom-call | flops 5765000192 | tf_op jit(solution)/shard_map/pallas_call | solution.py:183
  56.9 2.2 copy-done.1
  59.1 3.0 shard_map.266
  62.2 3.0 shard_map.267
  67.3 3.0 shard_map.268
  70.2 2.4 collective-permute-start.5
  72.7 3.2 shard_map.265.refs_1__0_
  76.6 11.3 %all-gather.6.cloned.1.call-done.refs_5_.refs_6_.refs_7_.refs_10_.refs_11_.refs_12_ = bf16[512,3584]{1,0:T(8,128)(2,1)} async-done(((bf16[64,3584]{1,0:T(8,128)(2,1)}), bf16[512,3584]{1,0:T(8,128)(2,1)}) %all-gather.6.cloned.1.call-update) | async-done | bytes 3670032 | tf_op jit(solution)/shard_map/all_gather | solution.py:955
  88.7 15.6 %shard_map.270 = (bf16[512,512]{1,0:T(8,128)(2,1)}, f32[512,512]{1,0:T(8,128)}, f32[512,512]{1,0:T(8,128)}, bf16[512,512]{1,0:T(8,128)(2,1)}, bf16[512,1536]{1,0...) custom-call(bf16[512,512]{1,0:T(8,128)(2,1)} %frames.5, ...), custom_call_target="tpu_custom_call" | custom-call | flops 23060000768 | tf_op jit(solution)/shard_map/pallas_call | solution.py:183
  113.2 3.4 collective-permute-start.12
  116.6 2.2 collective-permute-start.11
  123.1 5.1 %shard_map.271 = (bf16[512,512]{1,0:T(8,128)(2,1)}, f32[512,512]{1,0:T(8,128)}, bf16[256,512]{1,0:T(8,128)(2,1)}, bf16[256,512]{1,0:T(8,128)(2,1)}, bf16[256,512]{1,0:T(8,128)(2,1)}, /*index=5*/bf16[256,512]{1,0:T(8,128)(2,1)}) custom-call(f32[1]{0:T(128)} %bitcast.refs_0_, f32[512,512]{1,0:T(8,128)} %get-tuple-element.129.refs_1_.refs_7_.refs_2_, ...), custom_call_target="tpu_custom_call" | custom-call | flops 5765000192 | tf_op jit(solution)/shard_map/pallas_call | solution.py:183
  130.0 2.6 collective-permute-start.17
  132.7 7.2 %collective-permute-done.13.block = bf16[256,512]{1,0:T(8,128)(2,1)S(1)} collective-permute-done((bf16[256,512]{1,0:T(8,128)(2,1)}, bf16[256,512]{1,0:T(8,128)(2,1)S(1)}, u32[]{:S(2)}, u32[]{:S(2)}) %collective-permute-start.13) | collective-permute-done | bytes 262176 | tf_op jit(solution)/shard_map/ppermute | solution.py:77
  139.9 2.2 copy-done.3
  142.1 2.8 shard_map.273
  144.9 4.0 collective-permute-done.15.block
  148.9 2.8 shard_map.274
  151.8 2.8 shard_map.275
  154.6 3.0 collective-permute-start.18
  157.5 2.8 shard_map.272.refs_1__0_
  161.0 10.3 %collective-permute-done.16.refs_1__2_ = bf16[256,512]{1,0:T(8,128)(2,1)S(1)} collective-permute-done((bf16[256,512]{1,0:T(8,128)(2,1)S(1)}, bf16[256,512]{1,0:T(8,128)(2,1)S(1)}, u32[]{:S(2)}, u32[]{:S(2)}) %collective-permute-start.16) | collective-permute-done | bytes 262176 | tf_op jit(solution)/shard_map/ppermute | solution.py:77
  172.1 5.9 %shard_map.276 = (bf16[512,512]{1,0:T(8,128)(2,1)}, f32[512,512]{1,0:T(8,128)}, f32[512,1]{1,0:T(8,128)}, f32[1,512]{1,0:T(1,128)}, bf16[256,512]{1,0:T(8,128)(2...) custom-call(f32[512,512]{1,0:T(8,128)} %get-tuple-element.133.refs_0_.refs_4_, ...), custom_call_target="tpu_custom_call" | custom-call | flops 5765000192 | tf_op jit(solution)/shard_map/pallas_call | solution.py:183
  178.0 4.1 collective-permute-start.19
  184.6 2.2 copy-done.4
  187.7 4.1 shard_map.277
  191.8 6.6 %collective-permute-done.22.grad.grads_3_ = bf16[256,512]{1,0:T(8,128)(2,1)S(1)} collective-permute-done((bf16[256,512]{1,0:T(8,128)(2,1)}, bf16[256,512]{1,0:T(8,128)(2,1)S(1)}, u32[]{:S(2)}, u32[]{:S(2)}) %collective-permute-start.22) | collective-permute-done | bytes 262176 | tf_op jit(solution)/shard_map/ppermute | solution.py:77
  198.4 4.1 shard_map.280
  204.4 4.1 shard_map.279
  208.5 9.3 %collective-permute-start.23 = (bf16[256,512]{1,0:T(8,128)(2,1)S(1)}, bf16[256,512]{1,0:T(8,128)(2,1)S(1)}, u32[]{:S(2)}, u32[]{:S(2)}) collective-permute-start(bf16[256,512]{1,0:T(8,128)(2,1)S(1)} %get-tuple-element.161), channel_id=1, source_target_pairs={{0,2},{1,3},{2,0},{3,1},{4,6},{5,7},{6,4},{7,5},{8,10},{9,11},{10,... | collective-permute-start | bytes 786440 | tf_op jit(solution)/shard_map/ppermute | solution.py:77
  217.8 4.1 shard_map.278
  221.9 6.0 %shard_map.281 = bf16[8,512,512]{2,1,0:T(8,128)(2,1)S(1)} custom-call(s32[1]{0:T(128)} %bitcast.20.dp_index, bf16[256,512]{1,0:T(8,128)(2,1)S(1)} %get-tuple-element.146.inputs_0_, bf16[256,512]{1,0:T(8,128)(2,1)S(1)} %get-tuple-element.147.inputs_1_, bf16[256,512]{1,0:T(8,128)(2,1)S(1)} %get-tuple-element.149.inputs_2_, ...), custom_call_target="tpu_custom_call" | custom-call | flops 9223999488 | tf_op jit(solution)/shard_map/pallas_call | solution.py:183
  232.4 6.6 %shard_map.282 = (f32[512,512]{1,0:T(8,128)}, bf16[512,512]{1,0:T(8,128)(2,1)}, f32[512,512]{1,0:T(8,128)}, f32[8,512]{1,0:T(8,128)}) custom-call(f32[1]{0:T(128)} %bitcast.refs_0_, f32[512,512]{1,0:T(8,128)} %get-tuple-element.141.refs_1_, bf16[256,512]{1,0:T(8,128)(2,1)} %copy-done.5, bf16[256,512]{1,0:T(8,128)(2,1)} %copy-done.43, ...), custom_call_target="tpu_custom_call" | custom-call | flops 5765000192 | tf_op jit(solution)/shard_map/pallas_call | solution.py:183
  241.2 2.3 collective-permute-start.28
  249.3 3.2 collective-permute-start.29
  254.8 22.3 %shard_map.283 = (bf16[512,1024]{1,0:T(8,128)(2,1)}, bf16[512,512]{1,0:T(8,128)(2,1)}, bf16[512,1536]{1,0:T(8,128)(2,1)}, f32[512,512]{1,0:T(8,128)}, f32[512,1]...) custom-call(f32[1]{0:T(128)} %bitcast.refs_0_, ...), custom_call_target="tpu_custom_call" | custom-call | flops 34589999104 | tf_op jit(solution)/shard_map/pallas_call | solution.py:183
  277.1 10.7 %shard_map.288 = (bf16[512,4096]{1,0:T(8,128)(2,1)}, bf16[512,512]{1,0:T(8,128)(2,1)}, f32[128,512]{1,0:T(8,128)}) custom-call(bf16[512,512]{1,0:T(8,128)(2,1)} %get-tuple-element.181.refs_0_, bf16[512,1536]{1,0:T(8,128)(2,1)} %get-tuple-element.182.refs_1_, bf16[512,512]{1,0:T(8,128)(2,1)} %get-tuple-element.183.refs_2_, ...), custom_call_target="tpu_custom_call" | custom-call | flops 1152999936 | tf_op jit(solution)/shard_map/pallas_call | solution.py:183
  287.9 5.0 %all-to-all-start.2 = ((bf16[8,64,4096]{2,1,0:T(8,128)(2,1)}), bf16[8,64,4096]{2,1,0:T(8,128)(2,1)}, u32[]{:S(2)}, u32[]{:S(2)}) async-start(bf16[8,64,4096]{2,1,0:T(8,128)(2,1)} %bitcast.103), calls=%async_computation.3 | async-start | bytes 8388608 | tf_op jit(solution)/shard_map/all_to_all | solution.py:69
  292.8 2.1 collective-permute-start.32
  297.4 2.2 copy-done.2
  299.6 3.8 shard_map.284
  304.1 10.0 %collective-permute-done.36.grad.grads_3_ = bf16[256,512]{1,0:T(8,128)(2,1)S(1)} collective-permute-done((bf16[256,512]{1,0:T(8,128)(2,1)S(1)}, bf16[256,512]{1,0:T(8,128)(2,1)S(1)}, u32[]{:S(2)}, u32[]{:S(2)}) %collective-permute-start.36) | collective-permute-done | bytes 262176 | tf_op jit(solution)/shard_map/ppermute | solution.py:77
  314.1 3.8 shard_map.287
  317.9 2.7 collective-permute-start.37
  320.6 3.8 shard_map.286
  324.5 6.5 %collective-permute-start.35 = (bf16[256,512]{1,0:T(8,128)(2,1)S(1)}, bf16[256,512]{1,0:T(8,128)(2,1)S(1)}, u32[]{:S(2)}, u32[]{:S(2)}) collective-permute-start(bf16[256,512]{1,0:T(8,128)(2,1)S(1)} %get-tuple-element.177), channel_id=1, source_target_pairs={{0,2},{1,3},{2,0},{3,1},{4,6},{5,7},{6,4},{7,5},{8,10},{9,11},{10,... | collective-permute-start | bytes 786440 | tf_op jit(solution)/shard_map/ppermute | solution.py:77
  331.0 3.8 shard_map.285
  334.9 7.4 %shard_map.291 = (bf16[4,512,512]{2,1,0:T(8,128)(2,1)S(1)}, bf16[4,512,512]{2,1,0:T(8,128)(2,1)}) custom-call(s32[1]{0:T(128)} %bitcast.20.dp_index, bf16[256,512]{1,0:T(8,128)(2,1)S(1)} %get-tuple-element.208.inputs_0_, bf16[256,512]{1,0:T(8,128)(2,1)S(1)} %get-tuple-element.209.inputs_1_, bf16[256,512]{1,0:T(8,128)(2,1)S(1)} %get-tuple-element.210.inputs_2_, ...), custom_call_target="tpu_custom_call" | custom-call | flops 9223999488 | tf_op jit(solution)/shard_map/pallas_call | solution.py:183
  342.3 2.2 collective-permute-done.35.blocks_2_
  344.6 3.0 collective-permute-done.33.blocks_1_
  350.4 3.4 all-to-all-start.5
  353.8 3.8 reduce_sum.31
  357.6 6.4 %all-to-all-done.5 = f32[32,16,128]{2,1,0:T(8,128)S(1)} async-done(((f32[32,16,128]{2,1,0:T(8,128)}), f32[32,16,128]{2,1,0:T(8,128)S(1)}, u32[]{:S(2)}, u32[]{:S(2)}) %all-to-all-start.5) | async-done | bytes 262176 | tf_op jit(solution)/shard_map/all_to_all | solution.py:69
  364.0 3.5 all-to-all-start.3
  370.4 2.2 add_convert_fusion
  378.2 4.6 %all-to-all-done.3.arrived = bf16[4,16,4096]{2,1,0:T(8,128)(2,1)S(1)} async-done(((bf16[4,16,4096]{2,1,0:T(8,128)(2,1)}), bf16[4,16,4096]{2,1,0:T(8,128)(2,1)S(1)}, u32[]{:S(2)}, u32[]{:S(2)}) %all-to-all-start.3) | async-done | bytes 524320 | tf_op jit(solution)/shard_map/all_to_all | solution.py:1169
  386.9 2.6 all-to-all-start.4
  389.7 16.6 %collective-permute-done.41 = bf16[512,512]{1,0:T(8,128)(2,1)S(1)} collective-permute-done((bf16[512,512]{1,0:T(8,128)(2,1)S(1)}, bf16[512,512]{1,0:T(8,128)(2,1)S(1)}, u32[]{:S(2)}, u32[]{:S(2)}) %collective-permute-start.41) | collective-permute-done | bytes 524320 | tf_op jit(solution)/shard_map/ppermute | solution.py:1193
  413.3 4.7 %shard_map.289 = f32[512,512]{1,0:T(8,128)} custom-call(bf16[512,512]{1,0:T(8,128)(2,1)} %frames.5, bf16[256,512]{1,0:T(8,128)(2,1)} %copy-done.14, bf16[256,512]{1,0:T(8,128)(2,1)} %copy-done.36, bf16[256,512]{1,0:T(8,128)(2,1)} %copy-done.35, bf16[256,512]{1,0:T(8,128)(2,1)} %copy-done.34, s32[512,1]{1,0:T(8,128)} %get-tuple-element.123.refs_2_.slot_col, ...), custom_call_target="tpu_custom_call" | custom-call | flops 46120001536 | tf_op jit(solution)/shard_map/pallas_call | solution.py:183
  (240 shorter events, 79.5 us)
Async XLA Ops:
  7.2 49.7 %all-gather.8.cloned.1.call-start = ((), (), s32[]{:S(2)}) async-start(), calls=%async_computation.9 | async-start | bytes 4718592 | tf_op jit(solution)/shard_map/all_gather | solution.py:920
  8.3 21.5 %copy-start.30 = (bf16[2,16,4]{1,2,0:T(4,128)(2,1)S(1)}, bf16[2,16,4]{1,2,0:T(4,128)(2,1)}, u32[]{:S(2)}) copy-start(bf16[2,16,4]{1,2,0:T(4,128)(2,1)} %param.22) | copy-start | bytes 772
  8.4 21.6 %copy-start.31 = (bf16[6,16]{1,0:T(8,128)(2,1)S(1)}, bf16[6,16]{1,0:T(8,128)(2,1)}, u32[]{:S(2)}) copy-start(bf16[6,16]{1,0:T(8,128)(2,1)} %param.23) | copy-start | bytes 580
  8.4 21.7 %copy-start.26 = (bf16[15,16]{1,0:T(8,128)(2,1)S(1)}, bf16[15,16]{1,0:T(8,128)(2,1)}, u32[]{:S(2)}) copy-start(bf16[15,16]{1,0:T(8,128)(2,1)} %param.27) | copy-start | bytes 1444
  8.4 21.8 %copy-start.32 = (bf16[16]{0:T(256)(128)(2,1)S(1)}, bf16[16]{0:T(256)(128)(2,1)}, u32[]{:S(2)}) copy-start(bf16[16]{0:T(256)(128)(2,1)} %param.28) | copy-start | bytes 100
  8.4 21.9 %copy-start.27 = (s32[512,1]{0,1:T(1,128)S(1)}, s32[512,1]{0,1:T(1,128)}, u32[]{:S(2)}) copy-start(s32[512,1]{0,1:T(1,128)} %param.19) | copy-start | bytes 6148
  8.4 22.7 %copy-start.28 = (s32[512,1]{0,1:T(1,128)S(1)}, s32[512,1]{0,1:T(1,128)}, u32[]{:S(2)}) copy-start(s32[512,1]{0,1:T(1,128)} %param.20) | copy-start | bytes 6148
  10.4 77.4 %all-gather.6.cloned.1.call-start = ((), (), s32[]{:S(2)}) async-start(), calls=%async_computation.7 | async-start | bytes 4128768 | tf_op jit(solution)/shard_map/all_gather | solution.py:955
  32.1 13.1 %copy-start.25 = (s32[32,4]{0,1:T(4,128)S(1)}, s32[32,4]{0,1:T(4,128)}, u32[]{:S(2)}) copy-start(s32[32,4]{0,1:T(4,128)} %param.18) | copy-start | bytes 1540
  36.0 12.4 %all-to-all-start = ((bf16[32,16,128]{2,1,0:T(8,128)(2,1)}), bf16[32,16,128]{2,1,0:T(8,128)(2,1)S(1)}, u32[]{:S(2)}, u32[]{:S(2)}) async-start(bf16[32,16,128]{2,1,0:T(8,128)(2,1)} %broadcast_in_dim.44), calls=%async_computation | async-start | bytes 262144 | tf_op jit(solution)/shard_map/all_to_all | solution.py:65
  39.7 92.9 %all-gather.10.cloned.1.call-start = ((), (), s32[]{:S(2)}) async-start(), calls=%async_computation.10 | async-start | bytes 4718592 | tf_op jit(solution)/shard_map/all_gather | solution.py:958
  39.8 17.1 %collective-permute-start = (bf16[256,512]{1,0:T(8,128)(2,1)}, bf16[256,512]{1,0:T(8,128)(2,1)S(1)}, u32[]{:S(2)}, u32[]{:S(2)}) collective-permute-start(bf16[256,512]{1,0:T(8,128)(2,1)} %get-tuple-element.120), channel_id=1, source_target_pairs={{0,1},{1,0},{2,3},{3,2},{4,5},{5,4},{6,7},{7,6},{8,9},{9,8},{10,11... | collective-permute-start | bytes 786440 | tf_op jit(solution)/shard_map/ppermute | solution.py:77
  41.6 20.6 %collective-permute-start.2 = (bf16[256,512]{1,0:T(8,128)(2,1)}, bf16[256,512]{1,0:T(8,128)(2,1)S(1)}, u32[]{:S(2)}, u32[]{:S(2)}) collective-permute-start(bf16[256,512]{1,0:T(8,128)(2,1)} %get-tuple-element.121), channel_id=1, source_target_pairs={{0,2},{1,3},{2,0},{3,1},{4,6},{5,7},{6,4},{7,5},{8,10},{9,11},{10,... | collective-permute-start | bytes 786440 | tf_op jit(solution)/shard_map/ppermute | solution.py:77
  44.0 23.2 %collective-permute-start.4 = (bf16[256,512]{1,0:T(8,128)(2,1)}, bf16[256,512]{1,0:T(8,128)(2,1)S(1)}, u32[]{:S(2)}, u32[]{:S(2)}) collective-permute-start(bf16[256,512]{1,0:T(8,128)(2,1)} %get-tuple-element.122), channel_id=1, source_target_pairs={{0,3},{1,2},{2,1},{3,0},{4,7},{5,6},{6,5},{7,4},{8,11},{9,10},{10,... | collective-permute-start | bytes 786440 | tf_op jit(solution)/shard_map/ppermute | solution.py:77
  45.1 364.8 %reduce-scatter.2.cloned.1.call-start = ((), (), s32[]{:S(2)}) async-start(), calls=%async_computation.8 | async-start | bytes 4718592 | tf_op jit(solution)/shard_map/reduce_scatter | solution.py:1083
  62.1 25.7 %collective-permute-start.1 = (bf16[256,512]{1,0:T(8,128)(2,1)S(1)}, bf16[256,512]{1,0:T(8,128)(2,1)S(1)}, u32[]{:S(2)}, u32[]{:S(2)}) collective-permute-start(bf16[256,512]{1,0:T(8,128)(2,1)S(1)} %shard_map.266), channel_id=1, source_target_pairs={{0,1},{1,0},{2,3},{3,2},{4,5},{5,4},{6,7},{7,6},{8,9},{9,8},{10,11... | collective-permute-start | bytes 786440 | tf_op jit(solution)/shard_map/ppermute | solution.py:77
  65.2 22.6 %collective-permute-start.3 = (bf16[256,512]{1,0:T(8,128)(2,1)S(1)}, bf16[256,512]{1,0:T(8,128)(2,1)S(1)}, u32[]{:S(2)}, u32[]{:S(2)}) collective-permute-start(bf16[256,512]{1,0:T(8,128)(2,1)S(1)} %shard_map.267), channel_id=1, source_target_pairs={{0,2},{1,3},{2,0},{3,1},{4,6},{5,7},{6,4},{7,5},{8,10},{9,11},{10,... | collective-permute-start | bytes 786440 | tf_op jit(solution)/shard_map/ppermute | solution.py:77
  70.2 17.6 %collective-permute-start.5 = (bf16[256,512]{1,0:T(8,128)(2,1)S(1)}, bf16[256,512]{1,0:T(8,128)(2,1)S(1)}, u32[]{:S(2)}, u32[]{:S(2)}) collective-permute-start(bf16[256,512]{1,0:T(8,128)(2,1)S(1)} %shard_map.268), channel_id=1, source_target_pairs={{0,3},{1,2},{2,1},{3,0},{4,7},{5,6},{6,5},{7,4},{8,11},{9,10},{10,... | collective-permute-start | bytes 786440 | tf_op jit(solution)/shard_map/ppermute | solution.py:77
  104.3 1.5 collective-permute-start.6
  106.5 4.6 %collective-permute-start.9 = (f32[8,512]{1,0:T(8,128)S(1)}, f32[8,512]{1,0:T(8,128)S(1)}, u32[]{:S(2)}, u32[]{:S(2)}) collective-permute-start(f32[8,512]{1,0:T(8,128)S(1)} %add.78), channel_id=1, source_target_pairs={{0,24},{1,25},{2,26},{3,27},{4,28},{5,29},{6,30},{7,31},{8,16},{9,... | collective-permute-start | bytes 49160 | tf_op jit(solution)/shard_map/ppermute | solution.py:34
  108.0 3.7 collective-permute-start.8
  109.5 3.7 collective-permute-start.7
  113.2 6.9 %collective-permute-start.12 = (f32[8,512]{1,0:T(8,128)S(1)}, f32[8,512]{1,0:T(8,128)S(1)}, u32[]{:S(2)}, u32[]{:S(2)}) collective-permute-start(f32[8,512]{1,0:T(8,128)S(1)} %add_add_fusion.3), channel_id=1, source_target_pairs={{0,3},{1,2},{2,1},{3,0},{4,7},{5,6},{6,5},{7,4},{8,11},{9,10},{10,... | collective-permute-start | bytes 49160 | tf_op jit(solution)/shard_map/ppermute | solution.py:34
  116.6 4.6 %collective-permute-start.11 = (f32[8,512]{1,0:T(8,128)S(1)}, f32[8,512]{1,0:T(8,128)S(1)}, u32[]{:S(2)}, u32[]{:S(2)}) collective-permute-start(f32[8,512]{1,0:T(8,128)S(1)} %add_add_fusion.3), channel_id=1, source_target_pairs={{0,2},{1,3},{2,0},{3,1},{4,6},{5,7},{6,4},{7,5},{8,10},{9,11},{10,... | collective-permute-start | bytes 49160 | tf_op jit(solution)/shard_map/ppermute | solution.py:34
  118.8 3.7 collective-permute-start.10
  128.2 11.7 %collective-permute-start.13 = (bf16[256,512]{1,0:T(8,128)(2,1)}, bf16[256,512]{1,0:T(8,128)(2,1)S(1)}, u32[]{:S(2)}, u32[]{:S(2)}) collective-permute-start(bf16[256,512]{1,0:T(8,128)(2,1)} %get-tuple-element.135), channel_id=1, source_target_pairs={{0,1},{1,0},{2,3},{3,2},{4,5},{5,4},{6,7},{7,6},{8,9},{9,8},{10,11... | collective-permute-start | bytes 786440 | tf_op jit(solution)/shard_map/ppermute | solution.py:77
  128.5 20.4 %collective-permute-start.15 = (bf16[256,512]{1,0:T(8,128)(2,1)}, bf16[256,512]{1,0:T(8,128)(2,1)S(1)}, u32[]{:S(2)}, u32[]{:S(2)}) collective-permute-start(bf16[256,512]{1,0:T(8,128)(2,1)} %get-tuple-element.136), channel_id=1, source_target_pairs={{0,2},{1,3},{2,0},{3,1},{4,6},{5,7},{6,4},{7,5},{8,10},{9,11},{10,... | collective-permute-start | bytes 786440 | tf_op jit(solution)/shard_map/ppermute | solution.py:77
  130.0 21.7 %collective-permute-start.17 = (bf16[256,512]{1,0:T(8,128)(2,1)}, bf16[256,512]{1,0:T(8,128)(2,1)S(1)}, u32[]{:S(2)}, u32[]{:S(2)}) collective-permute-start(bf16[256,512]{1,0:T(8,128)(2,1)} %get-tuple-element.137), channel_id=1, source_target_pairs={{0,3},{1,2},{2,1},{3,0},{4,7},{5,6},{6,5},{7,4},{8,11},{9,10},{10,... | collective-permute-start | bytes 786440 | tf_op jit(solution)/shard_map/ppermute | solution.py:77
  144.9 16.2 %collective-permute-start.14 = (bf16[256,512]{1,0:T(8,128)(2,1)S(1)}, bf16[256,512]{1,0:T(8,128)(2,1)S(1)}, u32[]{:S(2)}, u32[]{:S(2)}) collective-permute-start(bf16[256,512]{1,0:T(8,128)(2,1)S(1)} %shard_map.273), channel_id=1, source_target_pairs={{0,1},{1,0},{2,3},{3,2},{4,5},{5,4},{6,7},{7,6},{8,9},{9,8},{10,11... | collective-permute-start | bytes 786440 | tf_op jit(solution)/shard_map/ppermute | solution.py:77
  151.7 19.6 %collective-permute-start.16 = (bf16[256,512]{1,0:T(8,128)(2,1)S(1)}, bf16[256,512]{1,0:T(8,128)(2,1)S(1)}, u32[]{:S(2)}, u32[]{:S(2)}) collective-permute-start(bf16[256,512]{1,0:T(8,128)(2,1)S(1)} %shard_map.274), channel_id=1, source_target_pairs={{0,2},{1,3},{2,0},{3,1},{4,6},{5,7},{6,4},{7,5},{8,10},{9,11},{10,... | collective-permute-start | bytes 786440 | tf_op jit(solution)/shard_map/ppermute | solution.py:77
  154.6 16.8 %collective-permute-start.18 = (bf16[256,512]{1,0:T(8,128)(2,1)S(1)}, bf16[256,512]{1,0:T(8,128)(2,1)S(1)}, u32[]{:S(2)}, u32[]{:S(2)}) collective-permute-start(bf16[256,512]{1,0:T(8,128)(2,1)S(1)} %shard_map.275), channel_id=1, source_target_pairs={{0,3},{1,2},{2,1},{3,0},{4,7},{5,6},{6,5},{7,4},{8,11},{9,10},{10,... | collective-permute-start | bytes 786440 | tf_op jit(solution)/shard_map/ppermute | solution.py:77
  161.0 10.3 %copy-start.44 = (bf16[256,512]{1,0:T(8,128)(2,1)}, bf16[256,512]{1,0:T(8,128)(2,1)S(1)}, u32[]{:S(2)}) copy-start(bf16[256,512]{1,0:T(8,128)(2,1)S(1)} %collective-permute-done.14.refs_1__1_) | copy-start | bytes 786436
  178.0 39.8 %collective-permute-start.19 = (bf16[256,512]{1,0:T(8,128)(2,1)}, bf16[256,512]{1,0:T(8,128)(2,1)S(1)}, u32[]{:S(2)}, u32[]{:S(2)}) collective-permute-start(bf16[256,512]{1,0:T(8,128)(2,1)} %get-tuple-element.144), channel_id=1, source_target_pairs={{0,1},{1,0},{2,3},{3,2},{4,5},{5,4},{6,7},{7,6},{8,9},{9,8},{10,11... | collective-permute-start | bytes 786440 | tf_op jit(solution)/shard_map/ppermute | solution.py:77
  182.1 22.2 %collective-permute-start.21 = (bf16[256,512]{1,0:T(8,128)(2,1)}, bf16[256,512]{1,0:T(8,128)(2,1)S(1)}, u32[]{:S(2)}, u32[]{:S(2)}) collective-permute-start(bf16[256,512]{1,0:T(8,128)(2,1)} %get-tuple-element.148), channel_id=1, source_target_pairs={{0,2},{1,3},{2,0},{3,1},{4,6},{5,7},{6,4},{7,5},{8,10},{9,11},{10,... | collective-permute-start | bytes 786440 | tf_op jit(solution)/shard_map/ppermute | solution.py:77
  183.0 15.4 %collective-permute-start.22 = (bf16[256,512]{1,0:T(8,128)(2,1)}, bf16[256,512]{1,0:T(8,128)(2,1)S(1)}, u32[]{:S(2)}, u32[]{:S(2)}) collective-permute-start(bf16[256,512]{1,0:T(8,128)(2,1)} %get-tuple-element.150), channel_id=1, source_target_pairs={{0,3},{1,2},{2,1},{3,0},{4,7},{5,6},{6,5},{7,4},{8,11},{9,10},{10,... | collective-permute-start | bytes 786440 | tf_op jit(solution)/shard_map/ppermute | solution.py:77
  191.8 10.7 %copy-start.5 = (bf16[256,512]{1,0:T(8,128)(2,1)}, bf16[256,512]{1,0:T(8,128)(2,1)S(1)}, u32[]{:S(2)}) copy-start(bf16[256,512]{1,0:T(8,128)(2,1)S(1)} %get-tuple-element.143.refs_2__0_) | copy-start | bytes 786436
  202.5 29.0 %collective-permute-start.24 = (bf16[256,512]{1,0:T(8,128)(2,1)S(1)}, bf16[256,512]{1,0:T(8,128)(2,1)S(1)}, u32[]{:S(2)}, u32[]{:S(2)}) collective-permute-start(bf16[256,512]{1,0:T(8,128)(2,1)S(1)} %get-tuple-element.162), channel_id=1, source_target_pairs={{0,3},{1,2},{2,1},{3,0},{4,7},{5,6},{6,5},{7,4},{8,11},{9,10},{10,... | collective-permute-start | bytes 786440 | tf_op jit(solution)/shard_map/ppermute | solution.py:77
  208.5 13.4 %copy-start.8 = (bf16[256,512]{1,0:T(8,128)(2,1)S(1)}, bf16[256,512]{1,0:T(8,128)(2,1)}, u32[]{:S(2)}) copy-start(bf16[256,512]{1,0:T(8,128)(2,1)} %get-tuple-element.142.grad.grads_0_) | copy-start | bytes 786436
  208.5 23.0 %collective-permute-start.23 = (bf16[256,512]{1,0:T(8,128)(2,1)S(1)}, bf16[256,512]{1,0:T(8,128)(2,1)S(1)}, u32[]{:S(2)}, u32[]{:S(2)}) collective-permute-start(bf16[256,512]{1,0:T(8,128)(2,1)S(1)} %get-tuple-element.161), channel_id=1, source_target_pairs={{0,2},{1,3},{2,0},{3,1},{4,6},{5,7},{6,4},{7,5},{8,10},{9,11},{10,... | collective-permute-start | bytes 786440 | tf_op jit(solution)/shard_map/ppermute | solution.py:77
  221.9 9.6 %collective-permute-start.20 = (bf16[256,512]{1,0:T(8,128)(2,1)S(1)}, bf16[256,512]{1,0:T(8,128)(2,1)S(1)}, u32[]{:S(2)}, u32[]{:S(2)}) collective-permute-start(bf16[256,512]{1,0:T(8,128)(2,1)S(1)} %get-tuple-element.145), channel_id=1, source_target_pairs={{0,1},{1,0},{2,3},{3,2},{4,5},{5,4},{6,7},{7,6},{8,9},{9,8},{10,11... | collective-permute-start | bytes 786440 | tf_op jit(solution)/shard_map/ppermute | solution.py:77
  239.0 1.5 collective-permute-start.25
  241.2 4.6 %collective-permute-start.28 = (f32[8,512]{1,0:T(8,128)S(1)}, f32[8,512]{1,0:T(8,128)S(1)}, u32[]{:S(2)}, u32[]{:S(2)}) collective-permute-start(f32[8,512]{1,0:T(8,128)S(1)} %add.85), channel_id=1, source_target_pairs={{0,24},{1,25},{2,26},{3,27},{4,28},{5,29},{6,30},{7,31},{8,16},{9,... | collective-permute-start | bytes 49160 | tf_op jit(solution)/shard_map/ppermute | solution.py:34
  243.5 3.7 collective-permute-start.27
  244.3 3.7 collective-permute-start.26
  248.0 5.6 %collective-permute-start.31 = (f32[8,512]{1,0:T(8,128)S(1)}, f32[8,512]{1,0:T(8,128)S(1)}, u32[]{:S(2)}, u32[]{:S(2)}) collective-permute-start(f32[8,512]{1,0:T(8,128)S(1)} %add_add_fusion.1), channel_id=1, source_target_pairs={{0,3},{1,2},{2,1},{3,0},{4,7},{5,6},{6,5},{7,4},{8,11},{9,10},{10,... | collective-permute-start | bytes 49160 | tf_op jit(solution)/shard_map/ppermute | solution.py:34
  249.1 4.8 %collective-permute-start.30 = (f32[8,512]{1,0:T(8,128)S(1)}, f32[8,512]{1,0:T(8,128)S(1)}, u32[]{:S(2)}, u32[]{:S(2)}) collective-permute-start(f32[8,512]{1,0:T(8,128)S(1)} %add_add_fusion.1), channel_id=1, source_target_pairs={{0,2},{1,3},{2,0},{3,1},{4,6},{5,7},{6,4},{7,5},{8,10},{9,11},{10,... | collective-permute-start | bytes 49160 | tf_op jit(solution)/shard_map/ppermute | solution.py:34
  249.3 4.9 %collective-permute-start.29 = (f32[8,512]{1,0:T(8,128)S(1)}, f32[8,512]{1,0:T(8,128)S(1)}, u32[]{:S(2)}, u32[]{:S(2)}) collective-permute-start(f32[8,512]{1,0:T(8,128)S(1)} %add_add_fusion.1), channel_id=1, source_target_pairs={{0,1},{1,0},{2,3},{3,2},{4,5},{5,4},{6,7},{7,6},{8,9},{9,8},{10,11... | collective-permute-start | bytes 49160 | tf_op jit(solution)/shard_map/ppermute | solution.py:34
  287.8 9.6 %copy-start.11 = (bf16[256,512]{1,0:T(8,128)(2,1)S(1)}, bf16[256,512]{1,0:T(8,128)(2,1)}, u32[]{:S(2)}) copy-start(bf16[256,512]{1,0:T(8,128)(2,1)} %get-tuple-element.118.block) | copy-start | bytes 786436
  287.9 62.5 %all-to-all-start.2 = ((bf16[8,64,4096]{2,1,0:T(8,128)(2,1)}), bf16[8,64,4096]{2,1,0:T(8,128)(2,1)}, u32[]{:S(2)}, u32[]{:S(2)}) async-start(bf16[8,64,4096]{2,1,0:T(8,128)(2,1)} %bitcast.103), calls=%async_computation.3 | async-start | bytes 8388608 | tf_op jit(solution)/shard_map/all_to_all | solution.py:69
  292.8 38.1 %collective-permute-start.32 = (bf16[256,512]{1,0:T(8,128)(2,1)S(1)}, bf16[256,512]{1,0:T(8,128)(2,1)S(1)}, u32[]{:S(2)}, u32[]{:S(2)}) collective-permute-start(bf16[256,512]{1,0:T(8,128)(2,1)S(1)} %copy-done.37), channel_id=1, source_target_pairs={{0,1},{1,0},{2,3},{3,2},{4,5},{5,4},{6,7},{7,6},{8,9},{9,8},{10,11... | collective-permute-start | bytes 786440 | tf_op jit(solution)/shard_map/ppermute | solution.py:77
  295.0 25.7 %collective-permute-start.34 = (bf16[256,512]{1,0:T(8,128)(2,1)S(1)}, bf16[256,512]{1,0:T(8,128)(2,1)S(1)}, u32[]{:S(2)}, u32[]{:S(2)}) collective-permute-start(bf16[256,512]{1,0:T(8,128)(2,1)S(1)} %copy-done.38), channel_id=1, source_target_pairs={{0,2},{1,3},{2,0},{3,1},{4,6},{5,7},{6,4},{7,5},{8,10},{9,11},{10,... | collective-permute-start | bytes 786440 | tf_op jit(solution)/shard_map/ppermute | solution.py:77
  296.0 18.1 %collective-permute-start.36 = (bf16[256,512]{1,0:T(8,128)(2,1)S(1)}, bf16[256,512]{1,0:T(8,128)(2,1)S(1)}, u32[]{:S(2)}, u32[]{:S(2)}) collective-permute-start(bf16[256,512]{1,0:T(8,128)(2,1)S(1)} %copy-done.40), channel_id=1, source_target_pairs={{0,3},{1,2},{2,1},{3,0},{4,7},{5,6},{6,5},{7,4},{8,11},{9,10},{10,... | collective-permute-start | bytes 786440 | tf_op jit(solution)/shard_map/ppermute | solution.py:77
  317.9 24.4 %collective-permute-start.37 = (bf16[256,512]{1,0:T(8,128)(2,1)S(1)}, bf16[256,512]{1,0:T(8,128)(2,1)S(1)}, u32[]{:S(2)}, u32[]{:S(2)}) collective-permute-start(bf16[256,512]{1,0:T(8,128)(2,1)S(1)} %get-tuple-element.179), channel_id=1, source_target_pairs={{0,3},{1,2},{2,1},{3,0},{4,7},{5,6},{6,5},{7,4},{8,11},{9,10},{10,... | collective-permute-start | bytes 786440 | tf_op jit(solution)/shard_map/ppermute | solution.py:77
  324.5 20.1 %collective-permute-start.35 = (bf16[256,512]{1,0:T(8,128)(2,1)S(1)}, bf16[256,512]{1,0:T(8,128)(2,1)S(1)}, u32[]{:S(2)}, u32[]{:S(2)}) collective-permute-start(bf16[256,512]{1,0:T(8,128)(2,1)S(1)} %get-tuple-element.177), channel_id=1, source_target_pairs={{0,2},{1,3},{2,0},{3,1},{4,6},{5,7},{6,4},{7,5},{8,10},{9,11},{10,... | collective-permute-start | bytes 786440 | tf_op jit(solution)/shard_map/ppermute | solution.py:77
  334.8 12.8 %collective-permute-start.33 = (bf16[256,512]{1,0:T(8,128)(2,1)S(1)}, bf16[256,512]{1,0:T(8,128)(2,1)S(1)}, u32[]{:S(2)}, u32[]{:S(2)}) collective-permute-start(bf16[256,512]{1,0:T(8,128)(2,1)S(1)} %get-tuple-element.175), channel_id=1, source_target_pairs={{0,1},{1,0},{2,3},{3,2},{4,5},{5,4},{6,7},{7,6},{8,9},{9,8},{10,11... | collective-permute-start | bytes 786440 | tf_op jit(solution)/shard_map/ppermute | solution.py:77
  334.9 13.6 %copy-start.22 = (f32[24,512]{1,0:T(8,128)S(1)}, f32[24,512]{1,0:T(8,128)}, u32[]{:S(2)}) copy-start(f32[24,512]{1,0:T(8,128)} %get-tuple-element.201) | copy-start | bytes 147460
  334.9 14.3 %copy-start.29 = (f32[1,512]{1,0:T(1,128)S(1)}, f32[1,512]{1,0:T(1,128)}, u32[]{:S(2)}) copy-start(f32[1,512]{1,0:T(1,128)} %get-tuple-element.202) | copy-start | bytes 6148
  347.6 22.8 %collective-permute-start.38 = (bf16[4,512,512]{2,1,0:T(8,128)(2,1)}, bf16[4,512,512]{2,1,0:T(8,128)(2,1)}, u32[]{:S(2)}, u32[]{:S(2)}) collective-permute-start(bf16[4,512,512]{2,1,0:T(8,128)(2,1)} %get-tuple-element.222), channel_id=1, source_target_pairs={{0,4},{4,0},{8,12},{12,8},{16,20},{20,16},{24,28},{28,24},{1,5},{5... | collective-permute-start | bytes 6291464 | tf_op jit(solution)/shard_map/ppermute | solution.py:1193
  350.4 13.6 %all-to-all-start.5 = ((f32[32,16,128]{2,1,0:T(8,128)}), f32[32,16,128]{2,1,0:T(8,128)S(1)}, u32[]{:S(2)}, u32[]{:S(2)}) async-start(f32[32,16,128]{2,1,0:T(8,128)} %bitcast.26), calls=%async_computation.6 | async-start | bytes 524288 | tf_op jit(solution)/shard_map/all_to_all | solution.py:69
  364.0 18.8 %all-to-all-start.3 = ((bf16[4,16,4096]{2,1,0:T(8,128)(2,1)}), bf16[4,16,4096]{2,1,0:T(8,128)(2,1)S(1)}, u32[]{:S(2)}, u32[]{:S(2)}) async-start(bf16[4,16,4096]{2,1,0:T(8,128)(2,1)} %bitcast.23), calls=%async_computation.4 | async-start | bytes 1048576 | tf_op jit(solution)/shard_map/all_to_all | solution.py:1169
  374.7 14.9 %collective-permute-start.39 = (bf16[512,512]{1,0:T(8,128)(2,1)}, bf16[512,512]{1,0:T(8,128)(2,1)S(1)}, u32[]{:S(2)}, u32[]{:S(2)}) collective-permute-start(bf16[512,512]{1,0:T(8,128)(2,1)} %get-tuple-element.275), channel_id=1, source_target_pairs={{0,8},{4,12},{8,0},{12,4},{16,24},{20,28},{24,16},{28,20},{1,9},{5... | collective-permute-start | bytes 1572872 | tf_op jit(solution)/shard_map/ppermute | solution.py:1193
  375.8 30.5 %collective-permute-start.41 = (bf16[512,512]{1,0:T(8,128)(2,1)S(1)}, bf16[512,512]{1,0:T(8,128)(2,1)S(1)}, u32[]{:S(2)}, u32[]{:S(2)}) collective-permute-start(bf16[512,512]{1,0:T(8,128)(2,1)S(1)} %get-tuple-element.276), channel_id=1, source_target_pairs={{0,24},{4,28},{8,16},{12,20},{16,8},{20,12},{24,0},{28,4},{1,25},{... | collective-permute-start | bytes 1572872 | tf_op jit(solution)/shard_map/ppermute | solution.py:1193
  377.3 30.0 %collective-permute-start.40 = (bf16[512,512]{1,0:T(8,128)(2,1)S(1)}, bf16[512,512]{1,0:T(8,128)(2,1)S(1)}, u32[]{:S(2)}, u32[]{:S(2)}) collective-permute-start(bf16[512,512]{1,0:T(8,128)(2,1)S(1)} %get-tuple-element.277), channel_id=1, source_target_pairs={{0,16},{4,20},{8,24},{12,28},{16,0},{20,4},{24,8},{28,12},{1,17},{... | collective-permute-start | bytes 1572872 | tf_op jit(solution)/shard_map/ppermute | solution.py:1193
  386.9 21.8 %all-to-all-start.4 = ((bf16[32,16,512]{2,1,0:T(8,128)(2,1)}), bf16[32,16,512]{2,1,0:T(8,128)(2,1)S(1)}, u32[]{:S(2)}, u32[]{:S(2)}) async-start(bf16[32,16,512]{2,1,0:T(8,128)(2,1)} %broadcast_in_dim.47), calls=%async_computation.5 | async-start | bytes 1048576 | tf_op jit(solution)/shard_map/all_to_all | solution.py:65
  (36 other events, 104.5 us)
Sparse Core Ops, SparseCore 0:
  10.5 40.8 all-gather.7
  53.3 34.5 all-gather.5
  89.7 36.7 all-gather.9
  252.6 55.1 reduce-scatter.1

commit v4 on v3

--- a/solution.py
+++ b/solution.py
@@ -468,17 +468,25 @@
 
 def dense_grad_kernel(
     experts, stream, ua, dproj, attended, dat, uc, dgin, swish, dco, gate_grad1, gate1, col1, gate_grad2, gate2, col2,
-    probs, routers, pre, embedded, frames, out, dz, router_terms, logits,
+    dp_index, probs, routers, pre, embedded, frames, kept, moved, dz, router_terms, logits, term,
 ):
     width = ua.shape[1]
+    count = 2 * kept.shape[0]
+    part_rows = width // count
+
+    def place(left, right, tile):
+        for column in range(right.shape[1] // width):
+            term[...] = dot_tn(left[...], right[:, pl.ds(column * width, width)]).astype(BF16)
+            for number in range(count):
+                source = pl.multiple_of((dp_index[0] ^ number) * part_rows, part_rows)
+                target = moved if number % 2 else kept
+                target[number // 2, pl.ds((tile + column) * part_rows, part_rows), :] = term[pl.ds(source, part_rows), :]
+
     rows = frames.shape[0]
     stream.ready(0)
     stream.ready(1)
-    start = 0
-    for left, right in ((ua, dproj), (attended, dat)):
-        for column in range(0, right.shape[1], width):
-            out[:, pl.ds(start, width)] = dot_tn(left[...], right[:, pl.ds(column, width)]).astype(BF16)
-            start += width
+    place(ua, dproj, 0)
+    place(attended, dat, 3)
     stream.ready(2)
     for part in chunks(rows, 256):
         lane = iota((256, LANES), 1)
@@ -498,11 +506,30 @@
         logits[...], embedded[...], (((0,), (0,)), ((), ())), precision=HIGHEST, preferred_element_type=F32
     )
     stream.flush(dz, router_terms)
-    for left, right in ((uc, dgin), (swish, dco), (frames, dz)):
-        for column in range(0, right.shape[1], width):
-            out[:, pl.ds(start, width)] = dot_tn(left[...], right[:, pl.ds(column, width)]).astype(BF16)
-            start += width
-    stream.flush(out)
+    place(uc, dgin, 4)
+    place(swish, dco, 6)
+    place(frames, dz, 7)
+    stream.flush(kept, moved)
+
+
+def pair_kernel(kept, moved, *outs):
+    for number, out in enumerate(outs):
+        out[...] = (kept[number].astype(F32) + moved[number].astype(F32)).astype(BF16)
+
+
+def experts_out_kernel(parts, second, in_out, out_out):
+    _, _, in_rows, hidden = in_out.shape
+    width = out_out.shape[3]
+    half = out_out.shape[2]
+
+    first = parts[0][...].astype(F32)
+    for part in parts[1:]:
+        first = first + part[...].astype(F32)
+    for layer, values in ((0, first), (1, second[...].astype(F32))):
+        out_out[layer, 0] = values[:half]
+        for tile in range(hidden // width):
+            rows = values[half + tile * in_rows : half + (tile + 1) * in_rows]
+            in_out[layer, 0, :, tile * width : (tile + 1) * width] = rows
 
 
 def dense_out_kernel(arrived, *outs):
@@ -1139,9 +1166,13 @@
     )
     first_grads = swap_blocks(sent)
 
-    dense_terms, dz, router_terms = call(
+    def dp_exchange(values, mask):
+        return lax.ppermute(values, "dp", [(i, i ^ mask) for i in range(dp_count)])
+
+    dense_part = shaped((dp_count // 2, 8 * width // dp_count, width), BF16)
+    kept, moved, dz, router_terms = call(
         functools.partial(dense_grad_kernel, experts),
-        (shaped((width, 8 * width), BF16), low, shaped((LANES, width), F32)),
+        (dense_part, dense_part, low, shaped((LANES, width), F32)),
         ua,
         dproj,
         attended,
@@ -1156,16 +1187,29 @@
         gate_grad2,
         gate2,
         choice_second,
+        dp_index,
         probs,
         router_table,
         embed_pre,
         embedded,
         frames,
-        stages=[0, 0, 1, 1, 2, 2, 2, 2] + [None] * 7 + [None, 2, 2, 2],
+        specs=[None] * 14 + [SMEM] + [None] * 5,
+        stages=[0, 0, 1, 1, 2, 2, 2, 2] + [None] * 8 + [None, 2, 2, 2],
         cost=1,
-        scratch=[pltpu.VMEM((rows, LANES), F32)],
-    )
-    dense_own = sum_to_owners(dense_terms.reshape(dp_count, -1, 8 * width), "dp").astype(BF16)
+        scratch=[pltpu.VMEM((rows, LANES), F32), pltpu.VMEM((width, width), BF16)],
+    )
+    pairs = call(
+        pair_kernel,
+        [shaped(kept.shape[1:], BF16)] * (dp_count // 2),
+        kept,
+        dp_exchange(moved, 1),
+        vmem=16,
+        cost=10,
+    )
+    dense_own = pairs[0].astype(F32)
+    for pair, mask in zip(pairs[1:], chip_masks()[1:]):
+        dense_own = dense_own + dp_exchange(pair, mask).astype(F32)
+    dense_own = dense_own.astype(BF16).reshape(8, peers, slice_width, width).transpose(1, 2, 0, 3)
     dense_own = lax.all_to_all(
         dense_own.reshape(peers, slice_width, 8 * width), "expert", split_axis=0, concat_axis=0, tiled=True
     )
@@ -1174,11 +1218,9 @@
         dense_out_kernel,
         (*owned, shaped((slice_width, width), BF16)),
         dense_own,
+        vmem=8,
         cost=10,
     )
-    embed_total = gather_everywhere(embed_own)
-    embed_total = embed_total.reshape(width, width).astype(F32)
-
     backs = [
         expert_backward(block, grad, gain(0), first_weights, hidden, True)
         for block, grad in zip(first_blocks, first_grads)
@@ -1189,14 +1231,25 @@
     kept, moved = weight_grads(dp_index, inputs, first_grads, hid, pre_grads, dp_count, True)
     moved = after(moved, *first_back[1:])
 
-    def dp_exchange(values, mask):
-        return lax.ppermute(values, "dp", [(i, i ^ mask) for i in range(dp_count)])
-
-    pair_sum = (kept.astype(F32) + dp_exchange(moved, 1).astype(F32)).astype(BF16)
-    first_own = pair_sum[0].astype(F32)
-    for number, mask in enumerate(chip_masks()):
-        if mask:
-            first_own = first_own + dp_exchange(pair_sum[number], mask).astype(F32)
+    pairs = call(
+        pair_kernel,
+        [shaped(kept.shape[1:], BF16)] * (dp_count // 2),
+        kept,
+        dp_exchange(moved, 1),
+        vmem=16,
+        cost=20,
+    )
+    first_parts = [
+        dp_exchange(pair, mask) if mask else pair for pair, mask in zip(pairs, chip_masks())
+    ]
+    in_grad, out_grad = call(
+        experts_out_kernel,
+        (shaped((layers, 1, width // dp_count, hidden), F32), shaped((layers, 1, hidden // dp_count, width), F32)),
+        first_parts,
+        second_own,
+        vmem=24,
+        cost=10,
+    )
 
     small_terms = jnp.concatenate(
         [
@@ -1211,8 +1264,21 @@
         ],
         0,
     )
-    small_terms = jnp.pad(small_terms.T, ((0, 0), (0, LANES - small_width)))
-    small_sums = sum_to_owners(small_terms.reshape(-1, slice_width, LANES), AXES).T
+    small_terms = jnp.pad(small_terms.T, ((0, 0), (0, -small_width % 32)))
+    lanes = small_terms.shape[1] * slice_width
+    small_terms = jnp.pad(small_terms.reshape(-1, lanes), ((0, 0), (0, -lanes % width)))
+    high = lax.reduce_precision(small_terms, 8, 7)
+    split = jnp.stack([high, small_terms - high], 1).astype(BF16)
+    split = split.reshape(split.shape[0], -1, width)
+    split = jnp.pad(split, ((0, 0), (0, -split.shape[1] % 16), (0, 0)))
+    mixed = jnp.concatenate([split, jnp.broadcast_to(embed_own[None], (split.shape[0],) + embed_own.shape)], 1)
+    mixed = lax.all_to_all(mixed, AXES, split_axis=0, concat_axis=0, tiled=True)
+    embed_total = mixed[:, split.shape[1] :].reshape(width, width).astype(F32)
+    small_sums = jnp.sum(mixed[:, : split.shape[1]].astype(F32), 0)
+    count = -(-lanes // width)
+    small_sums = (small_sums[:count] + small_sums[count : 2 * count]).reshape(-1)[:lanes]
+    small_sums = small_sums.reshape(slice_width, -1).T
+
     frames_grad = call(
         final_kernel,
         wide,
@@ -1227,12 +1293,6 @@
         specs=[None] * 7 + [ANY],
         cost=40,
     )
-    def matrices(own):
-        half = own.shape[0] // 2
-        first = jnp.concatenate(jnp.split(own[half:], hidden // width, 0), 1)
-        return first, own[:half]
-
-    first_pair, second_pair = matrices(first_own), matrices(second_own.astype(F32))
     return (
         block_out,
         frames_grad,
@@ -1245,8 +1305,8 @@
         small_sums[gains : gains + taps],
         small_sums[gains + taps],
         dense_own[3],
-        jnp.stack([first_pair[0], second_pair[0]])[:, None],
-        jnp.stack([first_pair[1], second_pair[1]])[:, None],
+        in_grad,
+        out_grad,
     )
 
 

time: 433 us -> 421 us (0.972)
  starting transfers between devices: 87.4 us -> 78.9 us
  other arithmetic: 18.3 us -> 9.98 us
    ppermute x24, waiting for transfers between devices: 44.8 us -> 32.7 us  [swap_blocks(): lax.ppermute(blocks[k], 'expert', [(i, i ^ k) for i in range(total)])]
    all_to_all x2 -> x1, waiting for transfers between devices: 6.36 us -> 17.1 us  [shards(): mixed = lax.all_to_all(mixed, AXES, split_axis=0, concat_axis=0, tiled=True)]
    all_to_all x1, waiting for transfers between devices: 4.57 us -> 10.3 us  [shards(): lax.all_to_all(dense_own.reshape(peers, slice_width, 8 * width), 'expert'...]
    all_to_all x2 -> x1, starting transfers between devices: 8.37 us -> 3.39 us  [shards(): mixed = lax.all_to_all(mixed, AXES, split_axis=0, concat_axis=0, tiled=True)]
    ppermute x24, starting transfers between devices: 48.2 us -> 43.5 us  [swap_blocks(): lax.ppermute(blocks[k], 'expert', [(i, i ^ k) for i in range(total)])]
    ppermute x4 -> x8, waiting for transfers between devices: 17.8 us -> 13.9 us  [dp_exchange(): return lax.ppermute(values, 'dp', [(i, i ^ mask) for i in range(dp_count)])]
    pallas_call x28 -> x31, Pallas kernels: 149 us -> 151 us  [call(): pl.pallas_call(wrapped, out_shape=outs, in_specs=specs, out_specs=out_spe...]
    unnamed x111 -> x119, local copies, waits for them, and re-layouts: 24.6 us -> 26 us
  transfers between devices with their start and end apart: 51 -> 53, of which waited for: 28 -> 26; matrix products, arithmetic and copies ran while one was open for 6% -> 6% of each run, Pallas kernels for 31% -> 33%
where the time goes in v4:
time: 421 us; the launch traced here: 413 us
  Pallas kernels  151 us (36%)
  waiting for transfers between devices  100 us (24%)
  starting transfers between devices  78.9 us (19%)
  local copies, waits for them, and re-layouts  37.4 us (9%)
  blocking collectives  19.3 us (5%)
  between operations  15.8 us (4%)
  other arithmetic  9.98 us (2%)
    pallas_call x31, Pallas kernels, call(): pl.pallas_call(wrapped, out_shape=outs, in_specs=specs, out_specs=out_spe...  151 us
    ppermute x24, starting transfers between devices, swap_blocks(): lax.ppermute(blocks[k], 'expert', [(i, i ^ k) for i in range(total)])  43.5 us
    ppermute x24, waiting for transfers between devices, swap_blocks(): lax.ppermute(blocks[k], 'expert', [(i, i ^ k) for i in range(total)])  32.7 us
    unnamed x119, local copies, waits for them, and re-layouts  26 us
    all_to_all x1, blocking collectives, shards(): lax.all_to_all(jnp.broadcast_to(dense[None], (peers,) + dense.shape), 'ex...  19.3 us
    ppermute x14, starting transfers between devices, exchange(): return lax.ppermute(values, axes, [(i, i ^ mask) for i in range(total)])  17.5 us
    all_to_all x1, waiting for transfers between devices, shards(): mixed = lax.all_to_all(mixed, AXES, split_axis=0, concat_axis=0, tiled=True)  17.1 us
    ppermute x8, waiting for transfers between devices, dp_exchange(): return lax.ppermute(values, 'dp', [(i, i ^ mask) for i in range(dp_count)])  13.9 us
  transfers between devices with their start and end apart: 53, of which 26 were waited for; matrix products, arithmetic and copies ran while one was open for 6% of the time, Pallas kernels for 33%

profile of v4, /device:TPU:0, one launch (start us, length us, event | category | flops | bytes accessed | tf_op | source)
XLA Modules:
  0.0 412.7 jit_solution(612052817114339866)
XLA Ops:
  10.5 19.3 %all_to_all.20 = bf16[4,16,3584]{2,1,0:T(8,128)(2,1)} all-to-all(bf16[4,16,3584]{2,1,0:T(8,128)(2,1)S(1)} %broadcast_in_dim.39), channel_id=1, replica_groups=mesh['dp'=8,'expert'=4] {'expert'}, dimensions={0} | all-to-all | bytes 917504 | tf_op jit(solution)/shard_map/all_to_all | solution.py:979
  32.1 3.2 shard_map.264
  36.0 3.7 all-to-all-start
  41.6 2.4 collective-permute-start.2
  46.2 2.2 all-to-all-done
  49.4 4.6 %shard_map.269 = (f32[512,512]{1,0:T(8,128)}, f32[512,512]{1,0:T(8,128)}, f32[512,128]{1,0:T(8,128)}, f32[512,1]{1,0:T(8,128)}, f32[512,1]{1,0:T(8,128)}, /*inde...) custom-call(s32[3]{0:T(128)} %slice_bitcast_fusion.2.ends, bf16[512,512]{1,0:T(8,128)(2,1)} %frames.5, ...), custom_call_target="tpu_custom_call" | custom-call | flops 5765000192 | tf_op jit(solution)/shard_map/pallas_call | solution.py:183
  55.1 1.8 fusion.3
  56.9 2.2 copy-done.1
  59.1 3.0 shard_map.266
  62.2 3.0 shard_map.267
  65.2 2.0 collective-permute-start.3
  67.3 3.0 shard_map.268
  70.2 2.4 collective-permute-start.5
  72.7 3.2 shard_map.265.refs_1__0_
  76.6 11.2 %all-gather.6.cloned.1.call-done.refs_5_.refs_6_.refs_7_.refs_10_.refs_11_.refs_12_ = bf16[512,3584]{1,0:T(8,128)(2,1)} async-done(((bf16[64,3584]{1,0:T(8,128)(2,1)}), bf16[512,3584]{1,0:T(8,128)(2,1)}) %all-gather.6.cloned.1.call-update) | async-done | bytes 3670032 | tf_op jit(solution)/shard_map/all_gather | solution.py:982
  88.7 15.7 %shard_map.270 = (bf16[512,512]{1,0:T(8,128)(2,1)}, f32[512,512]{1,0:T(8,128)}, f32[512,512]{1,0:T(8,128)}, bf16[512,512]{1,0:T(8,128)(2,1)}, bf16[512,1536]{1,0...) custom-call(bf16[512,512]{1,0:T(8,128)(2,1)} %frames.5, ...), custom_call_target="tpu_custom_call" | custom-call | flops 23060000768 | tf_op jit(solution)/shard_map/pallas_call | solution.py:183
  113.2 3.4 collective-permute-start.12
  116.6 2.3 collective-permute-start.11
  123.2 5.0 %shard_map.271 = (bf16[512,512]{1,0:T(8,128)(2,1)}, f32[512,512]{1,0:T(8,128)}, bf16[256,512]{1,0:T(8,128)(2,1)}, bf16[256,512]{1,0:T(8,128)(2,1)}, bf16[256,512]{1,0:T(8,128)(2,1)}, /*index=5*/bf16[256,512]{1,0:T(8,128)(2,1)}) custom-call(f32[1]{0:T(128)} %bitcast.refs_0_, f32[512,512]{1,0:T(8,128)} %get-tuple-element.140.refs_1_.refs_7_.refs_2_, ...), custom_call_target="tpu_custom_call" | custom-call | flops 5765000192 | tf_op jit(solution)/shard_map/pallas_call | solution.py:183
  130.1 2.6 collective-permute-start.17
  132.7 7.2 %collective-permute-done.13.block = bf16[256,512]{1,0:T(8,128)(2,1)S(1)} collective-permute-done((bf16[256,512]{1,0:T(8,128)(2,1)}, bf16[256,512]{1,0:T(8,128)(2,1)S(1)}, u32[]{:S(2)}, u32[]{:S(2)}) %collective-permute-start.13) | collective-permute-done | bytes 262176 | tf_op jit(solution)/shard_map/ppermute | solution.py:77
  139.9 2.2 copy-done.3
  142.1 2.8 shard_map.273
  145.0 4.1 collective-permute-done.15.block
  149.1 2.8 shard_map.274
  152.0 2.8 shard_map.275
  154.8 2.8 collective-permute-start.18
  157.6 2.8 shard_map.272.refs_1__0_
  161.0 10.3 %collective-permute-done.16.refs_1__2_ = bf16[256,512]{1,0:T(8,128)(2,1)S(1)} collective-permute-done((bf16[256,512]{1,0:T(8,128)(2,1)S(1)}, bf16[256,512]{1,0:T(8,128)(2,1)S(1)}, u32[]{:S(2)}, u32[]{:S(2)}) %collective-permute-start.16) | collective-permute-done | bytes 262176 | tf_op jit(solution)/shard_map/ppermute | solution.py:77
  172.1 5.9 %shard_map.276 = (bf16[512,512]{1,0:T(8,128)(2,1)}, f32[512,512]{1,0:T(8,128)}, f32[512,1]{1,0:T(8,128)}, f32[1,512]{1,0:T(1,128)}, bf16[256,512]{1,0:T(8,128)(2...) custom-call(f32[512,512]{1,0:T(8,128)} %get-tuple-element.144.refs_0_.refs_4_, ...), custom_call_target="tpu_custom_call" | custom-call | flops 5765000192 | tf_op jit(solution)/shard_map/pallas_call | solution.py:183
  178.0 4.2 %collective-permute-start.19 = (bf16[256,512]{1,0:T(8,128)(2,1)}, bf16[256,512]{1,0:T(8,128)(2,1)S(1)}, u32[]{:S(2)}, u32[]{:S(2)}) collective-permute-start(bf16[256,512]{1,0:T(8,128)(2,1)} %get-tuple-element.155), channel_id=1, source_target_pairs={{0,1},{1,0},{2,3},{3,2},{4,5},{5,4},{6,7},{7,6},{8,9},{9,8},{10,11... | collective-permute-start | bytes 786440 | tf_op jit(solution)/shard_map/ppermute | solution.py:77
  184.6 2.2 copy-done.4
  187.8 4.1 shard_map.277
  191.9 6.5 %collective-permute-done.22.grad.grads_3_ = bf16[256,512]{1,0:T(8,128)(2,1)S(1)} collective-permute-done((bf16[256,512]{1,0:T(8,128)(2,1)}, bf16[256,512]{1,0:T(8,128)(2,1)S(1)}, u32[]{:S(2)}, u32[]{:S(2)}) %collective-permute-start.22) | collective-permute-done | bytes 262176 | tf_op jit(solution)/shard_map/ppermute | solution.py:77
  198.4 4.1 shard_map.280
  202.5 1.9 collective-permute-start.24
  204.4 4.1 shard_map.279
  208.5 9.3 %collective-permute-start.23 = (bf16[256,512]{1,0:T(8,128)(2,1)S(1)}, bf16[256,512]{1,0:T(8,128)(2,1)S(1)}, u32[]{:S(2)}, u32[]{:S(2)}) collective-permute-start(bf16[256,512]{1,0:T(8,128)(2,1)S(1)} %get-tuple-element.172), channel_id=1, source_target_pairs={{0,2},{1,3},{2,0},{3,1},{4,6},{5,7},{6,4},{7,5},{8,10},{9,11},{10,... | collective-permute-start | bytes 786440 | tf_op jit(solution)/shard_map/ppermute | solution.py:77
  217.8 4.1 shard_map.278
  221.9 6.0 %shard_map.281 = bf16[8,512,512]{2,1,0:T(8,128)(2,1)S(1)} custom-call(s32[1]{0:T(128)} %bitcast.20.dp_index.refs_14_, bf16[256,512]{1,0:T(8,128)(2,1)S(1)} %get-tuple-element.157.inputs_0_, bf16[256,512]{1,0:T(8,128)(2,1)S(1)} %get-tuple-element.158.inputs_1_, bf16[256,512]{1,0:T(8,128)(2,1)S(1)} %get-tuple-element.160.inputs_2_, ...), custom_call_target="tpu_custom_call" | custom-call | flops 9223999488 | tf_op jit(solution)/shard_map/pallas_call | solution.py:183
  227.9 2.0 copy-done
  232.4 6.6 %shard_map.282 = (f32[512,512]{1,0:T(8,128)}, bf16[512,512]{1,0:T(8,128)(2,1)}, f32[512,512]{1,0:T(8,128)}, f32[8,512]{1,0:T(8,128)}) custom-call(f32[1]{0:T(128)} %bitcast.refs_0_, f32[512,512]{1,0:T(8,128)} %get-tuple-element.152.refs_1_, bf16[256,512]{1,0:T(8,128)(2,1)} %copy-done.11, bf16[256,512]{1,0:T(8,128)(2,1)} %copy-done.47, ...), custom_call_target="tpu_custom_call" | custom-call | flops 5765000192 | tf_op jit(solution)/shard_map/pallas_call | solution.py:183
  241.1 2.0 collective-permute-start.28
  246.9 1.9 collective-permute-start.31
  248.9 2.5 collective-permute-start.29
  254.1 22.5 %shard_map.283 = (bf16[512,1024]{1,0:T(8,128)(2,1)}, bf16[512,512]{1,0:T(8,128)(2,1)}, bf16[512,1536]{1,0:T(8,128)(2,1)}, f32[512,512]{1,0:T(8,128)}, f32[512,1]...) custom-call(f32[1]{0:T(128)} %bitcast.refs_0_, ...), custom_call_target="tpu_custom_call" | custom-call | flops 34589999104 | tf_op jit(solution)/shard_map/pallas_call | solution.py:183
  279.0 2.1 collective-permute-start.36
  281.1 11.0 %shard_map.288 = (bf16[4,512,512]{2,1,0:T(8,128)(2,1)}, bf16[4,512,512]{2,1,0:T(8,128)(2,1)}, bf16[512,512]{1,0:T(8,128)(2,1)}, f32[128,512]{1,0:T(8,128)}) custom-call(bf16[512,512]{1,0:T(8,128)(2,1)} %get-tuple-element.192.refs_0_, bf16[512,1536]{1,0:T(8,128)(2,1)} %get-tuple-element.193.refs_1_, bf16[512,512]{1,0:T(8,128)(2,1)} %get-tuple-element.194.refs_2_, ...), custom_call_target="tpu_custom_call" | custom-call | flops 1152999936 | tf_op jit(solution)/shard_map/pallas_call | solution.py:183
  292.2 2.5 copy-done.2
  294.8 3.9 shard_map.284
  298.6 3.9 shard_map.287
  303.8 3.8 shard_map.286
  307.7 3.5 collective-permute-start.35
  311.2 3.8 shard_map.285
  319.2 6.1 %shard_map.292 = (bf16[4,512,512]{2,1,0:T(8,128)(2,1)S(1)}, bf16[4,512,512]{2,1,0:T(8,128)(2,1)S(1)}) custom-call(s32[1]{0:T(128)} %bitcast.20.dp_index.refs_14_, bf16[256,512]{1,0:T(8,128)(2,1)S(1)} %get-tuple-element.224.inputs_0_, bf16[256,512]{1,0:T(8,128)(2,1)S(1)} %get-tuple-element.225.inputs_1_, bf16[256,512]{1,0:T(8,128)(2,1)S(1)} %get-tuple-element.226.inputs_2_, ...), custom_call_target="tpu_custom_call" | custom-call | flops 9223999488 | tf_op jit(solution)/shard_map/pallas_call | solution.py:183
  325.3 3.0 collective-permute-done.35.blocks_2_
  328.5 2.1 collective-permute-done.39
  330.6 9.6 %collective-permute-done.40 = bf16[512,512]{1,0:T(8,128)(2,1)S(1)} collective-permute-done((bf16[512,512]{1,0:T(8,128)(2,1)S(1)}, bf16[512,512]{1,0:T(8,128)(2,1)S(1)}, u32[]{:S(2)}, u32[]{:S(2)}) %collective-permute-start.40) | collective-permute-done | bytes 524320 | tf_op jit(solution)/shard_map/ppermute | solution.py:1170
  342.9 3.5 all-to-all-start.2
  349.4 10.3 %all-to-all-done.2.arrived = bf16[4,16,4096]{2,1,0:T(8,128)(2,1)S(1)} async-done(((bf16[4,16,4096]{2,1,0:T(8,128)(2,1)}), bf16[4,16,4096]{2,1,0:T(8,128)(2,1)S(1)}, u32[]{:S(2)}, u32[]{:S(2)}) %all-to-all-start.2) | async-done | bytes 524320 | tf_op jit(solution)/shard_map/all_to_all | solution.py:1213
  362.5 3.4 all-to-all-start.3
  367.5 2.1 shard_map.293
  373.8 17.1 %all-to-all-done.3 = bf16[32,32,512]{2,1,0:T(8,128)(2,1)} async-done(((bf16[32,32,512]{2,1,0:T(8,128)(2,1)}), bf16[32,32,512]{2,1,0:T(8,128)(2,1)}, u32[]{:S(2)}, u32[]{:S(2)}) %all-to-all-start.3) | async-done | bytes 1048608 | tf_op jit(solution)/shard_map/all_to_all | solution.py:1275
  397.2 4.7 %shard_map.289 = f32[512,512]{1,0:T(8,128)} custom-call(bf16[512,512]{1,0:T(8,128)(2,1)} %frames.5, bf16[256,512]{1,0:T(8,128)(2,1)} %copy-done.22, bf16[256,512]{1,0:T(8,128)(2,1)} %copy-done.43, bf16[256,512]{1,0:T(8,128)(2,1)} %copy-done.42, bf16[256,512]{1,0:T(8,128)(2,1)} %copy-done.41, s32[512,1]{1,0:T(8,128)} %get-tuple-element.134.refs_2_.slot_col, ...), custom_call_target="tpu_custom_call" | custom-call | flops 46120001536 | tf_op jit(solution)/shard_map/pallas_call | solution.py:183
  (253 shorter events, 76.8 us)
Async XLA Ops:
  7.2 49.7 %all-gather.8.cloned.1.call-start = ((), (), s32[]{:S(2)}) async-start(), calls=%async_computation.7 | async-start | bytes 4718592 | tf_op jit(solution)/shard_map/all_gather | solution.py:947
  8.3 21.5 %copy-start.37 = (bf16[2,16,4]{1,2,0:T(4,128)(2,1)S(1)}, bf16[2,16,4]{1,2,0:T(4,128)(2,1)}, u32[]{:S(2)}) copy-start(bf16[2,16,4]{1,2,0:T(4,128)(2,1)} %param.22) | copy-start | bytes 772
  8.4 21.6 %copy-start.38 = (bf16[6,16]{1,0:T(8,128)(2,1)S(1)}, bf16[6,16]{1,0:T(8,128)(2,1)}, u32[]{:S(2)}) copy-start(bf16[6,16]{1,0:T(8,128)(2,1)} %param.23) | copy-start | bytes 580
  8.4 21.7 %copy-start.33 = (bf16[15,16]{1,0:T(8,128)(2,1)S(1)}, bf16[15,16]{1,0:T(8,128)(2,1)}, u32[]{:S(2)}) copy-start(bf16[15,16]{1,0:T(8,128)(2,1)} %param.27) | copy-start | bytes 1444
  8.4 21.8 %copy-start.39 = (bf16[16]{0:T(256)(128)(2,1)S(1)}, bf16[16]{0:T(256)(128)(2,1)}, u32[]{:S(2)}) copy-start(bf16[16]{0:T(256)(128)(2,1)} %param.28) | copy-start | bytes 100
  8.4 21.9 %copy-start.34 = (s32[512,1]{0,1:T(1,128)S(1)}, s32[512,1]{0,1:T(1,128)}, u32[]{:S(2)}) copy-start(s32[512,1]{0,1:T(1,128)} %param.19) | copy-start | bytes 6148
  8.4 22.7 %copy-start.35 = (s32[512,1]{0,1:T(1,128)S(1)}, s32[512,1]{0,1:T(1,128)}, u32[]{:S(2)}) copy-start(s32[512,1]{0,1:T(1,128)} %param.20) | copy-start | bytes 6148
  10.4 77.4 %all-gather.6.cloned.1.call-start = ((), (), s32[]{:S(2)}) async-start(), calls=%async_computation.5 | async-start | bytes 4128768 | tf_op jit(solution)/shard_map/all_gather | solution.py:982
  32.1 13.1 %copy-start.32 = (s32[32,4]{0,1:T(4,128)S(1)}, s32[32,4]{0,1:T(4,128)}, u32[]{:S(2)}) copy-start(s32[32,4]{0,1:T(4,128)} %param.18) | copy-start | bytes 1540
  36.0 12.4 %all-to-all-start = ((bf16[32,16,128]{2,1,0:T(8,128)(2,1)}), bf16[32,16,128]{2,1,0:T(8,128)(2,1)S(1)}, u32[]{:S(2)}, u32[]{:S(2)}) async-start(bf16[32,16,128]{2,1,0:T(8,128)(2,1)} %broadcast_in_dim.38), calls=%async_computation | async-start | bytes 262144 | tf_op jit(solution)/shard_map/all_to_all | solution.py:65
  39.7 93.0 %all-gather.10.cloned.1.call-start = ((), (), s32[]{:S(2)}) async-start(), calls=%async_computation.8 | async-start | bytes 4718592 | tf_op jit(solution)/shard_map/all_gather | solution.py:985
  39.8 17.1 %collective-permute-start = (bf16[256,512]{1,0:T(8,128)(2,1)}, bf16[256,512]{1,0:T(8,128)(2,1)S(1)}, u32[]{:S(2)}, u32[]{:S(2)}) collective-permute-start(bf16[256,512]{1,0:T(8,128)(2,1)} %get-tuple-element.131), channel_id=1, source_target_pairs={{0,1},{1,0},{2,3},{3,2},{4,5},{5,4},{6,7},{7,6},{8,9},{9,8},{10,11... | collective-permute-start | bytes 786440 | tf_op jit(solution)/shard_map/ppermute | solution.py:77
  41.6 20.6 %collective-permute-start.2 = (bf16[256,512]{1,0:T(8,128)(2,1)}, bf16[256,512]{1,0:T(8,128)(2,1)S(1)}, u32[]{:S(2)}, u32[]{:S(2)}) collective-permute-start(bf16[256,512]{1,0:T(8,128)(2,1)} %get-tuple-element.132), channel_id=1, source_target_pairs={{0,2},{1,3},{2,0},{3,1},{4,6},{5,7},{6,4},{7,5},{8,10},{9,11},{10,... | collective-permute-start | bytes 786440 | tf_op jit(solution)/shard_map/ppermute | solution.py:77
  44.0 23.2 %collective-permute-start.4 = (bf16[256,512]{1,0:T(8,128)(2,1)}, bf16[256,512]{1,0:T(8,128)(2,1)S(1)}, u32[]{:S(2)}, u32[]{:S(2)}) collective-permute-start(bf16[256,512]{1,0:T(8,128)(2,1)} %get-tuple-element.133), channel_id=1, source_target_pairs={{0,3},{1,2},{2,1},{3,0},{4,7},{5,6},{6,5},{7,4},{8,11},{9,10},{10,... | collective-permute-start | bytes 786440 | tf_op jit(solution)/shard_map/ppermute | solution.py:77
  45.1 352.1 %reduce-scatter.2.cloned.1.call-start = ((), (), s32[]{:S(2)}) async-start(), calls=%async_computation.6 | async-start | bytes 4718592 | tf_op jit(solution)/shard_map/reduce_scatter | solution.py:1110
  62.1 25.7 %collective-permute-start.1 = (bf16[256,512]{1,0:T(8,128)(2,1)S(1)}, bf16[256,512]{1,0:T(8,128)(2,1)S(1)}, u32[]{:S(2)}, u32[]{:S(2)}) collective-permute-start(bf16[256,512]{1,0:T(8,128)(2,1)S(1)} %shard_map.266), channel_id=1, source_target_pairs={{0,1},{1,0},{2,3},{3,2},{4,5},{5,4},{6,7},{7,6},{8,9},{9,8},{10,11... | collective-permute-start | bytes 786440 | tf_op jit(solution)/shard_map/ppermute | solution.py:77
  65.2 22.6 %collective-permute-start.3 = (bf16[256,512]{1,0:T(8,128)(2,1)S(1)}, bf16[256,512]{1,0:T(8,128)(2,1)S(1)}, u32[]{:S(2)}, u32[]{:S(2)}) collective-permute-start(bf16[256,512]{1,0:T(8,128)(2,1)S(1)} %shard_map.267), channel_id=1, source_target_pairs={{0,2},{1,3},{2,0},{3,1},{4,6},{5,7},{6,4},{7,5},{8,10},{9,11},{10,... | collective-permute-start | bytes 786440 | tf_op jit(solution)/shard_map/ppermute | solution.py:77
  70.2 17.6 %collective-permute-start.5 = (bf16[256,512]{1,0:T(8,128)(2,1)S(1)}, bf16[256,512]{1,0:T(8,128)(2,1)S(1)}, u32[]{:S(2)}, u32[]{:S(2)}) collective-permute-start(bf16[256,512]{1,0:T(8,128)(2,1)S(1)} %shard_map.268), channel_id=1, source_target_pairs={{0,3},{1,2},{2,1},{3,0},{4,7},{5,6},{6,5},{7,4},{8,11},{9,10},{10,... | collective-permute-start | bytes 786440 | tf_op jit(solution)/shard_map/ppermute | solution.py:77
  104.4 1.5 collective-permute-start.6
  106.5 4.6 %collective-permute-start.9 = (f32[8,512]{1,0:T(8,128)S(1)}, f32[8,512]{1,0:T(8,128)S(1)}, u32[]{:S(2)}, u32[]{:S(2)}) collective-permute-start(f32[8,512]{1,0:T(8,128)S(1)} %add.80), channel_id=1, source_target_pairs={{0,24},{1,25},{2,26},{3,27},{4,28},{5,29},{6,30},{7,31},{8,16},{9,... | collective-permute-start | bytes 49160 | tf_op jit(solution)/shard_map/ppermute | solution.py:34
  108.0 3.7 collective-permute-start.8
  109.5 3.7 collective-permute-start.7
  113.2 6.9 %collective-permute-start.12 = (f32[8,512]{1,0:T(8,128)S(1)}, f32[8,512]{1,0:T(8,128)S(1)}, u32[]{:S(2)}, u32[]{:S(2)}) collective-permute-start(f32[8,512]{1,0:T(8,128)S(1)} %add_add_fusion.3), channel_id=1, source_target_pairs={{0,3},{1,2},{2,1},{3,0},{4,7},{5,6},{6,5},{7,4},{8,11},{9,10},{10,... | collective-permute-start | bytes 49160 | tf_op jit(solution)/shard_map/ppermute | solution.py:34
  116.6 4.6 %collective-permute-start.11 = (f32[8,512]{1,0:T(8,128)S(1)}, f32[8,512]{1,0:T(8,128)S(1)}, u32[]{:S(2)}, u32[]{:S(2)}) collective-permute-start(f32[8,512]{1,0:T(8,128)S(1)} %add_add_fusion.3), channel_id=1, source_target_pairs={{0,2},{1,3},{2,0},{3,1},{4,6},{5,7},{6,4},{7,5},{8,10},{9,11},{10,... | collective-permute-start | bytes 49160 | tf_op jit(solution)/shard_map/ppermute | solution.py:34
  118.9 3.7 collective-permute-start.10
  128.3 11.7 %collective-permute-start.13 = (bf16[256,512]{1,0:T(8,128)(2,1)}, bf16[256,512]{1,0:T(8,128)(2,1)S(1)}, u32[]{:S(2)}, u32[]{:S(2)}) collective-permute-start(bf16[256,512]{1,0:T(8,128)(2,1)} %get-tuple-element.146), channel_id=1, source_target_pairs={{0,1},{1,0},{2,3},{3,2},{4,5},{5,4},{6,7},{7,6},{8,9},{9,8},{10,11... | collective-permute-start | bytes 786440 | tf_op jit(solution)/shard_map/ppermute | solution.py:77
  128.6 20.5 %collective-permute-start.15 = (bf16[256,512]{1,0:T(8,128)(2,1)}, bf16[256,512]{1,0:T(8,128)(2,1)S(1)}, u32[]{:S(2)}, u32[]{:S(2)}) collective-permute-start(bf16[256,512]{1,0:T(8,128)(2,1)} %get-tuple-element.147), channel_id=1, source_target_pairs={{0,2},{1,3},{2,0},{3,1},{4,6},{5,7},{6,4},{7,5},{8,10},{9,11},{10,... | collective-permute-start | bytes 786440 | tf_op jit(solution)/shard_map/ppermute | solution.py:77
  130.1 21.8 %collective-permute-start.17 = (bf16[256,512]{1,0:T(8,128)(2,1)}, bf16[256,512]{1,0:T(8,128)(2,1)S(1)}, u32[]{:S(2)}, u32[]{:S(2)}) collective-permute-start(bf16[256,512]{1,0:T(8,128)(2,1)} %get-tuple-element.148), channel_id=1, source_target_pairs={{0,3},{1,2},{2,1},{3,0},{4,7},{5,6},{6,5},{7,4},{8,11},{9,10},{10,... | collective-permute-start | bytes 786440 | tf_op jit(solution)/shard_map/ppermute | solution.py:77
  144.9 16.2 %collective-permute-start.14 = (bf16[256,512]{1,0:T(8,128)(2,1)S(1)}, bf16[256,512]{1,0:T(8,128)(2,1)S(1)}, u32[]{:S(2)}, u32[]{:S(2)}) collective-permute-start(bf16[256,512]{1,0:T(8,128)(2,1)S(1)} %shard_map.273), channel_id=1, source_target_pairs={{0,1},{1,0},{2,3},{3,2},{4,5},{5,4},{6,7},{7,6},{8,9},{9,8},{10,11... | collective-permute-start | bytes 786440 | tf_op jit(solution)/shard_map/ppermute | solution.py:77
  151.9 19.5 %collective-permute-start.16 = (bf16[256,512]{1,0:T(8,128)(2,1)S(1)}, bf16[256,512]{1,0:T(8,128)(2,1)S(1)}, u32[]{:S(2)}, u32[]{:S(2)}) collective-permute-start(bf16[256,512]{1,0:T(8,128)(2,1)S(1)} %shard_map.274), channel_id=1, source_target_pairs={{0,2},{1,3},{2,0},{3,1},{4,6},{5,7},{6,4},{7,5},{8,10},{9,11},{10,... | collective-permute-start | bytes 786440 | tf_op jit(solution)/shard_map/ppermute | solution.py:77
  154.8 16.6 %collective-permute-start.18 = (bf16[256,512]{1,0:T(8,128)(2,1)S(1)}, bf16[256,512]{1,0:T(8,128)(2,1)S(1)}, u32[]{:S(2)}, u32[]{:S(2)}) collective-permute-start(bf16[256,512]{1,0:T(8,128)(2,1)S(1)} %shard_map.275), channel_id=1, source_target_pairs={{0,3},{1,2},{2,1},{3,0},{4,7},{5,6},{6,5},{7,4},{8,11},{9,10},{10,... | collective-permute-start | bytes 786440 | tf_op jit(solution)/shard_map/ppermute | solution.py:77
  178.0 39.7 %collective-permute-start.19 = (bf16[256,512]{1,0:T(8,128)(2,1)}, bf16[256,512]{1,0:T(8,128)(2,1)S(1)}, u32[]{:S(2)}, u32[]{:S(2)}) collective-permute-start(bf16[256,512]{1,0:T(8,128)(2,1)} %get-tuple-element.155), channel_id=1, source_target_pairs={{0,1},{1,0},{2,3},{3,2},{4,5},{5,4},{6,7},{7,6},{8,9},{9,8},{10,11... | collective-permute-start | bytes 786440 | tf_op jit(solution)/shard_map/ppermute | solution.py:77
  182.2 22.2 %collective-permute-start.21 = (bf16[256,512]{1,0:T(8,128)(2,1)}, bf16[256,512]{1,0:T(8,128)(2,1)S(1)}, u32[]{:S(2)}, u32[]{:S(2)}) collective-permute-start(bf16[256,512]{1,0:T(8,128)(2,1)} %get-tuple-element.159), channel_id=1, source_target_pairs={{0,2},{1,3},{2,0},{3,1},{4,6},{5,7},{6,4},{7,5},{8,10},{9,11},{10,... | collective-permute-start | bytes 786440 | tf_op jit(solution)/shard_map/ppermute | solution.py:77
  183.0 15.4 %collective-permute-start.22 = (bf16[256,512]{1,0:T(8,128)(2,1)}, bf16[256,512]{1,0:T(8,128)(2,1)S(1)}, u32[]{:S(2)}, u32[]{:S(2)}) collective-permute-start(bf16[256,512]{1,0:T(8,128)(2,1)} %get-tuple-element.161), channel_id=1, source_target_pairs={{0,3},{1,2},{2,1},{3,0},{4,7},{5,6},{6,5},{7,4},{8,11},{9,10},{10,... | collective-permute-start | bytes 786440 | tf_op jit(solution)/shard_map/ppermute | solution.py:77
  202.5 29.0 %collective-permute-start.24 = (bf16[256,512]{1,0:T(8,128)(2,1)S(1)}, bf16[256,512]{1,0:T(8,128)(2,1)S(1)}, u32[]{:S(2)}, u32[]{:S(2)}) collective-permute-start(bf16[256,512]{1,0:T(8,128)(2,1)S(1)} %get-tuple-element.173), channel_id=1, source_target_pairs={{0,3},{1,2},{2,1},{3,0},{4,7},{5,6},{6,5},{7,4},{8,11},{9,10},{10,... | collective-permute-start | bytes 786440 | tf_op jit(solution)/shard_map/ppermute | solution.py:77
  208.5 13.4 %copy-start.14 = (bf16[256,512]{1,0:T(8,128)(2,1)S(1)}, bf16[256,512]{1,0:T(8,128)(2,1)}, u32[]{:S(2)}) copy-start(bf16[256,512]{1,0:T(8,128)(2,1)} %get-tuple-element.153.grad.grads_0_) | copy-start | bytes 786436
  208.5 23.0 %collective-permute-start.23 = (bf16[256,512]{1,0:T(8,128)(2,1)S(1)}, bf16[256,512]{1,0:T(8,128)(2,1)S(1)}, u32[]{:S(2)}, u32[]{:S(2)}) collective-permute-start(bf16[256,512]{1,0:T(8,128)(2,1)S(1)} %get-tuple-element.172), channel_id=1, source_target_pairs={{0,2},{1,3},{2,0},{3,1},{4,6},{5,7},{6,4},{7,5},{8,10},{9,11},{10,... | collective-permute-start | bytes 786440 | tf_op jit(solution)/shard_map/ppermute | solution.py:77
  221.9 9.6 %collective-permute-start.20 = (bf16[256,512]{1,0:T(8,128)(2,1)S(1)}, bf16[256,512]{1,0:T(8,128)(2,1)S(1)}, u32[]{:S(2)}, u32[]{:S(2)}) collective-permute-start(bf16[256,512]{1,0:T(8,128)(2,1)S(1)} %get-tuple-element.156), channel_id=1, source_target_pairs={{0,1},{1,0},{2,3},{3,2},{4,5},{5,4},{6,7},{7,6},{8,9},{9,8},{10,11... | collective-permute-start | bytes 786440 | tf_op jit(solution)/shard_map/ppermute | solution.py:77
  239.0 1.5 collective-permute-start.25
  241.1 4.7 %collective-permute-start.28 = (f32[8,512]{1,0:T(8,128)S(1)}, f32[8,512]{1,0:T(8,128)S(1)}, u32[]{:S(2)}, u32[]{:S(2)}) collective-permute-start(f32[8,512]{1,0:T(8,128)S(1)} %add.87), channel_id=1, source_target_pairs={{0,24},{1,25},{2,26},{3,27},{4,28},{5,29},{6,30},{7,31},{8,16},{9,... | collective-permute-start | bytes 49160 | tf_op jit(solution)/shard_map/ppermute | solution.py:34
  243.1 3.7 collective-permute-start.27
  243.2 3.7 collective-permute-start.26
  246.9 5.6 %collective-permute-start.31 = (f32[8,512]{1,0:T(8,128)S(1)}, f32[8,512]{1,0:T(8,128)S(1)}, u32[]{:S(2)}, u32[]{:S(2)}) collective-permute-start(f32[8,512]{1,0:T(8,128)S(1)} %add_add_fusion.1), channel_id=1, source_target_pairs={{0,3},{1,2},{2,1},{3,0},{4,7},{5,6},{6,5},{7,4},{8,11},{9,10},{10,... | collective-permute-start | bytes 49160 | tf_op jit(solution)/shard_map/ppermute | solution.py:34
  248.8 4.6 %collective-permute-start.30 = (f32[8,512]{1,0:T(8,128)S(1)}, f32[8,512]{1,0:T(8,128)S(1)}, u32[]{:S(2)}, u32[]{:S(2)}) collective-permute-start(f32[8,512]{1,0:T(8,128)S(1)} %add_add_fusion.1), channel_id=1, source_target_pairs={{0,2},{1,3},{2,0},{3,1},{4,6},{5,7},{6,4},{7,5},{8,10},{9,11},{10,... | collective-permute-start | bytes 49160 | tf_op jit(solution)/shard_map/ppermute | solution.py:34
  248.9 4.5 %collective-permute-start.29 = (f32[8,512]{1,0:T(8,128)S(1)}, f32[8,512]{1,0:T(8,128)S(1)}, u32[]{:S(2)}, u32[]{:S(2)}) collective-permute-start(f32[8,512]{1,0:T(8,128)S(1)} %add_add_fusion.1), channel_id=1, source_target_pairs={{0,1},{1,0},{2,3},{3,2},{4,5},{5,4},{6,7},{7,6},{8,9},{9,8},{10,11... | collective-permute-start | bytes 49160 | tf_op jit(solution)/shard_map/ppermute | solution.py:34
  276.6 34.6 %collective-permute-start.32 = (bf16[256,512]{1,0:T(8,128)(2,1)}, bf16[256,512]{1,0:T(8,128)(2,1)S(1)}, u32[]{:S(2)}, u32[]{:S(2)}) collective-permute-start(bf16[256,512]{1,0:T(8,128)(2,1)} %get-tuple-element.185), channel_id=1, source_target_pairs={{0,1},{1,0},{2,3},{3,2},{4,5},{5,4},{6,7},{7,6},{8,9},{9,8},{10,11... | collective-permute-start | bytes 786440 | tf_op jit(solution)/shard_map/ppermute | solution.py:77
  278.4 25.5 %collective-permute-start.34 = (bf16[256,512]{1,0:T(8,128)(2,1)}, bf16[256,512]{1,0:T(8,128)(2,1)S(1)}, u32[]{:S(2)}, u32[]{:S(2)}) collective-permute-start(bf16[256,512]{1,0:T(8,128)(2,1)} %get-tuple-element.187), channel_id=1, source_target_pairs={{0,2},{1,3},{2,0},{3,1},{4,6},{5,7},{6,4},{7,5},{8,10},{9,11},{10,... | collective-permute-start | bytes 786440 | tf_op jit(solution)/shard_map/ppermute | solution.py:77
  279.0 19.7 %collective-permute-start.36 = (bf16[256,512]{1,0:T(8,128)(2,1)}, bf16[256,512]{1,0:T(8,128)(2,1)S(1)}, u32[]{:S(2)}, u32[]{:S(2)}) collective-permute-start(bf16[256,512]{1,0:T(8,128)(2,1)} %get-tuple-element.189), channel_id=1, source_target_pairs={{0,3},{1,2},{2,1},{3,0},{4,7},{5,6},{6,5},{7,4},{8,11},{9,10},{10,... | collective-permute-start | bytes 786440 | tf_op jit(solution)/shard_map/ppermute | solution.py:77
  292.1 23.0 %collective-permute-start.38 = (bf16[4,512,512]{2,1,0:T(8,128)(2,1)}, bf16[4,512,512]{2,1,0:T(8,128)(2,1)S(1)}, u32[]{:S(2)}, u32[]{:S(2)}) collective-permute-start(bf16[4,512,512]{2,1,0:T(8,128)(2,1)} %get-tuple-element.214), channel_id=1, source_target_pairs={{0,4},{4,0},{8,12},{12,8},{16,20},{20,16},{24,28},{28,24},{1,5},{5... | collective-permute-start | bytes 6291464 | tf_op jit(solution)/shard_map/ppermute | solution.py:1170
  302.5 15.7 %collective-permute-start.37 = (bf16[256,512]{1,0:T(8,128)(2,1)S(1)}, bf16[256,512]{1,0:T(8,128)(2,1)S(1)}, u32[]{:S(2)}, u32[]{:S(2)}) collective-permute-start(bf16[256,512]{1,0:T(8,128)(2,1)S(1)} %get-tuple-element.190), channel_id=1, source_target_pairs={{0,3},{1,2},{2,1},{3,0},{4,7},{5,6},{6,5},{7,4},{8,11},{9,10},{10,... | collective-permute-start | bytes 786440 | tf_op jit(solution)/shard_map/ppermute | solution.py:77
  307.7 20.7 %collective-permute-start.35 = (bf16[256,512]{1,0:T(8,128)(2,1)S(1)}, bf16[256,512]{1,0:T(8,128)(2,1)S(1)}, u32[]{:S(2)}, u32[]{:S(2)}) collective-permute-start(bf16[256,512]{1,0:T(8,128)(2,1)S(1)} %get-tuple-element.188), channel_id=1, source_target_pairs={{0,2},{1,3},{2,0},{3,1},{4,6},{5,7},{6,4},{7,5},{8,10},{9,11},{10,... | collective-permute-start | bytes 786440 | tf_op jit(solution)/shard_map/ppermute | solution.py:77
  315.1 13.3 %collective-permute-start.33 = (bf16[256,512]{1,0:T(8,128)(2,1)S(1)}, bf16[256,512]{1,0:T(8,128)(2,1)S(1)}, u32[]{:S(2)}, u32[]{:S(2)}) collective-permute-start(bf16[256,512]{1,0:T(8,128)(2,1)S(1)} %get-tuple-element.186), channel_id=1, source_target_pairs={{0,1},{1,0},{2,3},{3,2},{4,5},{5,4},{6,7},{7,6},{8,9},{9,8},{10,11... | collective-permute-start | bytes 786440 | tf_op jit(solution)/shard_map/ppermute | solution.py:77
  315.7 14.9 %collective-permute-start.39 = (bf16[512,512]{1,0:T(8,128)(2,1)S(1)}, bf16[512,512]{1,0:T(8,128)(2,1)S(1)}, u32[]{:S(2)}, u32[]{:S(2)}) collective-permute-start(bf16[512,512]{1,0:T(8,128)(2,1)S(1)} %get-tuple-element.216), channel_id=1, source_target_pairs={{0,8},{4,12},{8,0},{12,4},{16,24},{20,28},{24,16},{28,20},{1,9},{5... | collective-permute-start | bytes 1572872 | tf_op jit(solution)/shard_map/ppermute | solution.py:1170
  316.7 23.4 %collective-permute-start.40 = (bf16[512,512]{1,0:T(8,128)(2,1)S(1)}, bf16[512,512]{1,0:T(8,128)(2,1)S(1)}, u32[]{:S(2)}, u32[]{:S(2)}) collective-permute-start(bf16[512,512]{1,0:T(8,128)(2,1)S(1)} %get-tuple-element.217), channel_id=1, source_target_pairs={{0,16},{4,20},{8,24},{12,28},{16,0},{20,4},{24,8},{28,12},{1,17},{... | collective-permute-start | bytes 1572872 | tf_op jit(solution)/shard_map/ppermute | solution.py:1170
  318.2 23.0 %collective-permute-start.41 = (bf16[512,512]{1,0:T(8,128)(2,1)S(1)}, bf16[512,512]{1,0:T(8,128)(2,1)S(1)}, u32[]{:S(2)}, u32[]{:S(2)}) collective-permute-start(bf16[512,512]{1,0:T(8,128)(2,1)S(1)} %get-tuple-element.218), channel_id=1, source_target_pairs={{0,24},{4,28},{8,16},{12,20},{16,8},{20,12},{24,0},{28,4},{1,25},{... | collective-permute-start | bytes 1572872 | tf_op jit(solution)/shard_map/ppermute | solution.py:1170
  325.3 16.2 %copy-start.9 = (bf16[4,512,512]{2,1,0:T(8,128)(2,1)}, bf16[4,512,512]{2,1,0:T(8,128)(2,1)S(1)}, u32[]{:S(2)}) copy-start(bf16[4,512,512]{2,1,0:T(8,128)(2,1)S(1)} %get-tuple-element.236.kept) | copy-start | bytes 6291460
  328.4 13.4 %copy-start.42 = (bf16[256,512]{1,0:T(8,128)(2,1)}, bf16[256,512]{1,0:T(8,128)(2,1)S(1)}, u32[]{:S(2)}) copy-start(bf16[256,512]{1,0:T(8,128)(2,1)S(1)} %collective-permute-done.35.blocks_2_) | copy-start | bytes 786436
  328.4 14.5 %copy-start.43 = (bf16[256,512]{1,0:T(8,128)(2,1)}, bf16[256,512]{1,0:T(8,128)(2,1)S(1)}, u32[]{:S(2)}) copy-start(bf16[256,512]{1,0:T(8,128)(2,1)S(1)} %collective-permute-done.33.blocks_1_) | copy-start | bytes 786436
  328.4 37.5 %collective-permute-start.42 = (bf16[4,512,512]{2,1,0:T(8,128)(2,1)S(1)}, bf16[4,512,512]{2,1,0:T(8,128)(2,1)}, u32[]{:S(2)}, u32[]{:S(2)}) collective-permute-start(bf16[4,512,512]{2,1,0:T(8,128)(2,1)S(1)} %get-tuple-element.238), channel_id=1, source_target_pairs={{0,4},{4,0},{8,12},{12,8},{16,20},{20,16},{24,28},{28,24},{1,5},{5... | collective-permute-start | bytes 6291464 | tf_op jit(solution)/shard_map/ppermute | solution.py:1170
  342.9 16.8 %all-to-all-start.2 = ((bf16[4,16,4096]{2,1,0:T(8,128)(2,1)}), bf16[4,16,4096]{2,1,0:T(8,128)(2,1)S(1)}, u32[]{:S(2)}, u32[]{:S(2)}) async-start(bf16[4,16,4096]{2,1,0:T(8,128)(2,1)} %reshape.103), calls=%async_computation.3 | async-start | bytes 1048576 | tf_op jit(solution)/shard_map/all_to_all | solution.py:1213
  362.5 28.4 %all-to-all-start.3 = ((bf16[32,32,512]{2,1,0:T(8,128)(2,1)}), bf16[32,32,512]{2,1,0:T(8,128)(2,1)}, u32[]{:S(2)}, u32[]{:S(2)}) async-start(bf16[32,32,512]{2,1,0:T(8,128)(2,1)} %copy.85), calls=%async_computation.4 | async-start | bytes 2097152 | tf_op jit(solution)/shard_map/all_to_all | solution.py:1275
  370.3 31.6 %collective-permute-start.43 = (bf16[512,512]{1,0:T(8,128)(2,1)S(1)}, bf16[512,512]{1,0:T(8,128)(2,1)S(1)}, u32[]{:S(2)}, u32[]{:S(2)}) collective-permute-start(bf16[512,512]{1,0:T(8,128)(2,1)S(1)} %get-tuple-element.240), channel_id=1, source_target_pairs={{0,8},{4,12},{8,0},{12,4},{16,24},{20,28},{24,16},{28,20},{1,9},{5... | collective-permute-start | bytes 1572872 | tf_op jit(solution)/shard_map/ppermute | solution.py:1170
  371.9 30.0 %collective-permute-start.44 = (bf16[512,512]{1,0:T(8,128)(2,1)S(1)}, bf16[512,512]{1,0:T(8,128)(2,1)S(1)}, u32[]{:S(2)}, u32[]{:S(2)}) collective-permute-start(bf16[512,512]{1,0:T(8,128)(2,1)S(1)} %get-tuple-element.241), channel_id=1, source_target_pairs={{0,16},{4,20},{8,24},{12,28},{16,0},{20,4},{24,8},{28,12},{1,17},{... | collective-permute-start | bytes 1572872 | tf_op jit(solution)/shard_map/ppermute | solution.py:1170
  373.4 29.7 %collective-permute-start.45 = (bf16[512,512]{1,0:T(8,128)(2,1)S(1)}, bf16[512,512]{1,0:T(8,128)(2,1)S(1)}, u32[]{:S(2)}, u32[]{:S(2)}) collective-permute-start(bf16[512,512]{1,0:T(8,128)(2,1)S(1)} %get-tuple-element.242), channel_id=1, source_target_pairs={{0,24},{4,28},{8,16},{12,20},{16,8},{20,12},{24,0},{28,4},{1,25},{... | collective-permute-start | bytes 1572872 | tf_op jit(solution)/shard_map/ppermute | solution.py:1170
  (42 other events, 144.9 us)
Sparse Core Ops, SparseCore 0:
  10.5 40.8 all-gather.7
  53.3 34.5 all-gather.5
  89.7 36.7 all-gather.9
  251.5 50.6 reduce-scatter.1

commit v5 on v4

--- a/solution.py
+++ b/solution.py
@@ -49,14 +49,21 @@
     return [low, high, low | high]
 
 
-def sum_everywhere(values):
-    for bits in device_groups():
+def terms_everywhere(values):
+    groups = device_groups()
+    for bits in groups[:-1]:
         arrived = [exchange(values, AXES, mask) for mask in masks_of(bits)]
         if len(arrived) == 1:
             values = values + arrived[0]
         else:
             values = (values + arrived[0]) + (arrived[1] + arrived[2])
-    return values
+    return [values] + [exchange(values, AXES, mask) for mask in masks_of(groups[-1])]
+
+
+def total_of(terms):
+    if len(terms) == 2:
+        return terms[0][...] + terms[1][...]
+    return (terms[0][...] + terms[1][...]) + (terms[2][...] + terms[3][...])
 
 
 def gather_everywhere(values):
@@ -88,8 +95,9 @@
 
 
 class Stream:
-    def __init__(self, arrivals, results):
+    def __init__(self, arrivals, results, spare):
         self.arrivals, self.results = arrivals, results
+        self.spare, self.spared = spare, 0
         self.waited, self.sent = set(), []
         self.begin(0)
         self.begin(1)
@@ -106,9 +114,19 @@
 
     def flush(self, *refs):
         for ref in refs:
-            copy = self.results[id(ref)]
-            copy.start()
-            self.sent.append(copy)
+            held, target, sem = self.results[id(ref)]
+            self.send(held, target, sem)
+
+    def flush_rows(self, ref, start, size):
+        held, target, _ = self.results[id(ref)]
+        rows = pl.ds(start, size)
+        self.send(held.at[:, rows], target.at[:, rows], self.spare.at[self.spared])
+        self.spared += 1
+
+    def send(self, held, target, sem):
+        copy = pltpu.make_async_copy(held, target, sem)
+        copy.start()
+        self.sent.append(copy)
 
     def finish(self):
         for copy in self.sent:
@@ -147,12 +165,12 @@
         out_leaves, out_tree = jax.tree.flatten(outs)
         buffers += [pltpu.VMEM(leaf.shape, leaf.dtype) for leaf in out_leaves]
         own_scratch, total = len(scratch), len(buffers)
-        scratch = scratch + buffers + [pltpu.SemaphoreType.DMA((total,))]
+        scratch = scratch + buffers + [pltpu.SemaphoreType.DMA((4,)), pltpu.SemaphoreType.DMA((total,))]
 
         def wrapped(*refs):
             refs = list(refs)
             ins, out_refs, rest = refs[: len(args)], refs[len(args) : len(args) + out_count], refs[len(args) + out_count :]
-            own, held, sems = rest[:own_scratch], rest[own_scratch:-1], rest[-1]
+            own, held, spare, sems = rest[:own_scratch], rest[own_scratch:-2], rest[-2], rest[-1]
             arrivals, given, used = {}, [], 0
             for ref, part, stage in zip(ins, columns, stages):
                 if stage is None:
@@ -170,10 +188,10 @@
                 given.append(jax.tree.unflatten(tree, landed))
             results, places = {}, []
             for ref in jax.tree.leaves(out_refs):
-                results[id(held[used])] = pltpu.make_async_copy(held[used], ref, sems.at[used])
+                results[id(held[used])] = (held[used], ref, sems.at[used])
                 places.append(held[used])
                 used += 1
-            stream = Stream(arrivals, results)
+            stream = Stream(arrivals, results, spare)
             given_outs = jax.tree.unflatten(out_tree, places)
             given_outs = list(given_outs) if isinstance(given_outs, (tuple, list)) else [given_outs]
             body(stream, *given, *given_outs, *own)
@@ -468,15 +486,16 @@
 
 def dense_grad_kernel(
     experts, stream, ua, dproj, attended, dat, uc, dgin, swish, dco, gate_grad1, gate1, col1, gate_grad2, gate2, col2,
-    dp_index, probs, routers, pre, embedded, frames, kept, moved, dz, router_terms, logits, term,
+    dp_index, probs, routers, pre, embedded, frames, kept, moved, dz, router_terms, logits, term, turned,
 ):
     width = ua.shape[1]
     count = 2 * kept.shape[0]
     part_rows = width // count
 
     def place(left, right, tile):
+        turned[...] = left[...].T
         for column in range(right.shape[1] // width):
-            term[...] = dot_tn(left[...], right[:, pl.ds(column * width, width)]).astype(BF16)
+            term[...] = dot(turned[...], right[:, pl.ds(column * width, width)]).astype(BF16)
             for number in range(count):
                 source = pl.multiple_of((dp_index[0] ^ number) * part_rows, part_rows)
                 target = moved if number % 2 else kept
@@ -487,6 +506,8 @@
     stream.ready(1)
     place(ua, dproj, 0)
     place(attended, dat, 3)
+    for ref in (kept, moved):
+        stream.flush_rows(ref, 0, 4 * part_rows)
     stream.ready(2)
     for part in chunks(rows, 256):
         lane = iota((256, LANES), 1)
@@ -497,19 +518,23 @@
             scale = gate_grad[part, :] * gate[part, :]
             grad = jnp.where(inside, scale * (hot - probs[part, :]), grad)
         logits[part, :] = grad
-        demb = lax.dot_general(
-            grad, routers[...], (((1,), (1,)), ((), ())), precision=HIGHEST, preferred_element_type=F32
-        )
+        demb = dot_nt(grad.astype(BF16), routers[...].astype(BF16))
         held = pre[part, :]
         dz[part, :] = (demb * slope(held, sigmoid(held))).astype(BF16)
-    router_terms[...] = lax.dot_general(
-        logits[...], embedded[...], (((0,), (0,)), ((), ())), precision=HIGHEST, preferred_element_type=F32
-    )
+    router_terms[...] = dot(logits[...].T.astype(BF16), embedded[...].astype(BF16))
     stream.flush(dz, router_terms)
     place(uc, dgin, 4)
     place(swish, dco, 6)
     place(frames, dz, 7)
-    stream.flush(kept, moved)
+    for ref in (kept, moved):
+        stream.flush_rows(ref, 4 * part_rows, 4 * part_rows)
+
+
+def sum_kernel(parts, out):
+    total = parts[0][...].astype(F32)
+    for part in parts[1:]:
+        total = total + part[...].astype(F32)
+    out[...] = total.astype(BF16)
 
 
 def pair_kernel(kept, moved, *outs):
@@ -697,9 +722,9 @@
     return mean, lax.rsqrt(variance + EPSILON)
 
 
-def middle_kernel(stream, frame_count, depth, moments, x2, table, conv_out, slot_row, swish_out, x3_out, sent, normed):
+def middle_kernel(frame_count, depth, terms, x2, table, conv_out, slot_row, swish_out, x3_out, moments, sent, normed):
     rows, width = depth.shape
-    stream.ready(0)
+    moments[...] = total_of(terms)
     mean, scale = batch_terms(moments, frame_count)
     for part in chunks(rows, 256):
         bn = (depth[part, :] - mean) * scale * table[pl.ds(5, 1), :] + table[pl.ds(21, 1), :]
@@ -709,18 +734,15 @@
         x3_out[part, :] = x3
         hat, _ = normalize(x3)
         normed[part, :] = (hat * table[pl.ds(3, 1), :]).astype(BF16)
-    stream.flush(swish_out, x3_out)
     scatter_to(slot_row, normed[...], sent)
-    stream.flush(*sent)
 
 
 def turn_kernel(
-    stream, x3, blocks, slot_col, slot_row, gate, table, cotangent, seg_col,
+    x3, blocks, slot_col, slot_row, gate, table, cotangent, seg_col,
     block_out, dx4_out, gate_grad, gain_out, sent, grads,
 ):
     rows, width = x3.shape
     gain = table[pl.ds(4, 1), :]
-    stream.ready(0)
     gain_sum = jnp.zeros((1, width), F32)
     for part in chunks(rows, 256):
         found = gathered(slot_col, blocks, part)
@@ -736,18 +758,15 @@
         gate_grad[part, :] = 0.5 * jnp.sum(found * dx4, 1, keepdims=True)
         grads[part, :] = (half * dx4).astype(BF16)
     gain_out[...] = gain_sum
-    stream.flush(block_out, dx4_out, gate_grad, gain_out)
     scatter_to(slot_row, grads[...], sent)
-    stream.flush(*sent)
 
 
 def conv_back_kernel(
-    stream, frame_count, dx4, blocks, slot_col, x3, table, conv_out, depth, moments,
+    frame_count, dx4, blocks, slot_col, x3, table, conv_out, depth, moments,
     dx3_out, dco_out, dh_out, sums,
 ):
     rows, width = x3.shape
     mean, scale = batch_terms(moments, frame_count)
-    stream.ready(0)
     total = jnp.zeros((1, width), F32)
     moment = jnp.zeros((1, width), F32)
     shift = jnp.zeros((1, width), F32)
@@ -774,18 +793,18 @@
     for number, row in enumerate((total, moment, shift, gain5, gain3)):
         sums[pl.ds(number, 1), :] = row
     sums[pl.ds(5, 3), :] = jnp.zeros((3, width), F32)
-    stream.flush(dx3_out, dco_out, dh_out, sums)
 
 
 def back_kernel(
-    stream, frame_count, dh, depth, moments, sums, dx3, gin, x2, x1, table, conv_in, attn_out, attn_in, qkv, lse,
+    stream, frame_count, dh, depth, moments, sum_terms, dx3, gin, x2, x1, table, conv_in, attn_out, attn_in, qkv, lse,
     cosine, sine, seg_col, seg_row, taps, expert, gate, slot_row,
     dgin_out, dat_out, dproj_out, dx1_out, gate_grad, terms, sent,
     padded, glu, grad_rows, dk, dv, rows_sent, flipped,
 ):
     rows, width = dh.shape
     mean, scale = batch_terms(moments, frame_count)
-    total, moment = sums[pl.ds(0, 1), :], sums[pl.ds(1, 1), :]
+    sums = total_of(sum_terms)
+    total, moment = sums[0:1], sums[1:2]
     var_grad = -0.5 * moment * scale * scale * scale
     mean_grad = -scale * total - 2.0 * mean * var_grad
     edge = jnp.zeros((8, width), F32)
@@ -1062,19 +1081,18 @@
         cost=20,
         scratch=[padded, pltpu.VMEM((width, rows), BF16)],
     )
-    moments = sum_everywhere(moments)
-    swish, x3, sent = call(
+    moment_terms = terms_everywhere(moments)
+    swish, x3, moments, sent = call(
         middle_kernel,
-        (low, wide, [block] * peers),
+        (low, wide, sums_shape, [block] * peers),
         frame_count,
         depth,
-        moments,
+        moment_terms,
         x2,
         table,
-        Columns(dense, 6 * width, width),
+        dense,
         slot_row2,
-        specs=[SMEM] + [None] * 6,
-        stages=[None, 0, None, 0, None, 0, None],
+        specs=[SMEM] + [None] * 4 + [conv_out_spec, None],
         scratch=[pltpu.VMEM((rows, width), BF16)],
     )
 
@@ -1093,7 +1111,6 @@
         table,
         cotangent,
         seg_col,
-        stages=[0, 0, None, None, None, None, 0, None],
         scratch=[pltpu.VMEM((rows, width), BF16)],
     )
     second_grads = swap_blocks(sent)
@@ -1118,13 +1135,12 @@
         slot_col2,
         x3,
         table,
-        Columns(dense, 6 * width, width),
+        dense,
         depth,
         moments,
-        specs=[SMEM] + [None] * 8,
-        stages=[None, 0, 0, None, 0, None, 0, 0, None],
-    )
-    all_sums = sum_everywhere(sums)
+        specs=[SMEM] + [None] * 5 + [conv_out_spec] + [None] * 2,
+    )
+    all_sums = terms_everywhere(sums)
     dgin, dat, dproj, dx1, gate_grad1, terms, sent = call(
         back_kernel,
         (
@@ -1196,7 +1212,7 @@
         specs=[None] * 14 + [SMEM] + [None] * 5,
         stages=[0, 0, 1, 1, 2, 2, 2, 2] + [None] * 8 + [None, 2, 2, 2],
         cost=1,
-        scratch=[pltpu.VMEM((rows, LANES), F32), pltpu.VMEM((width, width), BF16)],
+        scratch=[pltpu.VMEM((rows, LANES), F32), pltpu.VMEM((width, width), BF16), pltpu.VMEM((width, rows), BF16)],
     )
     pairs = call(
         pair_kernel,
@@ -1206,21 +1222,14 @@
         vmem=16,
         cost=10,
     )
-    dense_own = pairs[0].astype(F32)
-    for pair, mask in zip(pairs[1:], chip_masks()[1:]):
-        dense_own = dense_own + dp_exchange(pair, mask).astype(F32)
-    dense_own = dense_own.astype(BF16).reshape(8, peers, slice_width, width).transpose(1, 2, 0, 3)
-    dense_own = lax.all_to_all(
-        dense_own.reshape(peers, slice_width, 8 * width), "expert", split_axis=0, concat_axis=0, tiled=True
-    )
-    owned = [shaped((slice_width, count * width), F32) for count in (3, 1, 2, 1)]
-    *dense_own, embed_own = call(
-        dense_out_kernel,
-        (*owned, shaped((slice_width, width), BF16)),
-        dense_own,
+    dense_own = call(
+        sum_kernel,
+        shaped(pairs[0].shape, BF16),
+        [dp_exchange(pair, mask) if mask else pair for pair, mask in zip(pairs, chip_masks())],
         vmem=8,
-        cost=10,
-    )
+        cost=60,
+    )
+    dense_own = dense_own.reshape(8, peers, slice_width, width).transpose(1, 2, 0, 3)
     backs = [
         expert_backward(block, grad, gain(0), first_weights, hidden, True)
         for block, grad in zip(first_blocks, first_grads)
@@ -1239,9 +1248,21 @@
         vmem=16,
         cost=20,
     )
+    dense_own = after(dense_own, *pairs)
+    dense_own = lax.all_to_all(
+        dense_own.reshape(peers, slice_width, 8 * width), "expert", split_axis=0, concat_axis=0, tiled=True
+    )
     first_parts = [
         dp_exchange(pair, mask) if mask else pair for pair, mask in zip(pairs, chip_masks())
     ]
+    owned = [shaped((slice_width, count * width), F32) for count in (3, 1, 2, 1)]
+    *dense_own, embed_own = call(
+        dense_out_kernel,
+        (*owned, shaped((slice_width, width), BF16)),
+        dense_own,
+        vmem=8,
+        cost=10,
+    )
     in_grad, out_grad = call(
         experts_out_kernel,
         (shaped((layers, 1, width // dp_count, hidden), F32), shaped((layers, 1, hidden // dp_count, width), F32)),
@@ -1264,20 +1285,15 @@
         ],
         0,
     )
-    small_terms = jnp.pad(small_terms.T, ((0, 0), (0, -small_width % 32)))
-    lanes = small_terms.shape[1] * slice_width
-    small_terms = jnp.pad(small_terms.reshape(-1, lanes), ((0, 0), (0, -lanes % width)))
+    small_terms = small_terms.T
     high = lax.reduce_precision(small_terms, 8, 7)
-    split = jnp.stack([high, small_terms - high], 1).astype(BF16)
-    split = split.reshape(split.shape[0], -1, width)
-    split = jnp.pad(split, ((0, 0), (0, -split.shape[1] % 16), (0, 0)))
-    mixed = jnp.concatenate([split, jnp.broadcast_to(embed_own[None], (split.shape[0],) + embed_own.shape)], 1)
+    split = jnp.concatenate([high, small_terms - high], 1).astype(BF16)
+    split = jnp.pad(split, ((0, 0), (0, LANES - 2 * small_width))).reshape(-1, slice_width, LANES)
+    mixed = jnp.concatenate([jnp.broadcast_to(embed_own[None], (split.shape[0],) + embed_own.shape), split], 2)
     mixed = lax.all_to_all(mixed, AXES, split_axis=0, concat_axis=0, tiled=True)
-    embed_total = mixed[:, split.shape[1] :].reshape(width, width).astype(F32)
-    small_sums = jnp.sum(mixed[:, : split.shape[1]].astype(F32), 0)
-    count = -(-lanes // width)
-    small_sums = (small_sums[:count] + small_sums[count : 2 * count]).reshape(-1)[:lanes]
-    small_sums = small_sums.reshape(slice_width, -1).T
+    embed_total = mixed[:, :, :width].reshape(width, width).astype(F32)
+    small_sums = jnp.sum(mixed[:, :, width:].astype(F32), 0)
+    small_sums = (small_sums[:, :small_width] + small_sums[:, small_width : 2 * small_width]).T
 
     frames_grad = call(
         final_kernel,

time: 421 us -> 410 us (0.974)
  Pallas kernels: 151 us -> 145 us
    pallas_call x31 -> x32, Pallas kernels: 151 us -> 145 us  [call(): pl.pallas_call(wrapped, out_shape=outs, in_specs=specs, out_specs=out_spe...]
    unnamed x119 -> x129, local copies, waits for them, and re-layouts: 26 us -> 24.5 us
  transfers between devices with their start and end apart: 53 -> 53, of which waited for: 26 -> 26; matrix products, arithmetic and copies ran while one was open for 6% -> 5% of each run, Pallas kernels for 33% -> 33%
where the time goes in v5:
time: 410 us; the launch traced here: 402 us
  Pallas kernels  145 us (35%)
  waiting for transfers between devices  97.4 us (24%)
  starting transfers between devices  81.3 us (20%)
  local copies, waits for them, and re-layouts  34.2 us (8%)
  blocking collectives  19.3 us (5%)
  between operations  16.2 us (4%)
  other arithmetic  8.35 us (2%)
    pallas_call x32, Pallas kernels, call(): pl.pallas_call(wrapped, out_shape=outs, in_specs=specs, out_specs=out_spe...  145 us
    ppermute x24, starting transfers between devices, swap_blocks(): lax.ppermute(blocks[k], 'expert', [(i, i ^ k) for i in range(total)])  45.7 us
    ppermute x24, waiting for transfers between devices, swap_blocks(): lax.ppermute(blocks[k], 'expert', [(i, i ^ k) for i in range(total)])  32.1 us
    unnamed x129, local copies, waits for them, and re-layouts  24.5 us
    all_to_all x1, blocking collectives, shards(): lax.all_to_all(jnp.broadcast_to(dense[None], (peers,) + dense.shape), 'ex...  19.3 us
    ppermute x14, starting transfers between devices, exchange(): return lax.ppermute(values, axes, [(i, i ^ mask) for i in range(total)])  17.4 us
    ppermute x8, waiting for transfers between devices, dp_exchange(): return lax.ppermute(values, 'dp', [(i, i ^ mask) for i in range(dp_count)])  17.1 us
    all_to_all x1, waiting for transfers between devices, shards(): mixed = lax.all_to_all(mixed, AXES, split_axis=0, concat_axis=0, tiled=True)  13.4 us
  transfers between devices with their start and end apart: 53, of which 26 were waited for; matrix products, arithmetic and copies ran while one was open for 5% of the time, Pallas kernels for 33%

profile of v5, /device:TPU:0, one launch (start us, length us, event | category | flops | bytes accessed | tf_op | source)
XLA Modules:
  0.0 402.2 jit_solution(11800596505795975046)
XLA Ops:
  10.5 19.3 %all_to_all.20 = bf16[4,16,3584]{2,1,0:T(8,128)(2,1)} all-to-all(bf16[4,16,3584]{2,1,0:T(8,128)(2,1)S(1)} %broadcast_in_dim.39), channel_id=1, replica_groups=mesh['dp'=8,'expert'=4] {'expert'}, dimensions={0} | all-to-all | bytes 917504 | tf_op jit(solution)/shard_map/all_to_all | solution.py:998
  32.1 3.2 shard_map.264
  36.0 3.7 all-to-all-start
  39.8 1.8 collective-permute-start
  41.6 2.4 collective-permute-start.2
  46.2 2.2 all-to-all-done
  49.3 4.6 %shard_map.269 = (f32[512,512]{1,0:T(8,128)}, f32[512,512]{1,0:T(8,128)}, f32[512,128]{1,0:T(8,128)}, f32[512,1]{1,0:T(8,128)}, f32[512,1]{1,0:T(8,128)}, /*inde...) custom-call(s32[3]{0:T(128)} %slice_bitcast_fusion.2.ends, bf16[512,512]{1,0:T(8,128)(2,1)} %frames.5, ...), custom_call_target="tpu_custom_call" | custom-call | flops 5765000192 | tf_op jit(solution)/shard_map/pallas_call | solution.py:201
  55.1 1.8 fusion
  57.0 2.2 copy-done.1
  59.1 3.0 shard_map.266
  62.2 3.0 shard_map.267
  65.3 2.1 collective-permute-start.3
  67.3 3.0 shard_map.268
  70.3 2.4 collective-permute-start.5
  72.7 3.2 shard_map.265.refs_1__0_
  76.6 11.2 %all-gather.6.cloned.1.call-done.refs_5_.refs_6_.refs_7_.conv_out.refs_10_.refs_11_.refs_12_ = bf16[512,3584]{1,0:T(8,128)(2,1)} async-done(((bf16[64,3584]{1,0:T(8,128)(2,1)}), bf16[512,3584]{1,0:T(8,128)(2,1)}) %all-gather.6.cloned.1.call-update) | async-done | bytes 3670032 | tf_op jit(solution)/shard_map/all_gather | solution.py:1001
  88.7 15.7 %shard_map.270 = (bf16[512,512]{1,0:T(8,128)(2,1)}, f32[512,512]{1,0:T(8,128)}, f32[512,512]{1,0:T(8,128)}, bf16[512,512]{1,0:T(8,128)(2,1)}, bf16[512,1536]{1,0...) custom-call(bf16[512,512]{1,0:T(8,128)(2,1)} %frames.5, ...), custom_call_target="tpu_custom_call" | custom-call | flops 23060000768 | tf_op jit(solution)/shard_map/pallas_call | solution.py:201
  113.3 3.4 collective-permute-start.12
  116.7 2.2 collective-permute-start.11
  123.3 3.9 shard_map.271
  129.0 2.6 collective-permute-start.17
  131.6 7.2 %collective-permute-done.13.block = bf16[256,512]{1,0:T(8,128)(2,1)S(1)} collective-permute-done((bf16[256,512]{1,0:T(8,128)(2,1)}, bf16[256,512]{1,0:T(8,128)(2,1)S(1)}, u32[]{:S(2)}, u32[]{:S(2)}) %collective-permute-start.13) | collective-permute-done | bytes 262176 | tf_op jit(solution)/shard_map/ppermute | solution.py:84
  138.7 2.2 copy-done.3
  140.9 2.8 shard_map.273
  143.8 4.2 %collective-permute-done.15.block = bf16[256,512]{1,0:T(8,128)(2,1)S(1)} collective-permute-done((bf16[256,512]{1,0:T(8,128)(2,1)}, bf16[256,512]{1,0:T(8,128)(2,1)S(1)}, u32[]{:S(2)}, u32[]{:S(2)}) %collective-permute-start.15) | collective-permute-done | bytes 262176 | tf_op jit(solution)/shard_map/ppermute | solution.py:84
  148.0 2.8 shard_map.274
  150.9 2.8 shard_map.275
  153.7 2.7 collective-permute-start.18
  156.3 2.8 shard_map.272.blocks_0_
  159.8 10.3 %collective-permute-done.16.blocks_2_ = bf16[256,512]{1,0:T(8,128)(2,1)S(1)} collective-permute-done((bf16[256,512]{1,0:T(8,128)(2,1)S(1)}, bf16[256,512]{1,0:T(8,128)(2,1)S(1)}, u32[]{:S(2)}, u32[]{:S(2)}) %collective-permute-start.16) | collective-permute-done | bytes 262176 | tf_op jit(solution)/shard_map/ppermute | solution.py:84
  170.9 4.9 %shard_map.276 = (bf16[512,512]{1,0:T(8,128)(2,1)}, f32[512,512]{1,0:T(8,128)}, f32[512,1]{1,0:T(8,128)}, f32[1,512]{1,0:T(1,128)}, bf16[256,512]{1,0:T(8,128)(2...) custom-call(f32[512,512]{1,0:T(8,128)} %get-tuple-element.146.x3, ...), custom_call_target="tpu_custom_call" | custom-call | flops 5765000192 | tf_op jit(solution)/shard_map/pallas_call | solution.py:201
  175.8 4.1 %collective-permute-start.19 = (bf16[256,512]{1,0:T(8,128)(2,1)}, bf16[256,512]{1,0:T(8,128)(2,1)S(1)}, u32[]{:S(2)}, u32[]{:S(2)}) collective-permute-start(bf16[256,512]{1,0:T(8,128)(2,1)} %get-tuple-element.157), channel_id=1, source_target_pairs={{0,1},{1,0},{2,3},{3,2},{4,5},{5,4},{6,7},{7,6},{8,9},{9,8},{10,11... | collective-permute-start | bytes 786440 | tf_op jit(solution)/shard_map/ppermute | solution.py:84
  182.3 2.2 copy-done.4
  185.4 4.1 %shard_map.277 = (bf16[256,512]{1,0:T(8,128)(2,1)S(1)}, bf16[256,2048]{1,0:T(8,128)(2,1)S(1)}, bf16[256,2048]{1,0:T(8,128)(2,1)S(1)}, bf16[256,512]{1,0:T(8,128)(2,1)S(1)}, f32[1,512]{1,0:T(1,128)}) custom-call(bf16[256,512]{1,0:T(8,128)(2,1)S(1)} %copy-done.10, bf16[256,512]{1,0:T(8,128)(2,1)S(1)} %copy-done.11, f32[1,512]{1,0:T(1,128)S(1)} %get-tuple-element.281.gain, ...), custom_call_target="tpu_custom_call" | custom-call | flops 23060000768 | tf_op jit(solution)/shard_map/pallas_call | solution.py:201
  189.6 6.5 %collective-permute-done.22.grad.grads_3_ = bf16[256,512]{1,0:T(8,128)(2,1)S(1)} collective-permute-done((bf16[256,512]{1,0:T(8,128)(2,1)}, bf16[256,512]{1,0:T(8,128)(2,1)S(1)}, u32[]{:S(2)}, u32[]{:S(2)}) %collective-permute-start.22) | collective-permute-done | bytes 262176 | tf_op jit(solution)/shard_map/ppermute | solution.py:84
  196.0 4.1 %shard_map.280 = (bf16[256,512]{1,0:T(8,128)(2,1)S(1)}, bf16[256,2048]{1,0:T(8,128)(2,1)S(1)}, bf16[256,2048]{1,0:T(8,128)(2,1)S(1)}, bf16[256,512]{1,0:T(8,128)(2,1)S(1)}, f32[1,512]{1,0:T(1,128)}) custom-call(bf16[256,512]{1,0:T(8,128)(2,1)S(1)} %collective-permute-done.17.block, bf16[256,512]{1,0:T(8,128)(2,1)S(1)} %collective-permute-done.22.grad.grads_3_, ...), custom_call_target="tpu_custom_call" | custom-call | flops 23060000768 | tf_op jit(solution)/shard_map/pallas_call | solution.py:201
  200.1 2.0 collective-permute-start.24
  202.1 4.1 %shard_map.279 = (bf16[256,512]{1,0:T(8,128)(2,1)S(1)}, bf16[256,2048]{1,0:T(8,128)(2,1)S(1)}, bf16[256,2048]{1,0:T(8,128)(2,1)S(1)}, bf16[256,512]{1,0:T(8,128)(2,1)S(1)}, f32[1,512]{1,0:T(1,128)}) custom-call(bf16[256,512]{1,0:T(8,128)(2,1)S(1)} %collective-permute-done.15.block, bf16[256,512]{1,0:T(8,128)(2,1)S(1)} %collective-permute-done.21.grad.grads_2_, ...), custom_call_target="tpu_custom_call" | custom-call | flops 23060000768 | tf_op jit(solution)/shard_map/pallas_call | solution.py:201
  206.2 9.3 %collective-permute-start.23 = (bf16[256,512]{1,0:T(8,128)(2,1)S(1)}, bf16[256,512]{1,0:T(8,128)(2,1)S(1)}, u32[]{:S(2)}, u32[]{:S(2)}) collective-permute-start(bf16[256,512]{1,0:T(8,128)(2,1)S(1)} %get-tuple-element.174), channel_id=1, source_target_pairs={{0,2},{1,3},{2,0},{3,1},{4,6},{5,7},{6,4},{7,5},{8,10},{9,11},{10,... | collective-permute-start | bytes 786440 | tf_op jit(solution)/shard_map/ppermute | solution.py:84
  215.5 4.1 %shard_map.278 = (bf16[256,512]{1,0:T(8,128)(2,1)S(1)}, bf16[256,2048]{1,0:T(8,128)(2,1)S(1)}, bf16[256,2048]{1,0:T(8,128)(2,1)S(1)}, bf16[256,512]{1,0:T(8,128)(2,1)S(1)}, f32[1,512]{1,0:T(1,128)}) custom-call(bf16[256,512]{1,0:T(8,128)(2,1)S(1)} %collective-permute-done.13.block, bf16[256,512]{1,0:T(8,128)(2,1)S(1)} %collective-permute-done.19.grad.grads_1_, ...), custom_call_target="tpu_custom_call" | custom-call | flops 23060000768 | tf_op jit(solution)/shard_map/pallas_call | solution.py:201
  219.6 6.0 %shard_map.281 = bf16[8,512,512]{2,1,0:T(8,128)(2,1)S(1)} custom-call(s32[1]{0:T(128)} %bitcast.20.dp_index.refs_14_, bf16[256,512]{1,0:T(8,128)(2,1)S(1)} %get-tuple-element.159.inputs_0_, bf16[256,512]{1,0:T(8,128)(2,1)S(1)} %get-tuple-element.160.inputs_1_, bf16[256,512]{1,0:T(8,128)(2,1)S(1)} %get-tuple-element.162.inputs_2_, ...), custom_call_target="tpu_custom_call" | custom-call | flops 9223999488 | tf_op jit(solution)/shard_map/pallas_call | solution.py:201
  225.6 2.0 copy-done
  230.3 5.6 %shard_map.282 = (f32[512,512]{1,0:T(8,128)}, bf16[512,512]{1,0:T(8,128)(2,1)}, f32[512,512]{1,0:T(8,128)}, f32[8,512]{1,0:T(8,128)}) custom-call(f32[1]{0:T(128)} %bitcast.frame_count.refs_0_, f32[512,512]{1,0:T(8,128)} %get-tuple-element.154.dx4, bf16[256,512]{1,0:T(8,128)(2,1)} %copy-done.9, bf16[256,512]{1,0:T(8,128)(2,1)} %copy-done.46, ...), custom_call_target="tpu_custom_call" | custom-call | flops 5765000192 | tf_op jit(solution)/shard_map/pallas_call | solution.py:201
  245.5 2.5 collective-permute-start.29
  250.4 22.7 %shard_map.283 = (bf16[512,1024]{1,0:T(8,128)(2,1)}, bf16[512,512]{1,0:T(8,128)(2,1)}, bf16[512,1536]{1,0:T(8,128)(2,1)}, f32[512,512]{1,0:T(8,128)}, f32[512,1]...) custom-call(f32[1]{0:T(128)} %bitcast.frame_count.refs_0_, ...), custom_call_target="tpu_custom_call" | custom-call | flops 34589999104 | tf_op jit(solution)/shard_map/pallas_call | solution.py:201
  273.1 2.1 collective-permute-start.32
  275.7 1.9 collective-permute-start.36
  277.6 9.2 %shard_map.288 = (bf16[4,512,512]{2,1,0:T(8,128)(2,1)}, bf16[4,512,512]{2,1,0:T(8,128)(2,1)}, bf16[512,512]{1,0:T(8,128)(2,1)}, f32[128,512]{1,0:T(8,128)}) custom-call(bf16[512,512]{1,0:T(8,128)(2,1)} %get-tuple-element.195.refs_0_, bf16[512,1536]{1,0:T(8,128)(2,1)} %get-tuple-element.196.refs_1_, bf16[512,512]{1,0:T(8,128)(2,1)} %get-tuple-element.197.refs_2_, ...), custom_call_target="tpu_custom_call" | custom-call | flops 1152999936 | tf_op jit(solution)/shard_map/pallas_call | solution.py:201
  287.0 2.2 copy-done.2
  289.1 4.1 %shard_map.284 = (bf16[256,512]{1,0:T(8,128)(2,1)S(1)}, bf16[256,2048]{1,0:T(8,128)(2,1)S(1)}, bf16[256,2048]{1,0:T(8,128)(2,1)S(1)}, bf16[256,512]{1,0:T(8,128)(2,1)S(1)}, f32[1,512]{1,0:T(1,128)S(1)}) custom-call(bf16[256,512]{1,0:T(8,128)(2,1)S(1)} %copy-done.15, bf16[256,512]{1,0:T(8,128)(2,1)S(1)} %copy-done.16, f32[1,512]{1,0:T(1,128)S(1)} %get-tuple-element.282.gain, ...), custom_call_target="tpu_custom_call" | custom-call | flops 23060000768 | tf_op jit(solution)/shard_map/pallas_call | solution.py:201
  293.3 3.8 shard_map.287
  298.9 3.9 shard_map.286
  302.8 5.3 %collective-permute-start.35 = (bf16[256,512]{1,0:T(8,128)(2,1)S(1)}, bf16[256,512]{1,0:T(8,128)(2,1)S(1)}, u32[]{:S(2)}, u32[]{:S(2)}) collective-permute-start(bf16[256,512]{1,0:T(8,128)(2,1)S(1)} %get-tuple-element.191), channel_id=1, source_target_pairs={{0,2},{1,3},{2,0},{3,1},{4,6},{5,7},{6,4},{7,5},{8,10},{9,11},{10,... | collective-permute-start | bytes 786440 | tf_op jit(solution)/shard_map/ppermute | solution.py:84
  308.1 3.9 shard_map.285
  316.1 6.1 %shard_map.292 = (bf16[4,512,512]{2,1,0:T(8,128)(2,1)S(1)}, bf16[4,512,512]{2,1,0:T(8,128)(2,1)S(1)}) custom-call(s32[1]{0:T(128)} %bitcast.20.dp_index.refs_14_, bf16[256,512]{1,0:T(8,128)(2,1)S(1)} %get-tuple-element.215.inputs_0_, bf16[256,512]{1,0:T(8,128)(2,1)S(1)} %get-tuple-element.216.inputs_1_, bf16[256,512]{1,0:T(8,128)(2,1)S(1)} %get-tuple-element.217.inputs_2_, ...), custom_call_target="tpu_custom_call" | custom-call | flops 9223999488 | tf_op jit(solution)/shard_map/pallas_call | solution.py:201
  322.3 2.3 collective-permute-done.35.blocks_2_
  324.6 2.9 collective-permute-done.39.parts_1_
  327.5 7.4 %collective-permute-done.40.parts_2_ = bf16[512,512]{1,0:T(8,128)(2,1)S(1)} collective-permute-done((bf16[512,512]{1,0:T(8,128)(2,1)S(1)}, bf16[512,512]{1,0:T(8,128)(2,1)S(1)}, u32[]{:S(2)}, u32[]{:S(2)}) %collective-permute-start.40) | collective-permute-done | bytes 524320 | tf_op jit(solution)/shard_map/ppermute | solution.py:1186
  339.2 3.5 all-to-all-start.2
  344.8 9.4 %all-to-all-done.2.arrived = bf16[4,16,4096]{2,1,0:T(8,128)(2,1)S(1)} async-done(((bf16[4,16,4096]{2,1,0:T(8,128)(2,1)}), bf16[4,16,4096]{2,1,0:T(8,128)(2,1)S(1)}, u32[]{:S(2)}, u32[]{:S(2)}) %all-to-all-start.2) | async-done | bytes 524320 | tf_op jit(solution)/shard_map/all_to_all | solution.py:1252
  355.8 3.7 all-to-all-start.3
  363.0 13.4 %all-to-all-done.3 = bf16[32,16,640]{2,1,0:T(8,128)(2,1)} async-done(((bf16[32,16,640]{2,1,0:T(8,128)(2,1)}), bf16[32,16,640]{2,1,0:T(8,128)(2,1)}, u32[]{:S(2)}, u32[]{:S(2)}) %all-to-all-start.3) | async-done | bytes 655392 | tf_op jit(solution)/shard_map/all_to_all | solution.py:1293
  382.5 4.7 %shard_map.289 = f32[512,512]{1,0:T(8,128)} custom-call(bf16[512,512]{1,0:T(8,128)(2,1)} %frames.5, bf16[256,512]{1,0:T(8,128)(2,1)} %copy-done.20, bf16[256,512]{1,0:T(8,128)(2,1)} %copy-done.42, bf16[256,512]{1,0:T(8,128)(2,1)} %copy-done.41, bf16[256,512]{1,0:T(8,128)(2,1)} %copy-done.40, s32[512,1]{1,0:T(8,128)} %get-tuple-element.136.refs_2_.slot_col, ...), custom_call_target="tpu_custom_call" | custom-call | flops 46120001536 | tf_op jit(solution)/shard_map/pallas_call | solution.py:201
  387.3 5.4 %collective-permute-done.45.parts_3_ = bf16[512,512]{1,0:T(8,128)(2,1)S(1)} collective-permute-done((bf16[512,512]{1,0:T(8,128)(2,1)S(1)}, bf16[512,512]{1,0:T(8,128)(2,1)S(1)}, u32[]{:S(2)}, u32[]{:S(2)}) %collective-permute-start.45) | collective-permute-done | bytes 524320 | tf_op jit(solution)/shard_map/ppermute | solution.py:1186
  (258 shorter events, 72.4 us)
Async XLA Ops:
  7.2 49.7 %all-gather.8.cloned.1.call-start = ((), (), s32[]{:S(2)}) async-start(), calls=%async_computation.7 | async-start | bytes 4718592 | tf_op jit(solution)/shard_map/all_gather | solution.py:966
  8.3 21.5 %copy-start.36 = (bf16[2,16,4]{1,2,0:T(4,128)(2,1)S(1)}, bf16[2,16,4]{1,2,0:T(4,128)(2,1)}, u32[]{:S(2)}) copy-start(bf16[2,16,4]{1,2,0:T(4,128)(2,1)} %param.22) | copy-start | bytes 772
  8.4 21.6 %copy-start.37 = (bf16[6,16]{1,0:T(8,128)(2,1)S(1)}, bf16[6,16]{1,0:T(8,128)(2,1)}, u32[]{:S(2)}) copy-start(bf16[6,16]{1,0:T(8,128)(2,1)} %param.23) | copy-start | bytes 580
  8.4 21.7 %copy-start.32 = (bf16[15,16]{1,0:T(8,128)(2,1)S(1)}, bf16[15,16]{1,0:T(8,128)(2,1)}, u32[]{:S(2)}) copy-start(bf16[15,16]{1,0:T(8,128)(2,1)} %param.27) | copy-start | bytes 1444
  8.4 21.8 %copy-start.38 = (bf16[16]{0:T(256)(128)(2,1)S(1)}, bf16[16]{0:T(256)(128)(2,1)}, u32[]{:S(2)}) copy-start(bf16[16]{0:T(256)(128)(2,1)} %param.28) | copy-start | bytes 100
  8.4 21.9 %copy-start.33 = (s32[512,1]{0,1:T(1,128)S(1)}, s32[512,1]{0,1:T(1,128)}, u32[]{:S(2)}) copy-start(s32[512,1]{0,1:T(1,128)} %param.19) | copy-start | bytes 6148
  8.4 22.7 %copy-start.34 = (s32[512,1]{0,1:T(1,128)S(1)}, s32[512,1]{0,1:T(1,128)}, u32[]{:S(2)}) copy-start(s32[512,1]{0,1:T(1,128)} %param.20) | copy-start | bytes 6148
  10.4 77.4 %all-gather.6.cloned.1.call-start = ((), (), s32[]{:S(2)}) async-start(), calls=%async_computation.5 | async-start | bytes 4128768 | tf_op jit(solution)/shard_map/all_gather | solution.py:1001
  32.1 13.1 %copy-start.31 = (s32[32,4]{0,1:T(4,128)S(1)}, s32[32,4]{0,1:T(4,128)}, u32[]{:S(2)}) copy-start(s32[32,4]{0,1:T(4,128)} %param.18) | copy-start | bytes 1540
  36.0 12.4 %all-to-all-start = ((bf16[32,16,128]{2,1,0:T(8,128)(2,1)}), bf16[32,16,128]{2,1,0:T(8,128)(2,1)S(1)}, u32[]{:S(2)}, u32[]{:S(2)}) async-start(bf16[32,16,128]{2,1,0:T(8,128)(2,1)} %broadcast_in_dim.38), calls=%async_computation | async-start | bytes 262144 | tf_op jit(solution)/shard_map/all_to_all | solution.py:72
  39.8 91.8 %all-gather.10.cloned.1.call-start = ((), (), s32[]{:S(2)}) async-start(), calls=%async_computation.8 | async-start | bytes 4718592 | tf_op jit(solution)/shard_map/all_gather | solution.py:1004
  39.8 17.1 %collective-permute-start = (bf16[256,512]{1,0:T(8,128)(2,1)}, bf16[256,512]{1,0:T(8,128)(2,1)S(1)}, u32[]{:S(2)}, u32[]{:S(2)}) collective-permute-start(bf16[256,512]{1,0:T(8,128)(2,1)} %get-tuple-element.133), channel_id=1, source_target_pairs={{0,1},{1,0},{2,3},{3,2},{4,5},{5,4},{6,7},{7,6},{8,9},{9,8},{10,11... | collective-permute-start | bytes 786440 | tf_op jit(solution)/shard_map/ppermute | solution.py:84
  41.6 20.6 %collective-permute-start.2 = (bf16[256,512]{1,0:T(8,128)(2,1)}, bf16[256,512]{1,0:T(8,128)(2,1)S(1)}, u32[]{:S(2)}, u32[]{:S(2)}) collective-permute-start(bf16[256,512]{1,0:T(8,128)(2,1)} %get-tuple-element.134), channel_id=1, source_target_pairs={{0,2},{1,3},{2,0},{3,1},{4,6},{5,7},{6,4},{7,5},{8,10},{9,11},{10,... | collective-permute-start | bytes 786440 | tf_op jit(solution)/shard_map/ppermute | solution.py:84
  44.1 23.3 %collective-permute-start.4 = (bf16[256,512]{1,0:T(8,128)(2,1)}, bf16[256,512]{1,0:T(8,128)(2,1)S(1)}, u32[]{:S(2)}, u32[]{:S(2)}) collective-permute-start(bf16[256,512]{1,0:T(8,128)(2,1)} %get-tuple-element.135), channel_id=1, source_target_pairs={{0,3},{1,2},{2,1},{3,0},{4,7},{5,6},{6,5},{7,4},{8,11},{9,10},{10,... | collective-permute-start | bytes 786440 | tf_op jit(solution)/shard_map/ppermute | solution.py:84
  45.1 337.4 %reduce-scatter.2.cloned.1.call-start = ((), (), s32[]{:S(2)}) async-start(), calls=%async_computation.6 | async-start | bytes 4718592 | tf_op jit(solution)/shard_map/reduce_scatter | solution.py:1127
  62.1 25.7 %collective-permute-start.1 = (bf16[256,512]{1,0:T(8,128)(2,1)S(1)}, bf16[256,512]{1,0:T(8,128)(2,1)S(1)}, u32[]{:S(2)}, u32[]{:S(2)}) collective-permute-start(bf16[256,512]{1,0:T(8,128)(2,1)S(1)} %shard_map.266), channel_id=1, source_target_pairs={{0,1},{1,0},{2,3},{3,2},{4,5},{5,4},{6,7},{7,6},{8,9},{9,8},{10,11... | collective-permute-start | bytes 786440 | tf_op jit(solution)/shard_map/ppermute | solution.py:84
  65.3 22.6 %collective-permute-start.3 = (bf16[256,512]{1,0:T(8,128)(2,1)S(1)}, bf16[256,512]{1,0:T(8,128)(2,1)S(1)}, u32[]{:S(2)}, u32[]{:S(2)}) collective-permute-start(bf16[256,512]{1,0:T(8,128)(2,1)S(1)} %shard_map.267), channel_id=1, source_target_pairs={{0,2},{1,3},{2,0},{3,1},{4,6},{5,7},{6,4},{7,5},{8,10},{9,11},{10,... | collective-permute-start | bytes 786440 | tf_op jit(solution)/shard_map/ppermute | solution.py:84
  70.3 17.5 %collective-permute-start.5 = (bf16[256,512]{1,0:T(8,128)(2,1)S(1)}, bf16[256,512]{1,0:T(8,128)(2,1)S(1)}, u32[]{:S(2)}, u32[]{:S(2)}) collective-permute-start(bf16[256,512]{1,0:T(8,128)(2,1)S(1)} %shard_map.268), channel_id=1, source_target_pairs={{0,3},{1,2},{2,1},{3,0},{4,7},{5,6},{6,5},{7,4},{8,11},{9,10},{10,... | collective-permute-start | bytes 786440 | tf_op jit(solution)/shard_map/ppermute | solution.py:84
  104.4 1.5 collective-permute-start.6
  106.6 4.6 %collective-permute-start.9 = (f32[8,512]{1,0:T(8,128)S(1)}, f32[8,512]{1,0:T(8,128)S(1)}, u32[]{:S(2)}, u32[]{:S(2)}) collective-permute-start(f32[8,512]{1,0:T(8,128)S(1)} %add.51), channel_id=1, source_target_pairs={{0,24},{1,25},{2,26},{3,27},{4,28},{5,29},{6,30},{7,31},{8,16},{9,... | collective-permute-start | bytes 49160 | tf_op jit(solution)/shard_map/ppermute | solution.py:34
  108.1 3.7 collective-permute-start.8
  109.5 3.7 collective-permute-start.7
  113.3 6.9 %collective-permute-start.12 = (f32[8,512]{1,0:T(8,128)S(1)}, f32[8,512]{1,0:T(8,128)S(1)}, u32[]{:S(2)}, u32[]{:S(2)}) collective-permute-start(f32[8,512]{1,0:T(8,128)S(1)} %add_add_fusion.1.terms_0_), channel_id=1, source_target_pairs={{0,3},{1,2},{2,1},{3,0},{4,7},{5,6},{6,5},{7,4},{8,11},{9,10},{10,... | collective-permute-start | bytes 49160 | tf_op jit(solution)/shard_map/ppermute | solution.py:34
  116.7 4.6 %collective-permute-start.11 = (f32[8,512]{1,0:T(8,128)S(1)}, f32[8,512]{1,0:T(8,128)S(1)}, u32[]{:S(2)}, u32[]{:S(2)}) collective-permute-start(f32[8,512]{1,0:T(8,128)S(1)} %add_add_fusion.1.terms_0_), channel_id=1, source_target_pairs={{0,2},{1,3},{2,0},{3,1},{4,6},{5,7},{6,4},{7,5},{8,10},{9,11},{10,... | collective-permute-start | bytes 49160 | tf_op jit(solution)/shard_map/ppermute | solution.py:34
  118.9 3.7 collective-permute-start.10
  127.2 11.5 %collective-permute-start.13 = (bf16[256,512]{1,0:T(8,128)(2,1)}, bf16[256,512]{1,0:T(8,128)(2,1)S(1)}, u32[]{:S(2)}, u32[]{:S(2)}) collective-permute-start(bf16[256,512]{1,0:T(8,128)(2,1)} %get-tuple-element.148), channel_id=1, source_target_pairs={{0,1},{1,0},{2,3},{3,2},{4,5},{5,4},{6,7},{7,6},{8,9},{9,8},{10,11... | collective-permute-start | bytes 786440 | tf_op jit(solution)/shard_map/ppermute | solution.py:84
  127.4 20.6 %collective-permute-start.15 = (bf16[256,512]{1,0:T(8,128)(2,1)}, bf16[256,512]{1,0:T(8,128)(2,1)S(1)}, u32[]{:S(2)}, u32[]{:S(2)}) collective-permute-start(bf16[256,512]{1,0:T(8,128)(2,1)} %get-tuple-element.149), channel_id=1, source_target_pairs={{0,2},{1,3},{2,0},{3,1},{4,6},{5,7},{6,4},{7,5},{8,10},{9,11},{10,... | collective-permute-start | bytes 786440 | tf_op jit(solution)/shard_map/ppermute | solution.py:84
  129.0 21.9 %collective-permute-start.17 = (bf16[256,512]{1,0:T(8,128)(2,1)}, bf16[256,512]{1,0:T(8,128)(2,1)S(1)}, u32[]{:S(2)}, u32[]{:S(2)}) collective-permute-start(bf16[256,512]{1,0:T(8,128)(2,1)} %get-tuple-element.150), channel_id=1, source_target_pairs={{0,3},{1,2},{2,1},{3,0},{4,7},{5,6},{6,5},{7,4},{8,11},{9,10},{10,... | collective-permute-start | bytes 786440 | tf_op jit(solution)/shard_map/ppermute | solution.py:84
  143.7 16.1 %collective-permute-start.14 = (bf16[256,512]{1,0:T(8,128)(2,1)S(1)}, bf16[256,512]{1,0:T(8,128)(2,1)S(1)}, u32[]{:S(2)}, u32[]{:S(2)}) collective-permute-start(bf16[256,512]{1,0:T(8,128)(2,1)S(1)} %shard_map.273), channel_id=1, source_target_pairs={{0,1},{1,0},{2,3},{3,2},{4,5},{5,4},{6,7},{7,6},{8,9},{9,8},{10,11... | collective-permute-start | bytes 786440 | tf_op jit(solution)/shard_map/ppermute | solution.py:84
  150.8 19.3 %collective-permute-start.16 = (bf16[256,512]{1,0:T(8,128)(2,1)S(1)}, bf16[256,512]{1,0:T(8,128)(2,1)S(1)}, u32[]{:S(2)}, u32[]{:S(2)}) collective-permute-start(bf16[256,512]{1,0:T(8,128)(2,1)S(1)} %shard_map.274), channel_id=1, source_target_pairs={{0,2},{1,3},{2,0},{3,1},{4,6},{5,7},{6,4},{7,5},{8,10},{9,11},{10,... | collective-permute-start | bytes 786440 | tf_op jit(solution)/shard_map/ppermute | solution.py:84
  153.7 16.5 %collective-permute-start.18 = (bf16[256,512]{1,0:T(8,128)(2,1)S(1)}, bf16[256,512]{1,0:T(8,128)(2,1)S(1)}, u32[]{:S(2)}, u32[]{:S(2)}) collective-permute-start(bf16[256,512]{1,0:T(8,128)(2,1)S(1)} %shard_map.275), channel_id=1, source_target_pairs={{0,3},{1,2},{2,1},{3,0},{4,7},{5,6},{6,5},{7,4},{8,11},{9,10},{10,... | collective-permute-start | bytes 786440 | tf_op jit(solution)/shard_map/ppermute | solution.py:84
  175.8 39.7 %collective-permute-start.19 = (bf16[256,512]{1,0:T(8,128)(2,1)}, bf16[256,512]{1,0:T(8,128)(2,1)S(1)}, u32[]{:S(2)}, u32[]{:S(2)}) collective-permute-start(bf16[256,512]{1,0:T(8,128)(2,1)} %get-tuple-element.157), channel_id=1, source_target_pairs={{0,1},{1,0},{2,3},{3,2},{4,5},{5,4},{6,7},{7,6},{8,9},{9,8},{10,11... | collective-permute-start | bytes 786440 | tf_op jit(solution)/shard_map/ppermute | solution.py:84
  179.9 22.3 %collective-permute-start.21 = (bf16[256,512]{1,0:T(8,128)(2,1)}, bf16[256,512]{1,0:T(8,128)(2,1)S(1)}, u32[]{:S(2)}, u32[]{:S(2)}) collective-permute-start(bf16[256,512]{1,0:T(8,128)(2,1)} %get-tuple-element.161), channel_id=1, source_target_pairs={{0,2},{1,3},{2,0},{3,1},{4,6},{5,7},{6,4},{7,5},{8,10},{9,11},{10,... | collective-permute-start | bytes 786440 | tf_op jit(solution)/shard_map/ppermute | solution.py:84
  180.7 15.3 %collective-permute-start.22 = (bf16[256,512]{1,0:T(8,128)(2,1)}, bf16[256,512]{1,0:T(8,128)(2,1)S(1)}, u32[]{:S(2)}, u32[]{:S(2)}) collective-permute-start(bf16[256,512]{1,0:T(8,128)(2,1)} %get-tuple-element.163), channel_id=1, source_target_pairs={{0,3},{1,2},{2,1},{3,0},{4,7},{5,6},{6,5},{7,4},{8,11},{9,10},{10,... | collective-permute-start | bytes 786440 | tf_op jit(solution)/shard_map/ppermute | solution.py:84
  189.6 10.6 %copy-start.9 = (bf16[256,512]{1,0:T(8,128)(2,1)}, bf16[256,512]{1,0:T(8,128)(2,1)S(1)}, u32[]{:S(2)}) copy-start(bf16[256,512]{1,0:T(8,128)(2,1)S(1)} %get-tuple-element.156.blocks_0_) | copy-start | bytes 786436
  200.1 29.3 %collective-permute-start.24 = (bf16[256,512]{1,0:T(8,128)(2,1)S(1)}, bf16[256,512]{1,0:T(8,128)(2,1)S(1)}, u32[]{:S(2)}, u32[]{:S(2)}) collective-permute-start(bf16[256,512]{1,0:T(8,128)(2,1)S(1)} %get-tuple-element.175), channel_id=1, source_target_pairs={{0,3},{1,2},{2,1},{3,0},{4,7},{5,6},{6,5},{7,4},{8,11},{9,10},{10,... | collective-permute-start | bytes 786440 | tf_op jit(solution)/shard_map/ppermute | solution.py:84
  206.2 13.4 %copy-start.12 = (bf16[256,512]{1,0:T(8,128)(2,1)S(1)}, bf16[256,512]{1,0:T(8,128)(2,1)}, u32[]{:S(2)}) copy-start(bf16[256,512]{1,0:T(8,128)(2,1)} %get-tuple-element.155.grad.grads_0_) | copy-start | bytes 786436
  206.2 23.2 %collective-permute-start.23 = (bf16[256,512]{1,0:T(8,128)(2,1)S(1)}, bf16[256,512]{1,0:T(8,128)(2,1)S(1)}, u32[]{:S(2)}, u32[]{:S(2)}) collective-permute-start(bf16[256,512]{1,0:T(8,128)(2,1)S(1)} %get-tuple-element.174), channel_id=1, source_target_pairs={{0,2},{1,3},{2,0},{3,1},{4,6},{5,7},{6,4},{7,5},{8,10},{9,11},{10,... | collective-permute-start | bytes 786440 | tf_op jit(solution)/shard_map/ppermute | solution.py:84
  219.6 9.8 %collective-permute-start.20 = (bf16[256,512]{1,0:T(8,128)(2,1)S(1)}, bf16[256,512]{1,0:T(8,128)(2,1)S(1)}, u32[]{:S(2)}, u32[]{:S(2)}) collective-permute-start(bf16[256,512]{1,0:T(8,128)(2,1)S(1)} %get-tuple-element.158), channel_id=1, source_target_pairs={{0,1},{1,0},{2,3},{3,2},{4,5},{5,4},{6,7},{7,6},{8,9},{9,8},{10,11... | collective-permute-start | bytes 786440 | tf_op jit(solution)/shard_map/ppermute | solution.py:84
  235.9 1.4 collective-permute-start.25
  238.0 4.7 %collective-permute-start.28 = (f32[8,512]{1,0:T(8,128)S(1)}, f32[8,512]{1,0:T(8,128)S(1)}, u32[]{:S(2)}, u32[]{:S(2)}) collective-permute-start(f32[8,512]{1,0:T(8,128)S(1)} %add.55), channel_id=1, source_target_pairs={{0,24},{1,25},{2,26},{3,27},{4,28},{5,29},{6,30},{7,31},{8,16},{9,... | collective-permute-start | bytes 49160 | tf_op jit(solution)/shard_map/ppermute | solution.py:34
  239.8 3.7 collective-permute-start.27
  239.8 3.7 collective-permute-start.26
  243.6 5.6 %collective-permute-start.31 = (f32[8,512]{1,0:T(8,128)S(1)}, f32[8,512]{1,0:T(8,128)S(1)}, u32[]{:S(2)}, u32[]{:S(2)}) collective-permute-start(f32[8,512]{1,0:T(8,128)S(1)} %add_add_fusion.refs_4__0_), channel_id=1, source_target_pairs={{0,3},{1,2},{2,1},{3,0},{4,7},{5,6},{6,5},{7,4},{8,11},{9,10},{10,... | collective-permute-start | bytes 49160 | tf_op jit(solution)/shard_map/ppermute | solution.py:34
  245.0 4.6 %collective-permute-start.30 = (f32[8,512]{1,0:T(8,128)S(1)}, f32[8,512]{1,0:T(8,128)S(1)}, u32[]{:S(2)}, u32[]{:S(2)}) collective-permute-start(f32[8,512]{1,0:T(8,128)S(1)} %add_add_fusion.refs_4__0_), channel_id=1, source_target_pairs={{0,2},{1,3},{2,0},{3,1},{4,6},{5,7},{6,4},{7,5},{8,10},{9,11},{10,... | collective-permute-start | bytes 49160 | tf_op jit(solution)/shard_map/ppermute | solution.py:34
  245.5 4.3 %collective-permute-start.29 = (f32[8,512]{1,0:T(8,128)S(1)}, f32[8,512]{1,0:T(8,128)S(1)}, u32[]{:S(2)}, u32[]{:S(2)}) collective-permute-start(f32[8,512]{1,0:T(8,128)S(1)} %add_add_fusion.refs_4__0_), channel_id=1, source_target_pairs={{0,1},{1,0},{2,3},{3,2},{4,5},{5,4},{6,7},{7,6},{8,9},{9,8},{10,11... | collective-permute-start | bytes 49160 | tf_op jit(solution)/shard_map/ppermute | solution.py:34
  273.1 35.0 %collective-permute-start.32 = (bf16[256,512]{1,0:T(8,128)(2,1)}, bf16[256,512]{1,0:T(8,128)(2,1)S(1)}, u32[]{:S(2)}, u32[]{:S(2)}) collective-permute-start(bf16[256,512]{1,0:T(8,128)(2,1)} %get-tuple-element.188), channel_id=1, source_target_pairs={{0,1},{1,0},{2,3},{3,2},{4,5},{5,4},{6,7},{7,6},{8,9},{9,8},{10,11... | collective-permute-start | bytes 786440 | tf_op jit(solution)/shard_map/ppermute | solution.py:84
  275.2 23.7 %collective-permute-start.34 = (bf16[256,512]{1,0:T(8,128)(2,1)}, bf16[256,512]{1,0:T(8,128)(2,1)S(1)}, u32[]{:S(2)}, u32[]{:S(2)}) collective-permute-start(bf16[256,512]{1,0:T(8,128)(2,1)} %get-tuple-element.190), channel_id=1, source_target_pairs={{0,2},{1,3},{2,0},{3,1},{4,6},{5,7},{6,4},{7,5},{8,10},{9,11},{10,... | collective-permute-start | bytes 786440 | tf_op jit(solution)/shard_map/ppermute | solution.py:84
  275.7 17.5 %collective-permute-start.36 = (bf16[256,512]{1,0:T(8,128)(2,1)}, bf16[256,512]{1,0:T(8,128)(2,1)S(1)}, u32[]{:S(2)}, u32[]{:S(2)}) collective-permute-start(bf16[256,512]{1,0:T(8,128)(2,1)} %get-tuple-element.192), channel_id=1, source_target_pairs={{0,3},{1,2},{2,1},{3,0},{4,7},{5,6},{6,5},{7,4},{8,11},{9,10},{10,... | collective-permute-start | bytes 786440 | tf_op jit(solution)/shard_map/ppermute | solution.py:84
  286.9 25.2 %collective-permute-start.38 = (bf16[4,512,512]{2,1,0:T(8,128)(2,1)}, bf16[4,512,512]{2,1,0:T(8,128)(2,1)S(1)}, u32[]{:S(2)}, u32[]{:S(2)}) collective-permute-start(bf16[4,512,512]{2,1,0:T(8,128)(2,1)} %get-tuple-element.210), channel_id=1, source_target_pairs={{0,4},{4,0},{8,12},{12,8},{16,20},{20,16},{24,28},{28,24},{1,5},{5... | collective-permute-start | bytes 6291464 | tf_op jit(solution)/shard_map/ppermute | solution.py:1186
  297.1 18.2 %collective-permute-start.37 = (bf16[256,512]{1,0:T(8,128)(2,1)S(1)}, bf16[256,512]{1,0:T(8,128)(2,1)S(1)}, u32[]{:S(2)}, u32[]{:S(2)}) collective-permute-start(bf16[256,512]{1,0:T(8,128)(2,1)S(1)} %get-tuple-element.193), channel_id=1, source_target_pairs={{0,3},{1,2},{2,1},{3,0},{4,7},{5,6},{6,5},{7,4},{8,11},{9,10},{10,... | collective-permute-start | bytes 786440 | tf_op jit(solution)/shard_map/ppermute | solution.py:84
  302.8 21.7 %collective-permute-start.35 = (bf16[256,512]{1,0:T(8,128)(2,1)S(1)}, bf16[256,512]{1,0:T(8,128)(2,1)S(1)}, u32[]{:S(2)}, u32[]{:S(2)}) collective-permute-start(bf16[256,512]{1,0:T(8,128)(2,1)S(1)} %get-tuple-element.191), channel_id=1, source_target_pairs={{0,2},{1,3},{2,0},{3,1},{4,6},{5,7},{6,4},{7,5},{8,10},{9,11},{10,... | collective-permute-start | bytes 786440 | tf_op jit(solution)/shard_map/ppermute | solution.py:84
  312.0 12.5 %collective-permute-start.33 = (bf16[256,512]{1,0:T(8,128)(2,1)S(1)}, bf16[256,512]{1,0:T(8,128)(2,1)S(1)}, u32[]{:S(2)}, u32[]{:S(2)}) collective-permute-start(bf16[256,512]{1,0:T(8,128)(2,1)S(1)} %get-tuple-element.189), channel_id=1, source_target_pairs={{0,1},{1,0},{2,3},{3,2},{4,5},{5,4},{6,7},{7,6},{8,9},{9,8},{10,11... | collective-permute-start | bytes 786440 | tf_op jit(solution)/shard_map/ppermute | solution.py:84
  312.6 14.9 %collective-permute-start.39 = (bf16[512,512]{1,0:T(8,128)(2,1)S(1)}, bf16[512,512]{1,0:T(8,128)(2,1)S(1)}, u32[]{:S(2)}, u32[]{:S(2)}) collective-permute-start(bf16[512,512]{1,0:T(8,128)(2,1)S(1)} %get-tuple-element.212), channel_id=1, source_target_pairs={{0,8},{4,12},{8,0},{12,4},{16,24},{20,28},{24,16},{28,20},{1,9},{5... | collective-permute-start | bytes 1572872 | tf_op jit(solution)/shard_map/ppermute | solution.py:1186
  313.6 21.4 %collective-permute-start.40 = (bf16[512,512]{1,0:T(8,128)(2,1)S(1)}, bf16[512,512]{1,0:T(8,128)(2,1)S(1)}, u32[]{:S(2)}, u32[]{:S(2)}) collective-permute-start(bf16[512,512]{1,0:T(8,128)(2,1)S(1)} %get-tuple-element.213), channel_id=1, source_target_pairs={{0,16},{4,20},{8,24},{12,28},{16,0},{20,4},{24,8},{28,12},{1,17},{... | collective-permute-start | bytes 1572872 | tf_op jit(solution)/shard_map/ppermute | solution.py:1186
  315.3 21.0 %collective-permute-start.41 = (bf16[512,512]{1,0:T(8,128)(2,1)S(1)}, bf16[512,512]{1,0:T(8,128)(2,1)S(1)}, u32[]{:S(2)}, u32[]{:S(2)}) collective-permute-start(bf16[512,512]{1,0:T(8,128)(2,1)S(1)} %get-tuple-element.214), channel_id=1, source_target_pairs={{0,24},{4,28},{8,16},{12,20},{16,8},{20,12},{24,0},{28,4},{1,25},{... | collective-permute-start | bytes 1572872 | tf_op jit(solution)/shard_map/ppermute | solution.py:1186
  324.5 12.0 %copy-start.41 = (bf16[256,512]{1,0:T(8,128)(2,1)}, bf16[256,512]{1,0:T(8,128)(2,1)S(1)}, u32[]{:S(2)}) copy-start(bf16[256,512]{1,0:T(8,128)(2,1)S(1)} %collective-permute-done.35.blocks_2_) | copy-start | bytes 786436
  324.5 12.0 %copy-start.42 = (bf16[256,512]{1,0:T(8,128)(2,1)}, bf16[256,512]{1,0:T(8,128)(2,1)S(1)}, u32[]{:S(2)}) copy-start(bf16[256,512]{1,0:T(8,128)(2,1)S(1)} %collective-permute-done.33.blocks_1_) | copy-start | bytes 786436
  324.5 12.4 %collective-permute-start.42 = (bf16[4,512,512]{2,1,0:T(8,128)(2,1)S(1)}, bf16[4,512,512]{2,1,0:T(8,128)(2,1)S(1)}, u32[]{:S(2)}, u32[]{:S(2)}) collective-permute-start(bf16[4,512,512]{2,1,0:T(8,128)(2,1)S(1)} %get-tuple-element.229), channel_id=1, source_target_pairs={{0,4},{4,0},{8,12},{12,8},{16,20},{20,16},{24,28},{28,24},{1,5},{5... | collective-permute-start | bytes 6291464 | tf_op jit(solution)/shard_map/ppermute | solution.py:1186
  339.2 14.9 %all-to-all-start.2 = ((bf16[4,16,4096]{2,1,0:T(8,128)(2,1)}), bf16[4,16,4096]{2,1,0:T(8,128)(2,1)S(1)}, u32[]{:S(2)}, u32[]{:S(2)}) async-start(bf16[4,16,4096]{2,1,0:T(8,128)(2,1)} %reshape.79), calls=%async_computation.3 | async-start | bytes 1048576 | tf_op jit(solution)/shard_map/all_to_all | solution.py:1252
  355.8 20.6 %all-to-all-start.3 = ((bf16[32,16,640]{2,1,0:T(8,128)(2,1)}), bf16[32,16,640]{2,1,0:T(8,128)(2,1)}, u32[]{:S(2)}, u32[]{:S(2)}) async-start(bf16[32,16,640]{2,1,0:T(8,128)(2,1)} %pad_maximum_fusion), calls=%async_computation.4 | async-start | bytes 1310720 | tf_op jit(solution)/shard_map/all_to_all | solution.py:1293
  359.5 27.8 %collective-permute-start.43 = (bf16[512,512]{1,0:T(8,128)(2,1)S(1)}, bf16[512,512]{1,0:T(8,128)(2,1)S(1)}, u32[]{:S(2)}, u32[]{:S(2)}) collective-permute-start(bf16[512,512]{1,0:T(8,128)(2,1)S(1)} %get-tuple-element.231), channel_id=1, source_target_pairs={{0,8},{4,12},{8,0},{12,4},{16,24},{20,28},{24,16},{28,20},{1,9},{5... | collective-permute-start | bytes 1572872 | tf_op jit(solution)/shard_map/ppermute | solution.py:1186
  361.3 26.0 %collective-permute-start.44 = (bf16[512,512]{1,0:T(8,128)(2,1)S(1)}, bf16[512,512]{1,0:T(8,128)(2,1)S(1)}, u32[]{:S(2)}, u32[]{:S(2)}) collective-permute-start(bf16[512,512]{1,0:T(8,128)(2,1)S(1)} %get-tuple-element.232), channel_id=1, source_target_pairs={{0,16},{4,20},{8,24},{12,28},{16,0},{20,4},{24,8},{28,12},{1,17},{... | collective-permute-start | bytes 1572872 | tf_op jit(solution)/shard_map/ppermute | solution.py:1186
  362.7 29.9 %collective-permute-start.45 = (bf16[512,512]{1,0:T(8,128)(2,1)S(1)}, bf16[512,512]{1,0:T(8,128)(2,1)S(1)}, u32[]{:S(2)}, u32[]{:S(2)}) collective-permute-start(bf16[512,512]{1,0:T(8,128)(2,1)S(1)} %get-tuple-element.233), channel_id=1, source_target_pairs={{0,24},{4,28},{8,16},{12,20},{16,8},{20,12},{24,0},{28,4},{1,25},{... | collective-permute-start | bytes 1572872 | tf_op jit(solution)/shard_map/ppermute | solution.py:1186
  (47 other events, 162.8 us)
Sparse Core Ops, SparseCore 0:
  10.5 40.8 all-gather.7
  53.3 34.5 all-gather.5
  89.7 36.7 all-gather.9
  248.2 50.6 reduce-scatter.1
